TPU v7x, 32 devices: a whole 2x2x4 slice. The times are simulated.
32 devices in a mesh: task: 2 (over core), dp: 16 (over z, y, x).
Axes of the slice: x: 2, y: 2, z: 4, core: 2. Of those that a mesh axis runs over, the one named last changes fastest.
Arguments:
- entries: bfloat16 [294912, 64], P('dp'), may hold values from -6 to 6
- lengths: int32 [16, 12288], P('dp'), may hold values from 1 to 64, 18432 in all within a row
- labels: int32 [2, 24576], P('task', 'dp'), may hold values from 0 to 1
- spec_w1: bfloat16 [2, 2, 512, 256], P('task', None, 'dp'), may hold values from -0.25 to 0.25
- spec_w2: bfloat16 [2, 2, 256, 256], P('task', None, 'dp'), may hold values from -0.375 to 0.375
- spec_gain: bfloat16 [2, 2, 256], P('task'), may hold values from 0.5 to 1.5
- spec_shift: bfloat16 [2, 2, 256], P('task'), may hold values from -0.59765625 to 0.59765625
- shared_w1: bfloat16 [2, 512, 256], P('task', 'dp'), may hold values from -0.25 to 0.25
- shared_w2: bfloat16 [2, 256, 256], P('task', 'dp'), may hold values from -0.375 to 0.375
- shared_gain: bfloat16 [2, 256], P('task'), may hold values from 0.5 to 1.5
- shared_shift: bfloat16 [2, 256], P('task'), may hold values from -0.59765625 to 0.59765625
- gate_w: bfloat16 [2, 512, 4], P('task'), may hold values from -0.25 to 0.25
- tower_w1: bfloat16 [2, 256, 128], P('task'), may hold values from -0.375 to 0.375
- tower_w2: bfloat16 [2, 128, 64], P('task'), may hold values from -0.5 to 0.5
- tower_w3: bfloat16 [2, 64], P('task'), may hold values from -0.75 to 0.75
Outputs:
- predictions: float32 [2, 24576], P('task', 'dp')
- entry_grads: bfloat16 [294912, 64], P('dp')
- spec_w1_grad: float32 [2, 2, 512, 256], P('task', None, 'dp')
- spec_w2_grad: float32 [2, 2, 256, 256], P('task', None, 'dp')
- spec_gain_grad: float32 [2, 2, 256], P('task')
- spec_shift_grad: float32 [2, 2, 256], P('task')
- shared_w1_grad: float32 [2, 512, 256], P('task', 'dp')
- shared_w2_grad: float32 [2, 256, 256], P('task', 'dp')
- shared_gain_grad: float32 [2, 256], P('task')
- shared_shift_grad: float32 [2, 256], P('task')
- gate_grad: float32 [2, 512, 4], P('task')
- tower1_grad: float32 [2, 256, 128], P('task')
- tower2_grad: float32 [2, 128, 64], P('task')
- tower3_grad: float32 [2, 64], P('task')
Inputs may be any that keep to these rules, and one draw needn't show every extreme that they name: Each index of dp: its 12288 bag lengths sum to exactly 18432, and its longest bag has exactly 64 rows.
All inputs are finite; a program needn't handle non-finite values.
Results may differ from a plain program's by a relative error of at most 0.012.
Values may be sent and summed in bfloat16 or wider, within the bound.
No kernel may reach another device: no remote copies, remote signals or barrier semaphores. Data moves between devices by JAX's collectives and lax.ppermute only.
A program may use at most 128 MiB of HBM per device.

v0:
```python
import jax
import jax.numpy as jnp
from jax import lax
from jax.sharding import PartitionSpec as P

EXPERTS = 2
GATES = 4
D = 512
HID = 256
TOWER1 = 128
TOWER2 = 64
MB = 2


EPSILON = 1e-05


def swapped(value, axis, bit):
    mask = 2**bit
    pairs = [(source, source ^ mask) for source in range(lax.axis_size(axis))]
    return lax.ppermute(value, axis, pairs)


def gelu_act(value):
    return jax.nn.gelu(value, approximate=True)


def gelu_grad(value, upstream):
    _, back_fn = jax.vjp(gelu_act, value)
    return back_fn(upstream)[0]


def contract_rows(left, right):
    return lax.dot_general(
        left, right, (((0,), (0,)), ((), ())), preferred_element_type=jnp.float32
    )


def contract_cols(left, right):
    return lax.dot_general(
        left, right, (((1,), (1,)), ((), ())), preferred_element_type=jnp.float32
    )


def expert_forward(features, first_w, second_w, gain_vec, shift_vec):
    pre_one = jnp.dot(features, first_w, preferred_element_type=jnp.float32)
    hidden_one = gelu_act(pre_one).astype(jnp.bfloat16)
    pre_two = jnp.dot(hidden_one, second_w, preferred_element_type=jnp.float32)
    act_two = gelu_act(pre_two)
    centered = act_two - jnp.mean(act_two, axis=-1, keepdims=True)
    inv_scale = lax.rsqrt(jnp.mean(centered * centered, axis=-1, keepdims=True) + EPSILON)
    normed = centered * inv_scale
    return (normed * gain_vec + shift_vec, (pre_one, hidden_one, pre_two, normed, inv_scale))


def expert_backward(upstream, kept, features, second_w, gain_vec):
    pre_one, hidden_one, pre_two, normed, inv_scale = kept
    shift_grad = jnp.sum(upstream, axis=0)
    gain_grad = jnp.sum(upstream * normed, axis=0)
    normed_grad = upstream * gain_vec
    act_grad = inv_scale * (
        normed_grad
        - jnp.mean(normed_grad, axis=-1, keepdims=True)
        - normed * jnp.mean(normed_grad * normed, axis=-1, keepdims=True)
    )
    pre_two_grad = gelu_grad(pre_two, act_grad).astype(jnp.bfloat16)
    second_grad = contract_rows(hidden_one, pre_two_grad)
    hidden_grad = contract_cols(pre_two_grad, second_w)
    pre_one_grad = gelu_grad(pre_one, hidden_grad).astype(jnp.bfloat16)
    first_grad = contract_rows(features, pre_one_grad)
    return (pre_one_grad, first_grad, second_grad, gain_grad, shift_grad)


def input_from(spec_codes, own_code, gate_code, spec_first, own_first, gate_matrix):
    total = contract_cols(gate_code, gate_matrix) + contract_cols(own_code, own_first)
    for member in range(EXPERTS):
        total = total + contract_cols(spec_codes[member], spec_first[member])
    return total


def per_device(
    entries,
    lengths,
    labels,
    spec_w1,
    spec_w2,
    spec_gain,
    spec_shift,
    shared_w1,
    shared_w2,
    shared_gain,
    shared_shift,
    gate_w,
    tower_w1,
    tower_w2,
    tower_w3,
):
    position = lax.axis_index("task")
    bag_count = lengths.shape[1]
    segment_ids = jnp.repeat(
        jnp.arange(bag_count, dtype=jnp.int32), lengths[0], total_repeat_length=entries.shape[0]
    )
    bag_sums = jax.ops.segment_sum(
        entries.astype(jnp.float32), segment_ids, num_segments=bag_count, indices_are_sorted=True
    )
    events = labels.shape[1]
    pooled = bag_sums.reshape(events, D)
    micro_rows = events // MB
    spec_gains = spec_gain[0].astype(jnp.float32)
    spec_shifts = spec_shift[0].astype(jnp.float32)
    own_gain = shared_gain[0].astype(jnp.float32)
    own_shift = shared_shift[0].astype(jnp.float32)
    gate_matrix = gate_w[0]
    tower_first = tower_w1[0]
    tower_second = tower_w2[0]
    tower_third = tower_w3[0]
    label_float = labels[0].astype(jnp.float32)
    big_totals = tuple(
        (
            jnp.zeros(weight.shape, jnp.float32)
            for weight in (spec_w1, spec_w2, shared_w1, shared_w2)
        )
    )
    small_totals = (
        jnp.zeros((EXPERTS, HID), jnp.float32),
        jnp.zeros((EXPERTS, HID), jnp.float32),
        jnp.zeros((HID,), jnp.float32),
        jnp.zeros((HID,), jnp.float32),
        jnp.zeros((D, GATES), jnp.float32),
        jnp.zeros((HID, TOWER1), jnp.float32),
        jnp.zeros((TOWER1, TOWER2), jnp.float32),
        jnp.zeros((TOWER2,), jnp.float32),
    )
    prediction_parts = []
    input_parts = []
    for batch_index in range(MB):
        gathered = (
            lax.all_gather(spec_w1, "dp", axis=2, tiled=True),
            lax.all_gather(spec_w2, "dp", axis=2, tiled=True),
            lax.all_gather(shared_w1, "dp", axis=1, tiled=True),
            lax.all_gather(shared_w2, "dp", axis=1, tiled=True),
        )
        spec_first = gathered[0][0]
        spec_second = gathered[1][0]
        own_first = gathered[2][0]
        own_second = gathered[3][0]
        lower = batch_index * micro_rows
        features = pooled[lower : lower + micro_rows].astype(jnp.bfloat16)
        labels_now = label_float[lower : lower + micro_rows]
        specific = [
            expert_forward(
                features,
                spec_first[member],
                spec_second[member],
                spec_gains[member],
                spec_shifts[member],
            )
            for member in range(EXPERTS)
        ]
        own_out, own_kept = expert_forward(features, own_first, own_second, own_gain, own_shift)
        own_low = own_out.astype(jnp.bfloat16)
        other_low = swapped(own_low, "task", 0)
        first_shared = jnp.where(position == 0, own_low, other_low).astype(jnp.float32)
        second_shared = jnp.where(position == 0, other_low, own_low).astype(jnp.float32)
        branches = [item[0] for item in specific] + [first_shared, second_shared]
        gate_logits = jnp.dot(features, gate_matrix, preferred_element_type=jnp.float32)
        gate_probs = jax.nn.softmax(gate_logits, axis=-1)
        mixture = gate_probs[:, 0:1] * branches[0]
        for member in range(1, GATES):
            mixture = mixture + gate_probs[:, member : member + 1] * branches[member]
        tower_in = mixture.astype(jnp.bfloat16)
        pre_three = jnp.dot(tower_in, tower_first, preferred_element_type=jnp.float32)
        act_three = gelu_act(pre_three).astype(jnp.bfloat16)
        pre_four = jnp.dot(act_three, tower_second, preferred_element_type=jnp.float32)
        act_four = gelu_act(pre_four).astype(jnp.bfloat16)
        logits = jnp.dot(act_four, tower_third, preferred_element_type=jnp.float32)
        probability = jax.nn.sigmoid(logits)
        prediction_parts.append(probability)
        logit_grad = probability - labels_now
        third_grad = jnp.dot(logit_grad, act_four.astype(jnp.float32))
        four_grad = logit_grad[:, None] * tower_third.astype(jnp.float32)[None, :]
        pre_four_grad = gelu_grad(pre_four, four_grad).astype(jnp.bfloat16)
        second_tower_grad = contract_rows(act_three, pre_four_grad)
        three_grad = contract_cols(pre_four_grad, tower_second)
        pre_three_grad = gelu_grad(pre_three, three_grad).astype(jnp.bfloat16)
        first_tower_grad = contract_rows(tower_in, pre_three_grad)
        mixture_grad = contract_cols(pre_three_grad, tower_first)
        prob_grad = jnp.stack(
            [jnp.sum(mixture_grad * branch, axis=-1) for branch in branches], axis=-1
        )
        logit_gate_grad = (
            gate_probs * (prob_grad - jnp.sum(gate_probs * prob_grad, axis=-1, keepdims=True))
        ).astype(jnp.bfloat16)
        gate_grad = contract_rows(features, logit_gate_grad)
        branch_grads = [
            gate_probs[:, member : member + 1] * mixture_grad for member in range(GATES)
        ]
        own_grad = jnp.where(position == 0, branch_grads[EXPERTS], branch_grads[EXPERTS + 1])
        sent_grad = jnp.where(position == 0, branch_grads[EXPERTS + 1], branch_grads[EXPERTS])
        received = swapped(sent_grad.astype(jnp.bfloat16), "task", 0).astype(sent_grad.dtype)
        own_back = expert_backward(own_grad + received, own_kept, features, own_second, own_gain)
        spec_backs = [
            expert_backward(
                branch_grads[member],
                specific[member][1],
                features,
                spec_second[member],
                spec_gains[member],
            )
            for member in range(EXPERTS)
        ]
        spec_codes = jnp.stack([item[0] for item in spec_backs])
        input_part = input_from(
            spec_codes, own_back[0], logit_gate_grad, spec_first, own_first, gate_matrix
        )
        input_total = lax.psum(input_part.astype(jnp.bfloat16), "task").astype(jnp.float32)
        input_parts.append(input_total)
        big_terms = (
            jnp.stack([item[1] for item in spec_backs])[None],
            jnp.stack([item[2] for item in spec_backs])[None],
            own_back[1][None],
            own_back[2][None],
        )
        scattered = (
            lax.psum_scatter(big_terms[0], "dp", scatter_dimension=2, tiled=True),
            lax.psum_scatter(big_terms[1], "dp", scatter_dimension=2, tiled=True),
            lax.psum_scatter(big_terms[2], "dp", scatter_dimension=1, tiled=True),
            lax.psum_scatter(big_terms[3], "dp", scatter_dimension=1, tiled=True),
        )
        big_totals = tuple((running + fresh for running, fresh in zip(big_totals, scattered)))
        small_terms = (
            jnp.stack([item[3] for item in spec_backs]),
            jnp.stack([item[4] for item in spec_backs]),
            own_back[3],
            own_back[4],
            gate_grad,
            first_tower_grad,
            second_tower_grad,
            third_grad,
        )
        small_totals = tuple((running + fresh for running, fresh in zip(small_totals, small_terms)))
    summed = lax.psum(
        (
            small_totals[0],
            small_totals[1],
            small_totals[2],
            small_totals[3],
            small_totals[4],
            small_totals[5],
            small_totals[6],
            small_totals[7],
        ),
        "dp",
    )
    input_all = jnp.concatenate(input_parts, axis=0).reshape(bag_count, -1)
    entry_grads = input_all[segment_ids].astype(jnp.bfloat16)
    predictions = jnp.concatenate(prediction_parts, axis=0)[None]
    return (
        predictions,
        entry_grads,
        big_totals[0],
        big_totals[1],
        summed[0][None],
        summed[1][None],
        big_totals[2],
        big_totals[3],
        summed[2][None],
        summed[3][None],
        summed[4][None],
        summed[5][None],
        summed[6][None],
        summed[7][None],
    )


def solution(mesh):
    placed = (
        P("dp", None),
        P("dp", None),
        P("task", "dp"),
        P("task", None, "dp", None),
        P("task", None, "dp", None),
        P("task", None, None),
        P("task", None, None),
        P("task", "dp", None),
        P("task", "dp", None),
        P("task", None),
        P("task", None),
        P("task", None, None),
        P("task", None, None),
        P("task", None, None),
        P("task", None),
    )
    return jax.shard_map(
        per_device,
        mesh=mesh,
        in_specs=placed,
        out_specs=(
            P("task", "dp"),
            P("dp", None),
            P("task", None, "dp", None),
            P("task", None, "dp", None),
            P("task", None, None),
            P("task", None, None),
            P("task", "dp", None),
            P("task", "dp", None),
            P("task", None),
            P("task", None),
            P("task", None, None),
            P("task", None, None),
            P("task", None, None),
            P("task", None),
        ),
        check_vma=False,
    )
```

profile of v0, /device:TPU:0, one launch (start us, length us, event | category | flops | bytes accessed | tf_op | source)
XLA Modules:
  0.0 975.5 jit_solution(16007190267330515198)
XLA Ops:
  12.2 85.2 %scatter_custom_fusion = s32[18432]{0:T(1024)S(1)} fusion(s32[12288]{0:T(1024)S(1)} %bitcast.262, s32[12288]{0:T(1024)S(1)} %broadcast.436, s32[]{:T(128)} %constant.118.clone.1), kind=kCustom, calls=%fused_computation.333 | custom fusion | flops 12288 | bytes 73732 | tf_op jit(solution)/shard_map/scatter-add | solution.py:100
  98.8 101.8 %gather_fusion = s32[18432]{0:T(1024)S(1)} fusion(s32[12288]{0:T(1024)S(1)} %iota.3, s32[18432]{0:T(1024)S(1)} %broadcast_clamp_fusion.1), kind=kCustom, calls=%fused_computation | custom fusion | bytes 221184 | tf_op jit(solution)/shard_map/jit(_take)/gather | solution.py:100
  200.8 43.1 %all_gather.19 = bf16[1,256,256]{2,1,0:T(8,128)(2,1)S(1)} all-gather(bf16[1,16,256]{2,1,0:T(8,128)(2,1)S(1)} %copy-done.57), channel_id=1, replica_groups=mesh['task'=2,'dp'=16] {'dp'}, dimensions={1}, use_global_device_ids=true | all-gather | bytes 139264 | tf_op jit(solution)/shard_map/all_gather | solution.py:141
  243.8 36.8 %all_gather.18 = bf16[1,512,256]{2,1,0:T(8,128)(2,1)S(1)} all-gather(bf16[1,32,256]{2,1,0:T(8,128)(2,1)S(1)} %copy-done.55), channel_id=1, replica_groups=mesh['task'=2,'dp'=16] {'dp'}, dimensions={1}, use_global_device_ids=true | all-gather | bytes 278528 | tf_op jit(solution)/shard_map/all_gather | solution.py:140
  280.7 5.1 copy.85
  285.8 103.1 %scatter_custom_fusion.1 = f32[12288,64]{1,0:T(8,128)} fusion(s32[18432]{0:T(1024)S(1)} %bitcast.260, f32[18432,64]{1,0:T(8,128)} %copy.85, f32[]{:T(128)} %constant.117.clone.1), kind=kCustom, calls=%fused_computation.6 | custom fusion | flops 1179648 | bytes 3146240 | tf_op jit(solution)/shard_map/scatter-add | solution.py:103
  388.9 4.9 fusion.216
  393.9 2.7 convert_element_type.177
  396.6 2.7 convert_element_type.190
  405.3 41.3 %all_gather.16 = bf16[1,2,512,256]{3,2,1,0:T(8,128)(2,1)S(1)} all-gather(bf16[1,2,32,256]{3,2,1,0:T(8,128)(2,1)S(1)} %copy-done.54), channel_id=1, replica_groups=mesh['task'=2,'dp'=16] {'dp'}, dimensions={2}, use_global_device_ids=true | all-gather | bytes 557056 | tf_op jit(solution)/shard_map/all_gather | solution.py:138
  451.8 36.9 %all_gather.17 = bf16[1,2,256,256]{3,2,1,0:T(8,128)(2,1)S(1)} all-gather(bf16[1,2,16,256]{3,2,1,0:T(8,128)(2,1)S(1)} %copy-done.56), channel_id=1, replica_groups=mesh['task'=2,'dp'=16] {'dp'}, dimensions={2}, use_global_device_ids=true | all-gather | bytes 278528 | tf_op jit(solution)/shard_map/all_gather | solution.py:139
  494.4 2.8 fusion.17
  498.0 2.8 fusion.12
  502.4 3.6 multiply_reduce_fusion.3
  506.7 3.6 multiply_reduce_fusion.5
  552.8 74.2 %all-reduce.2 = (f32[1,2,256]{2,1,0:T(2,128)}, f32[1,2,256]{2,1,0:T(2,128)}, f32[1,256]{1,0:T(1,128)}, f32[1,256]{1,0:T(1,128)}, f32[1,512,4]{1,2,0:T(4,128)}, /*index=5*/f32[1,128,64]{1,2,0:T(8,128)}, f32[1,64]{1,0:T(1,128)}) all-reduce(f32[1,2,256]{2,1,0:T(2,128)S(1)} %fusion.201, ...), channel_id=1, replica_groups=mesh['task'=2,'dp'=16] {'dp'}, use_global_device_ids=true, to_apply=%region_55.56 | all-reduce | flops 11840 | bytes 94720 | tf_op jit(solution)/shard_map/psum | solution.py:242
  627.0 2.6 maximum_convert_fusion
  629.7 3.9 reshape.382
  633.6 64.6 %gather_fusion.1 = bf16[18432,64]{1,0:T(8,128)(2,1)} fusion(bf16[12288,64]{1,0:T(8,128)(2,1)S(1)} %reshape.382, s32[18432]{0:T(1024)S(1)} %broadcast_clamp_fusion), kind=kCustom, calls=%fused_computation.1 | custom fusion | bytes 4792320 | tf_op jit(solution)/shard_map/gather | solution.py:256
  698.2 5.9 copy.138
  704.1 34.7 %reduce-scatter.11.cloned.1.call-done = f32[1,16,256]{2,1,0:T(8,128)} async-done(((f32[1,256,256]{2,1,0:T(8,128)}), f32[1,16,256]{2,1,0:T(8,128)}) %reduce-scatter.11.cloned.1.call-update) | async-done | bytes 16400 | tf_op jit(solution)/shard_map/reduce_scatter | solution.py:228
  738.8 75.6 %reduce-scatter.7.cloned.1.call-done = f32[1,2,16,256]{3,2,1,0:T(8,128)} async-done(((f32[1,2,256,256]{3,2,1,0:T(8,128)}), f32[1,2,16,256]{3,2,1,0:T(8,128)}) %reduce-scatter.7.cloned.1.call-update) | async-done | bytes 32784 | tf_op jit(solution)/shard_map/reduce_scatter | solution.py:226
  814.4 75.7 %reduce-scatter.9.cloned.1.call-done = f32[1,32,256]{2,1,0:T(8,128)} async-done(((f32[1,512,256]{2,1,0:T(8,128)}), f32[1,32,256]{2,1,0:T(8,128)}) %reduce-scatter.9.cloned.1.call-update) | async-done | bytes 32784 | tf_op jit(solution)/shard_map/reduce_scatter | solution.py:227
  890.0 76.9 %reduce-scatter.5.cloned.1.call-done = f32[1,2,32,256]{3,2,1,0:T(8,128)} async-done(((f32[1,2,512,256]{3,2,1,0:T(8,128)}), f32[1,2,32,256]{3,2,1,0:T(8,128)}) %reduce-scatter.5.cloned.1.call-update) | async-done | bytes 65552 | tf_op jit(solution)/shard_map/reduce_scatter | solution.py:225
  (307 shorter events, 69.3 us)
Async XLA Ops:
  7.2 490.1 %copy-start = (bf16[1,256,128]{2,1,0:T(8,128)(2,1)S(1)}, bf16[1,256,128]{2,1,0:T(8,128)(2,1)}, u32[]{:S(2)}) copy-start(bf16[1,256,128]{2,1,0:T(8,128)(2,1)} %param.29) | copy-start | bytes 196612
  7.2 619.8 %all-reduce.9.cloned.1.call-start = ((), (), s32[]{:S(2)}) async-start(), calls=%async_computation.9 | async-start | bytes 3145728 | tf_op jit(solution)/shard_map/psum | solution.py:216
  98.7 102.0 %copy-start.57 = (bf16[1,16,256]{2,1,0:T(8,128)(2,1)S(1)}, bf16[1,16,256]{2,1,0:T(8,128)(2,1)}, u32[]{:S(2)}) copy-start(bf16[1,16,256]{2,1,0:T(8,128)(2,1)} %param.25) | copy-start | bytes 24580
  98.7 145.1 %copy-start.55 = (bf16[1,32,256]{2,1,0:T(8,128)(2,1)S(1)}, bf16[1,32,256]{2,1,0:T(8,128)(2,1)}, u32[]{:S(2)}) copy-start(bf16[1,32,256]{2,1,0:T(8,128)(2,1)} %param.24) | copy-start | bytes 49156
  98.8 181.9 %copy-start.6 = (bf16[18432,64]{0,1:T(8,128)(2,1)S(1)}, bf16[18432,64]{0,1:T(8,128)(2,1)}, u32[]{:S(2)}) copy-start(bf16[18432,64]{0,1:T(8,128)(2,1)} %param.17) | copy-start | bytes 7077892
  243.8 157.5 %copy-start.47 = (bf16[1,256,256]{2,1,0:T(8,128)(2,1)}, bf16[1,256,256]{2,1,0:T(8,128)(2,1)S(1)}, u32[]{:S(2)}) copy-start(bf16[1,256,256]{2,1,0:T(8,128)(2,1)S(1)} %all_gather.19) | copy-start | bytes 393220
  404.1 93.9 %collective-permute-start = (bf16[768,256]{1,0:T(8,128)(2,1)}, bf16[768,256]{1,0:T(8,128)(2,1)}, u32[]{:S(2)}, u32[]{:S(2)}) collective-permute-start(bf16[768,256]{1,0:T(8,128)(2,1)} %get-tuple-element.135), channel_id=1, source_target_pairs={{0,16},{16,0},{1,17},{17,1},{2,18},{18,2},{3,19},{19,3},{4,20},{20... | collective-permute-start | bytes 1179656 | tf_op jit(solution)/shard_map/ppermute | solution.py:21
  404.1 90.3 %collective-permute-start.1 = (bf16[768,256]{1,0:T(8,128)(2,1)}, bf16[768,256]{1,0:T(8,128)(2,1)}, u32[]{:S(2)}, u32[]{:S(2)}) collective-permute-start(bf16[768,256]{1,0:T(8,128)(2,1)} %get-tuple-element.136), channel_id=1, source_target_pairs={{0,16},{16,0},{1,17},{17,1},{2,18},{18,2},{3,19},{19,3},{4,20},{20... | collective-permute-start | bytes 1179656 | tf_op jit(solution)/shard_map/ppermute | solution.py:21
  497.2 3.6 copy-start.4
  497.5 4.0 copy-start.28
  497.8 3.7 copy-start.63
  502.4 3.6 copy-start.46
  506.7 3.6 copy-start.44
  513.9 1.8 collective-permute-start.2
  514.0 4.4 collective-permute-start.3
  518.3 7.3 copy-start.34
  521.5 4.5 copy-start.36
  529.9 174.1 %all-reduce.7.cloned.1.call-start = ((), (), s32[]{:S(2)}) async-start(), calls=%async_computation.4 | async-start | bytes 262144 | tf_op jit(solution)/shard_map/psum | solution.py:242
  531.3 4.5 copy-start.21
  537.0 201.8 %reduce-scatter.11.cloned.1.call-start = ((), (), s32[]{:S(2)}) async-start(), calls=%async_computation.8 | async-start | bytes 278528 | tf_op jit(solution)/shard_map/reduce_scatter | solution.py:228
  541.0 273.4 %reduce-scatter.7.cloned.1.call-start = ((), (), s32[]{:S(2)}) async-start(), calls=%async_computation.6 | async-start | bytes 557056 | tf_op jit(solution)/shard_map/reduce_scatter | solution.py:226
  545.2 344.9 %reduce-scatter.9.cloned.1.call-start = ((), (), s32[]{:S(2)}) async-start(), calls=%async_computation.7 | async-start | bytes 557056 | tf_op jit(solution)/shard_map/reduce_scatter | solution.py:227
  547.2 419.7 %reduce-scatter.5.cloned.1.call-start = ((), (), s32[]{:S(2)}) async-start(), calls=%async_computation.5 | async-start | bytes 1114112 | tf_op jit(solution)/shard_map/reduce_scatter | solution.py:225
  698.2 270.3 %copy-start.1 = (bf16[1,256,128]{2,1,0:T(8,128)(2,1)S(1)}, bf16[1,256,128]{2,1,0:T(8,128)(2,1)}, u32[]{:S(2)}) copy-start(bf16[1,256,128]{2,1,0:T(8,128)(2,1)} %param.29) | copy-start | bytes 196612
  (51 other events, 85.1 us)
Sparse Core Ops, SparseCore 0:
  530.1 18.2 all-reduce.8
  555.3 105.3 all-reduce.6
  663.6 75.1 reduce-scatter.10
  741.4 72.8 reduce-scatter.6
  817.1 72.8 reduce-scatter.8
  892.7 74.1 reduce-scatter.4
where the time goes:
time: 991 us; the launch traced here: 976 us
  waiting for transfers between devices  263 us (27%)
  blocking collectives  232 us (23%)
  other arithmetic  215 us (22%)
  local copies, waits for them, and re-layouts  200 us (20%)
  matrix products  47.5 us (5%)
  between operations  15.8 us (2%)
    scatter-add x1, other arithmetic, per_device(): jax.ops.segment_sum(entries.astype(jnp.float32), segment_ids, num_segment...  103 us
    gather x1, local copies, waits for them, and re-layouts, per_device(): jnp.repeat(jnp.arange(bag_count, dtype=jnp.int32), lengths[0], total_repe...  102 us
    scatter-add x1, other arithmetic, per_device(): jnp.repeat(jnp.arange(bag_count, dtype=jnp.int32), lengths[0], total_repe...  85.2 us
    reduce_scatter x1, waiting for transfers between devices, per_device(): lax.psum_scatter(big_terms[0], 'dp', scatter_dimension=2, tiled=True)  76.9 us
    reduce_scatter x1, waiting for transfers between devices, per_device(): lax.psum_scatter(big_terms[2], 'dp', scatter_dimension=1, tiled=True)  75.7 us
    reduce_scatter x1, waiting for transfers between devices, per_device(): lax.psum_scatter(big_terms[1], 'dp', scatter_dimension=2, tiled=True)  75.6 us
    psum x1, blocking collectives, per_device(): lax.psum((small_totals[0], small_totals[1], small_totals[2], small_totals...  74.2 us
    gather x1, local copies, waits for them, and re-layouts, per_device(): entry_grads = input_all[segment_ids].astype(jnp.bfloat16)  64.6 us
  transfers between devices with their start and end apart: 10, of which 5 were waited for; matrix products, arithmetic and copies ran while one was open for 12% of the time, Pallas kernels for 0%

commit v1 on v0

v1 whole, which is shorter than its diff:
```python
import functools

import jax
import jax.numpy as jnp
from jax import lax
from jax.experimental import pallas as pl
from jax.experimental.pallas import tpu as pltpu
from jax.sharding import PartitionSpec as P

EXPERTS = 2
GATES = 4
D = 512
HID = 256
TOWER1 = 128
TOWER2 = 64
EMB = 64
FEATS = 8
LANES = 128
BAGS = 128
EVB = BAGS // FEATS
ROWS = 128
EPSILON = 1e-05
K0 = 0.7978845608028654
K1 = K0 * 0.044715
SLOTS = 3
BF = jnp.bfloat16
F32 = jnp.float32
VMEM_BYTES = 56 * 1024 * 1024

GATE_AT = 0
T1_AT = GATE_AT + D
T2_AT = T1_AT + HID
MISC_AT = T2_AT + TOWER1
LABEL_AT = MISC_AT + 16
GT1_AT = 0
GT2_AT = HID
GG_AT = GT2_AT + TOWER1 // 2
GM_AT = GG_AT + 32
G_ROWS = GM_AT + 16


def nn(left, right):
    return jnp.dot(left, right, preferred_element_type=F32)


def nt(left, right):
    return lax.dot_general(left, right, (((1,), (1,)), ((), ())), preferred_element_type=F32)


def tn(left, right):
    return lax.dot_general(left, right, (((0,), (0,)), ((), ())), preferred_element_type=F32)


def params(**kwargs):
    return pltpu.CompilerParams(vmem_limit_bytes=VMEM_BYTES, **kwargs)


def cost(flops, moved):
    return pl.CostEstimate(flops=int(flops), bytes_accessed=int(moved), transcendentals=0)


VSPEC = pl.BlockSpec(memory_space=pltpu.VMEM)
SSPEC = pl.BlockSpec(memory_space=pltpu.SMEM)


def one_hot(starts, ends, base):
    row = lax.broadcasted_iota(jnp.int32, (ROWS, 2 * BAGS), 0)
    inside = (row >= starts - base) & (row < ends - base)
    return jnp.where(inside, 1.0, 0.0).astype(BF)


def window(ref, block):
    first = ref[pl.ds(block, 1), :]
    second = ref[pl.ds(block + 1, 1), :]
    return jnp.concatenate([first, second], axis=1)


def pool_kernel(blocks, half_blocks, chunks, first_ref, begin_ref, pos_ref, len_ref, ent_ref, x_ref, st_ref, en_ref, acc_ref):
    position = pos_ref[0]
    k = lax.broadcasted_iota(jnp.int32, (BAGS, BAGS), 0)
    j = lax.broadcasted_iota(jnp.int32, (BAGS, BAGS), 1)
    natural = (j % EVB) * FEATS + j // EVB
    before = jnp.where(k < natural, 1.0, 0.0).astype(BF)
    same = jnp.where(k == natural, 1.0, 0.0).astype(BF)
    lens_f = len_ref[...].astype(F32)
    lens = lens_f.astype(BF)
    in_block = nn(lens, before)
    own = nn(lens, same)
    sums = jnp.sum(lens_f, axis=1, keepdims=True)
    high = jnp.floor(sums * (1.0 / 128.0))
    low = sums - high * 128.0
    bi = lax.broadcasted_iota(jnp.int32, (blocks, blocks), 0)
    bj = lax.broadcasted_iota(jnp.int32, (blocks, blocks), 1)
    lower = jnp.where(bj < bi, 1.0, 0.0).astype(BF)
    offset = 128.0 * nn(lower, jnp.broadcast_to(high, (blocks, BAGS)).astype(BF)) + nn(
        lower, jnp.broadcast_to(low, (blocks, BAGS)).astype(BF)
    )
    starts = offset + in_block
    st_ref[pl.ds(0, blocks), :] = starts.astype(jnp.int32)
    en_ref[pl.ds(0, blocks), :] = (starts + own).astype(jnp.int32)
    past = jnp.full((8, BAGS), chunks * ROWS, jnp.int32)
    st_ref[pl.ds(blocks, 8), :] = past
    en_ref[pl.ds(blocks, 8), :] = past

    base_block = position * half_blocks

    def clear(i, carry):
        at = pl.multiple_of((base_block + i) * BAGS, BAGS)
        acc_ref[pl.ds(at, BAGS), :] = jnp.zeros((BAGS, EMB), F32)
        return carry

    lax.fori_loop(0, half_blocks, clear, 0, unroll=4)

    low_chunk = begin_ref[base_block] // ROWS
    high_chunk = (begin_ref[base_block + half_blocks] + ROWS - 1) // ROWS
    step = 4

    def chunk(i, carry):
        for u in range(step):
            c = low_chunk + i * step + u
            inside = jnp.minimum(c, chunks - 1)
            block = first_ref[inside]
            at = pl.multiple_of(inside * ROWS, ROWS)
            picked = one_hot(window(st_ref, block), window(en_ref, block), c * ROWS)
            part = tn(picked, ent_ref[pl.ds(at, ROWS), :])
            to = pl.multiple_of(block * BAGS, BAGS)
            acc_ref[pl.ds(to, 2 * BAGS), :] += part
        return carry

    lax.fori_loop(0, (high_chunk - low_chunk + step - 1) // step, chunk, 0)

    def place(i, carry):
        at = pl.multiple_of((base_block + i) * BAGS, BAGS)
        to = pl.multiple_of(i * EVB, EVB)
        block = acc_ref[pl.ds(at, BAGS), :]
        for pair in range(FEATS // 2):
            left = block[2 * pair * EVB : (2 * pair + 1) * EVB]
            right = block[(2 * pair + 1) * EVB : (2 * pair + 2) * EVB]
            x_ref[pl.ds(to, EVB), pair * 2 * EMB : (pair + 1) * 2 * EMB] = jnp.concatenate(
                [left, right], axis=1
            ).astype(BF)
        return carry

    lax.fori_loop(0, half_blocks, place, 0, unroll=4)


def pool(first, begin, position, lengths, entries):
    blocks = lengths.shape[0]
    half_blocks = blocks // 2
    chunks = entries.shape[0] // ROWS
    return pl.pallas_call(
        functools.partial(pool_kernel, blocks, half_blocks, chunks),
        out_shape=(
            jax.ShapeDtypeStruct((half_blocks * EVB, D), BF),
            jax.ShapeDtypeStruct((blocks + 8, BAGS), jnp.int32),
            jax.ShapeDtypeStruct((blocks + 8, BAGS), jnp.int32),
        ),
        in_specs=[SSPEC, SSPEC, SSPEC, VSPEC, VSPEC],
        out_specs=(VSPEC, VSPEC, VSPEC),
        scratch_shapes=[pltpu.VMEM(((blocks + 1) * BAGS, EMB), F32)],
        compiler_params=params(),
        cost_estimate=cost(2e9, 5e6),
    )(first, begin, position, lengths, entries)


def expand_kernel(half_blocks, group, first_ref, pos_ref, st_ref, en_ref, own_ref, other_ref, out_ref, rows_ref):
    position = pos_ref[0]
    step = pl.program_id(0)

    @pl.when(step == 0)
    def _():
        for source, half in ((own_ref, position), (other_ref, 1 - position)):

            def place(i, carry):
                at = pl.multiple_of(i * EVB, EVB)
                to = pl.multiple_of((half * half_blocks + i) * BAGS, BAGS)
                for pair in range(FEATS // 2):
                    tile = source[pl.ds(at, EVB), pair * 2 * EMB : (pair + 1) * 2 * EMB]
                    rows_ref[pl.ds(to + 2 * pair * EVB, EVB), :] = tile[:, :EMB]
                    rows_ref[pl.ds(to + (2 * pair + 1) * EVB, EVB), :] = tile[:, EMB:]
                return carry

            lax.fori_loop(0, half_blocks, place, 0, unroll=4)
        rows_ref[pl.ds(2 * half_blocks * BAGS, BAGS), :] = jnp.zeros((BAGS, EMB), BF)

    for u in range(group):
        c = step * group + u
        block = first_ref[c]
        picked = one_hot(window(st_ref, block), window(en_ref, block), c * ROWS)
        at = pl.multiple_of(block * BAGS, BAGS)
        out_ref[u * ROWS : (u + 1) * ROWS, :] = nn(picked, rows_ref[pl.ds(at, 2 * BAGS), :]).astype(BF)


def expand(first, position, starts, ends, own, other, rows):
    blocks = starts.shape[0] - 8
    chunks = rows // ROWS
    group = 8
    while chunks % group:
        group //= 2
    return pl.pallas_call(
        functools.partial(expand_kernel, blocks // 2, group),
        grid=(chunks // group,),
        out_shape=jax.ShapeDtypeStruct((rows, EMB), BF),
        in_specs=[SSPEC, SSPEC, VSPEC, VSPEC, VSPEC, VSPEC],
        out_specs=pl.BlockSpec((group * ROWS, EMB), lambda i: (i, 0)),
        scratch_shapes=[pltpu.VMEM(((blocks + 1) * BAGS, EMB), BF)],
        compiler_params=params(dimension_semantics=("arbitrary",)),
        cost_estimate=cost(4e9, 6e6),
    )(first, position, starts, ends, own, other)


def gelu_both(v):
    square = v * v
    half = 0.5 * jnp.tanh(v * (K1 * square + K0)) + 0.5
    act = v * half
    slope = half + act * (1.0 - half) * (6.0 * K1 * square + 2.0 * K0)
    return act, slope


def row_mean(value):
    return jnp.mean(value, axis=-1, keepdims=True)


def row_sum(value):
    return jnp.sum(value, axis=-1, keepdims=True)


def col_sum(value):
    return jnp.sum(value, axis=0, keepdims=True)


def wide(ref, row):
    return jnp.concatenate([ref[row : row + 1, :], ref[row + 1 : row + 2, :]], axis=1)


def main_kernel(
    events,
    size,
    pos_ref,
    x_ref,
    own1_ref,
    own2_ref,
    oth1_ref,
    oth2_ref,
    own_ref,
    oth_ref,
    pred_ref,
    dx_ref,
    g1own_ref,
    g2own_ref,
    g1oth_ref,
    g2oth_ref,
    sown_ref,
    soth_ref,
    h_ref,
    e_ref,
    f_ref,
    n_ref,
    y_ref,
    s1_ref,
    s2_ref,
    q_ref,
    u1_ref,
    e2_ref,
    e1_ref,
    dl_ref,
    acc_ref,
    acc3_ref,
):
    position = pos_ref[0]
    first = (own1_ref, oth1_ref)
    second = (own2_ref, oth2_ref)
    packs = (own_ref, oth_ref)
    misc = [ref[MISC_AT : MISC_AT + 16, :].astype(F32) for ref in packs]
    gains = [[wide(misc[t], 2 * s) for s in range(SLOTS)] for t in range(2)]
    shifts = [[wide(misc[t], 2 * SLOTS + 2 * s) for s in range(SLOTS)] for t in range(2)]
    thirds = [misc[t][12:13, :] for t in range(2)]
    lane = lax.broadcasted_iota(jnp.int32, (size, LANES), 1)
    eye = (
        lax.broadcasted_iota(jnp.int32, (LANES, LANES), 0)
        == lax.broadcasted_iota(jnp.int32, (LANES, LANES), 1)
    ).astype(F32)
    acc_ref[...] = jnp.zeros_like(acc_ref)
    acc3_ref[...] = jnp.zeros_like(acc3_ref)
    tiles = size // LANES
    half_tiles = events // LANES

    def block(i, carry):
        at = pl.multiple_of(i * size, size)
        here = pl.ds(at, size)
        x = x_ref[here, :]
        for t in range(2):
            for s in range(SLOTS):
                m = t * SLOTS + s
                act, slope = gelu_both(nn(x, first[t][s]))
                s1_ref[m] = slope
                hidden = act.astype(BF)
                h_ref[m, here, :] = hidden
                act, slope = gelu_both(nn(hidden, second[t][s]))
                centred = act - row_mean(act)
                scale = lax.rsqrt(row_mean(centred * centred) + EPSILON)
                normed = centred * scale
                n_ref[m] = normed
                s2_ref[m] = slope * scale
                out = normed * gains[t][s] + shifts[t][s]
                if s == SLOTS - 1:
                    out = out.astype(BF).astype(F32)
                y_ref[m] = out
        mix_grads, probs = [], []
        dx = jnp.zeros((size, D), F32)
        for t in range(2):
            order = (t * SLOTS, t * SLOTS + 1, t * SLOTS + 2, (1 - t) * SLOTS + 2)
            pack = packs[t]
            gate = pack[GATE_AT : GATE_AT + D, :]
            t1 = pack[T1_AT : T1_AT + HID, :]
            t2 = pack[T2_AT : T2_AT + TOWER1, :]
            logits = jnp.where(lane < GATES, nn(x, gate), -1e30)
            raised = jnp.exp(logits - jnp.max(logits, axis=-1, keepdims=True))
            prob = raised / row_sum(raised)
            cols = [prob[:, k : k + 1] for k in range(GATES)]
            mixture = cols[0] * y_ref[order[0]]
            for k in range(1, GATES):
                mixture = mixture + cols[k] * y_ref[order[k]]
            q = mixture.astype(BF)
            q_ref[t, here, :] = q
            act, slope3 = gelu_both(nn(q, t1))
            u1 = act.astype(BF)
            u1_ref[t, here, :] = u1
            act, slope4 = gelu_both(nn(u1, t2))
            u2 = act.astype(BF).astype(F32)
            logit = row_sum(u2 * thirds[t])
            prediction = 1.0 / (1.0 + jnp.exp(-logit))
            label_cols = []
            for b in range(tiles):
                row = pack[pl.ds(LABEL_AT, 16), :].astype(F32)
                wanted = position * half_tiles + i * tiles + b
                pick = lax.broadcasted_iota(jnp.int32, (16, LANES), 0) == wanted
                line = col_sum(jnp.where(pick, row, 0.0))
                label_cols.append(row_sum(eye * line))
                part = prediction[b * LANES : (b + 1) * LANES]
                pred_ref[t, pl.ds(i * tiles + b, 1), :] = col_sum(eye * part)
            label = jnp.concatenate(label_cols, axis=0)
            d_logit = prediction - label
            acc3_ref[t : t + 1, :] += col_sum(d_logit * u2)
            e2 = (slope4 * (d_logit * thirds[t])).astype(BF)
            e2_ref[t, here, :] = e2
            e1 = (slope3 * nt(e2, t2)).astype(BF)
            e1_ref[t, here, :] = e1
            d_mix = nt(e1, t1)
            d_prob = [row_sum(d_mix * y_ref[order[k]]) for k in range(GATES)]
            weighted = cols[0] * d_prob[0]
            for k in range(1, GATES):
                weighted = weighted + cols[k] * d_prob[k]
            d_gate = jnp.zeros((size, LANES), F32)
            for k in range(GATES):
                d_gate = jnp.where(lane == k, cols[k] * (d_prob[k] - weighted), d_gate)
            d_gate = d_gate.astype(BF)
            dl_ref[t, here, :] = d_gate
            dx = dx + nt(d_gate, gate)
            mix_grads.append(d_mix)
            probs.append(cols)
        for t in range(2):
            for s in range(SLOTS):
                m = t * SLOTS + s
                up = probs[t][s] * mix_grads[t]
                if s == SLOTS - 1:
                    up = up + probs[1 - t][SLOTS] * mix_grads[1 - t]
                normed = n_ref[m]
                up_normed = up * normed
                acc_ref[m : m + 1, :] += col_sum(up_normed)
                acc_ref[8 + m : 9 + m, :] += col_sum(up)
                d_normed = up * gains[t][s]
                mean_one = row_mean(d_normed)
                mean_two = row_mean(up_normed * gains[t][s])
                e = (s2_ref[m] * (d_normed - mean_one - normed * mean_two)).astype(BF)
                e_ref[m, here, :] = e
                f = (s1_ref[m] * nt(e, second[t][s])).astype(BF)
                f_ref[m, here, :] = f
                dx = dx + nt(f, first[t][s])
        dx_ref[here, :] = dx.astype(BF)
        return carry

    lax.fori_loop(0, events // size, block, 0)

    x = x_ref[...]
    for t, (g1_ref, g2_ref, small_ref) in enumerate(
        ((g1own_ref, g2own_ref, sown_ref), (g1oth_ref, g2oth_ref, soth_ref))
    ):
        for s in range(SLOTS):
            m = t * SLOTS + s
            g2_ref[s] = tn(h_ref[m], e_ref[m]).astype(BF)
            g1_ref[s] = tn(x, f_ref[m]).astype(BF)
        small_ref[GT1_AT : GT1_AT + HID, :] = tn(q_ref[t], e1_ref[t]).astype(BF)
        grad2 = tn(u1_ref[t], e2_ref[t])
        half = TOWER1 // 2
        lanes = lax.broadcasted_iota(jnp.int32, (half, LANES), 1)
        small_ref[GT2_AT : GT2_AT + half, :] = jnp.where(
            lanes < TOWER2, grad2[:half], pltpu.roll(grad2[half:], TOWER2, 1)
        ).astype(BF)
        gate_grad = tn(dl_ref[t], x)[:8]
        for k in range(D // LANES):
            small_ref[GG_AT + 8 * k : GG_AT + 8 * (k + 1), :] = gate_grad[
                :, k * LANES : (k + 1) * LANES
            ].astype(BF)
        lines = []
        for kind in range(2):
            for s in range(SLOTS):
                m = 8 * kind + t * SLOTS + s
                for part in range(2):
                    lines.append(acc_ref[m : m + 1, part * LANES : (part + 1) * LANES])
        lines.append(acc3_ref[t : t + 1, :])
        lines.append(jnp.zeros((3, LANES), F32))
        small_ref[GM_AT : GM_AT + 16, :] = jnp.concatenate(lines, axis=0).astype(BF)


def layer(position, x, own1, own2, oth1, oth2, own_pack, oth_pack):
    events = x.shape[0]
    size = 128
    big = 2 * SLOTS
    grads1 = jax.ShapeDtypeStruct((SLOTS, D, HID), BF)
    grads2 = jax.ShapeDtypeStruct((SLOTS, HID, HID), BF)
    small = jax.ShapeDtypeStruct((G_ROWS, LANES), BF)
    return pl.pallas_call(
        functools.partial(main_kernel, events, size),
        out_shape=(
            jax.ShapeDtypeStruct((2, events // LANES, LANES), F32),
            jax.ShapeDtypeStruct((events, D), BF),
            grads1,
            grads2,
            grads1,
            grads2,
            small,
            small,
        ),
        in_specs=[SSPEC] + [VSPEC] * 7,
        out_specs=(VSPEC,) * 8,
        scratch_shapes=[
            pltpu.VMEM((big, events, HID), BF),
            pltpu.VMEM((big, events, HID), BF),
            pltpu.VMEM((big, events, HID), BF),
            pltpu.VMEM((big, size, HID), F32),
            pltpu.VMEM((big, size, HID), F32),
            pltpu.VMEM((big, size, HID), F32),
            pltpu.VMEM((big, size, HID), F32),
            pltpu.VMEM((2, events, HID), BF),
            pltpu.VMEM((2, events, TOWER1), BF),
            pltpu.VMEM((2, events, LANES), BF),
            pltpu.VMEM((2, events, TOWER1), BF),
            pltpu.VMEM((2, events, LANES), BF),
            pltpu.VMEM((16, HID), F32),
            pltpu.VMEM((8, LANES), F32),
        ],
        compiler_params=params(),
        cost_estimate=cost(events * big * 196608 * 6, 10e6),
    )(position, x, own1, own2, oth1, oth2, own_pack, oth_pack)


def sibling(value):
    return lax.ppermute(value, "task", [(0, 1), (1, 0)])


def flipped(value, mask):
    pairs = [(i, i ^ mask) for i in range(lax.axis_size("dp"))]
    return lax.ppermute(value, "dp", pairs)


def crossed(value, masks):
    n = lax.axis_size("dp")
    pairs = [(t * n + i, t * n + (i ^ masks[t])) for t in range(2) for i in range(n)]
    return lax.ppermute(value, ("task", "dp"), pairs)


def assemble_kernel(rows1, rows2, at_ref, *refs):
    pieces, (w1_ref, w2_ref) = refs[:-2], refs[-2:]
    for p, piece in enumerate(pieces):
        d = at_ref[p]
        for s in range(SLOTS):
            w1_ref[s, pl.ds(pl.multiple_of(d * rows1, rows1), rows1), :] = piece[s * rows1 : (s + 1) * rows1, :]
            low = SLOTS * rows1 + s * rows2
            w2_ref[s, pl.ds(pl.multiple_of(d * rows2, rows2), rows2), :] = piece[low : low + rows2, :]


def gather_weights(pack, rows1, rows2, me, position):
    n = lax.axis_size("dp")
    if rows2 % 16 or n < 4:
        every = lax.all_gather(pack, "dp", axis=0)
        cut = SLOTS * rows1
        w1 = every[:, :cut].reshape(n, SLOTS, rows1, HID).swapaxes(0, 1).reshape(SLOTS, D, HID)
        w2 = every[:, cut:].reshape(n, SLOTS, rows2, HID).swapaxes(0, 1).reshape(SLOTS, HID, HID)
        return w1, w2
    far = [pack] + [flipped(pack, 4 * k) for k in range(1, n // 4)]
    mid = [crossed(piece, (1, 2)) for piece in far]
    near = [crossed(piece, (2, 1)) for piece in far + mid]
    pieces = far + mid + near
    one, two = 1 + position, 2 - position
    at = [me ^ (4 * k) for k in range(n // 4)]
    at = at + [d ^ one for d in at]
    at = at + [d ^ two for d in at]
    return pl.pallas_call(
        functools.partial(assemble_kernel, rows1, rows2),
        out_shape=(
            jax.ShapeDtypeStruct((SLOTS, D, HID), BF),
            jax.ShapeDtypeStruct((SLOTS, HID, HID), BF),
        ),
        in_specs=[SSPEC] + [VSPEC] * n,
        out_specs=(VSPEC, VSPEC),
        compiler_params=params(),
        cost_estimate=cost(0, 3e6),
    )(jnp.stack(at), *pieces)


def sort_kernel(n, rows1, rows2, at_ref, a1_ref, a2_ref, b1_ref, b2_ref, keep_ref, send_ref):
    quarter = n // 4
    for p in range(n):
        out = keep_ref if p < n // 2 else send_ref
        q = p % (n // 2)
        d = at_ref[p]
        one = pl.ds(pl.multiple_of(d * rows1, rows1), rows1)
        two = pl.ds(pl.multiple_of(d * rows2, rows2), rows2)
        for s in range(SLOTS):
            total = a1_ref[s, one, :].astype(F32) + b1_ref[s, one, :].astype(F32)
            out[q // quarter, q % quarter, s * rows1 : (s + 1) * rows1, :] = total.astype(BF)
            total = a2_ref[s, two, :].astype(F32) + b2_ref[s, two, :].astype(F32)
            low = SLOTS * rows1 + s * rows2
            out[q // quarter, q % quarter, low : low + rows2, :] = total.astype(BF)


def added(one, two):
    return one.astype(F32) + two.astype(F32)


def scatter_grads(own1, own2, got1, got2, small, rows1, rows2, me, position):
    n = lax.axis_size("dp")
    if rows2 % 16 or n < 4:
        g1 = lax.psum_scatter(added(own1, got1), "dp", scatter_dimension=1, tiled=True)
        g2 = lax.psum_scatter(added(own2, got2), "dp", scatter_dimension=1, tiled=True)
        return g1, g2, lax.psum(small, "dp")
    quarter = n // 4
    one, two = 1 + position, 2 - position
    at = [me ^ (4 * k) for k in range(quarter)]
    at = at + [d ^ two for d in at]
    at = at + [d ^ one for d in at]
    rows = SLOTS * (rows1 + rows2)
    half = jax.ShapeDtypeStruct((2, quarter, rows, HID), BF)
    keep, send = pl.pallas_call(
        functools.partial(sort_kernel, n, rows1, rows2),
        out_shape=(half, half),
        in_specs=[SSPEC] + [VSPEC] * 4,
        out_specs=(VSPEC, VSPEC),
        compiler_params=params(),
        cost_estimate=cost(0, 5e6),
    )(jnp.stack(at), own1, own2, got1, got2)
    small = small.astype(BF)
    small = added(small, crossed(small, (1, 2))).astype(BF)
    total = added(keep, crossed(send, (1, 2))).astype(BF)
    small = added(small, crossed(small, (2, 1))).astype(BF)
    total = added(total[0], crossed(total[1], (2, 1))).astype(BF)
    mine, tiny = total[0].astype(F32), small.astype(F32)
    for k in range(1, quarter):
        tiny = tiny + flipped(small, 4 * k).astype(F32)
        mine = mine + flipped(total[k], 4 * k).astype(F32)
    cut = SLOTS * rows1
    return mine[:cut].reshape(SLOTS, rows1, HID), mine[cut:].reshape(SLOTS, rows2, HID), tiny


def swap_shared(gate, position):
    return jnp.where(position == 0, gate, gate[:, jnp.array([0, 1, 3, 2])])


def pack_small(labels, spec_gain, spec_shift, shared_gain, shared_shift, gate_w, tower_w1, tower_w2, tower_w3, position):
    gate = jnp.pad(swap_shared(gate_w[0], position), ((0, 0), (0, LANES - GATES)))
    second = jnp.pad(tower_w2[0], ((0, 0), (0, LANES - TOWER2)))
    third = jnp.pad(tower_w3, ((0, 3), (0, LANES - TOWER2)))
    lines = [
        part.reshape(-1, LANES)
        for part in (spec_gain[0], shared_gain[0], spec_shift[0], shared_shift[0])
    ]
    label = labels[0].astype(BF).reshape(-1, LANES)
    label = jnp.pad(label, ((0, 16 - label.shape[0]), (0, 0)))
    return jnp.concatenate([gate, tower_w1[0], second, *lines, third, label], axis=0)


def per_device(
    entries,
    lengths,
    labels,
    spec_w1,
    spec_w2,
    spec_gain,
    spec_shift,
    shared_w1,
    shared_w2,
    shared_gain,
    shared_shift,
    gate_w,
    tower_w1,
    tower_w2,
    tower_w3,
):
    position = lax.axis_index("task")
    me = lax.axis_index("dp")
    pos = position.reshape(1)
    rows1, rows2 = spec_w1.shape[2], spec_w2.shape[2]
    pack = jnp.concatenate(
        [part.reshape(-1, HID) for part in (spec_w1, shared_w1, spec_w2, shared_w2)], axis=0
    )
    small = pack_small(
        labels, spec_gain, spec_shift, shared_gain, shared_shift, gate_w, tower_w1, tower_w2, tower_w3, position
    )
    other_small = sibling(small)

    blocked = lengths.reshape(-1, BAGS)
    chunks = entries.shape[0] // ROWS
    ends = jnp.cumsum(jnp.sum(blocked, axis=1))
    begin = jnp.concatenate([jnp.zeros((1,), jnp.int32), ends])
    tops = jnp.arange(chunks, dtype=jnp.int32)[:, None] * ROWS
    first = jnp.sum((ends[None, :] <= tops).astype(jnp.int32), axis=1)
    x, starts, stops = pool(first, begin, pos, blocked, entries)

    own1, own2 = gather_weights(pack, rows1, rows2, me, position)
    oth1, oth2 = sibling(own1), sibling(own2)
    pred, dx, g1, g2, h1, h2, sown, soth = layer(pos, x, own1, own2, oth1, oth2, small, other_small)

    got1, got2, got_small = sibling(h1), sibling(h2), sibling(soth)
    w1_grad, w2_grad, tiny = scatter_grads(
        g1, g2, got1, got2, added(sown, got_small), rows1, rows2, me, position
    )
    entry_grads = expand(first, pos, starts, stops, dx, sibling(dx), entries.shape[0])

    mine = pred[0].reshape(-1)
    theirs = sibling(pred[1]).reshape(-1)
    predictions = jnp.where(
        position == 0, jnp.concatenate([mine, theirs]), jnp.concatenate([theirs, mine])
    )[None]

    t1 = tiny[GT1_AT : GT1_AT + HID]
    half = tiny[GT2_AT : GT2_AT + TOWER1 // 2]
    t2 = jnp.concatenate([half[:, :TOWER2], half[:, TOWER2:]], axis=0)
    gate = tiny[GG_AT : GG_AT + 32].reshape(D // LANES, 8, LANES)[:, :GATES]
    gate = swap_shared(gate.transpose(0, 2, 1).reshape(D, GATES), position)
    misc = tiny[GM_AT : GM_AT + 12].reshape(2, SLOTS, HID)
    t3 = tiny[GM_AT + 12 : GM_AT + 13, :TOWER2]
    return (
        predictions,
        entry_grads,
        w1_grad[None, :EXPERTS],
        w2_grad[None, :EXPERTS],
        misc[0, :EXPERTS][None],
        misc[1, :EXPERTS][None],
        w1_grad[EXPERTS:],
        w2_grad[EXPERTS:],
        misc[0, EXPERTS:],
        misc[1, EXPERTS:],
        gate[None],
        t1[None],
        t2[None],
        t3,
    )


def solution(mesh):
    placed = (
        P("dp", None),
        P("dp", None),
        P("task", "dp"),
        P("task", None, "dp", None),
        P("task", None, "dp", None),
        P("task", None, None),
        P("task", None, None),
        P("task", "dp", None),
        P("task", "dp", None),
        P("task", None),
        P("task", None),
        P("task", None, None),
        P("task", None, None),
        P("task", None, None),
        P("task", None),
    )
    return jax.shard_map(
        per_device,
        mesh=mesh,
        in_specs=placed,
        out_specs=(
            P("task", "dp"),
            P("dp", None),
            P("task", None, "dp", None),
            P("task", None, "dp", None),
            P("task", None, None),
            P("task", None, None),
            P("task", "dp", None),
            P("task", "dp", None),
            P("task", None),
            P("task", None),
            P("task", None, None),
            P("task", None, None),
            P("task", None, None),
            P("task", None),
        ),
        check_vma=False,
    )
```

time: 991 us -> 162 us (0.16); the launches traced: 976 us -> 162 us
  waiting for transfers between devices: 263 us -> 25.8 us
  blocking collectives: 232 us -> 0 us
  other arithmetic: 215 us -> 9.11 us
  local copies, waits for them, and re-layouts: 200 us -> 25.5 us
  Pallas kernels: 0 us -> 65.5 us
  matrix products: 47.5 us -> 0 us
  starting transfers between devices: 1.32 us -> 34.5 us
  between operations: 15.8 us -> 1 us
    reduce_scatter x4 -> x0, waiting for transfers between devices: 263 us -> none  [the longest x1 76.9 us: per_device(): lax.psum_scatter(big_terms[0], 'dp', scatter_dimension=2, tiled=True)]
    scatter-add x2 -> x0, other arithmetic: 188 us -> none  [the longest x1 103 us: per_device(): jax.ops.segment_sum(entries.astype(jnp.float32), segment_ids, num_segment...]
    gather x2 -> x3, local copies, waits for them, and re-layouts: 166 us -> 1.3 us  [swap_shared(): return jnp.where(position == 0, gate, gate[:, jnp.array([0, 1, 3, 2])])]
    all_gather x4 -> x0, blocking collectives: 158 us -> none  [the longest x1 43.1 us: per_device(): lax.all_gather(shared_w2, 'dp', axis=1, tiled=True)]
    psum x1 -> x0, blocking collectives: 74.2 us -> none  [per_device(): lax.psum((small_totals[0], small_totals[1], small_totals[2], small_totals...]
    pallas_call x0 -> x5, Pallas kernels: none -> 65.5 us  [the longest x1 36.8 us: layer(): pl.pallas_call(functools.partial(main_kernel, events, size), out_shape=(j...]
    dot_general x58 -> x0, matrix products: 47.5 us -> none  [the longest x18 17.3 us: contract_cols(): lax.dot_general(left, right, (((1,), (1,)), ((), ())), preferred_element_...]
    ppermute x4 -> x33, starting transfers between devices: 1.08 us -> 34.5 us  [the longest x16 18 us: crossed(): return lax.ppermute(value, ('task', 'dp'), pairs)]
  transfers between devices with their start and end apart: 10 -> 33, of which waited for: 5 -> 9; matrix products, arithmetic and copies ran while one was open for 12% -> 17% of each run, Pallas kernels for 0% -> 16%
where the time goes in v1:
time: 162 us
  Pallas kernels  65.5 us (40%)
  starting transfers between devices  34.5 us (21%)
  waiting for transfers between devices  25.8 us (16%)
  local copies, waits for them, and re-layouts  25.5 us (16%)
  other arithmetic  9.11 us (6%)
    pallas_call x1, Pallas kernels, layer(): pl.pallas_call(functools.partial(main_kernel, events, size), out_shape=(j...  36.8 us
    ppermute x16, starting transfers between devices, crossed(): return lax.ppermute(value, ('task', 'dp'), pairs)  18 us
    ppermute x16, waiting for transfers between devices, crossed(): return lax.ppermute(value, ('task', 'dp'), pairs)  18 us
    unnamed x50, local copies, waits for them, and re-layouts  16 us
    ppermute x9, starting transfers between devices, flipped(): return lax.ppermute(value, 'dp', pairs)  14.6 us
    pallas_call x1, Pallas kernels, expand(): pl.pallas_call(functools.partial(expand_kernel, blocks // 2, group), grid...  13.3 us
    pallas_call x1, Pallas kernels, pool(): pl.pallas_call(functools.partial(pool_kernel, blocks, half_blocks, chunks...  10.2 us
    ppermute x9, waiting for transfers between devices, flipped(): return lax.ppermute(value, 'dp', pairs)  6.65 us
  transfers between devices with their start and end apart: 33, of which 9 were waited for; matrix products, arithmetic and copies ran while one was open for 17% of the time, Pallas kernels for 16%

profile of v1, /device:TPU:0, one launch (start us, length us, event | category | flops | bytes accessed | tf_op | source)
XLA Modules:
  0.0 161.5 jit_solution(12873357597934664522)
XLA Ops:
  1.6 3.1 %collective-permute-start = (bf16[144,256]{1,0:T(8,128)(2,1)S(1)}, bf16[144,256]{1,0:T(8,128)(2,1)S(1)}, u32[]{:S(2)}, u32[]{:S(2)}) collective-permute-start(bf16[144,256]{1,0:T(8,128)(2,1)S(1)} %pad_maximum_fusion.refs_0_), channel_id=1, source_target_pairs={{0,4},{1,5},{2,6},{3,7},{4,0},{5,1},{6,2},{7,3},{8,12},{9,13},{10,... | collective-permute-start | bytes 221192 | tf_op jit(solution)/shard_map/ppermute | solution.py:464
  4.7 2.6 %collective-permute-start.1 = (bf16[144,256]{1,0:T(8,128)(2,1)S(1)}, bf16[144,256]{1,0:T(8,128)(2,1)S(1)}, u32[]{:S(2)}, u32[]{:S(2)}) collective-permute-start(bf16[144,256]{1,0:T(8,128)(2,1)S(1)} %pad_maximum_fusion.refs_0_), channel_id=1, source_target_pairs={{0,8},{1,9},{2,10},{3,11},{4,12},{5,13},{6,14},{7,15},{8,0},{9,1},... | collective-permute-start | bytes 221192 | tf_op jit(solution)/shard_map/ppermute | solution.py:464
  7.3 1.7 %collective-permute-start.3 = (bf16[144,256]{1,0:T(8,128)(2,1)S(1)}, bf16[144,256]{1,0:T(8,128)(2,1)S(1)}, u32[]{:S(2)}, u32[]{:S(2)}) collective-permute-start(bf16[144,256]{1,0:T(8,128)(2,1)S(1)} %pad_maximum_fusion.refs_0_), channel_id=1, source_target_pairs={{0,1},{1,0},{2,3},{3,2},{4,5},{5,4},{6,7},{7,6},{8,9},{9,8},{10,11... | collective-permute-start | bytes 221192 | tf_op jit(solution)/shard_map/ppermute | solution.py:470
  9.0 1.5 collective-permute-start.7
  12.5 1.5 collective-permute-start.5
  15.1 1.5 collective-permute-start.10
  18.1 1.6 collective-permute-start.9
  20.2 1.5 collective-permute-start.12
  22.2 1.5 collective-permute-start.14
  27.3 2.5 %shard_map.273 = (bf16[3,512,256]{2,1,0:T(8,128)(2,1)}, bf16[3,256,256]{2,1,0:T(8,128)(2,1)}) custom-call(s32[16]{0:T(128)} %stack.94.at_ref, bf16[144,256]{1,0:T(8,128)(2,1)} %copy-done.3, bf16[144,256]{1,0:T(8,128)(2,1)} %copy-done.5, bf16[144,256]{1,0:T(8,128)(2,1)} %copy-done.6, bf16[144,256]{1,0:T(8,128)(2,1)} %copy-done.7, bf16[144,256]{1,0:T(8,128)(2,1)} %copy-done.8, ...), custom_call_target="tpu_custom_call" | custom-call | bytes 3000000 | tf_op jit(solution)/shard_map/pallas_call | solution.py:499
  37.0 4.1 %copy.48.ent_ref = bf16[18432,64]{1,0:T(8,128)(2,1)} copy(bf16[18432,64]{0,1:T(8,128)(2,1)S(1)} %copy-done) | data formatting | bytes 4718592 | tf_op args[0]
  41.0 10.2 %shard_map.272 = (bf16[768,512]{1,0:T(8,128)(2,1)}, s32[104,128]{1,0:T(8,128)}, s32[104,128]{1,0:T(8,128)}) custom-call(s32[144]{0:T(256)} %convert_reduce_fusion.first_ref, s32[97]{0:T(128)} %pad_add_fusion.begin_ref, s32[1]{0:T(128)} %bitcast.pos_ref, s32[96,128]{1,0:T(8,128)} %bitcast.98, bf16[18432,64]{1,0:T(8,128)(2,1)} %copy.48.ent_ref), custom_call_target="tpu_custom_call" | custom-call | flops 2000000000 | bytes 5000000 | tf_op jit(solution)/shard_map/pallas_call | solution.py:151
  52.1 36.8 %shard_map.274 = (f32[2,6,128]{2,1,0:T(8,128)}, bf16[768,512]{1,0:T(8,128)(2,1)}, bf16[3,512,256]{2,1,0:T(8,128)(2,1)}, bf16[3,256,256]{2,1,0:T(8,128)(2,1)}, bf...) custom-call(s32[1]{0:T(128)} %bitcast.pos_ref, ...), custom_call_target="tpu_custom_call" | custom-call | flops 5435817984 | bytes 10000000 | tf_op jit(solution)/shard_map/pallas_call | solution.py:423
  92.6 3.7 %collective-permute-done.28 = bf16[368,128]{1,0:T(8,128)(2,1)S(1)} collective-permute-done((bf16[368,128]{1,0:T(8,128)(2,1)S(1)}, bf16[368,128]{1,0:T(8,128)(2,1)S(1)}, u32[]{:S(2)}, u32[]{:S(2)}) %collective-permute-start.28) | collective-permute-done | bytes 94240 | tf_op jit(solution)/shard_map/ppermute | solution.py:470
  99.2 1.7 %collective-permute-done.29 = bf16[368,128]{1,0:T(8,128)(2,1)S(1)} collective-permute-done((bf16[368,128]{1,0:T(8,128)(2,1)S(1)}, bf16[368,128]{1,0:T(8,128)(2,1)S(1)}, u32[]{:S(2)}, u32[]{:S(2)}) %collective-permute-start.29) | collective-permute-done | bytes 94240 | tf_op jit(solution)/shard_map/ppermute | solution.py:470
  102.1 2.1 %collective-permute-start.31 = (bf16[368,128]{1,0:T(8,128)(2,1)S(1)}, bf16[368,128]{1,0:T(8,128)(2,1)S(1)}, u32[]{:S(2)}, u32[]{:S(2)}) collective-permute-start(bf16[368,128]{1,0:T(8,128)(2,1)S(1)} %add_convert_fusion.1), channel_id=1, source_target_pairs={{0,8},{1,9},{2,10},{3,11},{4,12},{5,13},{6,14},{7,15},{8,0},{9,1},... | collective-permute-start | bytes 282632 | tf_op jit(solution)/shard_map/ppermute | solution.py:464
  106.0 5.2 %collective-permute-done.31 = bf16[368,128]{1,0:T(8,128)(2,1)S(1)} collective-permute-done((bf16[368,128]{1,0:T(8,128)(2,1)S(1)}, bf16[368,128]{1,0:T(8,128)(2,1)S(1)}, u32[]{:S(2)}, u32[]{:S(2)}) %collective-permute-start.31) | collective-permute-done | bytes 94240 | tf_op jit(solution)/shard_map/ppermute | solution.py:464
  114.0 2.8 %shard_map.276 = (bf16[2,4,144,256]{3,2,1,0:T(8,128)(2,1)}, bf16[2,4,144,256]{3,2,1,0:T(8,128)(2,1)}) custom-call(s32[16]{0:T(128)} %stack.99.at_ref, bf16[3,512,256]{2,1,0:T(8,128)(2,1)} %get-tuple-element.36.a1_ref, bf16[3,256,256]{2,1,0:T(8,128)(2,1)} %get-tuple-element.37.a2_ref, bf16[3,512,256]{2,1,0:T(8,128)(2,1)} %copy-done.1, ...), custom_call_target="tpu_custom_call" | custom-call | bytes 5000000 | tf_op jit(solution)/shard_map/pallas_call | solution.py:545
  119.1 7.8 %collective-permute-done.22 = bf16[2,4,144,256]{3,2,1,0:T(8,128)(2,1)S(1)} collective-permute-done((bf16[2,4,144,256]{3,2,1,0:T(8,128)(2,1)}, bf16[2,4,144,256]{3,2,1,0:T(8,128)(2,1)S(1)}, u32[]{:S(2)}, u32[]{:S(2)}) %collective-permute-start.22) | collective-permute-done | bytes 589856 | tf_op jit(solution)/shard_map/ppermute | solution.py:470
  130.5 4.4 %collective-permute-done.23 = bf16[4,144,256]{2,1,0:T(8,128)(2,1)S(1)} collective-permute-done((bf16[4,144,256]{2,1,0:T(8,128)(2,1)S(1)}, bf16[4,144,256]{2,1,0:T(8,128)(2,1)S(1)}, u32[]{:S(2)}, u32[]{:S(2)}) %collective-permute-start.23) | collective-permute-done | bytes 294944 | tf_op jit(solution)/shard_map/ppermute | solution.py:470
  135.0 1.6 %collective-permute-start.24 = (bf16[144,256]{1,0:T(8,128)(2,1)S(1)}, bf16[144,256]{1,0:T(8,128)(2,1)S(1)}, u32[]{:S(2)}, u32[]{:S(2)}) collective-permute-start(bf16[144,256]{1,0:T(8,128)(2,1)S(1)} %get-tuple-element.86), channel_id=1, source_target_pairs={{0,4},{1,5},{2,6},{3,7},{4,0},{5,1},{6,2},{7,3},{8,12},{9,13},{10,... | collective-permute-start | bytes 221192 | tf_op jit(solution)/shard_map/ppermute | solution.py:464
  138.0 1.5 collective-permute-start.26
  140.4 13.3 %shard_map.275 = bf16[18432,64]{1,0:T(8,128)(2,1)} custom-call(s32[144]{0:T(256)} %convert_reduce_fusion.first_ref, s32[1]{0:T(128)} %bitcast.pos_ref, s32[104,128]{1,0:T(8,128)} %get-tuple-element.33.st_ref, s32[104,128]{1,0:T(8,128)} %get-tuple-element.34.en_ref, bf16[768,512]{1,0:T(8,128)(2,1)} %get-tuple-element.35.own_ref, bf16[768,512]{1,0:T(8,128)(2,1)} %copy-done.18), custom_call_target="tpu_custom_call" | custom-call | flops 4000000000 | bytes 6000000 | tf_op jit(solution)/shard_map/pallas_call | solution.py:200
  153.7 5.9 %copy.53 = bf16[18432,64]{0,1:T(8,128)(2,1)} copy(bf16[18432,64]{1,0:T(8,128)(2,1)} %shard_map.275) | data formatting | bytes 4718592
  (147 shorter events, 40.5 us)
Async XLA Ops:
  1.6 8.9 %collective-permute-start = (bf16[144,256]{1,0:T(8,128)(2,1)S(1)}, bf16[144,256]{1,0:T(8,128)(2,1)S(1)}, u32[]{:S(2)}, u32[]{:S(2)}) collective-permute-start(bf16[144,256]{1,0:T(8,128)(2,1)S(1)} %pad_maximum_fusion.refs_0_), channel_id=1, source_target_pairs={{0,4},{1,5},{2,6},{3,7},{4,0},{5,1},{6,2},{7,3},{8,12},{9,13},{10,... | collective-permute-start | bytes 221192 | tf_op jit(solution)/shard_map/ppermute | solution.py:464
  4.7 7.8 %collective-permute-start.1 = (bf16[144,256]{1,0:T(8,128)(2,1)S(1)}, bf16[144,256]{1,0:T(8,128)(2,1)S(1)}, u32[]{:S(2)}, u32[]{:S(2)}) collective-permute-start(bf16[144,256]{1,0:T(8,128)(2,1)S(1)} %pad_maximum_fusion.refs_0_), channel_id=1, source_target_pairs={{0,8},{1,9},{2,10},{3,11},{4,12},{5,13},{6,14},{7,15},{8,0},{9,1},... | collective-permute-start | bytes 221192 | tf_op jit(solution)/shard_map/ppermute | solution.py:464
  7.3 6.7 %collective-permute-start.2 = (bf16[144,256]{1,0:T(8,128)(2,1)S(1)}, bf16[144,256]{1,0:T(8,128)(2,1)S(1)}, u32[]{:S(2)}, u32[]{:S(2)}) collective-permute-start(bf16[144,256]{1,0:T(8,128)(2,1)S(1)} %pad_maximum_fusion.refs_0_), channel_id=1, source_target_pairs={{0,12},{1,13},{2,14},{3,15},{4,8},{5,9},{6,10},{7,11},{8,4},{9,5},... | collective-permute-start | bytes 221192 | tf_op jit(solution)/shard_map/ppermute | solution.py:464
  7.3 7.8 %collective-permute-start.3 = (bf16[144,256]{1,0:T(8,128)(2,1)S(1)}, bf16[144,256]{1,0:T(8,128)(2,1)S(1)}, u32[]{:S(2)}, u32[]{:S(2)}) collective-permute-start(bf16[144,256]{1,0:T(8,128)(2,1)S(1)} %pad_maximum_fusion.refs_0_), channel_id=1, source_target_pairs={{0,1},{1,0},{2,3},{3,2},{4,5},{5,4},{6,7},{7,6},{8,9},{9,8},{10,11... | collective-permute-start | bytes 221192 | tf_op jit(solution)/shard_map/ppermute | solution.py:470
  9.0 7.6 %collective-permute-start.7 = (bf16[144,256]{1,0:T(8,128)(2,1)S(1)}, bf16[144,256]{1,0:T(8,128)(2,1)S(1)}, u32[]{:S(2)}, u32[]{:S(2)}) collective-permute-start(bf16[144,256]{1,0:T(8,128)(2,1)S(1)} %pad_maximum_fusion.refs_0_), channel_id=1, source_target_pairs={{0,2},{1,3},{2,0},{3,1},{4,6},{5,7},{6,4},{7,5},{8,10},{9,11},{10,... | collective-permute-start | bytes 221192 | tf_op jit(solution)/shard_map/ppermute | solution.py:470
  10.6 7.5 %collective-permute-start.4 = (bf16[144,256]{1,0:T(8,128)(2,1)S(1)}, bf16[144,256]{1,0:T(8,128)(2,1)S(1)}, u32[]{:S(2)}, u32[]{:S(2)}) collective-permute-start(bf16[144,256]{1,0:T(8,128)(2,1)S(1)} %collective-permute-done.refs_1_), channel_id=1, source_target_pairs={{0,1},{1,0},{2,3},{3,2},{4,5},{5,4},{6,7},{7,6},{8,9},{9,8},{10,11... | collective-permute-start | bytes 221192 | tf_op jit(solution)/shard_map/ppermute | solution.py:470
  12.5 7.2 %collective-permute-start.5 = (bf16[144,256]{1,0:T(8,128)(2,1)S(1)}, bf16[144,256]{1,0:T(8,128)(2,1)S(1)}, u32[]{:S(2)}, u32[]{:S(2)}) collective-permute-start(bf16[144,256]{1,0:T(8,128)(2,1)S(1)} %collective-permute-done.1.refs_2_), channel_id=1, source_target_pairs={{0,1},{1,0},{2,3},{3,2},{4,5},{5,4},{6,7},{7,6},{8,9},{9,8},{10,11... | collective-permute-start | bytes 221192 | tf_op jit(solution)/shard_map/ppermute | solution.py:470
  15.1 6.6 %collective-permute-start.10 = (bf16[144,256]{1,0:T(8,128)(2,1)S(1)}, bf16[144,256]{1,0:T(8,128)(2,1)S(1)}, u32[]{:S(2)}, u32[]{:S(2)}) collective-permute-start(bf16[144,256]{1,0:T(8,128)(2,1)S(1)} %collective-permute-done.2.refs_3_), channel_id=1, source_target_pairs={{0,2},{1,3},{2,0},{3,1},{4,6},{5,7},{6,4},{7,5},{8,10},{9,11},{10,... | collective-permute-start | bytes 221192 | tf_op jit(solution)/shard_map/ppermute | solution.py:470
  18.1 8.5 %collective-permute-start.9 = (bf16[144,256]{1,0:T(8,128)(2,1)S(1)}, bf16[144,256]{1,0:T(8,128)(2,1)S(1)}, u32[]{:S(2)}, u32[]{:S(2)}) collective-permute-start(bf16[144,256]{1,0:T(8,128)(2,1)S(1)} %collective-permute-done.1.refs_2_), channel_id=1, source_target_pairs={{0,2},{1,3},{2,0},{3,1},{4,6},{5,7},{6,4},{7,5},{8,10},{9,11},{10,... | collective-permute-start | bytes 221192 | tf_op jit(solution)/shard_map/ppermute | solution.py:470
  19.7 7.0 %collective-permute-start.11 = (bf16[144,256]{1,0:T(8,128)(2,1)S(1)}, bf16[144,256]{1,0:T(8,128)(2,1)}, u32[]{:S(2)}, u32[]{:S(2)}) collective-permute-start(bf16[144,256]{1,0:T(8,128)(2,1)S(1)} %collective-permute-done.3.refs_4_), channel_id=1, source_target_pairs={{0,2},{1,3},{2,0},{3,1},{4,6},{5,7},{6,4},{7,5},{8,10},{9,11},{10,... | collective-permute-start | bytes 221192 | tf_op jit(solution)/shard_map/ppermute | solution.py:470
  20.2 6.4 %collective-permute-start.12 = (bf16[144,256]{1,0:T(8,128)(2,1)S(1)}, bf16[144,256]{1,0:T(8,128)(2,1)}, u32[]{:S(2)}, u32[]{:S(2)}) collective-permute-start(bf16[144,256]{1,0:T(8,128)(2,1)S(1)} %collective-permute-done.4.refs_5_), channel_id=1, source_target_pairs={{0,2},{1,3},{2,0},{3,1},{4,6},{5,7},{6,4},{7,5},{8,10},{9,11},{10,... | collective-permute-start | bytes 221192 | tf_op jit(solution)/shard_map/ppermute | solution.py:470
  29.7 21.5 %collective-permute-start.15 = (bf16[3,512,256]{2,1,0:T(8,128)(2,1)}, bf16[3,512,256]{2,1,0:T(8,128)(2,1)}, u32[]{:S(2)}, u32[]{:S(2)}) collective-permute-start(bf16[3,512,256]{2,1,0:T(8,128)(2,1)} %get-tuple-element.30.own1_ref), channel_id=1, source_target_pairs={{0,16},{16,0},{1,17},{17,1},{2,18},{18,2},{3,19},{19,3},{4,20},{20... | collective-permute-start | bytes 2359304 | tf_op jit(solution)/shard_map/ppermute | solution.py:459
  33.7 17.5 %collective-permute-start.17 = (bf16[928,128]{1,0:T(8,128)(2,1)S(1)}, bf16[928,128]{1,0:T(8,128)(2,1)S(1)}, u32[]{:S(2)}, u32[]{:S(2)}) collective-permute-start(bf16[928,128]{1,0:T(8,128)(2,1)S(1)} %concatenate.38.own_ref), channel_id=1, source_target_pairs={{0,16},{16,0},{1,17},{17,1},{2,18},{18,2},{3,19},{19,3},{4,20},{20... | collective-permute-start | bytes 712712 | tf_op jit(solution)/shard_map/ppermute | solution.py:459
  35.5 15.7 %collective-permute-start.16 = (bf16[3,256,256]{2,1,0:T(8,128)(2,1)}, bf16[3,256,256]{2,1,0:T(8,128)(2,1)S(1)}, u32[]{:S(2)}, u32[]{:S(2)}) collective-permute-start(bf16[3,256,256]{2,1,0:T(8,128)(2,1)} %get-tuple-element.31.own2_ref), channel_id=1, source_target_pairs={{0,16},{16,0},{1,17},{17,1},{2,18},{18,2},{3,19},{19,3},{4,20},{20... | collective-permute-start | bytes 1179656 | tf_op jit(solution)/shard_map/ppermute | solution.py:459
  98.6 14.4 %collective-permute-start.20 = (bf16[3,512,256]{2,1,0:T(8,128)(2,1)}, bf16[3,512,256]{2,1,0:T(8,128)(2,1)S(1)}, u32[]{:S(2)}, u32[]{:S(2)}) collective-permute-start(bf16[3,512,256]{2,1,0:T(8,128)(2,1)} %get-tuple-element.38), channel_id=1, source_target_pairs={{0,16},{16,0},{1,17},{17,1},{2,18},{18,2},{3,19},{19,3},{4,20},{20... | collective-permute-start | bytes 2359304 | tf_op jit(solution)/shard_map/ppermute | solution.py:459
  99.1 13.9 %collective-permute-start.21 = (bf16[3,256,256]{2,1,0:T(8,128)(2,1)}, bf16[3,256,256]{2,1,0:T(8,128)(2,1)S(1)}, u32[]{:S(2)}, u32[]{:S(2)}) collective-permute-start(bf16[3,256,256]{2,1,0:T(8,128)(2,1)} %get-tuple-element.39), channel_id=1, source_target_pairs={{0,16},{16,0},{1,17},{17,1},{2,18},{18,2},{3,19},{19,3},{4,20},{20... | collective-permute-start | bytes 1179656 | tf_op jit(solution)/shard_map/ppermute | solution.py:459
  102.1 9.1 %collective-permute-start.31 = (bf16[368,128]{1,0:T(8,128)(2,1)S(1)}, bf16[368,128]{1,0:T(8,128)(2,1)S(1)}, u32[]{:S(2)}, u32[]{:S(2)}) collective-permute-start(bf16[368,128]{1,0:T(8,128)(2,1)S(1)} %add_convert_fusion.1), channel_id=1, source_target_pairs={{0,8},{1,9},{2,10},{3,11},{4,12},{5,13},{6,14},{7,15},{8,0},{9,1},... | collective-permute-start | bytes 282632 | tf_op jit(solution)/shard_map/ppermute | solution.py:464
  104.3 7.0 %collective-permute-start.32 = (bf16[368,128]{1,0:T(8,128)(2,1)S(1)}, bf16[368,128]{1,0:T(8,128)(2,1)S(1)}, u32[]{:S(2)}, u32[]{:S(2)}) collective-permute-start(bf16[368,128]{1,0:T(8,128)(2,1)S(1)} %add_convert_fusion.1), channel_id=1, source_target_pairs={{0,12},{1,13},{2,14},{3,15},{4,8},{5,9},{6,10},{7,11},{8,4},{9,5},... | collective-permute-start | bytes 282632 | tf_op jit(solution)/shard_map/ppermute | solution.py:464
  106.0 33.4 %collective-permute-start.19 = (bf16[768,512]{1,0:T(8,128)(2,1)}, bf16[768,512]{1,0:T(8,128)(2,1)S(1)}, u32[]{:S(2)}, u32[]{:S(2)}) collective-permute-start(bf16[768,512]{1,0:T(8,128)(2,1)} %get-tuple-element.35.own_ref), channel_id=1, source_target_pairs={{0,16},{16,0},{1,17},{17,1},{2,18},{18,2},{3,19},{19,3},{4,20},{20... | collective-permute-start | bytes 2359304 | tf_op jit(solution)/shard_map/ppermute | solution.py:459
  116.8 10.1 %collective-permute-start.22 = (bf16[2,4,144,256]{3,2,1,0:T(8,128)(2,1)}, bf16[2,4,144,256]{3,2,1,0:T(8,128)(2,1)S(1)}, u32[]{:S(2)}, u32[]{:S(2)}) collective-permute-start(bf16[2,4,144,256]{3,2,1,0:T(8,128)(2,1)} %get-tuple-element.41), channel_id=1, source_target_pairs={{0,1},{1,0},{2,3},{3,2},{4,5},{5,4},{6,7},{7,6},{8,9},{9,8},{10,11... | collective-permute-start | bytes 1769480 | tf_op jit(solution)/shard_map/ppermute | solution.py:470
  128.1 6.8 %collective-permute-start.23 = (bf16[4,144,256]{2,1,0:T(8,128)(2,1)S(1)}, bf16[4,144,256]{2,1,0:T(8,128)(2,1)S(1)}, u32[]{:S(2)}, u32[]{:S(2)}) collective-permute-start(bf16[4,144,256]{2,1,0:T(8,128)(2,1)S(1)} %slice_bitcast_fusion), channel_id=1, source_target_pairs={{0,2},{1,3},{2,0},{3,1},{4,6},{5,7},{6,4},{7,5},{8,10},{9,11},{10,... | collective-permute-start | bytes 884744 | tf_op jit(solution)/shard_map/ppermute | solution.py:470
  135.0 24.5 %collective-permute-start.24 = (bf16[144,256]{1,0:T(8,128)(2,1)S(1)}, bf16[144,256]{1,0:T(8,128)(2,1)S(1)}, u32[]{:S(2)}, u32[]{:S(2)}) collective-permute-start(bf16[144,256]{1,0:T(8,128)(2,1)S(1)} %get-tuple-element.86), channel_id=1, source_target_pairs={{0,4},{1,5},{2,6},{3,7},{4,0},{5,1},{6,2},{7,3},{8,12},{9,13},{10,... | collective-permute-start | bytes 221192 | tf_op jit(solution)/shard_map/ppermute | solution.py:464
  136.7 22.9 %collective-permute-start.25 = (bf16[144,256]{1,0:T(8,128)(2,1)S(1)}, bf16[144,256]{1,0:T(8,128)(2,1)S(1)}, u32[]{:S(2)}, u32[]{:S(2)}) collective-permute-start(bf16[144,256]{1,0:T(8,128)(2,1)S(1)} %get-tuple-element.88), channel_id=1, source_target_pairs={{0,8},{1,9},{2,10},{3,11},{4,12},{5,13},{6,14},{7,15},{8,0},{9,1},... | collective-permute-start | bytes 221192 | tf_op jit(solution)/shard_map/ppermute | solution.py:464
  138.0 21.6 %collective-permute-start.26 = (bf16[144,256]{1,0:T(8,128)(2,1)S(1)}, bf16[144,256]{1,0:T(8,128)(2,1)S(1)}, u32[]{:S(2)}, u32[]{:S(2)}) collective-permute-start(bf16[144,256]{1,0:T(8,128)(2,1)S(1)} %get-tuple-element.87), channel_id=1, source_target_pairs={{0,12},{1,13},{2,14},{3,15},{4,8},{5,9},{6,10},{7,11},{8,4},{9,5},... | collective-permute-start | bytes 221192 | tf_op jit(solution)/shard_map/ppermute | solution.py:464
  (30 other events, 271.2 us)

commit v2 on v0

v2 whole, which is shorter than its diff:
```python
import functools

import jax
import jax.numpy as jnp
from jax import lax
from jax.experimental import pallas as pl
from jax.experimental.pallas import tpu as pltpu
from jax.sharding import PartitionSpec as P

EXPERTS = 2
GATES = 4
D = 512
HID = 256
TOWER1 = 128
TOWER2 = 64
EMB = 64
FEATS = 8
LANES = 128
BAGS = 128
EVB = BAGS // FEATS
ROWS = 128
EPSILON = 1e-05
K0 = 0.7978845608028654
K1 = K0 * 0.044715
SLOTS = 3
BIG = 2 * SLOTS
WIDE = BIG * HID
BF = jnp.bfloat16
F32 = jnp.float32
VMEM_BYTES = 56 * 1024 * 1024

T1_AT = 0
T2_AT = T1_AT + HID
GATE_AT = T2_AT + TOWER2
MISC_AT = GATE_AT + GATES * (D // LANES)
LABEL_AT = MISC_AT + 16
G_ROWS = LABEL_AT


def nn(left, right):
    return jnp.dot(left, right, preferred_element_type=F32)


def nt(left, right):
    return lax.dot_general(left, right, (((1,), (1,)), ((), ())), preferred_element_type=F32)


def tn(left, right):
    return lax.dot_general(left, right, (((0,), (0,)), ((), ())), preferred_element_type=F32)


def params(**kwargs):
    return pltpu.CompilerParams(vmem_limit_bytes=VMEM_BYTES, **kwargs)


def cost(flops, moved):
    return pl.CostEstimate(flops=int(flops), bytes_accessed=int(moved), transcendentals=0)


def shape(dims, kind=BF):
    return jax.ShapeDtypeStruct(dims, kind)


VSPEC = pl.BlockSpec(memory_space=pltpu.VMEM)
SSPEC = pl.BlockSpec(memory_space=pltpu.SMEM)
ASPEC = pl.BlockSpec(memory_space=pl.ANY)


def line(ref, row):
    both = ref[row : row + 1, :].astype(F32)
    return [both[:, :LANES], both[:, LANES:]]


def prep_kernel(
    blocks,
    chunks,
    pos_ref,
    len_ref,
    label_ref,
    sgain_ref,
    sshift_ref,
    ogain_ref,
    oshift_ref,
    gate_ref,
    t1_ref,
    t2_ref,
    t3_ref,
    st_ref,
    en_ref,
    meta_ref,
    small_ref,
):
    k = lax.broadcasted_iota(jnp.int32, (BAGS, BAGS), 0)
    j = lax.broadcasted_iota(jnp.int32, (BAGS, BAGS), 1)
    natural = (j % EVB) * FEATS + j // EVB
    before = jnp.where(k < natural, 1.0, 0.0).astype(BF)
    same = jnp.where(k == natural, 1.0, 0.0).astype(BF)
    lens_f = jnp.concatenate(
        [len_ref[:, b * BAGS : (b + 1) * BAGS] for b in range(blocks)], axis=0
    ).astype(F32)
    lens = lens_f.astype(BF)
    in_block = nn(lens, before)
    own = nn(lens, same)
    sums = jnp.sum(lens_f, axis=1, keepdims=True)
    high = jnp.floor(sums * (1.0 / 128.0))
    low = sums - high * 128.0
    bi = lax.broadcasted_iota(jnp.int32, (blocks, blocks), 0)
    bj = lax.broadcasted_iota(jnp.int32, (blocks, blocks), 1)
    lower = jnp.where(bj < bi, 1.0, 0.0).astype(BF)
    offset = 128.0 * nn(lower, jnp.broadcast_to(high, (blocks, BAGS)).astype(BF)) + nn(
        lower, jnp.broadcast_to(low, (blocks, BAGS)).astype(BF)
    )
    starts = offset + in_block
    st_ref[pl.ds(0, blocks), :] = starts.astype(jnp.int32)
    en_ref[pl.ds(0, blocks), :] = (starts + own).astype(jnp.int32)
    past = jnp.full((8, BAGS), chunks * ROWS, jnp.int32)
    st_ref[pl.ds(blocks, 8), :] = past
    en_ref[pl.ds(blocks, 8), :] = past
    lanes = meta_ref.shape[1]
    begins = jnp.concatenate([offset] * (lanes // BAGS), axis=1)
    row = lax.broadcasted_iota(jnp.int32, (blocks, lanes), 0)
    col = lax.broadcasted_iota(jnp.int32, (blocks, lanes), 1)
    begin = jnp.sum(jnp.where(row == col, begins, 0.0), axis=0, keepdims=True)
    spot = lax.broadcasted_iota(jnp.int32, (1, lanes), 1)
    begin = jnp.where(spot >= blocks, float(chunks * ROWS), begin)
    reached = jnp.where(begins <= (col * ROWS).astype(F32), 1.0, 0.0)
    first = jnp.sum(reached, axis=0, keepdims=True) - 1.0
    meta_ref[0:1, :] = begin.astype(jnp.int32)
    meta_ref[1:2, :] = first.astype(jnp.int32)
    small_ref[T1_AT : T1_AT + HID, :] = t1_ref[...]
    small_ref[T2_AT : T2_AT + TOWER2, :] = t2_ref[...]
    gate = gate_ref[...].astype(F32)
    turned = jnp.concatenate([gate[0:2], gate[3:4], gate[2:3]], axis=0)
    gate = jnp.where(pos_ref[0] == 0, gate, turned)
    lines = [gate[g : g + 1, p * LANES : (p + 1) * LANES] for g in range(GATES) for p in range(D // LANES)]
    lines += line(sgain_ref, 0) + line(sgain_ref, 1) + line(ogain_ref, 0)
    lines += line(sshift_ref, 0) + line(sshift_ref, 1) + line(oshift_ref, 0)
    lines += [jnp.concatenate([t3_ref[...].astype(F32)] * 2, axis=1), jnp.zeros((3, LANES), F32)]
    events = label_ref.shape[1]
    lines += [label_ref[:, p * LANES : (p + 1) * LANES].astype(F32) for p in range(events // LANES)]
    lines += [jnp.zeros((16 - events // LANES, LANES), F32)]
    small_ref[pl.ds(GATE_AT, 48), :] = jnp.concatenate(lines, axis=0).astype(BF)


def prepare(pos, lengths, labels, spec_gain, spec_shift, shared_gain, shared_shift, gate, t1, t2, t3, chunks):
    blocks = lengths.shape[1] // BAGS
    lanes = -(-max(blocks + 1, chunks) // LANES) * LANES
    return pl.pallas_call(
        functools.partial(prep_kernel, blocks, chunks),
        out_shape=(
            shape((blocks + 8, BAGS), jnp.int32),
            shape((blocks + 8, BAGS), jnp.int32),
            shape((2, lanes), jnp.int32),
            shape((LABEL_AT + 16, LANES)),
        ),
        in_specs=[SSPEC] + [VSPEC] * 10,
        out_specs=(VSPEC,) * 4,
        compiler_params=params(),
        cost_estimate=cost(1e9, 1e6),
    )(pos, lengths, labels, spec_gain, spec_shift, shared_gain, shared_shift, gate, t1, t2, t3)


def one_hot(starts, ends, base):
    row = lax.broadcasted_iota(jnp.int32, (ROWS, 2 * BAGS), 0)
    inside = (row >= starts - base) & (row < ends - base)
    return jnp.where(inside, 1.0, 0.0).astype(BF)


def window(ref, block):
    first = ref[pl.ds(block, 1), :]
    second = ref[pl.ds(block + 1, 1), :]
    return jnp.concatenate([first, second], axis=1)


def pool_kernel(skip, count, half_blocks, chunks, pos_ref, meta_ref, st_ref, en_ref, ent_ref, x_ref, acc_ref):
    base_block = pos_ref[0] * half_blocks + skip

    def clear(i, carry):
        at = pl.multiple_of((base_block + i) * BAGS, BAGS)
        acc_ref[:, pl.ds(at, BAGS)] = jnp.zeros((EMB, BAGS), F32)
        return carry

    lax.fori_loop(0, count, clear, 0, unroll=4)

    low_chunk = meta_ref[0, base_block] // ROWS
    high_chunk = (meta_ref[0, base_block + count] + ROWS - 1) // ROWS
    step = 4

    def chunk(i, carry):
        for u in range(step):
            c = low_chunk + i * step + u
            inside = jnp.minimum(c, chunks - 1)
            block = meta_ref[1, inside]
            at = pl.multiple_of(inside * ROWS, ROWS)
            picked = one_hot(window(st_ref, block), window(en_ref, block), c * ROWS)
            part = nn(ent_ref[:, pl.ds(at, ROWS)], picked)
            to = pl.multiple_of(block * BAGS, BAGS)
            acc_ref[:, pl.ds(to, 2 * BAGS)] += part
        return carry

    lax.fori_loop(0, (high_chunk - low_chunk + step - 1) // step, chunk, 0)

    def place(i, carry):
        at = pl.multiple_of((base_block + i) * BAGS, BAGS)
        to = pl.multiple_of(i * EVB, EVB)
        block = acc_ref[:, pl.ds(at, BAGS)].T
        for pair in range(FEATS // 2):
            left = block[2 * pair * EVB : (2 * pair + 1) * EVB]
            right = block[(2 * pair + 1) * EVB : (2 * pair + 2) * EVB]
            x_ref[pl.ds(to, EVB), pair * 2 * EMB : (pair + 1) * 2 * EMB] = jnp.concatenate(
                [left, right], axis=1
            ).astype(BF)
        return carry

    lax.fori_loop(0, count, place, 0, unroll=4)


def pool(part, parts, pos, meta, starts, ends, entries):
    blocks = starts.shape[0] - 8
    half_blocks = blocks // 2
    count = half_blocks // parts
    chunks = entries.shape[1] // ROWS
    return pl.pallas_call(
        functools.partial(pool_kernel, part * count, count, half_blocks, chunks),
        out_shape=shape((count * EVB, D)),
        in_specs=[SSPEC, SSPEC, VSPEC, VSPEC, VSPEC],
        out_specs=VSPEC,
        scratch_shapes=[pltpu.VMEM((EMB, (blocks + 1) * BAGS), F32)],
        compiler_params=params(),
        cost_estimate=cost(4e9, 5e6),
    )(pos, meta, starts, ends, entries)


def expand_kernel(half_blocks, group, pos_ref, meta_ref, st_ref, en_ref, own_ref, other_ref, out_ref, rows_ref):
    position = pos_ref[0]
    step = pl.program_id(0)

    @pl.when(step == 0)
    def _():
        for source, half in ((own_ref, position), (other_ref, 1 - position)):

            def place(i, carry):
                at = pl.multiple_of(i * EVB, EVB)
                to = pl.multiple_of((half * half_blocks + i) * BAGS, BAGS)
                parts = []
                for pair in range(FEATS // 2):
                    tile = source[pl.ds(at, EVB), pair * 2 * EMB : (pair + 1) * 2 * EMB]
                    parts += [tile[:, :EMB], tile[:, EMB:]]
                rows_ref[:, pl.ds(to, BAGS)] = jnp.concatenate(parts, axis=0).T
                return carry

            lax.fori_loop(0, half_blocks, place, 0, unroll=4)
        rows_ref[:, pl.ds(2 * half_blocks * BAGS, BAGS)] = jnp.zeros((EMB, BAGS), BF)

    for u in range(group):
        c = step * group + u
        block = meta_ref[1, c]
        picked = one_hot(window(st_ref, block), window(en_ref, block), c * ROWS)
        at = pl.multiple_of(block * BAGS, BAGS)
        out_ref[:, u * ROWS : (u + 1) * ROWS] = nt(rows_ref[:, pl.ds(at, 2 * BAGS)], picked).astype(BF)


def expand(pos, meta, starts, ends, own, other, rows):
    blocks = starts.shape[0] - 8
    chunks = rows // ROWS
    group = 16
    while chunks % group:
        group //= 2
    return pl.pallas_call(
        functools.partial(expand_kernel, blocks // 2, group),
        grid=(chunks // group,),
        out_shape=shape((EMB, rows)),
        in_specs=[SSPEC, SSPEC, VSPEC, VSPEC, VSPEC, VSPEC],
        out_specs=pl.BlockSpec((EMB, group * ROWS), lambda i: (0, i)),
        scratch_shapes=[pltpu.VMEM((EMB, (blocks + 1) * BAGS), BF)],
        compiler_params=params(dimension_semantics=("arbitrary",)),
        cost_estimate=cost(8e9, 6e6),
    )(pos, meta, starts, ends, own, other)


def gelu_both(v):
    square = v * v
    half = 0.5 * jnp.tanh(v * (K1 * square + K0)) + 0.5
    act = v * half
    slope = half + act * (1.0 - half) * (6.0 * K1 * square + 2.0 * K0)
    return act, slope


def col_sum(value):
    return jnp.sum(value, axis=0, keepdims=True)


def lane_tiles(events, body):
    def step(j, carry):
        body(j, pl.ds(pl.multiple_of(j * LANES, LANES), LANES))
        return carry

    lax.fori_loop(0, events // LANES, step, 0)


def main_kernel(xs, groups, outs, rows1, rows2, pos_ref, at_ref, *refs):
    refs = list(refs)
    take = lambda n: [refs.pop(0) for _ in range(n)]
    x_parts = take(xs)
    own_groups, oth_groups = take(groups), take(groups)
    packs = take(2)
    pred_ref, dx_ref = take(2)
    own_outs, oth_outs = take(outs), take(outs)
    smalls = take(2)
    x_ref, wc_ref, w2_ref, gain_ref, third_ref, lab_ref, pc_ref, pb_ref, s2_ref, y_ref, h_ref, e_ref, fc_ref = take(13)
    lg_ref, prob_ref, q_ref, pt_ref, u1_ref, p4_ref, e2_ref, e1_ref, du_ref, dm_ref, dmb_ref, acc_ref, acc3_ref, g_ref = take(14)
    position = pos_ref[0]
    events = x_ref.shape[1]

    def part(m):
        return slice(m * HID, (m + 1) * HID)

    size = events // xs
    for k, piece in enumerate(x_parts):
        x_ref[:, k * size : (k + 1) * size] = piece[...].T
    for t, whole in enumerate((own_groups, oth_groups)):
        p = 0
        for group in whole:
            for g in range(group.shape[0]):
                d = at_ref[t, p]
                p += 1
                one = pl.ds(pl.multiple_of(d * rows1, rows1), rows1)
                two = pl.ds(pl.multiple_of(d * rows2, rows2), rows2)
                for s in range(SLOTS):
                    wc_ref[one, part(t * SLOTS + s)] = group[g, s * rows1 : (s + 1) * rows1, :]
                    low = SLOTS * rows1 + s * rows2
                    w2_ref[t * SLOTS + s, two, :] = group[g, low : low + rows2, :]
    lines = []
    for t in range(2):
        block = packs[t][GATE_AT : GATE_AT + 16, :].astype(F32)
        for g in range(GATES):
            lines.append(
                jnp.concatenate([block[4 * g + p : 4 * g + p + 1, :] for p in range(D // LANES)], axis=1)
            )
        lines.append(jnp.zeros((8 - GATES, D), F32))
    gates = jnp.concatenate(lines, axis=0).astype(BF)
    wc_ref[:, WIDE:] = jnp.concatenate([gates, jnp.zeros((LANES - 16, D), BF)], axis=0).T
    fc_ref[WIDE:, :] = jnp.zeros((LANES, events), BF)
    acc_ref[...] = jnp.zeros_like(acc_ref)
    acc3_ref[...] = jnp.zeros_like(acc3_ref)
    for t in range(2):
        misc = packs[t][MISC_AT : MISC_AT + 16, :].astype(F32)
        for s in range(SLOTS):
            for kind in range(2):
                for half in range(2):
                    at = 2 * (kind * SLOTS + s) + half
                    to = ((kind * 2 + t) * SLOTS + s) * HID + half * LANES
                    gain_ref[to : to + LANES, :] = jnp.broadcast_to(misc[at : at + 1, :], (LANES, LANES)).T
        third = jnp.broadcast_to(misc[12:13, :], (LANES, LANES)).T
        third_ref[t * TOWER2 : (t + 1) * TOWER2, :] = third[:TOWER2]
        lab_ref[t * 16 : (t + 1) * 16, :] = packs[t][LABEL_AT : LABEL_AT + 16, :].astype(F32)

    for m in range(BIG):
        pc_ref[part(m), :] = tn(wc_ref[:, part(m)], x_ref[...])
    lg_ref[...] = nn(gates, x_ref[...])

    def first_gelu(j, here):
        for m in range(BIG):
            act, slope = gelu_both(pc_ref[part(m), here])
            pc_ref[part(m), here] = slope
            h_ref[part(m), here] = act.astype(BF)

    lane_tiles(events, first_gelu)
    for m in range(BIG):
        pb_ref[part(m), :] = tn(w2_ref[m], h_ref[part(m), :])

    def second_gelu(j, here):
        for m in range(BIG):
            act, slope = gelu_both(pb_ref[part(m), here])
            centred = act - col_sum(act) * (1.0 / HID)
            scale = lax.rsqrt(col_sum(centred * centred) * (1.0 / HID) + EPSILON)
            normed = centred * scale
            pb_ref[part(m), here] = normed
            s2_ref[part(m), here] = slope * scale
            out = normed * gain_ref[part(m), :] + gain_ref[part(BIG + m), :]
            if m % SLOTS == SLOTS - 1:
                out = out.astype(BF).astype(F32)
            y_ref[part(m), here] = out

    lane_tiles(events, second_gelu)
    orders = [(t * SLOTS, t * SLOTS + 1, t * SLOTS + 2, (1 - t) * SLOTS + 2) for t in range(2)]

    def mix(j, here):
        for t in range(2):
            logits = [lg_ref[8 * t + k : 8 * t + k + 1, here] for k in range(GATES)]
            top = jnp.maximum(jnp.maximum(logits[0], logits[1]), jnp.maximum(logits[2], logits[3]))
            raised = [jnp.exp(logit - top) for logit in logits]
            scale = 1.0 / (raised[0] + raised[1] + raised[2] + raised[3])
            mixture = None
            for k in range(GATES):
                prob = raised[k] * scale
                prob_ref[8 * t + k : 8 * t + k + 1, here] = prob
                term = prob * y_ref[part(orders[t][k]), here]
                mixture = term if mixture is None else mixture + term
            q_ref[part(t), here] = mixture.astype(BF)

    lane_tiles(events, mix)
    for t in range(2):
        pt_ref[t * TOWER1 : (t + 1) * TOWER1, :] = tn(packs[t][T1_AT : T1_AT + HID, :], q_ref[part(t), :])

    def tower_gelu(j, here):
        act, slope = gelu_both(pt_ref[:, here])
        pt_ref[:, here] = slope
        u1_ref[:, here] = act.astype(BF)

    lane_tiles(events, tower_gelu)
    for t in range(2):
        p4_ref[t * TOWER2 : (t + 1) * TOWER2, :] = nn(
            packs[t][T2_AT : T2_AT + TOWER2, :], u1_ref[t * TOWER1 : (t + 1) * TOWER1, :]
        )

    def head(j, here):
        act, slope = gelu_both(p4_ref[:, here])
        u2 = act.astype(BF).astype(F32)
        product = u2 * third_ref[...]
        deltas = []
        for t in range(2):
            logit = col_sum(product[t * TOWER2 : (t + 1) * TOWER2])
            prediction = 1.0 / (1.0 + jnp.exp(-logit))
            pred_ref[t, pl.ds(j, 1), :] = prediction
            label = lab_ref[pl.ds(t * 16 + position * (events // LANES) + j, 1), :]
            deltas.append(jnp.broadcast_to(prediction - label, (TOWER2, LANES)))
        delta = jnp.concatenate(deltas, axis=0)
        acc3_ref[...] += delta * u2
        e2_ref[:, here] = (slope * (delta * third_ref[...])).astype(BF)

    lane_tiles(events, head)
    for t in range(2):
        du_ref[t * TOWER1 : (t + 1) * TOWER1, :] = tn(
            packs[t][T2_AT : T2_AT + TOWER2, :], e2_ref[t * TOWER2 : (t + 1) * TOWER2, :]
        )

    def tower_back(j, here):
        e1_ref[:, here] = (pt_ref[:, here] * du_ref[:, here]).astype(BF)

    lane_tiles(events, tower_back)
    for t in range(2):
        dm_ref[part(t), :] = nn(packs[t][T1_AT : T1_AT + HID, :], e1_ref[t * TOWER1 : (t + 1) * TOWER1, :])

    def mix_back(j, here):
        codes = []
        probs = [[prob_ref[8 * t + k : 8 * t + k + 1, here] for k in range(GATES)] for t in range(2)]
        for t in range(2):
            mixed = dm_ref[part(t), here]
            dmb_ref[part(t), here] = mixed.astype(BF)
            d_prob = [col_sum(mixed * y_ref[part(orders[t][k]), here]) for k in range(GATES)]
            weighted = probs[t][0] * d_prob[0]
            for k in range(1, GATES):
                weighted = weighted + probs[t][k] * d_prob[k]
            codes += [probs[t][k] * (d_prob[k] - weighted) for k in range(GATES)]
            codes.append(jnp.zeros((8 - GATES, LANES), F32))
        fc_ref[WIDE : WIDE + 16, here] = jnp.concatenate(codes, axis=0).astype(BF)
        for m in range(BIG):
            t, s = divmod(m, SLOTS)
            up = probs[t][s] * dm_ref[part(t), here]
            if s == SLOTS - 1:
                up = up + probs[1 - t][SLOTS] * dm_ref[part(1 - t), here]
            normed = pb_ref[part(m), here]
            up_normed = up * normed
            acc_ref[part(m), :] += up_normed
            gain = gain_ref[part(m), :]
            d_normed = up * gain
            mean_one = col_sum(d_normed) * (1.0 / HID)
            mean_two = col_sum(d_normed * normed) * (1.0 / HID)
            e_ref[part(m), here] = (s2_ref[part(m), here] * (d_normed - mean_one - normed * mean_two)).astype(BF)

    lane_tiles(events, mix_back)
    for m in range(BIG):
        s2_ref[part(m), :] = nn(w2_ref[m], e_ref[part(m), :])

    def first_back(j, here):
        for m in range(BIG):
            fc_ref[part(m), here] = (pc_ref[part(m), here] * s2_ref[part(m), here]).astype(BF)

    lane_tiles(events, first_back)
    dx_ref[...] = nn(wc_ref[...], fc_ref[...]).astype(BF).T

    for t, outputs in enumerate((own_outs, oth_outs)):
        for s in range(SLOTS):
            m = t * SLOTS + s
            g_ref[:D, :] = nt(x_ref[...], fc_ref[part(m), :])
            g_ref[D:, :] = nt(h_ref[part(m), :], e_ref[part(m), :])
            p = 0
            for out in outputs:
                for g in range(out.shape[0]):
                    d = at_ref[t, p]
                    p += 1
                    one = pl.ds(pl.multiple_of(d * rows1, rows1), rows1)
                    two = pl.ds(pl.multiple_of(D + d * rows2, rows2), rows2)
                    out[g, s * rows1 : (s + 1) * rows1, :] = g_ref[one, :].astype(BF)
                    low = SLOTS * rows1 + s * rows2
                    out[g, low : low + rows2, :] = g_ref[two, :].astype(BF)
    gate_grad = nt(fc_ref[WIDE : WIDE + 16, :], x_ref[...])
    weights = prob_ref[...].astype(BF)
    shifts = [nt(weights, dmb_ref[part(t), :]) for t in range(2)]
    third_grad = col_sum(acc3_ref[...].T)
    for t in range(2):
        small = smalls[t]
        tower = slice(t * TOWER1, (t + 1) * TOWER1)
        half = slice(t * TOWER2, (t + 1) * TOWER2)
        small[T1_AT : T1_AT + HID, :] = nt(q_ref[part(t), :], e1_ref[tower, :]).astype(BF)
        small[T2_AT : T2_AT + TOWER2, :] = nt(e2_ref[half, :], u1_ref[tower, :]).astype(BF)
        lines = []
        for g in range(GATES):
            row = gate_grad[8 * t + g : 8 * t + g + 1, :]
            lines += [row[:, p * LANES : (p + 1) * LANES] for p in range(D // LANES)]
        for s in range(SLOTS):
            for k in range(2):
                at = (t * SLOTS + s) * HID + k * LANES
                lines.append(col_sum(acc_ref[at : at + LANES, :].T))
        for s in range(SLOTS):
            row = shifts[t][8 * t + s : 8 * t + s + 1, :]
            if s == SLOTS - 1:
                row = row + shifts[1 - t][8 * (1 - t) + SLOTS : 8 * (1 - t) + SLOTS + 1, :]
            lines += [row[:, :LANES], row[:, LANES:]]
        lines.append(third_grad if t == 0 else pltpu.roll(third_grad, TOWER2, 1))
        lines.append(jnp.zeros((3, LANES), F32))
        small[GATE_AT : GATE_AT + 32, :] = jnp.concatenate(lines, axis=0).astype(BF)


def layer(pos, at, x_parts, own_groups, oth_groups, own_pack, oth_pack, outs, rows1, rows2):
    events = sum(part.shape[0] for part in x_parts)
    rows = SLOTS * (rows1 + rows2)
    count, pieces = outs
    grads = (shape((pieces, rows, HID)),) * (2 * count)
    small = shape((G_ROWS, LANES))
    scratch = [
        ((D, events), BF),
        ((D, WIDE + LANES), BF),
        ((BIG, HID, HID), BF),
        ((2 * WIDE, LANES), F32),
        ((2 * TOWER2, LANES), F32),
        ((32, LANES), F32),
        ((WIDE, events), F32),
        ((WIDE, events), F32),
        ((WIDE, events), F32),
        ((WIDE, events), F32),
        ((WIDE, events), BF),
        ((WIDE, events), BF),
        ((WIDE + LANES, events), BF),
        ((16, events), F32),
        ((16, events), F32),
        ((2 * HID, events), BF),
        ((2 * TOWER1, events), F32),
        ((2 * TOWER1, events), BF),
        ((2 * TOWER2, events), F32),
        ((2 * TOWER2, events), BF),
        ((2 * TOWER1, events), BF),
        ((2 * TOWER1, events), F32),
        ((2 * HID, events), F32),
        ((2 * HID, events), BF),
        ((WIDE, LANES), F32),
        ((2 * TOWER2, LANES), F32),
        ((D + HID, HID), F32),
    ]
    n_in = len(x_parts) + len(own_groups) + len(oth_groups) + 2
    result = pl.pallas_call(
        functools.partial(main_kernel, len(x_parts), len(own_groups), count, rows1, rows2),
        out_shape=(shape((2, events // LANES, LANES), F32), shape((events, D))) + grads + (small, small),
        in_specs=[SSPEC, SSPEC] + [VSPEC] * n_in,
        out_specs=(VSPEC,) * (4 + 2 * count),
        scratch_shapes=[pltpu.VMEM(dims, kind) for dims, kind in scratch],
        compiler_params=params(),
        cost_estimate=cost(events * BIG * 196608 * 6, 10e6),
    )(pos, at, *x_parts, *own_groups, *oth_groups, own_pack, oth_pack)
    pred, dx = result[:2]
    return pred, dx, result[2 : 2 + count], result[2 + count : 2 + 2 * count], result[-2], result[-1]


def sibling(value):
    return lax.ppermute(value, "task", [(0, 1), (1, 0)])


def flipped(value, mask):
    pairs = [(i, i ^ mask) for i in range(lax.axis_size("dp"))]
    return lax.ppermute(value, "dp", pairs)


def crossed(value, masks):
    n = lax.axis_size("dp")
    pairs = [(t * n + i, t * n + (i ^ masks[t])) for t in range(2) for i in range(n)]
    return lax.ppermute(value, ("task", "dp"), pairs)


def stack_kernel(count, *refs):
    out = refs[-1]
    for k in range(count):
        out[k] = refs[k][...]


def stacked(pieces, after):
    return pl.pallas_call(
        functools.partial(stack_kernel, len(pieces)),
        out_shape=shape((len(pieces),) + pieces[0].shape, pieces[0].dtype),
        in_specs=[VSPEC] * len(pieces) + [ASPEC] * len(after),
        out_specs=VSPEC,
        compiler_params=params(),
        cost_estimate=cost(0, 1e6),
    )(*pieces, *after)


def table(me, position, quarter):
    one, two = 1 + position, 2 - position
    near = [me ^ (4 * k) for k in range(quarter)]
    return near + [d ^ two for d in near] + [d ^ one for d in near] + [d ^ one ^ two for d in near]


def sum_kernel(count, pieces, *refs):
    refs = list(refs)
    for terms, split in zip(count, pieces):
        arrays = [refs.pop(0) for _ in range(terms)]
        total = arrays[0][...].astype(F32)
        for array in arrays[1:]:
            total = total + array[...].astype(F32)
        refs.append((total, split))
    lists = refs[-len(count) :]
    outs = refs[: -len(count)]
    for total, split in lists:
        for cut in split:
            out = outs.pop(0)
            out[...] = (total if cut is None else total[cut]).astype(out.dtype)


def summed(lists, splits, outs):
    flat = [array for arrays in lists for array in arrays]
    return pl.pallas_call(
        functools.partial(sum_kernel, [len(arrays) for arrays in lists], splits),
        out_shape=tuple(outs),
        in_specs=[VSPEC] * len(flat),
        out_specs=(VSPEC,) * len(outs),
        compiler_params=params(),
        cost_estimate=cost(0, 4e6),
    )(*flat)


def last_kernel(quarter, rows1, rows2, pos_ref, *refs):
    refs = list(refs)
    total = refs[0][...].astype(F32)
    tiny = refs[quarter][...].astype(F32)
    for k in range(1, quarter):
        total = total + refs[k][...].astype(F32)
        tiny = tiny + refs[quarter + k][...].astype(F32)
    w1_ref, w2_ref, o1_ref, o2_ref, sg_ref, ss_ref, og_ref, os_ref, gate_ref, t1_ref, t2_ref, t3_ref = refs[2 * quarter :]
    cut = SLOTS * rows1
    for s in range(EXPERTS):
        w1_ref[s] = total[s * rows1 : (s + 1) * rows1]
        w2_ref[s] = total[cut + s * rows2 : cut + (s + 1) * rows2]
    o1_ref[...] = total[EXPERTS * rows1 : cut]
    o2_ref[...] = total[cut + EXPERTS * rows2 :]
    t1_ref[...] = tiny[T1_AT : T1_AT + HID]
    t2_ref[...] = tiny[T2_AT : T2_AT + TOWER2]
    gates = []
    for g in range(GATES):
        at = GATE_AT + 4 * g
        gates.append(jnp.concatenate([tiny[at + p : at + p + 1] for p in range(D // LANES)], axis=1))
    turned = pos_ref[0] != 0
    gate_ref[0:1, :] = gates[0]
    gate_ref[1:2, :] = gates[1]
    gate_ref[2:3, :] = jnp.where(turned, gates[3], gates[2])
    gate_ref[3:4, :] = jnp.where(turned, gates[2], gates[3])
    for kind, (spec, own) in enumerate(((sg_ref, og_ref), (ss_ref, os_ref))):
        for s in range(SLOTS):
            at = MISC_AT + 2 * (kind * SLOTS + s)
            row = jnp.concatenate([tiny[at : at + 1], tiny[at + 1 : at + 2]], axis=1)
            if s < EXPERTS:
                spec[s : s + 1, :] = row
            else:
                own[...] = row
    t3_ref[...] = tiny[MISC_AT + 12 : MISC_AT + 13, :TOWER2]


def finish(pos, parts, tinies, rows1, rows2):
    outs = (
        shape((EXPERTS, rows1, HID), F32),
        shape((EXPERTS, rows2, HID), F32),
        shape((rows1, HID), F32),
        shape((rows2, HID), F32),
        shape((EXPERTS, HID), F32),
        shape((EXPERTS, HID), F32),
        shape((1, HID), F32),
        shape((1, HID), F32),
        shape((GATES, D), F32),
        shape((HID, TOWER1), F32),
        shape((TOWER2, TOWER1), F32),
        shape((1, TOWER2), F32),
    )
    return pl.pallas_call(
        functools.partial(last_kernel, len(parts), rows1, rows2),
        out_shape=outs,
        in_specs=[SSPEC] + [VSPEC] * (2 * len(parts)),
        out_specs=(VSPEC,) * len(outs),
        compiler_params=params(),
        cost_estimate=cost(0, 4e6),
    )(pos, *parts, *tinies)


def per_device(
    entries,
    lengths,
    labels,
    spec_w1,
    spec_w2,
    spec_gain,
    spec_shift,
    shared_w1,
    shared_w2,
    shared_gain,
    shared_shift,
    gate_w,
    tower_w1,
    tower_w2,
    tower_w3,
):
    position = lax.axis_index("task")
    me = lax.axis_index("dp")
    n = lax.axis_size("dp")
    pos = position.reshape(1)
    rows1, rows2 = spec_w1.shape[2], spec_w2.shape[2]
    direct = rows2 % 16 == 0 and n % 4 == 0 and n & (n - 1) == 0
    pack = jnp.concatenate(
        [part.reshape(-1, HID) for part in (spec_w1, shared_w1, spec_w2, shared_w2)], axis=0
    )
    if direct:
        quarter = n // 4
        far = [pack] + [flipped(pack, 4 * k) for k in range(1, quarter)]

    rows = entries.shape[0]
    starts, ends, meta, small = prepare(
        pos,
        lengths,
        labels,
        spec_gain[0],
        spec_shift[0],
        shared_gain,
        shared_shift,
        gate_w[0].T,
        tower_w1[0],
        tower_w2[0].T,
        tower_w3,
        rows // ROWS,
    )
    other_small = sibling(small)
    turned = entries.T
    x_first = pool(0, 2, pos, meta, starts, ends, turned)
    x_second = pool(1, 2, pos, meta, starts, ends, turned)

    if direct:
        zc = stacked(far, [x_first])
        r1 = crossed(zc, (1, 2))
        r2 = crossed(zc, (2, 1))
        r3 = crossed(r1, (2, 1))
        own = [zc, r2, r1, r3]
        at = jnp.stack([jnp.stack(table(me, position, quarter)), jnp.stack(table(me, 1 - position, quarter))])
        outs, used1, used2 = (2, n // 2), rows1, rows2
    else:
        every = lax.all_gather(pack, "dp", axis=0)
        cut = SLOTS * rows1
        w1 = every[:, :cut].reshape(n, SLOTS, rows1, HID).swapaxes(0, 1).reshape(-1, HID)
        w2 = every[:, cut:].reshape(n, SLOTS, rows2, HID).swapaxes(0, 1).reshape(-1, HID)
        own = [jnp.concatenate([w1, w2], axis=0)[None]]
        at = jnp.zeros((2, 1), jnp.int32)
        outs, used1, used2 = (1, 1), D, HID
    other = [sibling(group) for group in own]
    pred, dx, own_grads, oth_grads, own_tiny, oth_tiny = layer(
        pos, at, [x_first, x_second], own, other, small, other_small, outs, used1, used2
    )

    got = [sibling(grad) for grad in oth_grads[::-1]][::-1]
    got_tiny = sibling(oth_tiny)
    other_dx = sibling(dx)
    if direct:
        block = (quarter, SLOTS * (rows1 + rows2), HID)
        tiny_out = shape((G_ROWS, LANES))
        keep, send = own_grads
        send, tiny = summed([[send, got[1]], [own_tiny, got_tiny]], [[None], [None]], [shape(send.shape), tiny_out])
        other_tiny = crossed(tiny, (1, 2))
        arrived = crossed(send, (1, 2))
        keep, send, tiny = summed(
            [[keep, got[0], arrived], [tiny, other_tiny]],
            [[slice(0, quarter), slice(quarter, 2 * quarter)], [None]],
            [shape(block), shape(block), tiny_out],
        )
        other_tiny = crossed(tiny, (2, 1))
        arrived = crossed(send, (2, 1))
        *parts, tiny = summed(
            [[keep, arrived], [tiny, other_tiny]],
            [list(range(quarter)), [None]],
            [shape(block[1:])] * quarter + [tiny_out],
        )
        tinies = [tiny] + [flipped(tiny, 4 * k) for k in range(1, quarter)]
        parts = [parts[0]] + [flipped(parts[k], 4 * k) for k in range(1, quarter)]
        grads = finish(pos, parts, tinies, rows1, rows2)
    else:
        whole = own_grads[0][0].astype(F32) + got[0][0].astype(F32)
        g1 = lax.psum_scatter(whole[: SLOTS * D].reshape(SLOTS, D, HID), "dp", scatter_dimension=1, tiled=True)
        g2 = lax.psum_scatter(whole[SLOTS * D :].reshape(SLOTS, HID, HID), "dp", scatter_dimension=1, tiled=True)
        part = jnp.concatenate([g1.reshape(-1, HID), g2.reshape(-1, HID)], axis=0)
        tiny = lax.psum(own_tiny.astype(F32) + got_tiny.astype(F32), "dp")
        grads = finish(pos, [part], [tiny], rows1, rows2)
    w1, w2, o1, o2, sg, ss, og, os, gate, t1, t2, t3 = grads
    entry_grads = expand(pos, meta, starts, ends, dx, other_dx, rows).T

    mine = pred[0].reshape(-1)
    theirs = sibling(pred[1]).reshape(-1)
    predictions = jnp.where(
        position == 0, jnp.concatenate([mine, theirs]), jnp.concatenate([theirs, mine])
    )[None]
    return (
        predictions,
        entry_grads,
        w1[None],
        w2[None],
        sg[None],
        ss[None],
        o1[None],
        o2[None],
        og,
        os,
        gate.T[None],
        t1[None],
        t2.T[None],
        t3,
    )


def solution(mesh):
    placed = (
        P("dp", None),
        P("dp", None),
        P("task", "dp"),
        P("task", None, "dp", None),
        P("task", None, "dp", None),
        P("task", None, None),
        P("task", None, None),
        P("task", "dp", None),
        P("task", "dp", None),
        P("task", None),
        P("task", None),
        P("task", None, None),
        P("task", None, None),
        P("task", None, None),
        P("task", None),
    )
    return jax.shard_map(
        per_device,
        mesh=mesh,
        in_specs=placed,
        out_specs=(
            P("task", "dp"),
            P("dp", None),
            P("task", None, "dp", None),
            P("task", None, "dp", None),
            P("task", None, None),
            P("task", None, None),
            P("task", "dp", None),
            P("task", "dp", None),
            P("task", None),
            P("task", None),
            P("task", None, None),
            P("task", None, None),
            P("task", None, None),
            P("task", None),
        ),
        check_vma=False,
    )
```

time: 991 us -> 122 us (0.12); the launches traced: 976 us -> 121 us
  waiting for transfers between devices: 263 us -> 29.1 us
  blocking collectives: 232 us -> 0 us
  other arithmetic: 215 us -> 1.99 us
  local copies, waits for them, and re-layouts: 200 us -> 6.27 us
  Pallas kernels: 0 us -> 59.4 us
  matrix products: 47.5 us -> 0 us
  starting transfers between devices: 1.32 us -> 23.4 us
  between operations: 15.8 us -> 0.91 us
    reduce_scatter x4 -> x0, waiting for transfers between devices: 263 us -> none  [the longest x1 76.9 us: per_device(): lax.psum_scatter(big_terms[0], 'dp', scatter_dimension=2, tiled=True)]
    scatter-add x2 -> x0, other arithmetic: 188 us -> none  [the longest x1 103 us: per_device(): jax.ops.segment_sum(entries.astype(jnp.float32), segment_ids, num_segment...]
    gather x2 -> x0, local copies, waits for them, and re-layouts: 166 us -> none  [the longest x1 102 us: per_device(): jnp.repeat(jnp.arange(bag_count, dtype=jnp.int32), lengths[0], total_repe...]
    all_gather x4 -> x0, blocking collectives: 158 us -> none  [the longest x1 43.1 us: per_device(): lax.all_gather(shared_w2, 'dp', axis=1, tiled=True)]
    psum x1 -> x0, blocking collectives: 74.2 us -> none  [per_device(): lax.psum((small_totals[0], small_totals[1], small_totals[2], small_totals...]
    pallas_call x0 -> x10, Pallas kernels: none -> 59.4 us  [the longest x1 23.9 us: layer(): pl.pallas_call(functools.partial(main_kernel, len(x_parts), len(own_group...]
    dot_general x58 -> x0, matrix products: 47.5 us -> none  [the longest x18 17.3 us: contract_cols(): lax.dot_general(left, right, (((1,), (1,)), ((), ())), preferred_element_...]
    ppermute x4 -> x26, waiting for transfers between devices: 0.31 us -> 29.1 us  [the longest x7 26.3 us: crossed(): return lax.ppermute(value, ('task', 'dp'), pairs)]
  transfers between devices with their start and end apart: 10 -> 26, of which waited for: 5 -> 6; matrix products, arithmetic and copies ran while one was open for 12% -> 1% of each run, Pallas kernels for 0% -> 26%
where the time goes in v2:
time: 122 us; the launch traced here: 121 us
  Pallas kernels  59.4 us (49%)
  waiting for transfers between devices  29.1 us (24%)
  starting transfers between devices  23.4 us (19%)
  local copies, waits for them, and re-layouts  6.27 us (5%)
  other arithmetic  1.99 us (2%)
    ppermute x7, waiting for transfers between devices, crossed(): return lax.ppermute(value, ('task', 'dp'), pairs)  26.3 us
    pallas_call x1, Pallas kernels, layer(): pl.pallas_call(functools.partial(main_kernel, len(x_parts), len(own_group...  23.9 us
    ppermute x9, starting transfers between devices, flipped(): return lax.ppermute(value, 'dp', pairs)  14.3 us
    pallas_call x2, Pallas kernels, pool(): pl.pallas_call(functools.partial(pool_kernel, part * count, count, half_b...  12 us
    pallas_call x1, Pallas kernels, expand(): pl.pallas_call(functools.partial(expand_kernel, blocks // 2, group), grid...  11.5 us
    ppermute x7, starting transfers between devices, crossed(): return lax.ppermute(value, ('task', 'dp'), pairs)  7.24 us
    pallas_call x3, Pallas kernels, summed(): pl.pallas_call(functools.partial(sum_kernel, [len(arrays) for arrays in l...  6.54 us
    unnamed x59, local copies, waits for them, and re-layouts  6.08 us
  transfers between devices with their start and end apart: 26, of which 6 were waited for; matrix products, arithmetic and copies ran while one was open for 1% of the time, Pallas kernels for 26%

profile of v2, /device:TPU:0, one launch (start us, length us, event | category | flops | bytes accessed | tf_op | source)
XLA Modules:
  0.0 121.1 jit_solution(16968975066341301413)
XLA Ops:
  1.5 3.1 %collective-permute-start = (bf16[144,256]{1,0:T(8,128)(2,1)S(1)}, bf16[144,256]{1,0:T(8,128)(2,1)S(1)}, u32[]{:S(2)}, u32[]{:S(2)}) collective-permute-start(bf16[144,256]{1,0:T(8,128)(2,1)S(1)} %pad_maximum_fusion.refs_0_), channel_id=1, source_target_pairs={{0,4},{1,5},{2,6},{3,7},{4,0},{5,1},{6,2},{7,3},{8,12},{9,13},{10,... | collective-permute-start | bytes 221192 | tf_op jit(solution)/shard_map/ppermute | solution.py:581
  4.5 2.6 %collective-permute-start.1 = (bf16[144,256]{1,0:T(8,128)(2,1)S(1)}, bf16[144,256]{1,0:T(8,128)(2,1)S(1)}, u32[]{:S(2)}, u32[]{:S(2)}) collective-permute-start(bf16[144,256]{1,0:T(8,128)(2,1)S(1)} %pad_maximum_fusion.refs_0_), channel_id=1, source_target_pairs={{0,8},{1,9},{2,10},{3,11},{4,12},{5,13},{6,14},{7,15},{8,0},{9,1},... | collective-permute-start | bytes 221192 | tf_op jit(solution)/shard_map/ppermute | solution.py:581
  7.1 1.8 %shard_map.254 = (s32[104,128]{1,0:T(8,128)}, s32[104,128]{1,0:T(8,128)}, s32[2,256]{1,0:T(2,128)}, bf16[368,128]{1,0:T(8,128)(2,1)}) custom-call(s32[1]{0:T(128)} %bitcast.pos_ref, s32[1,12288]{1,0:T(1,128)} %len_ref.1, s32[1,1536]{1,0:T(1,128)} %label_ref.1, bf16[2,256]{1,0:T(2,128)(2,1)} %bitcast.90, bf16[2,256]{1,0:T(2,128)(2,1)} %bitcast.91, ...), custom_call_target="tpu_custom_call" | custom-call | flops 1000000000 | bytes 1000000 | tf_op jit(solution)/shard_map/pallas_call | solution.py:148
  8.9 6.0 %shard_map.255.refs_4_.refs_0_ = bf16[384,512]{1,0:T(8,128)(2,1)} custom-call(s32[1]{0:T(128)} %bitcast.pos_ref, s32[2,256]{1,0:T(2,128)} %get-tuple-element.48.meta_ref, s32[104,128]{1,0:T(8,128)} %get-tuple-element.49.st_ref, s32[104,128]{1,0:T(8,128)} %get-tuple-element.50.en_ref, bf16[64,18432]{1,0:T(8,128)(2,1)} %bitcast.76), custom_call_target="tpu_custom_call" | custom-call | flops 4000000000 | bytes 5000000 | tf_op jit(solution)/shard_map/pallas_call | solution.py:223
  16.2 1.7 %shard_map.257.refs_2_ = bf16[4,144,256]{2,1,0:T(8,128)(2,1)} custom-call(bf16[144,256]{1,0:T(8,128)(2,1)} %copy-done.4, bf16[144,256]{1,0:T(8,128)(2,1)} %copy-done.14, bf16[144,256]{1,0:T(8,128)(2,1)} %copy-done.15, bf16[144,256]{1,0:T(8,128)(2,1)} %copy-done.16, bf16[384,512]{1,0:T(8,128)(2,1)} %shard_map.255.refs_4_.refs_0_), custom_call_target="tpu_custom_call" | custom-call | bytes 1000000 | tf_op jit(solution)/shard_map/pallas_call | solution.py:597
  17.9 1.5 %collective-permute-start.4 = (bf16[4,144,256]{2,1,0:T(8,128)(2,1)}, bf16[4,144,256]{2,1,0:T(8,128)(2,1)S(1)}, u32[]{:S(2)}, u32[]{:S(2)}) collective-permute-start(bf16[4,144,256]{2,1,0:T(8,128)(2,1)} %shard_map.257.refs_2_), channel_id=1, source_target_pairs={{0,1},{1,0},{2,3},{3,2},{4,5},{5,4},{6,7},{7,6},{8,9},{9,8},{10,11... | collective-permute-start | bytes 884744 | tf_op jit(solution)/shard_map/ppermute | solution.py:587
  19.4 1.5 %collective-permute-start.3 = (bf16[4,144,256]{2,1,0:T(8,128)(2,1)}, bf16[4,144,256]{2,1,0:T(8,128)(2,1)S(1)}, u32[]{:S(2)}, u32[]{:S(2)}) collective-permute-start(bf16[4,144,256]{2,1,0:T(8,128)(2,1)} %shard_map.257.refs_2_), channel_id=1, source_target_pairs={{0,2},{1,3},{2,0},{3,1},{4,6},{5,7},{6,4},{7,5},{8,10},{9,11},{10,... | collective-permute-start | bytes 884744 | tf_op jit(solution)/shard_map/ppermute | solution.py:587
  20.9 7.0 %collective-permute-done.4.refs_4_ = bf16[4,144,256]{2,1,0:T(8,128)(2,1)S(1)} collective-permute-done((bf16[4,144,256]{2,1,0:T(8,128)(2,1)}, bf16[4,144,256]{2,1,0:T(8,128)(2,1)S(1)}, u32[]{:S(2)}, u32[]{:S(2)}) %collective-permute-start.4) | collective-permute-done | bytes 294944 | tf_op jit(solution)/shard_map/ppermute | solution.py:587
  29.2 5.5 %collective-permute-done.5.refs_5_ = bf16[4,144,256]{2,1,0:T(8,128)(2,1)S(1)} collective-permute-done((bf16[4,144,256]{2,1,0:T(8,128)(2,1)S(1)}, bf16[4,144,256]{2,1,0:T(8,128)(2,1)S(1)}, u32[]{:S(2)}, u32[]{:S(2)}) %collective-permute-start.5) | collective-permute-done | bytes 294944 | tf_op jit(solution)/shard_map/ppermute | solution.py:587
  34.7 6.0 %shard_map.256.refs_1_ = bf16[384,512]{1,0:T(8,128)(2,1)} custom-call(s32[1]{0:T(128)} %bitcast.pos_ref, s32[2,256]{1,0:T(2,128)} %get-tuple-element.48.meta_ref, s32[104,128]{1,0:T(8,128)} %get-tuple-element.49.st_ref, s32[104,128]{1,0:T(8,128)} %get-tuple-element.50.en_ref, bf16[64,18432]{1,0:T(8,128)(2,1)} %bitcast.77), custom_call_target="tpu_custom_call" | custom-call | flops 4000000000 | bytes 5000000 | tf_op jit(solution)/shard_map/pallas_call | solution.py:223
  43.3 23.9 %shard_map.258 = (f32[2,6,128]{2,1,0:T(8,128)}, bf16[768,512]{1,0:T(8,128)(2,1)}, bf16[8,144,256]{2,1,0:T(8,128)(2,1)}, bf16[8,144,256]{2,1,0:T(8,128)(2,1)}, bf...) custom-call(s32[1]{0:T(128)} %bitcast.pos_ref, ...), custom_call_target="tpu_custom_call" | custom-call | flops 5435817984 | bytes 10000000 | tf_op jit(solution)/shard_map/pallas_call | solution.py:562
  68.0 1.6 %collective-permute-done.15.refs_3_ = bf16[352,128]{1,0:T(8,128)(2,1)S(1)} collective-permute-done((bf16[352,128]{1,0:T(8,128)(2,1)}, bf16[352,128]{1,0:T(8,128)(2,1)S(1)}, u32[]{:S(2)}, u32[]{:S(2)}) %collective-permute-start.15) | collective-permute-done | bytes 90144 | tf_op jit(solution)/shard_map/ppermute | solution.py:576
  70.5 2.3 %shard_map.260 = (bf16[8,144,256]{2,1,0:T(8,128)(2,1)}, bf16[352,128]{1,0:T(8,128)(2,1)}) custom-call(bf16[8,144,256]{2,1,0:T(8,128)(2,1)} %get-tuple-element.56.refs_0_, bf16[8,144,256]{2,1,0:T(8,128)(2,1)} %copy-done.2, bf16[352,128]{1,0:T(8,128)(2,1)} %get-tuple-element.58.refs_2_, bf16[352,128]{1,0:T(8,128)(2,1)} %copy-done.10), custom_call_target="tpu_custom_call" | custom-call | bytes 4000000 | tf_op jit(solution)/shard_map/pallas_call | solution.py:631
  72.8 1.5 %collective-permute-start.16 = (bf16[8,144,256]{2,1,0:T(8,128)(2,1)}, bf16[8,144,256]{2,1,0:T(8,128)(2,1)S(1)}, u32[]{:S(2)}, u32[]{:S(2)}) collective-permute-start(bf16[8,144,256]{2,1,0:T(8,128)(2,1)} %get-tuple-element.60), channel_id=1, source_target_pairs={{0,1},{1,0},{2,3},{3,2},{4,5},{5,4},{6,7},{7,6},{8,9},{9,8},{10,11... | collective-permute-start | bytes 1769480 | tf_op jit(solution)/shard_map/ppermute | solution.py:587
  74.8 9.0 %collective-permute-done.17.refs_4_ = bf16[352,128]{1,0:T(8,128)(2,1)S(1)} collective-permute-done((bf16[352,128]{1,0:T(8,128)(2,1)}, bf16[352,128]{1,0:T(8,128)(2,1)S(1)}, u32[]{:S(2)}, u32[]{:S(2)}) %collective-permute-start.17) | collective-permute-done | bytes 90144 | tf_op jit(solution)/shard_map/ppermute | solution.py:587
  84.7 2.4 %shard_map.261 = (bf16[4,144,256]{2,1,0:T(8,128)(2,1)}, bf16[4,144,256]{2,1,0:T(8,128)(2,1)}, bf16[352,128]{1,0:T(8,128)(2,1)}) custom-call(bf16[8,144,256]{2,1,0:T(8,128)(2,1)} %get-tuple-element.54.refs_0_, bf16[8,144,256]{2,1,0:T(8,128)(2,1)} %copy-done, bf16[8,144,256]{2,1,0:T(8,128)(2,1)} %copy-done.1, bf16[352,128]{1,0:T(8,128)(2,1)} %get-tuple-element.61.refs_3_, ...), custom_call_target="tpu_custom_call" | custom-call | bytes 4000000 | tf_op jit(solution)/shard_map/pallas_call | solution.py:631
  87.3 1.8 %collective-permute-start.19 = (bf16[352,128]{1,0:T(8,128)(2,1)}, bf16[352,128]{1,0:T(8,128)(2,1)S(1)}, u32[]{:S(2)}, u32[]{:S(2)}) collective-permute-start(bf16[352,128]{1,0:T(8,128)(2,1)} %get-tuple-element.64.refs_2_), channel_id=1, source_target_pairs={{0,2},{1,3},{2,0},{3,1},{4,6},{5,7},{6,4},{7,5},{8,10},{9,11},{10,... | collective-permute-start | bytes 270344 | tf_op jit(solution)/shard_map/ppermute | solution.py:587
  90.3 4.7 %collective-permute-done.19.refs_3_ = bf16[352,128]{1,0:T(8,128)(2,1)S(1)} collective-permute-done((bf16[352,128]{1,0:T(8,128)(2,1)}, bf16[352,128]{1,0:T(8,128)(2,1)S(1)}, u32[]{:S(2)}, u32[]{:S(2)}) %collective-permute-start.19) | collective-permute-done | bytes 90144 | tf_op jit(solution)/shard_map/ppermute | solution.py:587
  95.7 1.8 %shard_map.262 = (bf16[144,256]{1,0:T(8,128)(2,1)}, bf16[144,256]{1,0:T(8,128)(2,1)}, bf16[144,256]{1,0:T(8,128)(2,1)}, bf16[144,256]{1,0:T(8,128)(2,1)}, bf16[352,128]{1,0:T(8,128)(2,1)}) custom-call(bf16[4,144,256]{2,1,0:T(8,128)(2,1)} %get-tuple-element.62.refs_0_, bf16[4,144,256]{2,1,0:T(8,128)(2,1)} %copy-done.3, ...), custom_call_target="tpu_custom_call" | custom-call | bytes 4000000 | tf_op jit(solution)/shard_map/pallas_call | solution.py:631
  100.2 2.2 %collective-permute-start.24 = (bf16[352,128]{1,0:T(8,128)(2,1)}, bf16[352,128]{1,0:T(8,128)(2,1)S(1)}, u32[]{:S(2)}, u32[]{:S(2)}) collective-permute-start(bf16[352,128]{1,0:T(8,128)(2,1)} %get-tuple-element.69.refs_4_), channel_id=1, source_target_pairs={{0,8},{1,9},{2,10},{3,11},{4,12},{5,13},{6,14},{7,15},{8,0},{9,1},... | collective-permute-start | bytes 270344 | tf_op jit(solution)/shard_map/ppermute | solution.py:581
  102.4 1.5 %collective-permute-start.25 = (bf16[352,128]{1,0:T(8,128)(2,1)}, bf16[352,128]{1,0:T(8,128)(2,1)S(1)}, u32[]{:S(2)}, u32[]{:S(2)}) collective-permute-start(bf16[352,128]{1,0:T(8,128)(2,1)} %get-tuple-element.69.refs_4_), channel_id=1, source_target_pairs={{0,12},{1,13},{2,14},{3,15},{4,8},{5,9},{6,10},{7,11},{8,4},{9,5},... | collective-permute-start | bytes 270344 | tf_op jit(solution)/shard_map/ppermute | solution.py:581
  103.9 2.0 %collective-permute-start.21 = (bf16[144,256]{1,0:T(8,128)(2,1)}, bf16[144,256]{1,0:T(8,128)(2,1)S(1)}, u32[]{:S(2)}, u32[]{:S(2)}) collective-permute-start(bf16[144,256]{1,0:T(8,128)(2,1)} %get-tuple-element.67), channel_id=1, source_target_pairs={{0,8},{1,9},{2,10},{3,11},{4,12},{5,13},{6,14},{7,15},{8,0},{9,1},... | collective-permute-start | bytes 221192 | tf_op jit(solution)/shard_map/ppermute | solution.py:581
  106.9 11.5 %shard_map.259 = bf16[64,18432]{1,0:T(8,128)(2,1)} custom-call(s32[1]{0:T(128)} %bitcast.pos_ref, s32[2,256]{1,0:T(2,128)} %get-tuple-element.48.meta_ref, s32[104,128]{1,0:T(8,128)} %get-tuple-element.49.st_ref, s32[104,128]{1,0:T(8,128)} %get-tuple-element.50.en_ref, bf16[768,512]{1,0:T(8,128)(2,1)} %get-tuple-element.53.own_ref, bf16[768,512]{1,0:T(8,128)(2,1)} %copy-done.18), custom_call_target="tpu_custom_call" | custom-call | flops 8000000000 | bytes 6000000 | tf_op jit(solution)/shard_map/pallas_call | solution.py:269
  119.1 1.9 %shard_map.263 = (f32[2,32,256]{2,1,0:T(8,128)}, f32[2,16,256]{2,1,0:T(8,128)}, f32[32,256]{1,0:T(8,128)}, f32[16,256]{1,0:T(8,128)}, f32[2,256]{1,0:T(2,128)}, ...) custom-call(s32[1]{0:T(128)} %bitcast.pos_ref, ...), custom_call_target="tpu_custom_call" | custom-call | bytes 4000000 | tf_op jit(solution)/shard_map/pallas_call | solution.py:692
  (102 shorter events, 15.2 us)
Async XLA Ops:
  1.5 13.4 %collective-permute-start = (bf16[144,256]{1,0:T(8,128)(2,1)S(1)}, bf16[144,256]{1,0:T(8,128)(2,1)S(1)}, u32[]{:S(2)}, u32[]{:S(2)}) collective-permute-start(bf16[144,256]{1,0:T(8,128)(2,1)S(1)} %pad_maximum_fusion.refs_0_), channel_id=1, source_target_pairs={{0,4},{1,5},{2,6},{3,7},{4,0},{5,1},{6,2},{7,3},{8,12},{9,13},{10,... | collective-permute-start | bytes 221192 | tf_op jit(solution)/shard_map/ppermute | solution.py:581
  4.5 10.4 %collective-permute-start.1 = (bf16[144,256]{1,0:T(8,128)(2,1)S(1)}, bf16[144,256]{1,0:T(8,128)(2,1)S(1)}, u32[]{:S(2)}, u32[]{:S(2)}) collective-permute-start(bf16[144,256]{1,0:T(8,128)(2,1)S(1)} %pad_maximum_fusion.refs_0_), channel_id=1, source_target_pairs={{0,8},{1,9},{2,10},{3,11},{4,12},{5,13},{6,14},{7,15},{8,0},{9,1},... | collective-permute-start | bytes 221192 | tf_op jit(solution)/shard_map/ppermute | solution.py:581
  7.1 7.8 %collective-permute-start.2 = (bf16[144,256]{1,0:T(8,128)(2,1)S(1)}, bf16[144,256]{1,0:T(8,128)(2,1)S(1)}, u32[]{:S(2)}, u32[]{:S(2)}) collective-permute-start(bf16[144,256]{1,0:T(8,128)(2,1)S(1)} %pad_maximum_fusion.refs_0_), channel_id=1, source_target_pairs={{0,12},{1,13},{2,14},{3,15},{4,8},{5,9},{6,10},{7,11},{8,4},{9,5},... | collective-permute-start | bytes 221192 | tf_op jit(solution)/shard_map/ppermute | solution.py:581
  17.9 10.0 %collective-permute-start.4 = (bf16[4,144,256]{2,1,0:T(8,128)(2,1)}, bf16[4,144,256]{2,1,0:T(8,128)(2,1)S(1)}, u32[]{:S(2)}, u32[]{:S(2)}) collective-permute-start(bf16[4,144,256]{2,1,0:T(8,128)(2,1)} %shard_map.257.refs_2_), channel_id=1, source_target_pairs={{0,1},{1,0},{2,3},{3,2},{4,5},{5,4},{6,7},{7,6},{8,9},{9,8},{10,11... | collective-permute-start | bytes 884744 | tf_op jit(solution)/shard_map/ppermute | solution.py:587
  19.4 9.2 %collective-permute-start.3 = (bf16[4,144,256]{2,1,0:T(8,128)(2,1)}, bf16[4,144,256]{2,1,0:T(8,128)(2,1)S(1)}, u32[]{:S(2)}, u32[]{:S(2)}) collective-permute-start(bf16[4,144,256]{2,1,0:T(8,128)(2,1)} %shard_map.257.refs_2_), channel_id=1, source_target_pairs={{0,2},{1,3},{2,0},{3,1},{4,6},{5,7},{6,4},{7,5},{8,10},{9,11},{10,... | collective-permute-start | bytes 884744 | tf_op jit(solution)/shard_map/ppermute | solution.py:587
  28.0 6.7 %collective-permute-start.5 = (bf16[4,144,256]{2,1,0:T(8,128)(2,1)S(1)}, bf16[4,144,256]{2,1,0:T(8,128)(2,1)S(1)}, u32[]{:S(2)}, u32[]{:S(2)}) collective-permute-start(bf16[4,144,256]{2,1,0:T(8,128)(2,1)S(1)} %collective-permute-done.4.refs_4_), channel_id=1, source_target_pairs={{0,2},{1,3},{2,0},{3,1},{4,6},{5,7},{6,4},{7,5},{8,10},{9,11},{10,... | collective-permute-start | bytes 884744 | tf_op jit(solution)/shard_map/ppermute | solution.py:587
  28.1 13.4 %collective-permute-start.10 = (bf16[368,128]{1,0:T(8,128)(2,1)S(1)}, bf16[368,128]{1,0:T(8,128)(2,1)S(1)}, u32[]{:S(2)}, u32[]{:S(2)}) collective-permute-start(bf16[368,128]{1,0:T(8,128)(2,1)S(1)} %copy-done.26), channel_id=1, source_target_pairs={{0,16},{16,0},{1,17},{17,1},{2,18},{18,2},{3,19},{19,3},{4,20},{20... | collective-permute-start | bytes 282632 | tf_op jit(solution)/shard_map/ppermute | solution.py:576
  28.1 13.4 %collective-permute-start.6 = (bf16[4,144,256]{2,1,0:T(8,128)(2,1)}, bf16[4,144,256]{2,1,0:T(8,128)(2,1)S(1)}, u32[]{:S(2)}, u32[]{:S(2)}) collective-permute-start(bf16[4,144,256]{2,1,0:T(8,128)(2,1)} %shard_map.257.refs_2_), channel_id=1, source_target_pairs={{0,16},{16,0},{1,17},{17,1},{2,18},{18,2},{3,19},{19,3},{4,20},{20... | collective-permute-start | bytes 884744 | tf_op jit(solution)/shard_map/ppermute | solution.py:576
  28.6 12.9 %collective-permute-start.8 = (bf16[4,144,256]{2,1,0:T(8,128)(2,1)S(1)}, bf16[4,144,256]{2,1,0:T(8,128)(2,1)S(1)}, u32[]{:S(2)}, u32[]{:S(2)}) collective-permute-start(bf16[4,144,256]{2,1,0:T(8,128)(2,1)S(1)} %collective-permute-done.4.refs_4_), channel_id=1, source_target_pairs={{0,16},{16,0},{1,17},{17,1},{2,18},{18,2},{3,19},{19,3},{4,20},{20... | collective-permute-start | bytes 884744 | tf_op jit(solution)/shard_map/ppermute | solution.py:576
  28.7 12.9 %collective-permute-start.7 = (bf16[4,144,256]{2,1,0:T(8,128)(2,1)S(1)}, bf16[4,144,256]{2,1,0:T(8,128)(2,1)S(1)}, u32[]{:S(2)}, u32[]{:S(2)}) collective-permute-start(bf16[4,144,256]{2,1,0:T(8,128)(2,1)S(1)} %collective-permute-done.3.refs_3_), channel_id=1, source_target_pairs={{0,16},{16,0},{1,17},{17,1},{2,18},{18,2},{3,19},{19,3},{4,20},{20... | collective-permute-start | bytes 884744 | tf_op jit(solution)/shard_map/ppermute | solution.py:576
  34.7 6.9 %collective-permute-start.9 = (bf16[4,144,256]{2,1,0:T(8,128)(2,1)S(1)}, bf16[4,144,256]{2,1,0:T(8,128)(2,1)S(1)}, u32[]{:S(2)}, u32[]{:S(2)}) collective-permute-start(bf16[4,144,256]{2,1,0:T(8,128)(2,1)S(1)} %collective-permute-done.5.refs_5_), channel_id=1, source_target_pairs={{0,16},{16,0},{1,17},{17,1},{2,18},{18,2},{3,19},{19,3},{4,20},{20... | collective-permute-start | bytes 884744 | tf_op jit(solution)/shard_map/ppermute | solution.py:576
  67.2 2.4 %collective-permute-start.14 = (bf16[8,144,256]{2,1,0:T(8,128)(2,1)}, bf16[8,144,256]{2,1,0:T(8,128)(2,1)S(1)}, u32[]{:S(2)}, u32[]{:S(2)}) collective-permute-start(bf16[8,144,256]{2,1,0:T(8,128)(2,1)} %get-tuple-element.57), channel_id=1, source_target_pairs={{0,16},{16,0},{1,17},{17,1},{2,18},{18,2},{3,19},{19,3},{4,20},{20... | collective-permute-start | bytes 1769480 | tf_op jit(solution)/shard_map/ppermute | solution.py:576
  67.8 7.0 %collective-permute-start.13 = (bf16[8,144,256]{2,1,0:T(8,128)(2,1)}, bf16[8,144,256]{2,1,0:T(8,128)(2,1)S(1)}, u32[]{:S(2)}, u32[]{:S(2)}) collective-permute-start(bf16[8,144,256]{2,1,0:T(8,128)(2,1)} %get-tuple-element.55), channel_id=1, source_target_pairs={{0,16},{16,0},{1,17},{17,1},{2,18},{18,2},{3,19},{19,3},{4,20},{20... | collective-permute-start | bytes 1769480 | tf_op jit(solution)/shard_map/ppermute | solution.py:576
  72.8 11.1 %collective-permute-start.16 = (bf16[8,144,256]{2,1,0:T(8,128)(2,1)}, bf16[8,144,256]{2,1,0:T(8,128)(2,1)S(1)}, u32[]{:S(2)}, u32[]{:S(2)}) collective-permute-start(bf16[8,144,256]{2,1,0:T(8,128)(2,1)} %get-tuple-element.60), channel_id=1, source_target_pairs={{0,1},{1,0},{2,3},{3,2},{4,5},{5,4},{6,7},{7,6},{8,9},{9,8},{10,11... | collective-permute-start | bytes 1769480 | tf_op jit(solution)/shard_map/ppermute | solution.py:587
  74.2 29.7 %collective-permute-start.12 = (bf16[768,512]{1,0:T(8,128)(2,1)}, bf16[768,512]{1,0:T(8,128)(2,1)S(1)}, u32[]{:S(2)}, u32[]{:S(2)}) collective-permute-start(bf16[768,512]{1,0:T(8,128)(2,1)} %get-tuple-element.53.own_ref), channel_id=1, source_target_pairs={{0,16},{16,0},{1,17},{17,1},{2,18},{18,2},{3,19},{19,3},{4,20},{20... | collective-permute-start | bytes 2359304 | tf_op jit(solution)/shard_map/ppermute | solution.py:576
  74.2 9.6 %collective-permute-start.17 = (bf16[352,128]{1,0:T(8,128)(2,1)}, bf16[352,128]{1,0:T(8,128)(2,1)S(1)}, u32[]{:S(2)}, u32[]{:S(2)}) collective-permute-start(bf16[352,128]{1,0:T(8,128)(2,1)} %get-tuple-element.61.refs_3_), channel_id=1, source_target_pairs={{0,1},{1,0},{2,3},{3,2},{4,5},{5,4},{6,7},{7,6},{8,9},{9,8},{10,11... | collective-permute-start | bytes 270344 | tf_op jit(solution)/shard_map/ppermute | solution.py:587
  87.1 7.9 %collective-permute-start.18 = (bf16[4,144,256]{2,1,0:T(8,128)(2,1)}, bf16[4,144,256]{2,1,0:T(8,128)(2,1)S(1)}, u32[]{:S(2)}, u32[]{:S(2)}) collective-permute-start(bf16[4,144,256]{2,1,0:T(8,128)(2,1)} %get-tuple-element.63), channel_id=1, source_target_pairs={{0,2},{1,3},{2,0},{3,1},{4,6},{5,7},{6,4},{7,5},{8,10},{9,11},{10,... | collective-permute-start | bytes 884744 | tf_op jit(solution)/shard_map/ppermute | solution.py:587
  87.3 7.7 %collective-permute-start.19 = (bf16[352,128]{1,0:T(8,128)(2,1)}, bf16[352,128]{1,0:T(8,128)(2,1)S(1)}, u32[]{:S(2)}, u32[]{:S(2)}) collective-permute-start(bf16[352,128]{1,0:T(8,128)(2,1)} %get-tuple-element.64.refs_2_), channel_id=1, source_target_pairs={{0,2},{1,3},{2,0},{3,1},{4,6},{5,7},{6,4},{7,5},{8,10},{9,11},{10,... | collective-permute-start | bytes 270344 | tf_op jit(solution)/shard_map/ppermute | solution.py:587
  97.6 8.3 %collective-permute-start.20 = (bf16[144,256]{1,0:T(8,128)(2,1)}, bf16[144,256]{1,0:T(8,128)(2,1)S(1)}, u32[]{:S(2)}, u32[]{:S(2)}) collective-permute-start(bf16[144,256]{1,0:T(8,128)(2,1)} %get-tuple-element.66), channel_id=1, source_target_pairs={{0,4},{1,5},{2,6},{3,7},{4,0},{5,1},{6,2},{7,3},{8,12},{9,13},{10,... | collective-permute-start | bytes 221192 | tf_op jit(solution)/shard_map/ppermute | solution.py:581
  99.1 19.3 %collective-permute-start.23 = (bf16[352,128]{1,0:T(8,128)(2,1)}, bf16[352,128]{1,0:T(8,128)(2,1)S(1)}, u32[]{:S(2)}, u32[]{:S(2)}) collective-permute-start(bf16[352,128]{1,0:T(8,128)(2,1)} %get-tuple-element.69.refs_4_), channel_id=1, source_target_pairs={{0,4},{1,5},{2,6},{3,7},{4,0},{5,1},{6,2},{7,3},{8,12},{9,13},{10,... | collective-permute-start | bytes 270344 | tf_op jit(solution)/shard_map/ppermute | solution.py:581
  100.2 18.2 %collective-permute-start.24 = (bf16[352,128]{1,0:T(8,128)(2,1)}, bf16[352,128]{1,0:T(8,128)(2,1)S(1)}, u32[]{:S(2)}, u32[]{:S(2)}) collective-permute-start(bf16[352,128]{1,0:T(8,128)(2,1)} %get-tuple-element.69.refs_4_), channel_id=1, source_target_pairs={{0,8},{1,9},{2,10},{3,11},{4,12},{5,13},{6,14},{7,15},{8,0},{9,1},... | collective-permute-start | bytes 270344 | tf_op jit(solution)/shard_map/ppermute | solution.py:581
  102.4 16.0 %collective-permute-start.25 = (bf16[352,128]{1,0:T(8,128)(2,1)}, bf16[352,128]{1,0:T(8,128)(2,1)S(1)}, u32[]{:S(2)}, u32[]{:S(2)}) collective-permute-start(bf16[352,128]{1,0:T(8,128)(2,1)} %get-tuple-element.69.refs_4_), channel_id=1, source_target_pairs={{0,12},{1,13},{2,14},{3,15},{4,8},{5,9},{6,10},{7,11},{8,4},{9,5},... | collective-permute-start | bytes 270344 | tf_op jit(solution)/shard_map/ppermute | solution.py:581
  103.9 14.5 %collective-permute-start.21 = (bf16[144,256]{1,0:T(8,128)(2,1)}, bf16[144,256]{1,0:T(8,128)(2,1)S(1)}, u32[]{:S(2)}, u32[]{:S(2)}) collective-permute-start(bf16[144,256]{1,0:T(8,128)(2,1)} %get-tuple-element.67), channel_id=1, source_target_pairs={{0,8},{1,9},{2,10},{3,11},{4,12},{5,13},{6,14},{7,15},{8,0},{9,1},... | collective-permute-start | bytes 221192 | tf_op jit(solution)/shard_map/ppermute | solution.py:581
  105.9 12.5 %collective-permute-start.22 = (bf16[144,256]{1,0:T(8,128)(2,1)}, bf16[144,256]{1,0:T(8,128)(2,1)S(1)}, u32[]{:S(2)}, u32[]{:S(2)}) collective-permute-start(bf16[144,256]{1,0:T(8,128)(2,1)} %get-tuple-element.68), channel_id=1, source_target_pairs={{0,12},{1,13},{2,14},{3,15},{4,8},{5,9},{6,10},{7,11},{8,4},{9,5},... | collective-permute-start | bytes 221192 | tf_op jit(solution)/shard_map/ppermute | solution.py:581
  (30 other events, 126.7 us)

commit v3 on v2

--- a/solution.py
+++ b/solution.py
@@ -27,7 +27,6 @@
 WIDE = BIG * HID
 BF = jnp.bfloat16
 F32 = jnp.float32
-VMEM_BYTES = 56 * 1024 * 1024
 
 T1_AT = 0
 T2_AT = T1_AT + HID
@@ -35,6 +34,7 @@
 MISC_AT = GATE_AT + GATES * (D // LANES)
 LABEL_AT = MISC_AT + 16
 G_ROWS = LABEL_AT
+SMALL_ROWS = G_ROWS // 2
 
 
 def nn(left, right):
@@ -49,8 +49,8 @@
     return lax.dot_general(left, right, (((0,), (0,)), ((), ())), preferred_element_type=F32)
 
 
-def params(**kwargs):
-    return pltpu.CompilerParams(vmem_limit_bytes=VMEM_BYTES, **kwargs)
+def params(mib, **kwargs):
+    return pltpu.CompilerParams(vmem_limit_bytes=mib * 1024 * 1024, **kwargs)
 
 
 def cost(flops, moved):
@@ -74,7 +74,7 @@
 def prep_kernel(
     blocks,
     chunks,
-    pos_ref,
+    ids_ref,
     len_ref,
     label_ref,
     sgain_ref,
@@ -131,7 +131,7 @@
     small_ref[T2_AT : T2_AT + TOWER2, :] = t2_ref[...]
     gate = gate_ref[...].astype(F32)
     turned = jnp.concatenate([gate[0:2], gate[3:4], gate[2:3]], axis=0)
-    gate = jnp.where(pos_ref[0] == 0, gate, turned)
+    gate = jnp.where(ids_ref[0] == 0, gate, turned)
     lines = [gate[g : g + 1, p * LANES : (p + 1) * LANES] for g in range(GATES) for p in range(D // LANES)]
     lines += line(sgain_ref, 0) + line(sgain_ref, 1) + line(ogain_ref, 0)
     lines += line(sshift_ref, 0) + line(sshift_ref, 1) + line(oshift_ref, 0)
@@ -142,7 +142,7 @@
     small_ref[pl.ds(GATE_AT, 48), :] = jnp.concatenate(lines, axis=0).astype(BF)
 
 
-def prepare(pos, lengths, labels, spec_gain, spec_shift, shared_gain, shared_shift, gate, t1, t2, t3, chunks):
+def prepare(ids, lengths, labels, spec_gain, spec_shift, shared_gain, shared_shift, gate, t1, t2, t3, chunks):
     blocks = lengths.shape[1] // BAGS
     lanes = -(-max(blocks + 1, chunks) // LANES) * LANES
     return pl.pallas_call(
@@ -155,15 +155,16 @@
         ),
         in_specs=[SSPEC] + [VSPEC] * 10,
         out_specs=(VSPEC,) * 4,
-        compiler_params=params(),
+        compiler_params=params(56),
         cost_estimate=cost(1e9, 1e6),
-    )(pos, lengths, labels, spec_gain, spec_shift, shared_gain, shared_shift, gate, t1, t2, t3)
+    )(ids, lengths, labels, spec_gain, spec_shift, shared_gain, shared_shift, gate, t1, t2, t3)
 
 
 def one_hot(starts, ends, base):
-    row = lax.broadcasted_iota(jnp.int32, (ROWS, 2 * BAGS), 0)
-    inside = (row >= starts - base) & (row < ends - base)
-    return jnp.where(inside, 1.0, 0.0).astype(BF)
+    row = lax.broadcasted_iota(jnp.int32, (ROWS, 2 * BAGS), 0).astype(F32).astype(BF)
+    low = jnp.clip(starts - base, 0, ROWS).astype(F32).astype(BF)
+    high = jnp.clip(ends - base, 0, ROWS).astype(F32).astype(BF)
+    return jnp.where((row >= low) & (row < high), jnp.ones((), BF), jnp.zeros((), BF))
 
 
 def window(ref, block):
@@ -172,19 +173,20 @@
     return jnp.concatenate([first, second], axis=1)
 
 
-def pool_kernel(skip, count, half_blocks, chunks, pos_ref, meta_ref, st_ref, en_ref, ent_ref, x_ref, acc_ref):
-    base_block = pos_ref[0] * half_blocks + skip
+def pool_kernel(skip, count, half_blocks, chunks, ids_ref, meta_ref, st_ref, en_ref, ent_ref, *refs):
+    x_ref, acc_ref = refs[-2:]
+    base_block = ids_ref[0] * half_blocks + skip
 
     def clear(i, carry):
         at = pl.multiple_of((base_block + i) * BAGS, BAGS)
         acc_ref[:, pl.ds(at, BAGS)] = jnp.zeros((EMB, BAGS), F32)
         return carry
 
-    lax.fori_loop(0, count, clear, 0, unroll=4)
+    lax.fori_loop(0, count, clear, 0, unroll=True)
 
     low_chunk = meta_ref[0, base_block] // ROWS
     high_chunk = (meta_ref[0, base_block + count] + ROWS - 1) // ROWS
-    step = 4
+    step = 9
 
     def chunk(i, carry):
         for u in range(step):
@@ -212,10 +214,10 @@
             ).astype(BF)
         return carry
 
-    lax.fori_loop(0, count, place, 0, unroll=4)
-
-
-def pool(part, parts, pos, meta, starts, ends, entries):
+    lax.fori_loop(0, count, place, 0, unroll=12)
+
+
+def pool(part, parts, ids, meta, starts, ends, entries, *after):
     blocks = starts.shape[0] - 8
     half_blocks = blocks // 2
     count = half_blocks // parts
@@ -223,16 +225,16 @@
     return pl.pallas_call(
         functools.partial(pool_kernel, part * count, count, half_blocks, chunks),
         out_shape=shape((count * EVB, D)),
-        in_specs=[SSPEC, SSPEC, VSPEC, VSPEC, VSPEC],
+        in_specs=[SSPEC, SSPEC, VSPEC, VSPEC, VSPEC] + [ASPEC] * len(after),
         out_specs=VSPEC,
         scratch_shapes=[pltpu.VMEM((EMB, (blocks + 1) * BAGS), F32)],
-        compiler_params=params(),
-        cost_estimate=cost(4e9, 5e6),
-    )(pos, meta, starts, ends, entries)
-
-
-def expand_kernel(half_blocks, group, pos_ref, meta_ref, st_ref, en_ref, own_ref, other_ref, out_ref, rows_ref):
-    position = pos_ref[0]
+        compiler_params=params(16),
+        cost_estimate=cost(10e9, 5e6),
+    )(ids, meta, starts, ends, entries, *after)
+
+
+def expand_kernel(half_blocks, group, ids_ref, meta_ref, st_ref, en_ref, own_ref, other_ref, out_ref, rows_ref):
+    position = ids_ref[0]
     step = pl.program_id(0)
 
     @pl.when(step == 0)
@@ -242,40 +244,39 @@
             def place(i, carry):
                 at = pl.multiple_of(i * EVB, EVB)
                 to = pl.multiple_of((half * half_blocks + i) * BAGS, BAGS)
-                parts = []
                 for pair in range(FEATS // 2):
                     tile = source[pl.ds(at, EVB), pair * 2 * EMB : (pair + 1) * 2 * EMB]
-                    parts += [tile[:, :EMB], tile[:, EMB:]]
-                rows_ref[:, pl.ds(to, BAGS)] = jnp.concatenate(parts, axis=0).T
+                    rows_ref[pl.ds(to + 2 * pair * EVB, EVB), :] = tile[:, :EMB]
+                    rows_ref[pl.ds(to + (2 * pair + 1) * EVB, EVB), :] = tile[:, EMB:]
                 return carry
 
-            lax.fori_loop(0, half_blocks, place, 0, unroll=4)
-        rows_ref[:, pl.ds(2 * half_blocks * BAGS, BAGS)] = jnp.zeros((EMB, BAGS), BF)
+            lax.fori_loop(0, half_blocks, place, 0, unroll=12)
+        rows_ref[pl.ds(2 * half_blocks * BAGS, BAGS), :] = jnp.zeros((BAGS, EMB), BF)
 
     for u in range(group):
         c = step * group + u
         block = meta_ref[1, c]
         picked = one_hot(window(st_ref, block), window(en_ref, block), c * ROWS)
         at = pl.multiple_of(block * BAGS, BAGS)
-        out_ref[:, u * ROWS : (u + 1) * ROWS] = nt(rows_ref[:, pl.ds(at, 2 * BAGS)], picked).astype(BF)
-
-
-def expand(pos, meta, starts, ends, own, other, rows):
+        out_ref[:, u * ROWS : (u + 1) * ROWS] = nn(picked, rows_ref[pl.ds(at, 2 * BAGS), :]).astype(BF).T
+
+
+def expand(ids, meta, starts, ends, own, other, rows):
     blocks = starts.shape[0] - 8
     chunks = rows // ROWS
-    group = 16
+    group = 36
     while chunks % group:
-        group //= 2
+        group -= 1
     return pl.pallas_call(
         functools.partial(expand_kernel, blocks // 2, group),
         grid=(chunks // group,),
         out_shape=shape((EMB, rows)),
         in_specs=[SSPEC, SSPEC, VSPEC, VSPEC, VSPEC, VSPEC],
         out_specs=pl.BlockSpec((EMB, group * ROWS), lambda i: (0, i)),
-        scratch_shapes=[pltpu.VMEM((EMB, (blocks + 1) * BAGS), BF)],
-        compiler_params=params(dimension_semantics=("arbitrary",)),
-        cost_estimate=cost(8e9, 6e6),
-    )(pos, meta, starts, ends, own, other)
+        scratch_shapes=[pltpu.VMEM(((blocks + 1) * BAGS, EMB), BF)],
+        compiler_params=params(24, dimension_semantics=("arbitrary",)),
+        cost_estimate=cost(12e9, 6e6),
+    )(ids, meta, starts, ends, own, other)
 
 
 def gelu_both(v):
@@ -298,38 +299,65 @@
     lax.fori_loop(0, events // LANES, step, 0)
 
 
-def main_kernel(xs, groups, outs, rows1, rows2, pos_ref, at_ref, *refs):
+def main_kernel(xs, groups, plan, staged, rows1, rows2, ids_ref, *refs):
     refs = list(refs)
     take = lambda n: [refs.pop(0) for _ in range(n)]
-    x_parts = take(xs)
-    own_groups, oth_groups = take(groups), take(groups)
-    packs = take(2)
-    pred_ref, dx_ref = take(2)
-    own_outs, oth_outs = take(outs), take(outs)
-    smalls = take(2)
+    inputs = take(xs + 2 * groups + 2)
+    preds = take(2)
+    outputs = take(1 + 2 * len(plan))
+    staging = take(len(inputs))
+    sources = [pltpu.make_async_copy(a, b, refs[-1].at[k]) for k, (a, b) in enumerate(zip(inputs, staging))]
+    for copy in sources:
+        copy.start()
+    x_parts = [(staging[k], sources[k]) for k in range(xs)]
+    whole = list(zip(staging, sources))[xs : xs + 2 * groups]
+    own_groups, oth_groups = whole[:groups], whole[groups:]
+    packs = staging[-2:]
+    results = take(len(outputs))
+    targets = [pltpu.make_async_copy(a, b, refs[-2].at[k]) for k, (a, b) in enumerate(zip(results, outputs))]
+    dx_ref = results[0]
+    own_outs, oth_outs = results[1 : 1 + len(plan)], results[1 + len(plan) :]
+    own_sent, oth_sent = targets[1 : 1 + len(plan)], targets[1 + len(plan) :]
     x_ref, wc_ref, w2_ref, gain_ref, third_ref, lab_ref, pc_ref, pb_ref, s2_ref, y_ref, h_ref, e_ref, fc_ref = take(13)
-    lg_ref, prob_ref, q_ref, pt_ref, u1_ref, p4_ref, e2_ref, e1_ref, du_ref, dm_ref, dmb_ref, acc_ref, acc3_ref, g_ref = take(14)
-    position = pos_ref[0]
+    lg_ref, prob_ref, q_ref, pt_ref, u1_ref, p4_ref, e2_ref, e1_ref, du_ref, dm_ref, dmb_ref, acc_ref, acc3_ref, g1_ref, g2_ref = take(15)
+    position = ids_ref[0]
     events = x_ref.shape[1]
+    quarter = D // rows1 // 4
 
     def part(m):
         return slice(m * HID, (m + 1) * HID)
 
+    def rows_of(t, p):
+        if not quarter:
+            return pl.ds(0, rows1), pl.ds(0, rows2)
+        where = position if t == 0 else 1 - position
+        d = ids_ref[1] ^ (4 * (p % quarter))
+        if (p // quarter) & 1:
+            d = d ^ (2 - where)
+        if p // quarter >= 2:
+            d = d ^ (1 + where)
+        return (
+            pl.ds(pl.multiple_of(d * rows1, rows1), rows1),
+            pl.ds(pl.multiple_of(d * rows2, rows2), rows2),
+        )
+
     size = events // xs
-    for k, piece in enumerate(x_parts):
+    for k, (piece, copy) in enumerate(x_parts):
+        copy.wait()
         x_ref[:, k * size : (k + 1) * size] = piece[...].T
     for t, whole in enumerate((own_groups, oth_groups)):
         p = 0
-        for group in whole:
+        for group, copy in whole:
+            copy.wait()
             for g in range(group.shape[0]):
-                d = at_ref[t, p]
+                one, two = rows_of(t, p)
                 p += 1
-                one = pl.ds(pl.multiple_of(d * rows1, rows1), rows1)
-                two = pl.ds(pl.multiple_of(d * rows2, rows2), rows2)
                 for s in range(SLOTS):
                     wc_ref[one, part(t * SLOTS + s)] = group[g, s * rows1 : (s + 1) * rows1, :]
                     low = SLOTS * rows1 + s * rows2
                     w2_ref[t * SLOTS + s, two, :] = group[g, low : low + rows2, :]
+    sources[-2].wait()
+    sources[-1].wait()
     lines = []
     for t in range(2):
         block = packs[t][GATE_AT : GATE_AT + 16, :].astype(F32)
@@ -422,7 +450,7 @@
         for t in range(2):
             logit = col_sum(product[t * TOWER2 : (t + 1) * TOWER2])
             prediction = 1.0 / (1.0 + jnp.exp(-logit))
-            pred_ref[t, pl.ds(j, 1), :] = prediction
+            preds[t][pl.ds(j, 1), :] = prediction
             label = lab_ref[pl.ds(t * 16 + position * (events // LANES) + j, 1), :]
             deltas.append(jnp.broadcast_to(prediction - label, (TOWER2, LANES)))
         delta = jnp.concatenate(deltas, axis=0)
@@ -479,32 +507,28 @@
 
     lane_tiles(events, first_back)
     dx_ref[...] = nn(wc_ref[...], fc_ref[...]).astype(BF).T
-
-    for t, outputs in enumerate((own_outs, oth_outs)):
-        for s in range(SLOTS):
-            m = t * SLOTS + s
-            g_ref[:D, :] = nt(x_ref[...], fc_ref[part(m), :])
-            g_ref[D:, :] = nt(h_ref[part(m), :], e_ref[part(m), :])
-            p = 0
-            for out in outputs:
-                for g in range(out.shape[0]):
-                    d = at_ref[t, p]
-                    p += 1
-                    one = pl.ds(pl.multiple_of(d * rows1, rows1), rows1)
-                    two = pl.ds(pl.multiple_of(D + d * rows2, rows2), rows2)
-                    out[g, s * rows1 : (s + 1) * rows1, :] = g_ref[one, :].astype(BF)
-                    low = SLOTS * rows1 + s * rows2
-                    out[g, low : low + rows2, :] = g_ref[two, :].astype(BF)
+    targets[0].start()
+
     gate_grad = nt(fc_ref[WIDE : WIDE + 16, :], x_ref[...])
     weights = prob_ref[...].astype(BF)
     shifts = [nt(weights, dmb_ref[part(t), :]) for t in range(2)]
     third_grad = col_sum(acc3_ref[...].T)
-    for t in range(2):
-        small = smalls[t]
+    for t, results, sent in ((1, oth_outs, oth_sent), (0, own_outs, own_sent)):
+        for s in range(SLOTS):
+            m = t * SLOTS + s
+            g1_ref[...] = nt(x_ref[...], fc_ref[part(m), :])
+            g2_ref[...] = nt(h_ref[part(m), :], e_ref[part(m), :])
+            p = 0
+            for out, (pieces, small_first) in zip(results, plan):
+                for g in range(pieces):
+                    one, two = rows_of(t, p)
+                    p += 1
+                    at = g * SLOTS * (rows1 + rows2) + (SMALL_ROWS if small_first else 0)
+                    out[at + s * rows1 : at + (s + 1) * rows1, :] = g1_ref[one, :].astype(BF)
+                    at = at + SLOTS * rows1 + s * rows2
+                    out[at : at + rows2, :] = g2_ref[two, :].astype(BF)
         tower = slice(t * TOWER1, (t + 1) * TOWER1)
         half = slice(t * TOWER2, (t + 1) * TOWER2)
-        small[T1_AT : T1_AT + HID, :] = nt(q_ref[part(t), :], e1_ref[tower, :]).astype(BF)
-        small[T2_AT : T2_AT + TOWER2, :] = nt(e2_ref[half, :], u1_ref[tower, :]).astype(BF)
         lines = []
         for g in range(GATES):
             row = gate_grad[8 * t + g : 8 * t + g + 1, :]
@@ -520,15 +544,29 @@
             lines += [row[:, :LANES], row[:, LANES:]]
         lines.append(third_grad if t == 0 else pltpu.roll(third_grad, TOWER2, 1))
         lines.append(jnp.zeros((3, LANES), F32))
-        small[GATE_AT : GATE_AT + 32, :] = jnp.concatenate(lines, axis=0).astype(BF)
-
-
-def layer(pos, at, x_parts, own_groups, oth_groups, own_pack, oth_pack, outs, rows1, rows2):
+        small = jnp.concatenate(
+            [
+                nt(q_ref[part(t), :], e1_ref[tower, :]),
+                nt(e2_ref[half, :], u1_ref[tower, :]),
+                jnp.concatenate(lines, axis=0),
+            ],
+            axis=0,
+        )
+        small = jnp.concatenate([small[:SMALL_ROWS], small[SMALL_ROWS:]], axis=1).astype(BF)
+        for out, copy, (_, small_first) in list(zip(results, sent, plan))[::-1]:
+            if small_first:
+                out[:SMALL_ROWS, :] = small
+            copy.start()
+    for copy in targets:
+        copy.wait()
+
+
+def layer(ids, x_parts, own_groups, oth_groups, own_pack, oth_pack, plan, rows1, rows2):
     events = sum(part.shape[0] for part in x_parts)
     rows = SLOTS * (rows1 + rows2)
-    count, pieces = outs
-    grads = (shape((pieces, rows, HID)),) * (2 * count)
-    small = shape((G_ROWS, LANES))
+    grads = tuple(shape((pieces * rows + small * SMALL_ROWS, HID)) for pieces, small in plan)
+    pred = shape((events // LANES, LANES), F32)
+    results = (shape((events, D)),) + grads + grads
     scratch = [
         ((D, events), BF),
         ((D, WIDE + LANES), BF),
@@ -556,20 +594,22 @@
         ((2 * HID, events), BF),
         ((WIDE, LANES), F32),
         ((2 * TOWER2, LANES), F32),
-        ((D + HID, HID), F32),
+        ((D, HID), F32),
+        ((HID, HID), F32),
     ]
-    n_in = len(x_parts) + len(own_groups) + len(oth_groups) + 2
-    result = pl.pallas_call(
-        functools.partial(main_kernel, len(x_parts), len(own_groups), count, rows1, rows2),
-        out_shape=(shape((2, events // LANES, LANES), F32), shape((events, D))) + grads + (small, small),
-        in_specs=[SSPEC, SSPEC] + [VSPEC] * n_in,
-        out_specs=(VSPEC,) * (4 + 2 * count),
-        scratch_shapes=[pltpu.VMEM(dims, kind) for dims, kind in scratch],
-        compiler_params=params(),
+    arrays = [*x_parts, *own_groups, *oth_groups, own_pack, oth_pack]
+    staging = [(array.shape, array.dtype) for array in arrays] + [(r.shape, r.dtype) for r in results]
+    mine, theirs, dx, *grads = pl.pallas_call(
+        functools.partial(main_kernel, len(x_parts), len(own_groups), plan, len(arrays), rows1, rows2),
+        out_shape=(pred, pred) + results,
+        in_specs=[SSPEC] + [ASPEC] * len(arrays),
+        out_specs=(VSPEC, VSPEC) + (ASPEC,) * len(results),
+        scratch_shapes=[pltpu.VMEM(dims, kind) for dims, kind in staging + scratch]
+        + [pltpu.SemaphoreType.DMA((len(results),)), pltpu.SemaphoreType.DMA((len(arrays),))],
+        compiler_params=params(50),
         cost_estimate=cost(events * BIG * 196608 * 6, 10e6),
-    )(pos, at, *x_parts, *own_groups, *oth_groups, own_pack, oth_pack)
-    pred, dx = result[:2]
-    return pred, dx, result[2 : 2 + count], result[2 + count : 2 + 2 * count], result[-2], result[-1]
+    )(ids, *arrays)
+    return (mine, theirs), dx, grads[: len(plan)], grads[len(plan) :]
 
 
 def sibling(value):
@@ -588,64 +628,102 @@
 
 
 def stack_kernel(count, *refs):
-    out = refs[-1]
-    for k in range(count):
-        out[k] = refs[k][...]
-
-
-def stacked(pieces, after):
+    out, sems = refs[count], refs[count + 1]
+    copies = [pltpu.make_async_copy(refs[k], out.at[k], sems.at[k]) for k in range(count)]
+    for copy in copies:
+        copy.start()
+    for copy in copies:
+        copy.wait()
+
+
+def stacked(pieces):
     return pl.pallas_call(
         functools.partial(stack_kernel, len(pieces)),
         out_shape=shape((len(pieces),) + pieces[0].shape, pieces[0].dtype),
-        in_specs=[VSPEC] * len(pieces) + [ASPEC] * len(after),
+        in_specs=[ASPEC] * len(pieces),
         out_specs=VSPEC,
-        compiler_params=params(),
+        scratch_shapes=[pltpu.SemaphoreType.DMA((len(pieces),))],
+        compiler_params=params(4),
         cost_estimate=cost(0, 1e6),
-    )(*pieces, *after)
-
-
-def table(me, position, quarter):
-    one, two = 1 + position, 2 - position
-    near = [me ^ (4 * k) for k in range(quarter)]
-    return near + [d ^ two for d in near] + [d ^ one for d in near] + [d ^ one ^ two for d in near]
-
-
-def sum_kernel(count, pieces, *refs):
-    refs = list(refs)
-    for terms, split in zip(count, pieces):
-        arrays = [refs.pop(0) for _ in range(terms)]
-        total = arrays[0][...].astype(F32)
-        for array in arrays[1:]:
-            total = total + array[...].astype(F32)
-        refs.append((total, split))
-    lists = refs[-len(count) :]
-    outs = refs[: -len(count)]
-    for total, split in lists:
-        for cut in split:
-            out = outs.pop(0)
-            out[...] = (total if cut is None else total[cut]).astype(out.dtype)
-
-
-def summed(lists, splits, outs):
-    flat = [array for arrays in lists for array in arrays]
+    )(*pieces)
+
+
+def summed(*terms):
+    total = terms[0].astype(F32)
+    for term in terms[1:]:
+        total = total + term.astype(F32)
+    return total.astype(BF)
+
+
+def small_kernel(one_ref, two_ref, out_ref):
+    out_ref[...] = (one_ref[...].astype(F32) + two_ref[...].astype(F32)).astype(BF)
+
+
+def small_sum(one, two):
+    lead = pl.BlockSpec((SMALL_ROWS, HID), lambda i: (0, 0))
     return pl.pallas_call(
-        functools.partial(sum_kernel, [len(arrays) for arrays in lists], splits),
-        out_shape=tuple(outs),
-        in_specs=[VSPEC] * len(flat),
-        out_specs=(VSPEC,) * len(outs),
-        compiler_params=params(),
+        small_kernel,
+        grid=(1,),
+        out_shape=shape((SMALL_ROWS, HID)),
+        in_specs=[lead, lead],
+        out_specs=lead,
+        compiler_params=params(4),
+        cost_estimate=cost(8e9, 1e6),
+    )(one, two)
+
+
+def tie_kernel(*refs):
+    pass
+
+
+def tied(value, after):
+    return pl.pallas_call(
+        tie_kernel,
+        out_shape=shape(value.shape, value.dtype),
+        in_specs=[ASPEC, ASPEC],
+        out_specs=ASPEC,
+        input_output_aliases={0: 0},
+        compiler_params=params(1),
+        cost_estimate=cost(0, 1),
+    )(value, after)
+
+
+def far_kernel(quarter, rows, keep_ref, got_ref, mid_ref, near_ref, *outs):
+    for k, out in enumerate(outs):
+        here = slice(k * rows, (k + 1) * rows)
+        total = keep_ref[here, :].astype(F32) + got_ref[here, :].astype(F32)
+        at = SMALL_ROWS + k * rows
+        total = total + mid_ref[at : at + rows, :].astype(F32)
+        out[...] = (total + near_ref[here, :].astype(F32)).astype(BF)
+
+
+def far_messages(quarter, rows, keep, got, mid, near):
+    def lead(size):
+        return pl.BlockSpec((size, HID), lambda i: (0, 0))
+
+    size = quarter * rows
+    return pl.pallas_call(
+        functools.partial(far_kernel, quarter, rows),
+        grid=(1,),
+        out_shape=(shape((rows, HID)),) * quarter,
+        in_specs=[lead(size), lead(size), lead(size + SMALL_ROWS), lead(size)],
+        out_specs=(lead(rows),) * quarter,
+        compiler_params=params(12),
         cost_estimate=cost(0, 4e6),
-    )(*flat)
-
-
-def last_kernel(quarter, rows1, rows2, pos_ref, *refs):
-    refs = list(refs)
+    )(keep, got, mid, near)
+
+
+def last_kernel(count, rows1, rows2, ids_ref, *refs):
     total = refs[0][...].astype(F32)
-    tiny = refs[quarter][...].astype(F32)
-    for k in range(1, quarter):
+    for k in range(1, count):
         total = total + refs[k][...].astype(F32)
-        tiny = tiny + refs[quarter + k][...].astype(F32)
-    w1_ref, w2_ref, o1_ref, o2_ref, sg_ref, ss_ref, og_ref, os_ref, gate_ref, t1_ref, t2_ref, t3_ref = refs[2 * quarter :]
+    small = refs[count][...].astype(F32)
+    refs = refs[count + 1 :]
+    if len(refs) > 12:
+        small = small + refs[0][...].astype(F32)
+        refs = refs[1:]
+    w1_ref, w2_ref, o1_ref, o2_ref, sg_ref, ss_ref, og_ref, os_ref, gate_ref, t1_ref, t2_ref, t3_ref = refs
+    tiny = jnp.concatenate([small[:, :LANES], small[:, LANES:]], axis=0)
     cut = SLOTS * rows1
     for s in range(EXPERTS):
         w1_ref[s] = total[s * rows1 : (s + 1) * rows1]
@@ -658,7 +736,7 @@
     for g in range(GATES):
         at = GATE_AT + 4 * g
         gates.append(jnp.concatenate([tiny[at + p : at + p + 1] for p in range(D // LANES)], axis=1))
-    turned = pos_ref[0] != 0
+    turned = ids_ref[0] != 0
     gate_ref[0:1, :] = gates[0]
     gate_ref[1:2, :] = gates[1]
     gate_ref[2:3, :] = jnp.where(turned, gates[3], gates[2])
@@ -674,7 +752,7 @@
     t3_ref[...] = tiny[MISC_AT + 12 : MISC_AT + 13, :TOWER2]
 
 
-def finish(pos, parts, tinies, rows1, rows2):
+def finish(ids, parts, smalls, rows1, rows2):
     outs = (
         shape((EXPERTS, rows1, HID), F32),
         shape((EXPERTS, rows2, HID), F32),
@@ -692,11 +770,11 @@
     return pl.pallas_call(
         functools.partial(last_kernel, len(parts), rows1, rows2),
         out_shape=outs,
-        in_specs=[SSPEC] + [VSPEC] * (2 * len(parts)),
+        in_specs=[SSPEC] + [VSPEC] * (len(parts) + len(smalls)),
         out_specs=(VSPEC,) * len(outs),
-        compiler_params=params(),
+        compiler_params=params(8),
         cost_estimate=cost(0, 4e6),
-    )(pos, *parts, *tinies)
+    )(ids, *parts, *smalls)
 
 
 def per_device(
@@ -717,9 +795,8 @@
     tower_w3,
 ):
     position = lax.axis_index("task")
-    me = lax.axis_index("dp")
     n = lax.axis_size("dp")
-    pos = position.reshape(1)
+    ids = jnp.stack([position, lax.axis_index("dp")]).astype(jnp.int32)
     rows1, rows2 = spec_w1.shape[2], spec_w2.shape[2]
     direct = rows2 % 16 == 0 and n % 4 == 0 and n & (n - 1) == 0
     pack = jnp.concatenate(
@@ -731,7 +808,7 @@
 
     rows = entries.shape[0]
     starts, ends, meta, small = prepare(
-        pos,
+        ids,
         lengths,
         labels,
         spec_gain[0],
@@ -746,64 +823,57 @@
     )
     other_small = sibling(small)
     turned = entries.T
-    x_first = pool(0, 2, pos, meta, starts, ends, turned)
-    x_second = pool(1, 2, pos, meta, starts, ends, turned)
+    x_first = pool(0, 2, ids, meta, starts, ends, turned)
 
     if direct:
-        zc = stacked(far, [x_first])
-        r1 = crossed(zc, (1, 2))
+        zc = stacked(far)
+        r1 = tied(crossed(zc, (1, 2)), x_first)
         r2 = crossed(zc, (2, 1))
-        r3 = crossed(r1, (2, 1))
+        x_second = pool(1, 2, ids, meta, starts, ends, turned, r2)
+        r3 = tied(crossed(r1, (2, 1)), x_second)
         own = [zc, r2, r1, r3]
-        at = jnp.stack([jnp.stack(table(me, position, quarter)), jnp.stack(table(me, 1 - position, quarter))])
-        outs, used1, used2 = (2, n // 2), rows1, rows2
+        plan, used1, used2 = ((2 * quarter, 0), (2 * quarter, 1)), rows1, rows2
     else:
+        x_second = pool(1, 2, ids, meta, starts, ends, turned)
         every = lax.all_gather(pack, "dp", axis=0)
         cut = SLOTS * rows1
         w1 = every[:, :cut].reshape(n, SLOTS, rows1, HID).swapaxes(0, 1).reshape(-1, HID)
         w2 = every[:, cut:].reshape(n, SLOTS, rows2, HID).swapaxes(0, 1).reshape(-1, HID)
         own = [jnp.concatenate([w1, w2], axis=0)[None]]
-        at = jnp.zeros((2, 1), jnp.int32)
-        outs, used1, used2 = (1, 1), D, HID
+        plan, used1, used2 = ((1, 1),), D, HID
     other = [sibling(group) for group in own]
-    pred, dx, own_grads, oth_grads, own_tiny, oth_tiny = layer(
-        pos, at, [x_first, x_second], own, other, small, other_small, outs, used1, used2
+    pred, dx, own_grads, oth_grads = layer(
+        ids, [x_first, x_second], own, other, small, other_small, plan, used1, used2
     )
 
     got = [sibling(grad) for grad in oth_grads[::-1]][::-1]
-    got_tiny = sibling(oth_tiny)
     other_dx = sibling(dx)
+    turned = expand(ids, meta, starts, ends, dx, other_dx, rows)
+    piece = SLOTS * (rows1 + rows2)
     if direct:
-        block = (quarter, SLOTS * (rows1 + rows2), HID)
-        tiny_out = shape((G_ROWS, LANES))
         keep, send = own_grads
-        send, tiny = summed([[send, got[1]], [own_tiny, got_tiny]], [[None], [None]], [shape(send.shape), tiny_out])
-        other_tiny = crossed(tiny, (1, 2))
-        arrived = crossed(send, (1, 2))
-        keep, send, tiny = summed(
-            [[keep, got[0], arrived], [tiny, other_tiny]],
-            [[slice(0, quarter), slice(quarter, 2 * quarter)], [None]],
-            [shape(block), shape(block), tiny_out],
-        )
-        other_tiny = crossed(tiny, (2, 1))
-        arrived = crossed(send, (2, 1))
-        *parts, tiny = summed(
-            [[keep, arrived], [tiny, other_tiny]],
-            [list(range(quarter)), [None]],
-            [shape(block[1:])] * quarter + [tiny_out],
-        )
-        tinies = [tiny] + [flipped(tiny, 4 * k) for k in range(1, quarter)]
+        send = summed(send, got[1])
+        mid = tied(crossed(send, (1, 2)), turned)
+        cut = quarter * piece
+        small = small_sum(send, mid)
+        send = summed(keep[cut:], got[0][cut:], mid[SMALL_ROWS + cut :])
+        near = crossed(send, (2, 1))
+        parts = far_messages(quarter, piece, keep, got[0], mid, near)
+        smalls = [small] + [tied(flipped(small, 4 * k), parts[0]) for k in range(1, quarter)]
         parts = [parts[0]] + [flipped(parts[k], 4 * k) for k in range(1, quarter)]
-        grads = finish(pos, parts, tinies, rows1, rows2)
+        small = summed(*smalls)
+        grads = finish(ids, parts, [small, crossed(small, (2, 1))], rows1, rows2)
     else:
-        whole = own_grads[0][0].astype(F32) + got[0][0].astype(F32)
-        g1 = lax.psum_scatter(whole[: SLOTS * D].reshape(SLOTS, D, HID), "dp", scatter_dimension=1, tiled=True)
-        g2 = lax.psum_scatter(whole[SLOTS * D :].reshape(SLOTS, HID, HID), "dp", scatter_dimension=1, tiled=True)
+        whole = own_grads[0].astype(F32) + got[0].astype(F32)
+        small = lax.psum(whole[:SMALL_ROWS], "dp")
+        whole = whole[SMALL_ROWS:]
+        cut = SLOTS * D
+        g1 = lax.psum_scatter(whole[:cut].reshape(SLOTS, D, HID), "dp", scatter_dimension=1, tiled=True)
+        g2 = lax.psum_scatter(whole[cut:].reshape(SLOTS, HID, HID), "dp", scatter_dimension=1, tiled=True)
         part = jnp.concatenate([g1.reshape(-1, HID), g2.reshape(-1, HID)], axis=0)
-        tiny = lax.psum(own_tiny.astype(F32) + got_tiny.astype(F32), "dp")
-        grads = finish(pos, [part], [tiny], rows1, rows2)
+        grads = finish(ids, [part], [small], rows1, rows2)
     w1, w2, o1, o2, sg, ss, og, os, gate, t1, t2, t3 = grads
-    entry_grads = expand(pos, meta, starts, ends, dx, other_dx, rows).T
+    entry_grads = turned.T
 
     mine = pred[0].reshape(-1)
     theirs = sibling(pred[1]).reshape(-1)

time: 122 us -> 90.7 us (0.74)
  Pallas kernels: 59.4 us -> 40.2 us
  waiting for transfers between devices: 29.1 us -> 18.4 us
  local copies, waits for them, and re-layouts: 6.27 us -> 4 us
  other arithmetic: 1.99 us -> 3.46 us
    ppermute x7 -> x6, waiting for transfers between devices: 26.3 us -> 7.7 us  [crossed(): return lax.ppermute(value, ('task', 'dp'), pairs)]
    pallas_call x2, Pallas kernels: 12 us -> 5.21 us  [pool(): pl.pallas_call(functools.partial(pool_kernel, part * count, count, half_b...]
    ppermute x9, waiting for transfers between devices: 0.02 us -> 6.66 us  [flipped(): return lax.ppermute(value, 'dp', pairs)]
    pallas_call x3 -> x8, Pallas kernels: 6.54 us -> 0.19 us  [the longest x1 0.16 us: far_messages(): pl.pallas_call(functools.partial(far_kernel, quarter, rows), grid=(1,), o...]
    pallas_call x1, Pallas kernels: 11.5 us -> 6.58 us  [expand(): pl.pallas_call(functools.partial(expand_kernel, blocks // 2, group), grid...]
    unnamed x59 -> x24, local copies, waits for them, and re-layouts: 6.08 us -> 4 us
    convert_element_type x0 -> x3, other arithmetic: none -> 1.46 us  [summed(): return total.astype(BF)]
    pallas_call x1, Pallas kernels: 1.72 us -> 0.4 us  [stacked(): pl.pallas_call(functools.partial(stack_kernel, len(pieces)), out_shape=sh...]
  transfers between devices with their start and end apart: 26 -> 24, of which waited for: 6 -> 12; matrix products, arithmetic and copies ran while one was open for 1% -> 3% of each run, Pallas kernels for 26% -> 15%
where the time goes in v3:
time: 90.7 us; the launch traced here: 90.2 us
  Pallas kernels  40.2 us (44%)
  starting transfers between devices  23.3 us (26%)
  waiting for transfers between devices  18.4 us (20%)
  local copies, waits for them, and re-layouts  4 us (4%)
  other arithmetic  3.46 us (4%)
    pallas_call x1, Pallas kernels, layer(): pl.pallas_call(functools.partial(main_kernel, len(x_parts), len(own_group...  24.6 us
    ppermute x9, starting transfers between devices, flipped(): return lax.ppermute(value, 'dp', pairs)  14.6 us
    ppermute x6, waiting for transfers between devices, crossed(): return lax.ppermute(value, ('task', 'dp'), pairs)  7.7 us
    ppermute x9, waiting for transfers between devices, flipped(): return lax.ppermute(value, 'dp', pairs)  6.66 us
    pallas_call x1, Pallas kernels, expand(): pl.pallas_call(functools.partial(expand_kernel, blocks // 2, group), grid...  6.58 us
    ppermute x6, starting transfers between devices, crossed(): return lax.ppermute(value, ('task', 'dp'), pairs)  6.1 us
    pallas_call x2, Pallas kernels, pool(): pl.pallas_call(functools.partial(pool_kernel, part * count, count, half_b...  5.21 us
    ppermute x9, waiting for transfers between devices, sibling(): return lax.ppermute(value, 'task', [(0, 1), (1, 0)])  4.08 us
  transfers between devices with their start and end apart: 24, of which 12 were waited for; matrix products, arithmetic and copies ran while one was open for 3% of the time, Pallas kernels for 15%

profile of v3, /device:TPU:0, one launch (start us, length us, event | category | flops | bytes accessed | tf_op | source)
XLA Modules:
  0.0 90.2 jit_solution(2971406623495725916)
XLA Ops:
  1.5 5.0 %collective-permute-start.2 = (bf16[144,256]{1,0:T(8,128)(2,1)S(1)}, bf16[144,256]{1,0:T(8,128)(2,1)S(1)}, u32[]{:S(2)}, u32[]{:S(2)}) collective-permute-start(bf16[144,256]{1,0:T(8,128)(2,1)S(1)} %pad_maximum_fusion.refs_0_), channel_id=1, source_target_pairs={{0,12},{1,13},{2,14},{3,15},{4,8},{5,9},{6,10},{7,11},{8,4},{9,5},... | collective-permute-start | bytes 221192 | tf_op jit(solution)/shard_map/ppermute | solution.py:621
  7.7 1.9 %shard_map.254 = (s32[104,128]{1,0:T(8,128)}, s32[104,128]{1,0:T(8,128)}, s32[2,256]{1,0:T(2,128)}, bf16[368,128]{1,0:T(8,128)(2,1)}) custom-call(s32[2]{0:T(128)} %pad_add_fusion.ids_ref, s32[1,12288]{1,0:T(1,128)} %len_ref.1, s32[1,1536]{1,0:T(1,128)} %label_ref.1, bf16[2,256]{1,0:T(2,128)(2,1)} %bitcast.63, bf16[2,256]{1,0:T(2,128)(2,1)} %bitcast.64, ...), custom_call_target="tpu_custom_call" | custom-call | flops 1000000000 | bytes 1000000 | tf_op jit(solution)/shard_map/pallas_call | solution.py:148
  9.7 3.0 %collective-permute-done.1.refs_2_ = bf16[144,256]{1,0:T(8,128)(2,1)S(1)} collective-permute-done((bf16[144,256]{1,0:T(8,128)(2,1)S(1)}, bf16[144,256]{1,0:T(8,128)(2,1)S(1)}, u32[]{:S(2)}, u32[]{:S(2)}) %collective-permute-start.1) | collective-permute-done | bytes 73760 | tf_op jit(solution)/shard_map/ppermute | solution.py:621
  13.1 1.6 %collective-permute-start.4 = (bf16[4,144,256]{2,1,0:T(8,128)(2,1)S(1)}, bf16[4,144,256]{2,1,0:T(8,128)(2,1)S(1)}, u32[]{:S(2)}, u32[]{:S(2)}) collective-permute-start(bf16[4,144,256]{2,1,0:T(8,128)(2,1)S(1)} %shard_map.256.refs_2_), channel_id=1, source_target_pairs={{0,1},{1,0},{2,3},{3,2},{4,5},{5,4},{6,7},{7,6},{8,9},{9,8},{10,11... | collective-permute-start | bytes 884744 | tf_op jit(solution)/shard_map/ppermute | solution.py:627
  14.7 1.5 %collective-permute-start.3 = (bf16[4,144,256]{2,1,0:T(8,128)(2,1)S(1)}, bf16[4,144,256]{2,1,0:T(8,128)(2,1)S(1)}, u32[]{:S(2)}, u32[]{:S(2)}) collective-permute-start(bf16[4,144,256]{2,1,0:T(8,128)(2,1)S(1)} %shard_map.256.refs_2_), channel_id=1, source_target_pairs={{0,2},{1,3},{2,0},{3,1},{4,6},{5,7},{6,4},{7,5},{8,10},{9,11},{10,... | collective-permute-start | bytes 884744 | tf_op jit(solution)/shard_map/ppermute | solution.py:627
  18.5 2.7 %shard_map.255.refs_1_.refs_0_ = bf16[384,512]{1,0:T(8,128)(2,1)S(1)} custom-call(s32[2]{0:T(128)S(1)} %copy-done.1, s32[2,256]{1,0:T(2,128)S(1)} %copy-done.9, s32[104,128]{1,0:T(8,128)S(1)} %copy-done.5, s32[104,128]{1,0:T(8,128)S(1)} %copy-done.7, bf16[64,18432]{1,0:T(8,128)(2,1)S(1)} %bitcast.42), custom_call_target="tpu_custom_call" | custom-call | flops 10000000000 | bytes 5000000 | tf_op jit(solution)/shard_map/pallas_call | solution.py:225
  21.4 1.7 %collective-permute-done.4.refs_0_ = bf16[4,144,256]{2,1,0:T(8,128)(2,1)S(1)} collective-permute-done((bf16[4,144,256]{2,1,0:T(8,128)(2,1)S(1)}, bf16[4,144,256]{2,1,0:T(8,128)(2,1)S(1)}, u32[]{:S(2)}, u32[]{:S(2)}) %collective-permute-start.4) | collective-permute-done | bytes 294944 | tf_op jit(solution)/shard_map/ppermute | solution.py:627
  23.4 1.4 %collective-permute-start.7 = (bf16[4,144,256]{2,1,0:T(8,128)(2,1)S(1)}, bf16[4,144,256]{2,1,0:T(8,128)(2,1)S(1)}, u32[]{:S(2)}, u32[]{:S(2)}) collective-permute-start(bf16[4,144,256]{2,1,0:T(8,128)(2,1)S(1)} %collective-permute-done.3.refs_0_.refs_3_), channel_id=1, source_target_pairs={{0,16},{16,0},{1,17},{17,1},{2,18},{18,2},{3,19},{19,3},{4,20},{20... | collective-permute-start | bytes 884744 | tf_op jit(solution)/shard_map/ppermute | solution.py:616
  24.7 2.5 %shard_map.257.refs_1_ = bf16[384,512]{1,0:T(8,128)(2,1)S(1)} custom-call(s32[2]{0:T(128)S(1)} %copy-done.1, s32[2,256]{1,0:T(2,128)S(1)} %copy-done.10, s32[104,128]{1,0:T(8,128)S(1)} %copy-done.5, s32[104,128]{1,0:T(8,128)S(1)} %copy-done.7, bf16[64,18432]{1,0:T(8,128)(2,1)S(1)} %bitcast.43, bf16[4,144,256]{2,1,0:T(8,128)(2,1)S(1)} %collective-permute-done.3.refs_0_.refs_3_), custom_call_target="tpu_custom_call" | custom-call | flops 10000000000 | bytes 5000000 | tf_op jit(solution)/shard_map/pallas_call | solution.py:225
  27.2 2.5 %collective-permute-done.5.refs_0_ = bf16[4,144,256]{2,1,0:T(8,128)(2,1)S(1)} collective-permute-done((bf16[4,144,256]{2,1,0:T(8,128)(2,1)S(1)}, bf16[4,144,256]{2,1,0:T(8,128)(2,1)S(1)}, u32[]{:S(2)}, u32[]{:S(2)}) %collective-permute-start.5) | collective-permute-done | bytes 294944 | tf_op jit(solution)/shard_map/ppermute | solution.py:627
  30.3 1.2 %collective-permute-done.10.refs_11_ = bf16[368,128]{1,0:T(8,128)(2,1)S(1)} collective-permute-done((bf16[368,128]{1,0:T(8,128)(2,1)S(1)}, bf16[368,128]{1,0:T(8,128)(2,1)S(1)}, u32[]{:S(2)}, u32[]{:S(2)}) %collective-permute-start.10) | collective-permute-done | bytes 94240 | tf_op jit(solution)/shard_map/ppermute | solution.py:616
  31.5 24.6 %shard_map.260 = (f32[6,128]{1,0:T(8,128)S(1)}, f32[6,128]{1,0:T(8,128)S(1)}, bf16[768,512]{1,0:T(8,128)(2,1)}, bf16[1152,256]{1,0:T(8,128)(2,1)S(1)}, bf16[1328...) custom-call(s32[2]{0:T(128)S(1)} %copy-done.1, ...), custom_call_target="tpu_custom_call" | custom-call | flops 5435817984 | bytes 10000000 | tf_op jit(solution)/shard_map/pallas_call | solution.py:602
  56.8 1.7 %collective-permute-done.14 = bf16[1328,256]{1,0:T(8,128)(2,1)S(1)} collective-permute-done((bf16[1328,256]{1,0:T(8,128)(2,1)}, bf16[1328,256]{1,0:T(8,128)(2,1)S(1)}, u32[]{:S(2)}, u32[]{:S(2)}) %collective-permute-start.14) | collective-permute-done | bytes 679968 | tf_op jit(solution)/shard_map/ppermute | solution.py:616
  58.5 1.3 %add_convert_fusion.one_ref = bf16[1328,256]{1,0:T(8,128)(2,1)S(1)} fusion(bf16[1328,256]{1,0:T(8,128)(2,1)S(1)} %collective-permute-done.14, bf16[1328,256]{1,0:T(8,128)(2,1)} %get-tuple-element.50), kind=kLoop, calls=%fused_computation | loop fusion | flops 1359872 | bytes 2039808 | tf_op jit(solution)/shard_map/convert_element_type | solution.py:655
  59.8 1.6 %collective-permute-start.15 = (bf16[1328,256]{1,0:T(8,128)(2,1)S(1)}, bf16[1328,256]{1,0:T(8,128)(2,1)S(1)}, u32[]{:S(2)}, u32[]{:S(2)}) collective-permute-start(bf16[1328,256]{1,0:T(8,128)(2,1)S(1)} %add_convert_fusion.one_ref), channel_id=1, source_target_pairs={{0,1},{1,0},{2,3},{3,2},{4,5},{5,4},{6,7},{7,6},{8,9},{9,8},{10,11... | collective-permute-start | bytes 2039816 | tf_op jit(solution)/shard_map/ppermute | solution.py:627
  61.4 6.6 %shard_map.261.refs_1_ = bf16[64,18432]{1,0:T(8,128)(2,1)} custom-call(s32[2]{0:T(128)S(1)} %copy-done.1, s32[2,256]{1,0:T(2,128)S(1)} %copy-done.10, s32[104,128]{1,0:T(8,128)S(1)} %copy-done.6, s32[104,128]{1,0:T(8,128)S(1)} %copy-done.8, bf16[768,512]{1,0:T(8,128)(2,1)S(1)} %copy-done.3, bf16[768,512]{1,0:T(8,128)(2,1)S(1)} %collective-permute-done.12.other_ref), custom_call_target="tpu_custom_call" | custom-call | flops 12000000000 | bytes 6000000 | tf_op jit(solution)/shard_map/pallas_call | solution.py:270
  68.0 2.8 %collective-permute-done.15.refs_0_ = bf16[1328,256]{1,0:T(8,128)(2,1)S(1)} collective-permute-done((bf16[1328,256]{1,0:T(8,128)(2,1)S(1)}, bf16[1328,256]{1,0:T(8,128)(2,1)S(1)}, u32[]{:S(2)}, u32[]{:S(2)}) %collective-permute-start.15) | collective-permute-done | bytes 679968 | tf_op jit(solution)/shard_map/ppermute | solution.py:627
  70.7 1.7 %copy-done = bf16[64,18432]{1,0:T(8,128)(2,1)S(1)} copy-done((bf16[64,18432]{1,0:T(8,128)(2,1)S(1)}, bf16[64,18432]{1,0:T(8,128)(2,1)}, u32[]{:S(2)}) %copy-start) | copy-done | bytes 2359320
  73.0 1.8 %collective-permute-start.22 = (bf16[176,256]{1,0:T(8,128)(2,1)S(1)}, bf16[176,256]{1,0:T(8,128)(2,1)S(1)}, u32[]{:S(2)}, u32[]{:S(2)}) collective-permute-start(bf16[176,256]{1,0:T(8,128)(2,1)S(1)} %shard_map.264), channel_id=1, source_target_pairs={{0,12},{1,13},{2,14},{3,15},{4,8},{5,9},{6,10},{7,11},{8,4},{9,5},... | collective-permute-start | bytes 270344 | tf_op jit(solution)/shard_map/ppermute | solution.py:621
  74.8 2.7 %collective-permute-start.20 = (bf16[176,256]{1,0:T(8,128)(2,1)S(1)}, bf16[176,256]{1,0:T(8,128)(2,1)S(1)}, u32[]{:S(2)}, u32[]{:S(2)}) collective-permute-start(bf16[176,256]{1,0:T(8,128)(2,1)S(1)} %shard_map.264), channel_id=1, source_target_pairs={{0,4},{1,5},{2,6},{3,7},{4,0},{5,1},{6,2},{7,3},{8,12},{9,13},{10,... | collective-permute-start | bytes 270344 | tf_op jit(solution)/shard_map/ppermute | solution.py:621
  79.6 2.1 %collective-permute-start.18 = (bf16[144,256]{1,0:T(8,128)(2,1)S(1)}, bf16[144,256]{1,0:T(8,128)(2,1)S(1)}, u32[]{:S(2)}, u32[]{:S(2)}) collective-permute-start(bf16[144,256]{1,0:T(8,128)(2,1)S(1)} %get-tuple-element.54), channel_id=1, source_target_pairs={{0,8},{1,9},{2,10},{3,11},{4,12},{5,13},{6,14},{7,15},{8,0},{9,1},... | collective-permute-start | bytes 221192 | tf_op jit(solution)/shard_map/ppermute | solution.py:621
  81.7 2.2 %collective-permute-start.19 = (bf16[144,256]{1,0:T(8,128)(2,1)S(1)}, bf16[144,256]{1,0:T(8,128)(2,1)S(1)}, u32[]{:S(2)}, u32[]{:S(2)}) collective-permute-start(bf16[144,256]{1,0:T(8,128)(2,1)S(1)} %get-tuple-element.55), channel_id=1, source_target_pairs={{0,12},{1,13},{2,14},{3,15},{4,8},{5,9},{6,10},{7,11},{8,4},{9,5},... | collective-permute-start | bytes 221192 | tf_op jit(solution)/shard_map/ppermute | solution.py:621
  86.5 2.3 %collective-permute-done.18.refs_2_ = bf16[144,256]{1,0:T(8,128)(2,1)S(1)} collective-permute-done((bf16[144,256]{1,0:T(8,128)(2,1)S(1)}, bf16[144,256]{1,0:T(8,128)(2,1)S(1)}, u32[]{:S(2)}, u32[]{:S(2)}) %collective-permute-start.18) | collective-permute-done | bytes 73760 | tf_op jit(solution)/shard_map/ppermute | solution.py:621
  89.0 1.3 %shard_map.268 = (f32[2,32,256]{2,1,0:T(8,128)}, f32[2,16,256]{2,1,0:T(8,128)}, f32[32,256]{1,0:T(8,128)}, f32[16,256]{1,0:T(8,128)}, f32[2,256]{1,0:T(2,128)}, ...) custom-call(s32[2]{0:T(128)S(1)} %copy-done.1, ...), custom_call_target="tpu_custom_call" | custom-call | bytes 4000000 | tf_op jit(solution)/shard_map/pallas_call | solution.py:770
  (69 shorter events, 11.8 us)
Async XLA Ops:
  1.5 8.2 %collective-permute-start.2 = (bf16[144,256]{1,0:T(8,128)(2,1)S(1)}, bf16[144,256]{1,0:T(8,128)(2,1)S(1)}, u32[]{:S(2)}, u32[]{:S(2)}) collective-permute-start(bf16[144,256]{1,0:T(8,128)(2,1)S(1)} %pad_maximum_fusion.refs_0_), channel_id=1, source_target_pairs={{0,12},{1,13},{2,14},{3,15},{4,8},{5,9},{6,10},{7,11},{8,4},{9,5},... | collective-permute-start | bytes 221192 | tf_op jit(solution)/shard_map/ppermute | solution.py:621
  6.5 6.2 %collective-permute-start.1 = (bf16[144,256]{1,0:T(8,128)(2,1)S(1)}, bf16[144,256]{1,0:T(8,128)(2,1)S(1)}, u32[]{:S(2)}, u32[]{:S(2)}) collective-permute-start(bf16[144,256]{1,0:T(8,128)(2,1)S(1)} %pad_maximum_fusion.refs_0_), channel_id=1, source_target_pairs={{0,8},{1,9},{2,10},{3,11},{4,12},{5,13},{6,14},{7,15},{8,0},{9,1},... | collective-permute-start | bytes 221192 | tf_op jit(solution)/shard_map/ppermute | solution.py:621
  6.5 6.2 %collective-permute-start = (bf16[144,256]{1,0:T(8,128)(2,1)S(1)}, bf16[144,256]{1,0:T(8,128)(2,1)S(1)}, u32[]{:S(2)}, u32[]{:S(2)}) collective-permute-start(bf16[144,256]{1,0:T(8,128)(2,1)S(1)} %pad_maximum_fusion.refs_0_), channel_id=1, source_target_pairs={{0,4},{1,5},{2,6},{3,7},{4,0},{5,1},{6,2},{7,3},{8,12},{9,13},{10,... | collective-permute-start | bytes 221192 | tf_op jit(solution)/shard_map/ppermute | solution.py:621
  13.1 9.9 %collective-permute-start.4 = (bf16[4,144,256]{2,1,0:T(8,128)(2,1)S(1)}, bf16[4,144,256]{2,1,0:T(8,128)(2,1)S(1)}, u32[]{:S(2)}, u32[]{:S(2)}) collective-permute-start(bf16[4,144,256]{2,1,0:T(8,128)(2,1)S(1)} %shard_map.256.refs_2_), channel_id=1, source_target_pairs={{0,1},{1,0},{2,3},{3,2},{4,5},{5,4},{6,7},{7,6},{8,9},{9,8},{10,11... | collective-permute-start | bytes 884744 | tf_op jit(solution)/shard_map/ppermute | solution.py:627
  14.7 8.7 %collective-permute-start.3 = (bf16[4,144,256]{2,1,0:T(8,128)(2,1)S(1)}, bf16[4,144,256]{2,1,0:T(8,128)(2,1)S(1)}, u32[]{:S(2)}, u32[]{:S(2)}) collective-permute-start(bf16[4,144,256]{2,1,0:T(8,128)(2,1)S(1)} %shard_map.256.refs_2_), channel_id=1, source_target_pairs={{0,2},{1,3},{2,0},{3,1},{4,6},{5,7},{6,4},{7,5},{8,10},{9,11},{10,... | collective-permute-start | bytes 884744 | tf_op jit(solution)/shard_map/ppermute | solution.py:627
  21.3 10.2 %collective-permute-start.6 = (bf16[4,144,256]{2,1,0:T(8,128)(2,1)S(1)}, bf16[4,144,256]{2,1,0:T(8,128)(2,1)S(1)}, u32[]{:S(2)}, u32[]{:S(2)}) collective-permute-start(bf16[4,144,256]{2,1,0:T(8,128)(2,1)S(1)} %shard_map.256.refs_2_), channel_id=1, source_target_pairs={{0,16},{16,0},{1,17},{17,1},{2,18},{18,2},{3,19},{19,3},{4,20},{20... | collective-permute-start | bytes 884744 | tf_op jit(solution)/shard_map/ppermute | solution.py:616
  23.0 8.5 %collective-permute-start.8 = (bf16[4,144,256]{2,1,0:T(8,128)(2,1)S(1)}, bf16[4,144,256]{2,1,0:T(8,128)(2,1)S(1)}, u32[]{:S(2)}, u32[]{:S(2)}) collective-permute-start(bf16[4,144,256]{2,1,0:T(8,128)(2,1)S(1)} %shard_map.258.refs_4_), channel_id=1, source_target_pairs={{0,16},{16,0},{1,17},{17,1},{2,18},{18,2},{3,19},{19,3},{4,20},{20... | collective-permute-start | bytes 884744 | tf_op jit(solution)/shard_map/ppermute | solution.py:616
  23.0 6.7 %collective-permute-start.5 = (bf16[4,144,256]{2,1,0:T(8,128)(2,1)S(1)}, bf16[4,144,256]{2,1,0:T(8,128)(2,1)S(1)}, u32[]{:S(2)}, u32[]{:S(2)}) collective-permute-start(bf16[4,144,256]{2,1,0:T(8,128)(2,1)S(1)} %shard_map.258.refs_4_), channel_id=1, source_target_pairs={{0,2},{1,3},{2,0},{3,1},{4,6},{5,7},{6,4},{7,5},{8,10},{9,11},{10,... | collective-permute-start | bytes 884744 | tf_op jit(solution)/shard_map/ppermute | solution.py:627
  23.4 8.1 %collective-permute-start.7 = (bf16[4,144,256]{2,1,0:T(8,128)(2,1)S(1)}, bf16[4,144,256]{2,1,0:T(8,128)(2,1)S(1)}, u32[]{:S(2)}, u32[]{:S(2)}) collective-permute-start(bf16[4,144,256]{2,1,0:T(8,128)(2,1)S(1)} %collective-permute-done.3.refs_0_.refs_3_), channel_id=1, source_target_pairs={{0,16},{16,0},{1,17},{17,1},{2,18},{18,2},{3,19},{19,3},{4,20},{20... | collective-permute-start | bytes 884744 | tf_op jit(solution)/shard_map/ppermute | solution.py:616
  29.7 1.7 %collective-permute-start.9 = (bf16[4,144,256]{2,1,0:T(8,128)(2,1)S(1)}, bf16[4,144,256]{2,1,0:T(8,128)(2,1)S(1)}, u32[]{:S(2)}, u32[]{:S(2)}) collective-permute-start(bf16[4,144,256]{2,1,0:T(8,128)(2,1)S(1)} %shard_map.259.refs_5_), channel_id=1, source_target_pairs={{0,16},{16,0},{1,17},{17,1},{2,18},{18,2},{3,19},{19,3},{4,20},{20... | collective-permute-start | bytes 884744 | tf_op jit(solution)/shard_map/ppermute | solution.py:616
  29.8 1.7 %collective-permute-start.10 = (bf16[368,128]{1,0:T(8,128)(2,1)S(1)}, bf16[368,128]{1,0:T(8,128)(2,1)S(1)}, u32[]{:S(2)}, u32[]{:S(2)}) collective-permute-start(bf16[368,128]{1,0:T(8,128)(2,1)S(1)} %copy-done.4), channel_id=1, source_target_pairs={{0,16},{16,0},{1,17},{17,1},{2,18},{18,2},{3,19},{19,3},{4,20},{20... | collective-permute-start | bytes 282632 | tf_op jit(solution)/shard_map/ppermute | solution.py:616
  56.1 2.4 %collective-permute-start.14 = (bf16[1328,256]{1,0:T(8,128)(2,1)}, bf16[1328,256]{1,0:T(8,128)(2,1)S(1)}, u32[]{:S(2)}, u32[]{:S(2)}) collective-permute-start(bf16[1328,256]{1,0:T(8,128)(2,1)} %get-tuple-element.51), channel_id=1, source_target_pairs={{0,16},{16,0},{1,17},{17,1},{2,18},{18,2},{3,19},{19,3},{4,20},{20... | collective-permute-start | bytes 2039816 | tf_op jit(solution)/shard_map/ppermute | solution.py:616
  56.3 5.0 %collective-permute-start.12 = (bf16[768,512]{1,0:T(8,128)(2,1)}, bf16[768,512]{1,0:T(8,128)(2,1)S(1)}, u32[]{:S(2)}, u32[]{:S(2)}) collective-permute-start(bf16[768,512]{1,0:T(8,128)(2,1)} %get-tuple-element.47.own_ref), channel_id=1, source_target_pairs={{0,16},{16,0},{1,17},{17,1},{2,18},{18,2},{3,19},{19,3},{4,20},{20... | collective-permute-start | bytes 2359304 | tf_op jit(solution)/shard_map/ppermute | solution.py:616
  56.7 15.7 %collective-permute-start.13 = (bf16[1152,256]{1,0:T(8,128)(2,1)}, bf16[1152,256]{1,0:T(8,128)(2,1)S(1)}, u32[]{:S(2)}, u32[]{:S(2)}) collective-permute-start(bf16[1152,256]{1,0:T(8,128)(2,1)} %get-tuple-element.49), channel_id=1, source_target_pairs={{0,16},{16,0},{1,17},{17,1},{2,18},{18,2},{3,19},{19,3},{4,20},{20... | collective-permute-start | bytes 1769480 | tf_op jit(solution)/shard_map/ppermute | solution.py:616
  59.8 10.9 %collective-permute-start.15 = (bf16[1328,256]{1,0:T(8,128)(2,1)S(1)}, bf16[1328,256]{1,0:T(8,128)(2,1)S(1)}, u32[]{:S(2)}, u32[]{:S(2)}) collective-permute-start(bf16[1328,256]{1,0:T(8,128)(2,1)S(1)} %add_convert_fusion.one_ref), channel_id=1, source_target_pairs={{0,1},{1,0},{2,3},{3,2},{4,5},{5,4},{6,7},{7,6},{8,9},{9,8},{10,11... | collective-permute-start | bytes 2039816 | tf_op jit(solution)/shard_map/ppermute | solution.py:627
  72.5 6.8 %collective-permute-start.16 = (bf16[576,256]{1,0:T(8,128)(2,1)S(1)}, bf16[576,256]{1,0:T(8,128)(2,1)S(1)}, u32[]{:S(2)}, u32[]{:S(2)}) collective-permute-start(bf16[576,256]{1,0:T(8,128)(2,1)S(1)} %add_convert_fusion.1), channel_id=1, source_target_pairs={{0,2},{1,3},{2,0},{3,1},{4,6},{5,7},{6,4},{7,5},{8,10},{9,11},{10,... | collective-permute-start | bytes 884744 | tf_op jit(solution)/shard_map/ppermute | solution.py:627
  73.0 8.7 %collective-permute-start.22 = (bf16[176,256]{1,0:T(8,128)(2,1)S(1)}, bf16[176,256]{1,0:T(8,128)(2,1)S(1)}, u32[]{:S(2)}, u32[]{:S(2)}) collective-permute-start(bf16[176,256]{1,0:T(8,128)(2,1)S(1)} %shard_map.264), channel_id=1, source_target_pairs={{0,12},{1,13},{2,14},{3,15},{4,8},{5,9},{6,10},{7,11},{8,4},{9,5},... | collective-permute-start | bytes 270344 | tf_op jit(solution)/shard_map/ppermute | solution.py:621
  74.8 9.2 %collective-permute-start.21 = (bf16[176,256]{1,0:T(8,128)(2,1)S(1)}, bf16[176,256]{1,0:T(8,128)(2,1)S(1)}, u32[]{:S(2)}, u32[]{:S(2)}) collective-permute-start(bf16[176,256]{1,0:T(8,128)(2,1)S(1)} %shard_map.264), channel_id=1, source_target_pairs={{0,8},{1,9},{2,10},{3,11},{4,12},{5,13},{6,14},{7,15},{8,0},{9,1},... | collective-permute-start | bytes 270344 | tf_op jit(solution)/shard_map/ppermute | solution.py:621
  74.8 9.5 %collective-permute-start.20 = (bf16[176,256]{1,0:T(8,128)(2,1)S(1)}, bf16[176,256]{1,0:T(8,128)(2,1)S(1)}, u32[]{:S(2)}, u32[]{:S(2)}) collective-permute-start(bf16[176,256]{1,0:T(8,128)(2,1)S(1)} %shard_map.264), channel_id=1, source_target_pairs={{0,4},{1,5},{2,6},{3,7},{4,0},{5,1},{6,2},{7,3},{8,12},{9,13},{10,... | collective-permute-start | bytes 270344 | tf_op jit(solution)/shard_map/ppermute | solution.py:621
  77.4 1.2 %collective-permute-start.11 = (f32[6,128]{1,0:T(8,128)S(1)}, f32[6,128]{1,0:T(8,128)S(1)}, u32[]{:S(2)}, u32[]{:S(2)}) collective-permute-start(f32[6,128]{1,0:T(8,128)S(1)} %get-tuple-element.46), channel_id=1, source_target_pairs={{0,16},{16,0},{1,17},{17,1},{2,18},{18,2},{3,19},{19,3},{4,20},{20... | collective-permute-start | bytes 9224 | tf_op jit(solution)/shard_map/ppermute | solution.py:616
  79.5 7.1 %collective-permute-start.17 = (bf16[144,256]{1,0:T(8,128)(2,1)S(1)}, bf16[144,256]{1,0:T(8,128)(2,1)S(1)}, u32[]{:S(2)}, u32[]{:S(2)}) collective-permute-start(bf16[144,256]{1,0:T(8,128)(2,1)S(1)} %get-tuple-element.53), channel_id=1, source_target_pairs={{0,4},{1,5},{2,6},{3,7},{4,0},{5,1},{6,2},{7,3},{8,12},{9,13},{10,... | collective-permute-start | bytes 221192 | tf_op jit(solution)/shard_map/ppermute | solution.py:621
  79.6 9.3 %collective-permute-start.18 = (bf16[144,256]{1,0:T(8,128)(2,1)S(1)}, bf16[144,256]{1,0:T(8,128)(2,1)S(1)}, u32[]{:S(2)}, u32[]{:S(2)}) collective-permute-start(bf16[144,256]{1,0:T(8,128)(2,1)S(1)} %get-tuple-element.54), channel_id=1, source_target_pairs={{0,8},{1,9},{2,10},{3,11},{4,12},{5,13},{6,14},{7,15},{8,0},{9,1},... | collective-permute-start | bytes 221192 | tf_op jit(solution)/shard_map/ppermute | solution.py:621
  81.7 7.2 %collective-permute-start.19 = (bf16[144,256]{1,0:T(8,128)(2,1)S(1)}, bf16[144,256]{1,0:T(8,128)(2,1)S(1)}, u32[]{:S(2)}, u32[]{:S(2)}) collective-permute-start(bf16[144,256]{1,0:T(8,128)(2,1)S(1)} %get-tuple-element.55), channel_id=1, source_target_pairs={{0,12},{1,13},{2,14},{3,15},{4,8},{5,9},{6,10},{7,11},{8,4},{9,5},... | collective-permute-start | bytes 221192 | tf_op jit(solution)/shard_map/ppermute | solution.py:621
  84.4 4.6 %collective-permute-start.23 = (bf16[176,256]{1,0:T(8,128)(2,1)S(1)}, bf16[176,256]{1,0:T(8,128)(2,1)S(1)}, u32[]{:S(2)}, u32[]{:S(2)}) collective-permute-start(bf16[176,256]{1,0:T(8,128)(2,1)S(1)} %add_convert_fusion.2.refs_4_), channel_id=1, source_target_pairs={{0,2},{1,3},{2,0},{3,1},{4,6},{5,7},{6,4},{7,5},{8,10},{9,11},{10,... | collective-permute-start | bytes 270344 | tf_op jit(solution)/shard_map/ppermute | solution.py:627
  (11 other events, 49.7 us)

commit v4 on v3

--- a/solution.py
+++ b/solution.py
@@ -25,6 +25,7 @@
 SLOTS = 3
 BIG = 2 * SLOTS
 WIDE = BIG * HID
+PIECE = 32
 BF = jnp.bfloat16
 F32 = jnp.float32
 
@@ -71,25 +72,7 @@
     return [both[:, :LANES], both[:, LANES:]]
 
 
-def prep_kernel(
-    blocks,
-    chunks,
-    ids_ref,
-    len_ref,
-    label_ref,
-    sgain_ref,
-    sshift_ref,
-    ogain_ref,
-    oshift_ref,
-    gate_ref,
-    t1_ref,
-    t2_ref,
-    t3_ref,
-    st_ref,
-    en_ref,
-    meta_ref,
-    small_ref,
-):
+def bags_kernel(blocks, chunks, len_ref, st_ref, en_ref, meta_ref):
     k = lax.broadcasted_iota(jnp.int32, (BAGS, BAGS), 0)
     j = lax.broadcasted_iota(jnp.int32, (BAGS, BAGS), 1)
     natural = (j % EVB) * FEATS + j // EVB
@@ -127,6 +110,21 @@
     first = jnp.sum(reached, axis=0, keepdims=True) - 1.0
     meta_ref[0:1, :] = begin.astype(jnp.int32)
     meta_ref[1:2, :] = first.astype(jnp.int32)
+
+
+def small_kernel(
+    ids_ref,
+    label_ref,
+    sgain_ref,
+    sshift_ref,
+    ogain_ref,
+    oshift_ref,
+    gate_ref,
+    t1_ref,
+    t2_ref,
+    t3_ref,
+    small_ref,
+):
     small_ref[T1_AT : T1_AT + HID, :] = t1_ref[...]
     small_ref[T2_AT : T2_AT + TOWER2, :] = t2_ref[...]
     gate = gate_ref[...].astype(F32)
@@ -142,22 +140,29 @@
     small_ref[pl.ds(GATE_AT, 48), :] = jnp.concatenate(lines, axis=0).astype(BF)
 
 
-def prepare(ids, lengths, labels, spec_gain, spec_shift, shared_gain, shared_shift, gate, t1, t2, t3, chunks):
+def bags(lengths, chunks):
     blocks = lengths.shape[1] // BAGS
     lanes = -(-max(blocks + 1, chunks) // LANES) * LANES
+    bounds = shape((blocks + 8, BAGS), jnp.int32)
     return pl.pallas_call(
-        functools.partial(prep_kernel, blocks, chunks),
-        out_shape=(
-            shape((blocks + 8, BAGS), jnp.int32),
-            shape((blocks + 8, BAGS), jnp.int32),
-            shape((2, lanes), jnp.int32),
-            shape((LABEL_AT + 16, LANES)),
-        ),
-        in_specs=[SSPEC] + [VSPEC] * 10,
-        out_specs=(VSPEC,) * 4,
+        functools.partial(bags_kernel, blocks, chunks),
+        out_shape=(bounds, bounds, shape((2, lanes), jnp.int32)),
+        in_specs=[VSPEC],
+        out_specs=(VSPEC,) * 3,
+        compiler_params=params(4),
+        cost_estimate=cost(1e9, 1e6),
+    )(lengths)
+
+
+def pack_small(ids, *arrays):
+    return pl.pallas_call(
+        small_kernel,
+        out_shape=shape((LABEL_AT + 16, LANES)),
+        in_specs=[SSPEC] + [VSPEC] * len(arrays),
+        out_specs=VSPEC,
         compiler_params=params(56),
         cost_estimate=cost(1e9, 1e6),
-    )(ids, lengths, labels, spec_gain, spec_shift, shared_gain, shared_shift, gate, t1, t2, t3)
+    )(ids, *arrays)
 
 
 def one_hot(starts, ends, base):
@@ -233,9 +238,10 @@
     )(ids, meta, starts, ends, entries, *after)
 
 
-def expand_kernel(half_blocks, group, ids_ref, meta_ref, st_ref, en_ref, own_ref, other_ref, out_ref, rows_ref):
+def expand_kernel(half_blocks, group, ids_ref, meta_ref, st_ref, en_ref, own_ref, other_ref, out_ref, pred_ref, token_ref, rows_ref):
     position = ids_ref[0]
     step = pl.program_id(0)
+    events = half_blocks * EVB
 
     @pl.when(step == 0)
     def _():
@@ -252,6 +258,14 @@
 
             lax.fori_loop(0, half_blocks, place, 0, unroll=12)
         rows_ref[pl.ds(2 * half_blocks * BAGS, BAGS), :] = jnp.zeros((BAGS, EMB), BF)
+        own = own_ref[events : events + 16, : 2 * LANES].astype(F32)
+        other = other_ref[events : events + 16, : 2 * LANES].astype(F32)
+        mine = (own[:, :LANES] + own[:, LANES:])[:8]
+        theirs = (other[:, :LANES] + other[:, LANES:])[8:]
+        halves = (jnp.where(position == 0, mine, theirs), jnp.where(position == 0, theirs, mine))
+        tiles = events // LANES
+        token_ref[...] = mine
+        pred_ref[...] = jnp.concatenate([half[k : k + 1] for half in halves for k in range(tiles)], axis=1)
 
     for u in range(group):
         c = step * group + u
@@ -270,21 +284,47 @@
     return pl.pallas_call(
         functools.partial(expand_kernel, blocks // 2, group),
         grid=(chunks // group,),
-        out_shape=shape((EMB, rows)),
+        out_shape=(shape((EMB, rows)), shape((1, blocks * EVB), F32), shape((8, LANES), F32)),
         in_specs=[SSPEC, SSPEC, VSPEC, VSPEC, VSPEC, VSPEC],
-        out_specs=pl.BlockSpec((EMB, group * ROWS), lambda i: (0, i)),
+        out_specs=(
+            pl.BlockSpec((EMB, group * ROWS), lambda i: (0, i)),
+            pl.BlockSpec((1, blocks * EVB), lambda i: (0, 0)),
+            pl.BlockSpec((8, LANES), lambda i: (0, 0)),
+        ),
         scratch_shapes=[pltpu.VMEM(((blocks + 1) * BAGS, EMB), BF)],
         compiler_params=params(24, dimension_semantics=("arbitrary",)),
         cost_estimate=cost(12e9, 6e6),
     )(ids, meta, starts, ends, own, other)
 
 
+def gelu_twice(v):
+    cube = K1 * (v * v)
+    bend = jnp.tanh(v * (cube + K0))
+    rise = 1.0 + bend
+    act = v * rise
+    slope = rise + act * (1.0 - bend) * (3.0 * cube + K0)
+    return act, slope
+
+
 def gelu_both(v):
-    square = v * v
-    half = 0.5 * jnp.tanh(v * (K1 * square + K0)) + 0.5
-    act = v * half
-    slope = half + act * (1.0 - half) * (6.0 * K1 * square + 2.0 * K0)
-    return act, slope
+    act, slope = gelu_twice(v)
+    return 0.5 * act, 0.5 * slope
+
+
+def wide(block, row):
+    return jnp.concatenate([block[row : row + 1, :], block[row + 1 : row + 2, :]], axis=1)
+
+
+def by_eight(value):
+    return jnp.sum(value.reshape(-1, 8, value.shape[-1]), axis=0)
+
+
+def plus(total, term):
+    return term if total is None else total + term
+
+
+def pieces_of(m):
+    return [slice(at, at + PIECE) for at in range(m * HID, (m + 1) * HID, PIECE)]
 
 
 def col_sum(value):
@@ -299,27 +339,16 @@
     lax.fori_loop(0, events // LANES, step, 0)
 
 
-def main_kernel(xs, groups, plan, staged, rows1, rows2, ids_ref, *refs):
+def main_kernel(xs, groups, plan, rows1, rows2, ids_ref, *refs):
     refs = list(refs)
     take = lambda n: [refs.pop(0) for _ in range(n)]
-    inputs = take(xs + 2 * groups + 2)
-    preds = take(2)
-    outputs = take(1 + 2 * len(plan))
-    staging = take(len(inputs))
-    sources = [pltpu.make_async_copy(a, b, refs[-1].at[k]) for k, (a, b) in enumerate(zip(inputs, staging))]
-    for copy in sources:
-        copy.start()
-    x_parts = [(staging[k], sources[k]) for k in range(xs)]
-    whole = list(zip(staging, sources))[xs : xs + 2 * groups]
-    own_groups, oth_groups = whole[:groups], whole[groups:]
-    packs = staging[-2:]
-    results = take(len(outputs))
-    targets = [pltpu.make_async_copy(a, b, refs[-2].at[k]) for k, (a, b) in enumerate(zip(results, outputs))]
-    dx_ref = results[0]
-    own_outs, oth_outs = results[1 : 1 + len(plan)], results[1 + len(plan) :]
-    own_sent, oth_sent = targets[1 : 1 + len(plan)], targets[1 + len(plan) :]
+    x_parts = take(xs)
+    own_groups, oth_groups = take(groups), take(groups)
+    packs = take(2)
+    (dx_ref,) = take(1)
+    own_outs, oth_outs = take(len(plan)), take(len(plan))
     x_ref, wc_ref, w2_ref, gain_ref, third_ref, lab_ref, pc_ref, pb_ref, s2_ref, y_ref, h_ref, e_ref, fc_ref = take(13)
-    lg_ref, prob_ref, q_ref, pt_ref, u1_ref, p4_ref, e2_ref, e1_ref, du_ref, dm_ref, dmb_ref, acc_ref, acc3_ref, g1_ref, g2_ref = take(15)
+    scale_ref, lg_ref, prob_ref, q_ref, pt_ref, u1_ref, p4_ref, e2_ref, e1_ref, du_ref, dm_ref, dmb_ref, ds_ref, dn_ref, acc3_ref, pred_ref, g1_ref, g2_ref = take(18)
     position = ids_ref[0]
     events = x_ref.shape[1]
     quarter = D // rows1 // 4
@@ -342,22 +371,18 @@
         )
 
     size = events // xs
-    for k, (piece, copy) in enumerate(x_parts):
-        copy.wait()
+    for k, piece in enumerate(x_parts):
         x_ref[:, k * size : (k + 1) * size] = piece[...].T
     for t, whole in enumerate((own_groups, oth_groups)):
         p = 0
-        for group, copy in whole:
-            copy.wait()
+        for group in whole:
             for g in range(group.shape[0]):
                 one, two = rows_of(t, p)
                 p += 1
                 for s in range(SLOTS):
                     wc_ref[one, part(t * SLOTS + s)] = group[g, s * rows1 : (s + 1) * rows1, :]
                     low = SLOTS * rows1 + s * rows2
-                    w2_ref[t * SLOTS + s, two, :] = group[g, low : low + rows2, :]
-    sources[-2].wait()
-    sources[-1].wait()
+                    w2_ref[t * SLOTS + s, two, :] = (0.5 * group[g, low : low + rows2, :].astype(F32)).astype(BF)
     lines = []
     for t in range(2):
         block = packs[t][GATE_AT : GATE_AT + 16, :].astype(F32)
@@ -369,10 +394,10 @@
     gates = jnp.concatenate(lines, axis=0).astype(BF)
     wc_ref[:, WIDE:] = jnp.concatenate([gates, jnp.zeros((LANES - 16, D), BF)], axis=0).T
     fc_ref[WIDE:, :] = jnp.zeros((LANES, events), BF)
-    acc_ref[...] = jnp.zeros_like(acc_ref)
     acc3_ref[...] = jnp.zeros_like(acc3_ref)
+    miscs = [packs[t][MISC_AT : MISC_AT + 16, :].astype(F32) for t in range(2)]
     for t in range(2):
-        misc = packs[t][MISC_AT : MISC_AT + 16, :].astype(F32)
+        misc = miscs[t]
         for s in range(SLOTS):
             for kind in range(2):
                 for half in range(2):
@@ -389,29 +414,51 @@
 
     def first_gelu(j, here):
         for m in range(BIG):
-            act, slope = gelu_both(pc_ref[part(m), here])
-            pc_ref[part(m), here] = slope
-            h_ref[part(m), here] = act.astype(BF)
+            for rows in pieces_of(m):
+                act, slope = gelu_twice(pc_ref[rows, here])
+                pc_ref[rows, here] = slope
+                h_ref[rows, here] = act.astype(BF)
 
     lane_tiles(events, first_gelu)
     for m in range(BIG):
         pb_ref[part(m), :] = tn(w2_ref[m], h_ref[part(m), :])
 
     def second_gelu(j, here):
+        def front(m):
+            total = None
+            for rows in pieces_of(m):
+                act, slope = gelu_twice(pb_ref[rows, here])
+                pb_ref[rows, here] = act
+                s2_ref[rows, here] = slope
+                total = plus(total, by_eight(act))
+            return col_sum(total) * (1.0 / HID)
+
+        def back(m, mean):
+            total = None
+            for rows in pieces_of(m):
+                centred = pb_ref[rows, here] - mean
+                pb_ref[rows, here] = centred
+                total = plus(total, by_eight(centred * centred))
+            scale = lax.rsqrt(col_sum(total) * (1.0 / HID) + 4.0 * EPSILON)
+            scale_ref[m : m + 1, here] = scale
+            for rows in pieces_of(m):
+                normed = pb_ref[rows, here] * scale
+                pb_ref[rows, here] = normed
+                out = normed * gain_ref[rows, :] + gain_ref[slice(WIDE + rows.start, WIDE + rows.stop), :]
+                if m % SLOTS == SLOTS - 1:
+                    out = out.astype(BF).astype(F32)
+                y_ref[rows, here] = out
+
+        means = front(0)
         for m in range(BIG):
-            act, slope = gelu_both(pb_ref[part(m), here])
-            centred = act - col_sum(act) * (1.0 / HID)
-            scale = lax.rsqrt(col_sum(centred * centred) * (1.0 / HID) + EPSILON)
-            normed = centred * scale
-            pb_ref[part(m), here] = normed
-            s2_ref[part(m), here] = slope * scale
-            out = normed * gain_ref[part(m), :] + gain_ref[part(BIG + m), :]
-            if m % SLOTS == SLOTS - 1:
-                out = out.astype(BF).astype(F32)
-            y_ref[part(m), here] = out
+            ahead = front(m + 1) if m + 1 < BIG else None
+            back(m, means)
+            means = ahead
 
     lane_tiles(events, second_gelu)
     orders = [(t * SLOTS, t * SLOTS + 1, t * SLOTS + 2, (1 - t) * SLOTS + 2) for t in range(2)]
+
+    prob_ref[...] = jnp.ones_like(prob_ref)
 
     def mix(j, here):
         for t in range(2):
@@ -450,7 +497,7 @@
         for t in range(2):
             logit = col_sum(product[t * TOWER2 : (t + 1) * TOWER2])
             prediction = 1.0 / (1.0 + jnp.exp(-logit))
-            preds[t][pl.ds(j, 1), :] = prediction
+            pred_ref[pl.ds(8 * t + j, 1), :] = prediction
             label = lab_ref[pl.ds(t * 16 + position * (events // LANES) + j, 1), :]
             deltas.append(jnp.broadcast_to(prediction - label, (TOWER2, LANES)))
         delta = jnp.concatenate(deltas, axis=0)
@@ -468,34 +515,68 @@
 
     lane_tiles(events, tower_back)
     for t in range(2):
-        dm_ref[part(t), :] = nn(packs[t][T1_AT : T1_AT + HID, :], e1_ref[t * TOWER1 : (t + 1) * TOWER1, :])
+        mixed = nn(packs[t][T1_AT : T1_AT + HID, :], e1_ref[t * TOWER1 : (t + 1) * TOWER1, :])
+        dm_ref[part(t), :] = mixed
+        dmb_ref[part(t), :] = mixed.astype(BF)
+        rows = [wide(miscs[t], 2 * (SLOTS + s)) for s in range(EXPERTS)] + [jnp.zeros((8 - EXPERTS, HID), F32)]
+        ds_ref[8 * t : 8 * t + 8, :] = nn(jnp.concatenate(rows, axis=0).astype(BF), dmb_ref[part(t), :])
 
     def mix_back(j, here):
+        probs = [[prob_ref[8 * t + k : 8 * t + k + 1, here] for k in range(GATES)] for t in range(2)]
+        d_probs = [[None] * GATES for _ in range(2)]
+        for t in range(2):
+            for k in range(EXPERTS, GATES):
+                total = None
+                for mine, rows in zip(pieces_of(t), pieces_of(orders[t][k])):
+                    total = plus(total, by_eight(dm_ref[mine, here] * y_ref[rows, here]))
+                d_probs[t][k] = col_sum(total)
+
+        def turned_gain(m, rows):
+            t, s = divmod(m, SLOTS)
+            mine = slice(rows.start - m * HID + t * HID, rows.stop - m * HID + t * HID)
+            up = dm_ref[mine, here]
+            if s == SLOTS - 1:
+                theirs = slice(mine.start + (1 - 2 * t) * HID, mine.stop + (1 - 2 * t) * HID)
+                up = probs[t][s] * up + probs[1 - t][SLOTS] * dm_ref[theirs, here]
+            return up * gain_ref[rows, :]
+
+        def front(m):
+            one, two = None, None
+            for rows in pieces_of(m):
+                d_normed = turned_gain(m, rows)
+                y_ref[rows, here] = d_normed
+                product = d_normed * pb_ref[rows, here]
+                dn_ref[rows, here] = product.astype(BF)
+                one = plus(one, by_eight(d_normed))
+                two = plus(two, by_eight(product))
+            return col_sum(one), col_sum(two)
+
+        def back(m, one, two):
+            t, s = divmod(m, SLOTS)
+            one, two = one * (1.0 / HID), two * (1.0 / HID)
+            outer = scale_ref[m : m + 1, here]
+            if s < EXPERTS:
+                outer = outer * probs[t][s]
+            for rows in pieces_of(m):
+                inner = y_ref[rows, here] - one - pb_ref[rows, here] * two
+                e_ref[rows, here] = (s2_ref[rows, here] * outer * inner).astype(BF)
+
+        sums = front(0)
+        for m in range(BIG):
+            ahead = front(m + 1) if m + 1 < BIG else None
+            t, s = divmod(m, SLOTS)
+            if s < EXPERTS:
+                d_probs[t][s] = sums[1] + ds_ref[8 * t + s : 8 * t + s + 1, here]
+            back(m, *sums)
+            sums = ahead
         codes = []
-        probs = [[prob_ref[8 * t + k : 8 * t + k + 1, here] for k in range(GATES)] for t in range(2)]
         for t in range(2):
-            mixed = dm_ref[part(t), here]
-            dmb_ref[part(t), here] = mixed.astype(BF)
-            d_prob = [col_sum(mixed * y_ref[part(orders[t][k]), here]) for k in range(GATES)]
-            weighted = probs[t][0] * d_prob[0]
+            weighted = probs[t][0] * d_probs[t][0]
             for k in range(1, GATES):
-                weighted = weighted + probs[t][k] * d_prob[k]
-            codes += [probs[t][k] * (d_prob[k] - weighted) for k in range(GATES)]
+                weighted = weighted + probs[t][k] * d_probs[t][k]
+            codes += [probs[t][k] * (d_probs[t][k] - weighted) for k in range(GATES)]
             codes.append(jnp.zeros((8 - GATES, LANES), F32))
         fc_ref[WIDE : WIDE + 16, here] = jnp.concatenate(codes, axis=0).astype(BF)
-        for m in range(BIG):
-            t, s = divmod(m, SLOTS)
-            up = probs[t][s] * dm_ref[part(t), here]
-            if s == SLOTS - 1:
-                up = up + probs[1 - t][SLOTS] * dm_ref[part(1 - t), here]
-            normed = pb_ref[part(m), here]
-            up_normed = up * normed
-            acc_ref[part(m), :] += up_normed
-            gain = gain_ref[part(m), :]
-            d_normed = up * gain
-            mean_one = col_sum(d_normed) * (1.0 / HID)
-            mean_two = col_sum(d_normed * normed) * (1.0 / HID)
-            e_ref[part(m), here] = (s2_ref[part(m), here] * (d_normed - mean_one - normed * mean_two)).astype(BF)
 
     lane_tiles(events, mix_back)
     for m in range(BIG):
@@ -506,14 +587,17 @@
             fc_ref[part(m), here] = (pc_ref[part(m), here] * s2_ref[part(m), here]).astype(BF)
 
     lane_tiles(events, first_back)
-    dx_ref[...] = nn(wc_ref[...], fc_ref[...]).astype(BF).T
-    targets[0].start()
+    dx_ref[:events, :] = nn(wc_ref[...], fc_ref[...]).astype(BF).T
+    pred = pred_ref[...]
+    high = pred.astype(BF)
+    low = (pred - high.astype(F32)).astype(BF)
+    dx_ref[events:, :] = jnp.concatenate([high, low, high, low], axis=1)
 
     gate_grad = nt(fc_ref[WIDE : WIDE + 16, :], x_ref[...])
     weights = prob_ref[...].astype(BF)
     shifts = [nt(weights, dmb_ref[part(t), :]) for t in range(2)]
     third_grad = col_sum(acc3_ref[...].T)
-    for t, results, sent in ((1, oth_outs, oth_sent), (0, own_outs, own_sent)):
+    for t, results in enumerate((own_outs, oth_outs)):
         for s in range(SLOTS):
             m = t * SLOTS + s
             g1_ref[...] = nt(x_ref[...], fc_ref[part(m), :])
@@ -526,7 +610,7 @@
                     at = g * SLOTS * (rows1 + rows2) + (SMALL_ROWS if small_first else 0)
                     out[at + s * rows1 : at + (s + 1) * rows1, :] = g1_ref[one, :].astype(BF)
                     at = at + SLOTS * rows1 + s * rows2
-                    out[at : at + rows2, :] = g2_ref[two, :].astype(BF)
+                    out[at : at + rows2, :] = (0.5 * g2_ref[two, :]).astype(BF)
         tower = slice(t * TOWER1, (t + 1) * TOWER1)
         half = slice(t * TOWER2, (t + 1) * TOWER2)
         lines = []
@@ -534,9 +618,9 @@
             row = gate_grad[8 * t + g : 8 * t + g + 1, :]
             lines += [row[:, p * LANES : (p + 1) * LANES] for p in range(D // LANES)]
         for s in range(SLOTS):
-            for k in range(2):
-                at = (t * SLOTS + s) * HID + k * LANES
-                lines.append(col_sum(acc_ref[at : at + LANES, :].T))
+            at = 8 * t + (s if s < EXPERTS else GATES)
+            row = nt(weights, dn_ref[part(t * SLOTS + s), :])[at : at + 1, :] / wide(miscs[t], 2 * s)
+            lines += [row[:, :LANES], row[:, LANES:]]
         for s in range(SLOTS):
             row = shifts[t][8 * t + s : 8 * t + s + 1, :]
             if s == SLOTS - 1:
@@ -553,20 +637,16 @@
             axis=0,
         )
         small = jnp.concatenate([small[:SMALL_ROWS], small[SMALL_ROWS:]], axis=1).astype(BF)
-        for out, copy, (_, small_first) in list(zip(results, sent, plan))[::-1]:
+        for out, (_, small_first) in zip(results, plan):
             if small_first:
                 out[:SMALL_ROWS, :] = small
-            copy.start()
-    for copy in targets:
-        copy.wait()
 
 
 def layer(ids, x_parts, own_groups, oth_groups, own_pack, oth_pack, plan, rows1, rows2):
     events = sum(part.shape[0] for part in x_parts)
     rows = SLOTS * (rows1 + rows2)
     grads = tuple(shape((pieces * rows + small * SMALL_ROWS, HID)) for pieces, small in plan)
-    pred = shape((events // LANES, LANES), F32)
-    results = (shape((events, D)),) + grads + grads
+    results = (shape((events + 16, D)),) + grads + grads
     scratch = [
         ((D, events), BF),
         ((D, WIDE + LANES), BF),
@@ -581,6 +661,7 @@
         ((WIDE, events), BF),
         ((WIDE, events), BF),
         ((WIDE + LANES, events), BF),
+        ((8, events), F32),
         ((16, events), F32),
         ((16, events), F32),
         ((2 * HID, events), BF),
@@ -592,24 +673,24 @@
         ((2 * TOWER1, events), F32),
         ((2 * HID, events), F32),
         ((2 * HID, events), BF),
-        ((WIDE, LANES), F32),
+        ((16, events), F32),
+        ((WIDE, events), BF),
         ((2 * TOWER2, LANES), F32),
+        ((16, LANES), F32),
         ((D, HID), F32),
         ((HID, HID), F32),
     ]
     arrays = [*x_parts, *own_groups, *oth_groups, own_pack, oth_pack]
-    staging = [(array.shape, array.dtype) for array in arrays] + [(r.shape, r.dtype) for r in results]
-    mine, theirs, dx, *grads = pl.pallas_call(
-        functools.partial(main_kernel, len(x_parts), len(own_groups), plan, len(arrays), rows1, rows2),
-        out_shape=(pred, pred) + results,
-        in_specs=[SSPEC] + [ASPEC] * len(arrays),
-        out_specs=(VSPEC, VSPEC) + (ASPEC,) * len(results),
-        scratch_shapes=[pltpu.VMEM(dims, kind) for dims, kind in staging + scratch]
-        + [pltpu.SemaphoreType.DMA((len(results),)), pltpu.SemaphoreType.DMA((len(arrays),))],
-        compiler_params=params(50),
+    dx, *grads = pl.pallas_call(
+        functools.partial(main_kernel, len(x_parts), len(own_groups), plan, rows1, rows2),
+        out_shape=results,
+        in_specs=[SSPEC] + [VSPEC] * len(arrays),
+        out_specs=(VSPEC,) * len(results),
+        scratch_shapes=[pltpu.VMEM(dims, kind) for dims, kind in scratch],
+        compiler_params=params(46),
         cost_estimate=cost(events * BIG * 196608 * 6, 10e6),
     )(ids, *arrays)
-    return (mine, theirs), dx, grads[: len(plan)], grads[len(plan) :]
+    return dx, grads[: len(plan)], grads[len(plan) :]
 
 
 def sibling(value):
@@ -628,7 +709,7 @@
 
 
 def stack_kernel(count, *refs):
-    out, sems = refs[count], refs[count + 1]
+    out, sems = refs[-2:]
     copies = [pltpu.make_async_copy(refs[k], out.at[k], sems.at[k]) for k in range(count)]
     for copy in copies:
         copy.start()
@@ -655,14 +736,14 @@
     return total.astype(BF)
 
 
-def small_kernel(one_ref, two_ref, out_ref):
+def small_sum_kernel(one_ref, two_ref, out_ref):
     out_ref[...] = (one_ref[...].astype(F32) + two_ref[...].astype(F32)).astype(BF)
 
 
 def small_sum(one, two):
     lead = pl.BlockSpec((SMALL_ROWS, HID), lambda i: (0, 0))
     return pl.pallas_call(
-        small_kernel,
+        small_sum_kernel,
         grid=(1,),
         out_shape=shape((SMALL_ROWS, HID)),
         in_specs=[lead, lead],
@@ -713,23 +794,44 @@
     )(keep, got, mid, near)
 
 
-def last_kernel(count, rows1, rows2, ids_ref, *refs):
+def last_kernel(count, rows1, rows2, *refs):
     total = refs[0][...].astype(F32)
     for k in range(1, count):
         total = total + refs[k][...].astype(F32)
-    small = refs[count][...].astype(F32)
-    refs = refs[count + 1 :]
-    if len(refs) > 12:
-        small = small + refs[0][...].astype(F32)
-        refs = refs[1:]
-    w1_ref, w2_ref, o1_ref, o2_ref, sg_ref, ss_ref, og_ref, os_ref, gate_ref, t1_ref, t2_ref, t3_ref = refs
-    tiny = jnp.concatenate([small[:, :LANES], small[:, LANES:]], axis=0)
+    w1_ref, w2_ref, o1_ref, o2_ref, token_ref = refs[count:]
+    token_ref[...] = total[:8, :LANES]
     cut = SLOTS * rows1
     for s in range(EXPERTS):
         w1_ref[s] = total[s * rows1 : (s + 1) * rows1]
         w2_ref[s] = total[cut + s * rows2 : cut + (s + 1) * rows2]
     o1_ref[...] = total[EXPERTS * rows1 : cut]
     o2_ref[...] = total[cut + EXPERTS * rows2 :]
+
+
+def finish(parts, rows1, rows2):
+    outs = (
+        shape((EXPERTS, rows1, HID), F32),
+        shape((EXPERTS, rows2, HID), F32),
+        shape((rows1, HID), F32),
+        shape((rows2, HID), F32),
+        shape((8, LANES), F32),
+    )
+    return pl.pallas_call(
+        functools.partial(last_kernel, len(parts), rows1, rows2),
+        out_shape=outs,
+        in_specs=[VSPEC] * len(parts),
+        out_specs=(VSPEC,) * len(outs),
+        compiler_params=params(8),
+        cost_estimate=cost(10e9, 2e6),
+    )(*parts)
+
+
+def last_small_kernel(count, ids_ref, *refs):
+    small = refs[0][...].astype(F32)
+    for k in range(1, count):
+        small = small + refs[k][...].astype(F32)
+    sg_ref, ss_ref, og_ref, os_ref, gate_ref, t1_ref, t2_ref, t3_ref = refs[-8:]
+    tiny = jnp.concatenate([small[:, :LANES], small[:, LANES:]], axis=0)
     t1_ref[...] = tiny[T1_AT : T1_AT + HID]
     t2_ref[...] = tiny[T2_AT : T2_AT + TOWER2]
     gates = []
@@ -752,12 +854,8 @@
     t3_ref[...] = tiny[MISC_AT + 12 : MISC_AT + 13, :TOWER2]
 
 
-def finish(ids, parts, smalls, rows1, rows2):
+def finish_small(ids, parts, after):
     outs = (
-        shape((EXPERTS, rows1, HID), F32),
-        shape((EXPERTS, rows2, HID), F32),
-        shape((rows1, HID), F32),
-        shape((rows2, HID), F32),
         shape((EXPERTS, HID), F32),
         shape((EXPERTS, HID), F32),
         shape((1, HID), F32),
@@ -768,13 +866,13 @@
         shape((1, TOWER2), F32),
     )
     return pl.pallas_call(
-        functools.partial(last_kernel, len(parts), rows1, rows2),
+        functools.partial(last_small_kernel, len(parts)),
         out_shape=outs,
-        in_specs=[SSPEC] + [VSPEC] * (len(parts) + len(smalls)),
+        in_specs=[SSPEC] + [VSPEC] * len(parts) + [ASPEC],
         out_specs=(VSPEC,) * len(outs),
         compiler_params=params(8),
-        cost_estimate=cost(0, 4e6),
-    )(ids, *parts, *smalls)
+        cost_estimate=cost(0, 2e6),
+    )(ids, *parts, after)
 
 
 def per_device(
@@ -807,9 +905,9 @@
         far = [pack] + [flipped(pack, 4 * k) for k in range(1, quarter)]
 
     rows = entries.shape[0]
-    starts, ends, meta, small = prepare(
+    starts, ends, meta = bags(lengths, rows // ROWS)
+    small = pack_small(
         ids,
-        lengths,
         labels,
         spec_gain[0],
         spec_shift[0],
@@ -819,11 +917,10 @@
         tower_w1[0],
         tower_w2[0].T,
         tower_w3,
-        rows // ROWS,
     )
     other_small = sibling(small)
     turned = entries.T
-    x_first = pool(0, 2, ids, meta, starts, ends, turned)
+    x_first = pool(0, 2, ids, meta, starts, ends, turned, small)
 
     if direct:
         zc = stacked(far)
@@ -841,19 +938,18 @@
         w2 = every[:, cut:].reshape(n, SLOTS, rows2, HID).swapaxes(0, 1).reshape(-1, HID)
         own = [jnp.concatenate([w1, w2], axis=0)[None]]
         plan, used1, used2 = ((1, 1),), D, HID
-    other = [sibling(group) for group in own]
-    pred, dx, own_grads, oth_grads = layer(
-        ids, [x_first, x_second], own, other, small, other_small, plan, used1, used2
+    dx, own_grads, oth_grads = layer(
+        ids, [x_first, x_second], own, [sibling(group) for group in own], small, other_small, plan, used1, used2
     )
 
     got = [sibling(grad) for grad in oth_grads[::-1]][::-1]
     other_dx = sibling(dx)
-    turned = expand(ids, meta, starts, ends, dx, other_dx, rows)
+    turned, predictions, expanded = expand(ids, meta, starts, ends, dx, other_dx, rows)
     piece = SLOTS * (rows1 + rows2)
     if direct:
         keep, send = own_grads
         send = summed(send, got[1])
-        mid = tied(crossed(send, (1, 2)), turned)
+        mid = tied(crossed(send, (1, 2)), expanded)
         cut = quarter * piece
         small = small_sum(send, mid)
         send = summed(keep[cut:], got[0][cut:], mid[SMALL_ROWS + cut :])
@@ -862,7 +958,8 @@
         smalls = [small] + [tied(flipped(small, 4 * k), parts[0]) for k in range(1, quarter)]
         parts = [parts[0]] + [flipped(parts[k], 4 * k) for k in range(1, quarter)]
         small = summed(*smalls)
-        grads = finish(ids, parts, [small, crossed(small, (2, 1))], rows1, rows2)
+        *grads, summed_up = finish(parts, rows1, rows2)
+        grads += finish_small(ids, [small, crossed(small, (2, 1))], summed_up)
     else:
         whole = own_grads[0].astype(F32) + got[0].astype(F32)
         small = lax.psum(whole[:SMALL_ROWS], "dp")
@@ -871,15 +968,10 @@
         g1 = lax.psum_scatter(whole[:cut].reshape(SLOTS, D, HID), "dp", scatter_dimension=1, tiled=True)
         g2 = lax.psum_scatter(whole[cut:].reshape(SLOTS, HID, HID), "dp", scatter_dimension=1, tiled=True)
         part = jnp.concatenate([g1.reshape(-1, HID), g2.reshape(-1, HID)], axis=0)
-        grads = finish(ids, [part], [small], rows1, rows2)
+        *grads, summed_up = finish([part], rows1, rows2)
+        grads += finish_small(ids, [small], summed_up)
     w1, w2, o1, o2, sg, ss, og, os, gate, t1, t2, t3 = grads
     entry_grads = turned.T
-
-    mine = pred[0].reshape(-1)
-    theirs = sibling(pred[1]).reshape(-1)
-    predictions = jnp.where(
-        position == 0, jnp.concatenate([mine, theirs]), jnp.concatenate([theirs, mine])
-    )[None]
     return (
         predictions,
         entry_grads,

time: 90.7 us -> 84.6 us (0.933)
  Pallas kernels: 40.2 us -> 37.6 us
  local copies, waits for them, and re-layouts: 4 us -> 1.7 us
  starting transfers between devices: 23.3 us -> 25.1 us
  other arithmetic: 3.46 us -> 1.79 us
  waiting for transfers between devices: 18.4 us -> 17.3 us
    pallas_call x1, Pallas kernels: 24.6 us -> 21 us  [layer(): pl.pallas_call(functools.partial(main_kernel, len(x_parts), len(own_group...]
    ppermute x6, waiting for transfers between devices: 7.7 us -> 10.1 us  [crossed(): return lax.ppermute(value, ('task', 'dp'), pairs)]
    unnamed x24 -> x10, local copies, waits for them, and re-layouts: 4 us -> 1.7 us
    ppermute x9, waiting for transfers between devices: 6.66 us -> 4.52 us  [flipped(): return lax.ppermute(value, 'dp', pairs)]
    ppermute x6, starting transfers between devices: 6.1 us -> 7.88 us  [crossed(): return lax.ppermute(value, ('task', 'dp'), pairs)]
    pallas_call x2 -> x4, Pallas kernels: 1.96 us -> 3.33 us  [the longest x1 1.82 us: pack_small(): pl.pallas_call(small_kernel, out_shape=shape((LABEL_AT + 16, LANES)), in_...]
    ppermute x9 -> x8, waiting for transfers between devices: 4.08 us -> 2.72 us  [sibling(): return lax.ppermute(value, 'task', [(0, 1), (1, 0)])]
    convert_element_type x3, other arithmetic: 1.46 us -> 0.39 us  [summed(): return total.astype(BF)]
  transfers between devices with their start and end apart: 24 -> 23, of which waited for: 12 -> 9; matrix products, arithmetic and copies ran while one was open for 3% -> 1% of each run, Pallas kernels for 15% -> 18%
where the time goes in v4:
time: 84.6 us; the launch traced here: 84.3 us
  Pallas kernels  37.6 us (44%)
  starting transfers between devices  25.1 us (30%)
  waiting for transfers between devices  17.3 us (20%)
  other arithmetic  1.79 us (2%)
  local copies, waits for them, and re-layouts  1.7 us (2%)
    pallas_call x1, Pallas kernels, layer(): pl.pallas_call(functools.partial(main_kernel, len(x_parts), len(own_group...  21 us
    ppermute x9, starting transfers between devices, flipped(): return lax.ppermute(value, 'dp', pairs)  14.6 us
    ppermute x6, waiting for transfers between devices, crossed(): return lax.ppermute(value, ('task', 'dp'), pairs)  10.1 us
    ppermute x6, starting transfers between devices, crossed(): return lax.ppermute(value, ('task', 'dp'), pairs)  7.88 us
    pallas_call x1, Pallas kernels, expand(): pl.pallas_call(functools.partial(expand_kernel, blocks // 2, group), grid...  6.52 us
    pallas_call x2, Pallas kernels, pool(): pl.pallas_call(functools.partial(pool_kernel, part * count, count, half_b...  5.49 us
    ppermute x9, waiting for transfers between devices, flipped(): return lax.ppermute(value, 'dp', pairs)  4.52 us
    ppermute x8, waiting for transfers between devices, sibling(): return lax.ppermute(value, 'task', [(0, 1), (1, 0)])  2.72 us
  transfers between devices with their start and end apart: 23, of which 9 were waited for; matrix products, arithmetic and copies ran while one was open for 1% of the time, Pallas kernels for 18%

profile of v4, /device:TPU:0, one launch (start us, length us, event | category | flops | bytes accessed | tf_op | source)
XLA Modules:
  0.0 84.3 jit_solution(14973508945685486200)
XLA Ops:
  1.5 5.0 %collective-permute-start.2 = (bf16[144,256]{1,0:T(8,128)(2,1)S(1)}, bf16[144,256]{1,0:T(8,128)(2,1)S(1)}, u32[]{:S(2)}, u32[]{:S(2)}) collective-permute-start(bf16[144,256]{1,0:T(8,128)(2,1)S(1)} %pad_maximum_fusion.refs_0_), channel_id=1, source_target_pairs={{0,12},{1,13},{2,14},{3,15},{4,8},{5,9},{6,10},{7,11},{8,4},{9,5},... | collective-permute-start | bytes 221192 | tf_op jit(solution)/shard_map/ppermute | solution.py:702
  8.8 1.8 %shard_map.255.refs_0_.refs_10_ = bf16[368,128]{1,0:T(8,128)(2,1)} custom-call(s32[2]{0:T(128)} %pad_add_fusion.ids_ref, s32[1,1536]{1,0:T(1,128)} %label_ref.1, bf16[2,256]{1,0:T(2,128)(2,1)} %bitcast.44, bf16[2,256]{1,0:T(2,128)(2,1)} %bitcast.45, bf16[1,256]{1,0:T(2,128)(2,1)} %ogain_ref.1, bf16[1,256]{1,0:T(2,128)(2,1)} %oshift_ref.1, ...), custom_call_target="tpu_custom_call" | custom-call | flops 1000000000 | bytes 1000000 | tf_op jit(solution)/shard_map/pallas_call | solution.py:158
  10.6 2.1 %collective-permute-done.1.refs_2_ = bf16[144,256]{1,0:T(8,128)(2,1)S(1)} collective-permute-done((bf16[144,256]{1,0:T(8,128)(2,1)S(1)}, bf16[144,256]{1,0:T(8,128)(2,1)S(1)}, u32[]{:S(2)}, u32[]{:S(2)}) %collective-permute-start.1) | collective-permute-done | bytes 73760 | tf_op jit(solution)/shard_map/ppermute | solution.py:702
  13.1 1.6 %collective-permute-start.4 = (bf16[4,144,256]{2,1,0:T(8,128)(2,1)S(1)}, bf16[4,144,256]{2,1,0:T(8,128)(2,1)S(1)}, u32[]{:S(2)}, u32[]{:S(2)}) collective-permute-start(bf16[4,144,256]{2,1,0:T(8,128)(2,1)S(1)} %shard_map.257.refs_2_), channel_id=1, source_target_pairs={{0,1},{1,0},{2,3},{3,2},{4,5},{5,4},{6,7},{7,6},{8,9},{9,8},{10,11... | collective-permute-start | bytes 884744 | tf_op jit(solution)/shard_map/ppermute | solution.py:708
  14.7 1.5 %collective-permute-start.3 = (bf16[4,144,256]{2,1,0:T(8,128)(2,1)S(1)}, bf16[4,144,256]{2,1,0:T(8,128)(2,1)S(1)}, u32[]{:S(2)}, u32[]{:S(2)}) collective-permute-start(bf16[4,144,256]{2,1,0:T(8,128)(2,1)S(1)} %shard_map.257.refs_2_), channel_id=1, source_target_pairs={{0,2},{1,3},{2,0},{3,1},{4,6},{5,7},{6,4},{7,5},{8,10},{9,11},{10,... | collective-permute-start | bytes 884744 | tf_op jit(solution)/shard_map/ppermute | solution.py:708
  17.1 2.7 %shard_map.256.refs_1_.refs_0_ = bf16[384,512]{1,0:T(8,128)(2,1)S(1)} custom-call(s32[2]{0:T(128)S(1)} %copy-done, s32[2,256]{1,0:T(2,128)S(1)} %get-tuple-element.42.meta_ref, s32[104,128]{1,0:T(8,128)S(1)} %get-tuple-element.43.st_ref, s32[104,128]{1,0:T(8,128)S(1)} %get-tuple-element.44.en_ref, bf16[64,18432]{1,0:T(8,128)(2,1)S(1)} %bitcast.30, ...), custom_call_target="tpu_custom_call" | custom-call | flops 10000000000 | bytes 5000000 | tf_op jit(solution)/shard_map/pallas_call | solution.py:230
  20.0 3.1 %collective-permute-done.4.refs_0_ = bf16[4,144,256]{2,1,0:T(8,128)(2,1)S(1)} collective-permute-done((bf16[4,144,256]{2,1,0:T(8,128)(2,1)S(1)}, bf16[4,144,256]{2,1,0:T(8,128)(2,1)S(1)}, u32[]{:S(2)}, u32[]{:S(2)}) %collective-permute-start.4) | collective-permute-done | bytes 294944 | tf_op jit(solution)/shard_map/ppermute | solution.py:708
  23.4 1.4 %collective-permute-start.7 = (bf16[4,144,256]{2,1,0:T(8,128)(2,1)S(1)}, bf16[4,144,256]{2,1,0:T(8,128)(2,1)S(1)}, u32[]{:S(2)}, u32[]{:S(2)}) collective-permute-start(bf16[4,144,256]{2,1,0:T(8,128)(2,1)S(1)} %collective-permute-done.3.refs_0_.refs_3_), channel_id=1, source_target_pairs={{0,16},{16,0},{1,17},{17,1},{2,18},{18,2},{3,19},{19,3},{4,20},{20... | collective-permute-start | bytes 884744 | tf_op jit(solution)/shard_map/ppermute | solution.py:697
  24.7 2.7 %shard_map.258.refs_1_ = bf16[384,512]{1,0:T(8,128)(2,1)S(1)} custom-call(s32[2]{0:T(128)S(1)} %copy-done, s32[2,256]{1,0:T(2,128)S(1)} %get-tuple-element.42.meta_ref, s32[104,128]{1,0:T(8,128)S(1)} %get-tuple-element.43.st_ref, s32[104,128]{1,0:T(8,128)S(1)} %get-tuple-element.44.en_ref, bf16[64,18432]{1,0:T(8,128)(2,1)S(1)} %bitcast.31, ...), custom_call_target="tpu_custom_call" | custom-call | flops 10000000000 | bytes 5000000 | tf_op jit(solution)/shard_map/pallas_call | solution.py:230
  27.5 2.2 %collective-permute-done.5.refs_0_ = bf16[4,144,256]{2,1,0:T(8,128)(2,1)S(1)} collective-permute-done((bf16[4,144,256]{2,1,0:T(8,128)(2,1)S(1)}, bf16[4,144,256]{2,1,0:T(8,128)(2,1)S(1)}, u32[]{:S(2)}, u32[]{:S(2)}) %collective-permute-start.5) | collective-permute-done | bytes 294944 | tf_op jit(solution)/shard_map/ppermute | solution.py:708
  30.3 1.2 %collective-permute-done.10.refs_11_ = bf16[368,128]{1,0:T(8,128)(2,1)S(1)} collective-permute-done((bf16[368,128]{1,0:T(8,128)(2,1)S(1)}, bf16[368,128]{1,0:T(8,128)(2,1)S(1)}, u32[]{:S(2)}, u32[]{:S(2)}) %collective-permute-start.10) | collective-permute-done | bytes 94240 | tf_op jit(solution)/shard_map/ppermute | solution.py:697
  31.5 21.0 %shard_map.261 = (bf16[784,512]{1,0:T(8,128)(2,1)S(1)}, bf16[1152,256]{1,0:T(8,128)(2,1)S(1)}, bf16[1328,256]{1,0:T(8,128)(2,1)S(1)}, bf16[1152,256]{1,0:T(8,128)(2,1)S(1)}, bf16[1328,256]{1,0:T(8,128)(2,1)S(1)}) custom-call(s32[2]{0:T(128)S(1)} %copy-done, bf16[384,512]{1,0:T(8,128)(2,1)S(1)} %shard_map.256.refs_1_.refs_0_, ...), custom_call_target="tpu_custom_call" | custom-call | flops 5435817984 | bytes 10000000 | tf_op jit(solution)/shard_map/pallas_call | solution.py:684
  53.2 1.5 %collective-permute-done.13 = bf16[1328,256]{1,0:T(8,128)(2,1)S(1)} collective-permute-done((bf16[1328,256]{1,0:T(8,128)(2,1)S(1)}, bf16[1328,256]{1,0:T(8,128)(2,1)S(1)}, u32[]{:S(2)}, u32[]{:S(2)}) %collective-permute-start.13) | collective-permute-done | bytes 679968 | tf_op jit(solution)/shard_map/ppermute | solution.py:697
  54.9 1.5 %collective-permute-start.14 = (bf16[1328,256]{1,0:T(8,128)(2,1)S(1)}, bf16[1328,256]{1,0:T(8,128)(2,1)S(1)}, u32[]{:S(2)}, u32[]{:S(2)}) collective-permute-start(bf16[1328,256]{1,0:T(8,128)(2,1)S(1)} %add_convert_fusion.one_ref), channel_id=1, source_target_pairs={{0,1},{1,0},{2,3},{3,2},{4,5},{5,4},{6,7},{7,6},{8,9},{9,8},{10,11... | collective-permute-start | bytes 2039816 | tf_op jit(solution)/shard_map/ppermute | solution.py:708
  56.5 6.5 %shard_map.262 = (bf16[64,18432]{1,0:T(8,128)(2,1)}, f32[1,1536]{1,0:T(1,128)}, f32[8,128]{1,0:T(8,128)S(1)}) custom-call(s32[2]{0:T(128)S(1)} %copy-done, s32[2,256]{1,0:T(2,128)S(1)} %get-tuple-element.42.meta_ref, s32[104,128]{1,0:T(8,128)S(1)} %get-tuple-element.43.st_ref, s32[104,128]{1,0:T(8,128)S(1)} %get-tuple-element.44.en_ref, ...), custom_call_target="tpu_custom_call" | custom-call | flops 12000000000 | bytes 6000000 | tf_op jit(solution)/shard_map/pallas_call | solution.py:284
  63.0 2.8 %collective-permute-done.14.refs_0_ = bf16[1328,256]{1,0:T(8,128)(2,1)S(1)} collective-permute-done((bf16[1328,256]{1,0:T(8,128)(2,1)S(1)}, bf16[1328,256]{1,0:T(8,128)(2,1)S(1)}, u32[]{:S(2)}, u32[]{:S(2)}) %collective-permute-start.14) | collective-permute-done | bytes 679968 | tf_op jit(solution)/shard_map/ppermute | solution.py:708
  66.5 1.8 %collective-permute-start.21 = (bf16[176,256]{1,0:T(8,128)(2,1)S(1)}, bf16[176,256]{1,0:T(8,128)(2,1)S(1)}, u32[]{:S(2)}, u32[]{:S(2)}) collective-permute-start(bf16[176,256]{1,0:T(8,128)(2,1)S(1)} %shard_map.266), channel_id=1, source_target_pairs={{0,12},{1,13},{2,14},{3,15},{4,8},{5,9},{6,10},{7,11},{8,4},{9,5},... | collective-permute-start | bytes 270344 | tf_op jit(solution)/shard_map/ppermute | solution.py:702
  68.2 2.7 %collective-permute-start.19 = (bf16[176,256]{1,0:T(8,128)(2,1)S(1)}, bf16[176,256]{1,0:T(8,128)(2,1)S(1)}, u32[]{:S(2)}, u32[]{:S(2)}) collective-permute-start(bf16[176,256]{1,0:T(8,128)(2,1)S(1)} %shard_map.266), channel_id=1, source_target_pairs={{0,4},{1,5},{2,6},{3,7},{4,0},{5,1},{6,2},{7,3},{8,12},{9,13},{10,... | collective-permute-start | bytes 270344 | tf_op jit(solution)/shard_map/ppermute | solution.py:702
  70.9 1.9 %collective-permute-done.15.near_ref = bf16[576,256]{1,0:T(8,128)(2,1)S(1)} collective-permute-done((bf16[576,256]{1,0:T(8,128)(2,1)S(1)}, bf16[576,256]{1,0:T(8,128)(2,1)S(1)}, u32[]{:S(2)}, u32[]{:S(2)}) %collective-permute-start.15) | collective-permute-done | bytes 294944 | tf_op jit(solution)/shard_map/ppermute | solution.py:708
  73.0 2.1 %collective-permute-start.17 = (bf16[144,256]{1,0:T(8,128)(2,1)S(1)}, bf16[144,256]{1,0:T(8,128)(2,1)S(1)}, u32[]{:S(2)}, u32[]{:S(2)}) collective-permute-start(bf16[144,256]{1,0:T(8,128)(2,1)S(1)} %get-tuple-element.55), channel_id=1, source_target_pairs={{0,8},{1,9},{2,10},{3,11},{4,12},{5,13},{6,14},{7,15},{8,0},{9,1},... | collective-permute-start | bytes 221192 | tf_op jit(solution)/shard_map/ppermute | solution.py:702
  75.2 2.3 %collective-permute-start.18 = (bf16[144,256]{1,0:T(8,128)(2,1)S(1)}, bf16[144,256]{1,0:T(8,128)(2,1)S(1)}, u32[]{:S(2)}, u32[]{:S(2)}) collective-permute-start(bf16[144,256]{1,0:T(8,128)(2,1)S(1)} %get-tuple-element.56), channel_id=1, source_target_pairs={{0,12},{1,13},{2,14},{3,15},{4,8},{5,9},{6,10},{7,11},{8,4},{9,5},... | collective-permute-start | bytes 221192 | tf_op jit(solution)/shard_map/ppermute | solution.py:702
  77.8 2.5 %collective-permute-start.22 = (bf16[176,256]{1,0:T(8,128)(2,1)S(1)}, bf16[176,256]{1,0:T(8,128)(2,1)S(1)}, u32[]{:S(2)}, u32[]{:S(2)}) collective-permute-start(bf16[176,256]{1,0:T(8,128)(2,1)S(1)} %add_convert_fusion.2.refs_0_), channel_id=1, source_target_pairs={{0,2},{1,3},{2,0},{3,1},{4,6},{5,7},{6,4},{7,5},{8,10},{9,11},{10,... | collective-permute-start | bytes 270344 | tf_op jit(solution)/shard_map/ppermute | solution.py:708
  80.3 2.0 %collective-permute-done.17.refs_2_ = bf16[144,256]{1,0:T(8,128)(2,1)S(1)} collective-permute-done((bf16[144,256]{1,0:T(8,128)(2,1)S(1)}, bf16[144,256]{1,0:T(8,128)(2,1)S(1)}, u32[]{:S(2)}, u32[]{:S(2)}) %collective-permute-start.17) | collective-permute-done | bytes 73760 | tf_op jit(solution)/shard_map/ppermute | solution.py:702
  83.0 1.2 %shard_map.270 = (f32[2,256]{1,0:T(2,128)}, f32[2,256]{1,0:T(2,128)}, f32[1,256]{1,0:T(1,128)}, f32[1,256]{1,0:T(1,128)}, f32[4,512]{1,0:T(4,128)}, /*index=5*/f...) custom-call(s32[2]{0:T(128)S(1)} %copy-done, bf16[176,256]{1,0:T(8,128)(2,1)S(1)} %add_convert_fusion.2.refs_0_, ...), custom_call_target="tpu_custom_call" | custom-call | bytes 2000000 | tf_op jit(solution)/shard_map/pallas_call | solution.py:868
  (54 shorter events, 8.2 us)
Async XLA Ops:
  1.5 9.2 %collective-permute-start.2 = (bf16[144,256]{1,0:T(8,128)(2,1)S(1)}, bf16[144,256]{1,0:T(8,128)(2,1)S(1)}, u32[]{:S(2)}, u32[]{:S(2)}) collective-permute-start(bf16[144,256]{1,0:T(8,128)(2,1)S(1)} %pad_maximum_fusion.refs_0_), channel_id=1, source_target_pairs={{0,12},{1,13},{2,14},{3,15},{4,8},{5,9},{6,10},{7,11},{8,4},{9,5},... | collective-permute-start | bytes 221192 | tf_op jit(solution)/shard_map/ppermute | solution.py:702
  6.5 6.2 %collective-permute-start.1 = (bf16[144,256]{1,0:T(8,128)(2,1)S(1)}, bf16[144,256]{1,0:T(8,128)(2,1)S(1)}, u32[]{:S(2)}, u32[]{:S(2)}) collective-permute-start(bf16[144,256]{1,0:T(8,128)(2,1)S(1)} %pad_maximum_fusion.refs_0_), channel_id=1, source_target_pairs={{0,8},{1,9},{2,10},{3,11},{4,12},{5,13},{6,14},{7,15},{8,0},{9,1},... | collective-permute-start | bytes 221192 | tf_op jit(solution)/shard_map/ppermute | solution.py:702
  6.5 6.2 %collective-permute-start = (bf16[144,256]{1,0:T(8,128)(2,1)S(1)}, bf16[144,256]{1,0:T(8,128)(2,1)S(1)}, u32[]{:S(2)}, u32[]{:S(2)}) collective-permute-start(bf16[144,256]{1,0:T(8,128)(2,1)S(1)} %pad_maximum_fusion.refs_0_), channel_id=1, source_target_pairs={{0,4},{1,5},{2,6},{3,7},{4,0},{5,1},{6,2},{7,3},{8,12},{9,13},{10,... | collective-permute-start | bytes 221192 | tf_op jit(solution)/shard_map/ppermute | solution.py:702
  8.8 7.4 %copy-start.1 = (bf16[18432,64]{0,1:T(8,128)(2,1)S(1)}, bf16[18432,64]{0,1:T(8,128)(2,1)}, u32[]{:S(2)}) copy-start(bf16[18432,64]{0,1:T(8,128)(2,1)} %param.15) | copy-start | bytes 7077892
  13.1 9.9 %collective-permute-start.4 = (bf16[4,144,256]{2,1,0:T(8,128)(2,1)S(1)}, bf16[4,144,256]{2,1,0:T(8,128)(2,1)S(1)}, u32[]{:S(2)}, u32[]{:S(2)}) collective-permute-start(bf16[4,144,256]{2,1,0:T(8,128)(2,1)S(1)} %shard_map.257.refs_2_), channel_id=1, source_target_pairs={{0,1},{1,0},{2,3},{3,2},{4,5},{5,4},{6,7},{7,6},{8,9},{9,8},{10,11... | collective-permute-start | bytes 884744 | tf_op jit(solution)/shard_map/ppermute | solution.py:708
  14.7 8.7 %collective-permute-start.3 = (bf16[4,144,256]{2,1,0:T(8,128)(2,1)S(1)}, bf16[4,144,256]{2,1,0:T(8,128)(2,1)S(1)}, u32[]{:S(2)}, u32[]{:S(2)}) collective-permute-start(bf16[4,144,256]{2,1,0:T(8,128)(2,1)S(1)} %shard_map.257.refs_2_), channel_id=1, source_target_pairs={{0,2},{1,3},{2,0},{3,1},{4,6},{5,7},{6,4},{7,5},{8,10},{9,11},{10,... | collective-permute-start | bytes 884744 | tf_op jit(solution)/shard_map/ppermute | solution.py:708
  19.9 11.6 %collective-permute-start.6 = (bf16[4,144,256]{2,1,0:T(8,128)(2,1)S(1)}, bf16[4,144,256]{2,1,0:T(8,128)(2,1)S(1)}, u32[]{:S(2)}, u32[]{:S(2)}) collective-permute-start(bf16[4,144,256]{2,1,0:T(8,128)(2,1)S(1)} %shard_map.257.refs_2_), channel_id=1, source_target_pairs={{0,16},{16,0},{1,17},{17,1},{2,18},{18,2},{3,19},{19,3},{4,20},{20... | collective-permute-start | bytes 884744 | tf_op jit(solution)/shard_map/ppermute | solution.py:697
  23.0 8.5 %collective-permute-start.8 = (bf16[4,144,256]{2,1,0:T(8,128)(2,1)S(1)}, bf16[4,144,256]{2,1,0:T(8,128)(2,1)S(1)}, u32[]{:S(2)}, u32[]{:S(2)}) collective-permute-start(bf16[4,144,256]{2,1,0:T(8,128)(2,1)S(1)} %shard_map.259.refs_4_), channel_id=1, source_target_pairs={{0,16},{16,0},{1,17},{17,1},{2,18},{18,2},{3,19},{19,3},{4,20},{20... | collective-permute-start | bytes 884744 | tf_op jit(solution)/shard_map/ppermute | solution.py:697
  23.0 6.7 %collective-permute-start.5 = (bf16[4,144,256]{2,1,0:T(8,128)(2,1)S(1)}, bf16[4,144,256]{2,1,0:T(8,128)(2,1)S(1)}, u32[]{:S(2)}, u32[]{:S(2)}) collective-permute-start(bf16[4,144,256]{2,1,0:T(8,128)(2,1)S(1)} %shard_map.259.refs_4_), channel_id=1, source_target_pairs={{0,2},{1,3},{2,0},{3,1},{4,6},{5,7},{6,4},{7,5},{8,10},{9,11},{10,... | collective-permute-start | bytes 884744 | tf_op jit(solution)/shard_map/ppermute | solution.py:708
  23.4 8.1 %collective-permute-start.7 = (bf16[4,144,256]{2,1,0:T(8,128)(2,1)S(1)}, bf16[4,144,256]{2,1,0:T(8,128)(2,1)S(1)}, u32[]{:S(2)}, u32[]{:S(2)}) collective-permute-start(bf16[4,144,256]{2,1,0:T(8,128)(2,1)S(1)} %collective-permute-done.3.refs_0_.refs_3_), channel_id=1, source_target_pairs={{0,16},{16,0},{1,17},{17,1},{2,18},{18,2},{3,19},{19,3},{4,20},{20... | collective-permute-start | bytes 884744 | tf_op jit(solution)/shard_map/ppermute | solution.py:697
  29.7 1.7 %collective-permute-start.9 = (bf16[4,144,256]{2,1,0:T(8,128)(2,1)S(1)}, bf16[4,144,256]{2,1,0:T(8,128)(2,1)S(1)}, u32[]{:S(2)}, u32[]{:S(2)}) collective-permute-start(bf16[4,144,256]{2,1,0:T(8,128)(2,1)S(1)} %shard_map.260.refs_5_), channel_id=1, source_target_pairs={{0,16},{16,0},{1,17},{17,1},{2,18},{18,2},{3,19},{19,3},{4,20},{20... | collective-permute-start | bytes 884744 | tf_op jit(solution)/shard_map/ppermute | solution.py:697
  29.8 1.7 %collective-permute-start.10 = (bf16[368,128]{1,0:T(8,128)(2,1)S(1)}, bf16[368,128]{1,0:T(8,128)(2,1)S(1)}, u32[]{:S(2)}, u32[]{:S(2)}) collective-permute-start(bf16[368,128]{1,0:T(8,128)(2,1)S(1)} %copy-done.3), channel_id=1, source_target_pairs={{0,16},{16,0},{1,17},{17,1},{2,18},{18,2},{3,19},{19,3},{4,20},{20... | collective-permute-start | bytes 282632 | tf_op jit(solution)/shard_map/ppermute | solution.py:697
  52.5 2.2 %collective-permute-start.13 = (bf16[1328,256]{1,0:T(8,128)(2,1)S(1)}, bf16[1328,256]{1,0:T(8,128)(2,1)S(1)}, u32[]{:S(2)}, u32[]{:S(2)}) collective-permute-start(bf16[1328,256]{1,0:T(8,128)(2,1)S(1)} %get-tuple-element.51), channel_id=1, source_target_pairs={{0,16},{16,0},{1,17},{17,1},{2,18},{18,2},{3,19},{19,3},{4,20},{20... | collective-permute-start | bytes 2039816 | tf_op jit(solution)/shard_map/ppermute | solution.py:697
  52.7 3.8 %collective-permute-start.11 = (bf16[784,512]{1,0:T(8,128)(2,1)S(1)}, bf16[784,512]{1,0:T(8,128)(2,1)S(1)}, u32[]{:S(2)}, u32[]{:S(2)}) collective-permute-start(bf16[784,512]{1,0:T(8,128)(2,1)S(1)} %get-tuple-element.45.own_ref), channel_id=1, source_target_pairs={{0,16},{16,0},{1,17},{17,1},{2,18},{18,2},{3,19},{19,3},{4,20},{20... | collective-permute-start | bytes 2408456 | tf_op jit(solution)/shard_map/ppermute | solution.py:697
  53.1 12.7 %collective-permute-start.12 = (bf16[1152,256]{1,0:T(8,128)(2,1)S(1)}, bf16[1152,256]{1,0:T(8,128)(2,1)S(1)}, u32[]{:S(2)}, u32[]{:S(2)}) collective-permute-start(bf16[1152,256]{1,0:T(8,128)(2,1)S(1)} %get-tuple-element.49), channel_id=1, source_target_pairs={{0,16},{16,0},{1,17},{17,1},{2,18},{18,2},{3,19},{19,3},{4,20},{20... | collective-permute-start | bytes 1769480 | tf_op jit(solution)/shard_map/ppermute | solution.py:697
  54.9 10.9 %collective-permute-start.14 = (bf16[1328,256]{1,0:T(8,128)(2,1)S(1)}, bf16[1328,256]{1,0:T(8,128)(2,1)S(1)}, u32[]{:S(2)}, u32[]{:S(2)}) collective-permute-start(bf16[1328,256]{1,0:T(8,128)(2,1)S(1)} %add_convert_fusion.one_ref), channel_id=1, source_target_pairs={{0,1},{1,0},{2,3},{3,2},{4,5},{5,4},{6,7},{7,6},{8,9},{9,8},{10,11... | collective-permute-start | bytes 2039816 | tf_op jit(solution)/shard_map/ppermute | solution.py:708
  66.0 6.8 %collective-permute-start.15 = (bf16[576,256]{1,0:T(8,128)(2,1)S(1)}, bf16[576,256]{1,0:T(8,128)(2,1)S(1)}, u32[]{:S(2)}, u32[]{:S(2)}) collective-permute-start(bf16[576,256]{1,0:T(8,128)(2,1)S(1)} %add_convert_fusion.1), channel_id=1, source_target_pairs={{0,2},{1,3},{2,0},{3,1},{4,6},{5,7},{6,4},{7,5},{8,10},{9,11},{10,... | collective-permute-start | bytes 884744 | tf_op jit(solution)/shard_map/ppermute | solution.py:708
  66.5 8.7 %collective-permute-start.21 = (bf16[176,256]{1,0:T(8,128)(2,1)S(1)}, bf16[176,256]{1,0:T(8,128)(2,1)S(1)}, u32[]{:S(2)}, u32[]{:S(2)}) collective-permute-start(bf16[176,256]{1,0:T(8,128)(2,1)S(1)} %shard_map.266), channel_id=1, source_target_pairs={{0,12},{1,13},{2,14},{3,15},{4,8},{5,9},{6,10},{7,11},{8,4},{9,5},... | collective-permute-start | bytes 270344 | tf_op jit(solution)/shard_map/ppermute | solution.py:702
  68.2 9.2 %collective-permute-start.20 = (bf16[176,256]{1,0:T(8,128)(2,1)S(1)}, bf16[176,256]{1,0:T(8,128)(2,1)S(1)}, u32[]{:S(2)}, u32[]{:S(2)}) collective-permute-start(bf16[176,256]{1,0:T(8,128)(2,1)S(1)} %shard_map.266), channel_id=1, source_target_pairs={{0,8},{1,9},{2,10},{3,11},{4,12},{5,13},{6,14},{7,15},{8,0},{9,1},... | collective-permute-start | bytes 270344 | tf_op jit(solution)/shard_map/ppermute | solution.py:702
  68.2 9.5 %collective-permute-start.19 = (bf16[176,256]{1,0:T(8,128)(2,1)S(1)}, bf16[176,256]{1,0:T(8,128)(2,1)S(1)}, u32[]{:S(2)}, u32[]{:S(2)}) collective-permute-start(bf16[176,256]{1,0:T(8,128)(2,1)S(1)} %shard_map.266), channel_id=1, source_target_pairs={{0,4},{1,5},{2,6},{3,7},{4,0},{5,1},{6,2},{7,3},{8,12},{9,13},{10,... | collective-permute-start | bytes 270344 | tf_op jit(solution)/shard_map/ppermute | solution.py:702
  73.0 7.4 %collective-permute-start.16 = (bf16[144,256]{1,0:T(8,128)(2,1)S(1)}, bf16[144,256]{1,0:T(8,128)(2,1)S(1)}, u32[]{:S(2)}, u32[]{:S(2)}) collective-permute-start(bf16[144,256]{1,0:T(8,128)(2,1)S(1)} %get-tuple-element.54), channel_id=1, source_target_pairs={{0,4},{1,5},{2,6},{3,7},{4,0},{5,1},{6,2},{7,3},{8,12},{9,13},{10,... | collective-permute-start | bytes 221192 | tf_op jit(solution)/shard_map/ppermute | solution.py:702
  73.0 9.3 %collective-permute-start.17 = (bf16[144,256]{1,0:T(8,128)(2,1)S(1)}, bf16[144,256]{1,0:T(8,128)(2,1)S(1)}, u32[]{:S(2)}, u32[]{:S(2)}) collective-permute-start(bf16[144,256]{1,0:T(8,128)(2,1)S(1)} %get-tuple-element.55), channel_id=1, source_target_pairs={{0,8},{1,9},{2,10},{3,11},{4,12},{5,13},{6,14},{7,15},{8,0},{9,1},... | collective-permute-start | bytes 221192 | tf_op jit(solution)/shard_map/ppermute | solution.py:702
  75.2 7.2 %collective-permute-start.18 = (bf16[144,256]{1,0:T(8,128)(2,1)S(1)}, bf16[144,256]{1,0:T(8,128)(2,1)S(1)}, u32[]{:S(2)}, u32[]{:S(2)}) collective-permute-start(bf16[144,256]{1,0:T(8,128)(2,1)S(1)} %get-tuple-element.56), channel_id=1, source_target_pairs={{0,12},{1,13},{2,14},{3,15},{4,8},{5,9},{6,10},{7,11},{8,4},{9,5},... | collective-permute-start | bytes 221192 | tf_op jit(solution)/shard_map/ppermute | solution.py:702
  77.8 5.2 %collective-permute-start.22 = (bf16[176,256]{1,0:T(8,128)(2,1)S(1)}, bf16[176,256]{1,0:T(8,128)(2,1)S(1)}, u32[]{:S(2)}, u32[]{:S(2)}) collective-permute-start(bf16[176,256]{1,0:T(8,128)(2,1)S(1)} %add_convert_fusion.2.refs_0_), channel_id=1, source_target_pairs={{0,2},{1,3},{2,0},{3,1},{4,6},{5,7},{6,4},{7,5},{8,10},{9,11},{10,... | collective-permute-start | bytes 270344 | tf_op jit(solution)/shard_map/ppermute | solution.py:708
  (4 other events, 15.9 us)

commit v5 on v4

--- a/solution.py
+++ b/solution.py
@@ -26,6 +26,7 @@
 BIG = 2 * SLOTS
 WIDE = BIG * HID
 PIECE = 32
+SPAN = 256
 BF = jnp.bfloat16
 F32 = jnp.float32
 
@@ -339,31 +340,30 @@
     lax.fori_loop(0, events // LANES, step, 0)
 
 
-def main_kernel(xs, groups, plan, rows1, rows2, ids_ref, *refs):
+def main_kernel(xs, given, plan, rows1, rows2, ids_ref, *refs):
     refs = list(refs)
     take = lambda n: [refs.pop(0) for _ in range(n)]
     x_parts = take(xs)
-    own_groups, oth_groups = take(groups), take(groups)
+    own_groups, oth_groups = take(len(given)), take(len(given))
     packs = take(2)
     (dx_ref,) = take(1)
     own_outs, oth_outs = take(len(plan)), take(len(plan))
     x_ref, wc_ref, w2_ref, gain_ref, third_ref, lab_ref, pc_ref, pb_ref, s2_ref, y_ref, h_ref, e_ref, fc_ref = take(13)
-    scale_ref, lg_ref, prob_ref, q_ref, pt_ref, u1_ref, p4_ref, e2_ref, e1_ref, du_ref, dm_ref, dmb_ref, ds_ref, dn_ref, acc3_ref, pred_ref, g1_ref, g2_ref = take(18)
+    scale_ref, lg_ref, prob_ref, q_ref, pt_ref, u1_ref, p4_ref, e2_ref, e1_ref, du_ref, dm_ref, dmb_ref, ds_ref, dn_ref, acc3_ref, pred_ref, g1_ref, g2_ref, dp_ref = take(19)
     position = ids_ref[0]
     events = x_ref.shape[1]
-    quarter = D // rows1 // 4
 
     def part(m):
         return slice(m * HID, (m + 1) * HID)
 
-    def rows_of(t, p):
-        if not quarter:
+    def rows_of(t, piece):
+        if piece is None:
             return pl.ds(0, rows1), pl.ds(0, rows2)
         where = position if t == 0 else 1 - position
-        d = ids_ref[1] ^ (4 * (p % quarter))
-        if (p // quarter) & 1:
+        d = ids_ref[1] ^ (4 * piece[2])
+        if piece[1]:
             d = d ^ (2 - where)
-        if p // quarter >= 2:
+        if piece[0]:
             d = d ^ (1 + where)
         return (
             pl.ds(pl.multiple_of(d * rows1, rows1), rows1),
@@ -374,11 +374,9 @@
     for k, piece in enumerate(x_parts):
         x_ref[:, k * size : (k + 1) * size] = piece[...].T
     for t, whole in enumerate((own_groups, oth_groups)):
-        p = 0
-        for group in whole:
-            for g in range(group.shape[0]):
-                one, two = rows_of(t, p)
-                p += 1
+        for group, pieces in zip(whole, given):
+            for g, piece in enumerate(pieces):
+                one, two = rows_of(t, piece)
                 for s in range(SLOTS):
                     wc_ref[one, part(t * SLOTS + s)] = group[g, s * rows1 : (s + 1) * rows1, :]
                     low = SLOTS * rows1 + s * rows2
@@ -408,54 +406,56 @@
         third_ref[t * TOWER2 : (t + 1) * TOWER2, :] = third[:TOWER2]
         lab_ref[t * 16 : (t + 1) * 16, :] = packs[t][LABEL_AT : LABEL_AT + 16, :].astype(F32)
 
-    for m in range(BIG):
+    lg_ref[...] = nn(gates, x_ref[...])
+    span = next(size for size in (SPAN, 2 * LANES, LANES) if events % size == 0)
+    spans = [slice(at, at + span) for at in range(0, events, span)]
+
+    def first_sums(m):
         pc_ref[part(m), :] = tn(wc_ref[:, part(m)], x_ref[...])
-    lg_ref[...] = nn(gates, x_ref[...])
-
-    def first_gelu(j, here):
-        for m in range(BIG):
+
+    def first_gelu(m):
+        for here in spans:
             for rows in pieces_of(m):
                 act, slope = gelu_twice(pc_ref[rows, here])
                 pc_ref[rows, here] = slope
                 h_ref[rows, here] = act.astype(BF)
 
-    lane_tiles(events, first_gelu)
-    for m in range(BIG):
-        pb_ref[part(m), :] = tn(w2_ref[m], h_ref[part(m), :])
-
-    def second_gelu(j, here):
-        def front(m):
-            total = None
-            for rows in pieces_of(m):
-                act, slope = gelu_twice(pb_ref[rows, here])
-                pb_ref[rows, here] = act
-                s2_ref[rows, here] = slope
-                total = plus(total, by_eight(act))
-            return col_sum(total) * (1.0 / HID)
-
-        def back(m, mean):
-            total = None
-            for rows in pieces_of(m):
-                centred = pb_ref[rows, here] - mean
-                pb_ref[rows, here] = centred
-                total = plus(total, by_eight(centred * centred))
-            scale = lax.rsqrt(col_sum(total) * (1.0 / HID) + 4.0 * EPSILON)
-            scale_ref[m : m + 1, here] = scale
-            for rows in pieces_of(m):
-                normed = pb_ref[rows, here] * scale
-                pb_ref[rows, here] = normed
-                out = normed * gain_ref[rows, :] + gain_ref[slice(WIDE + rows.start, WIDE + rows.stop), :]
+    def second_gelu(m, here):
+        total = None
+        for rows in pieces_of(m):
+            act, slope = gelu_twice(pb_ref[rows, here])
+            pb_ref[rows, here] = act
+            s2_ref[rows, here] = slope
+            total = plus(total, by_eight(act))
+        mean = col_sum(total) * (1.0 / HID)
+        total = None
+        for rows in pieces_of(m):
+            centred = pb_ref[rows, here] - mean
+            pb_ref[rows, here] = centred
+            total = plus(total, by_eight(centred * centred))
+        scale = lax.rsqrt(col_sum(total) * (1.0 / HID) + 4.0 * EPSILON)
+        scale_ref[m : m + 1, here] = scale
+        for rows in pieces_of(m):
+            normed = pb_ref[rows, here] * scale
+            pb_ref[rows, here] = normed
+            for lanes in range(here.start, here.stop, LANES):
+                block = slice(lanes, lanes + LANES)
+                out = pb_ref[rows, block] * gain_ref[rows, :] + gain_ref[slice(WIDE + rows.start, WIDE + rows.stop), :]
                 if m % SLOTS == SLOTS - 1:
                     out = out.astype(BF).astype(F32)
-                y_ref[rows, here] = out
-
-        means = front(0)
-        for m in range(BIG):
-            ahead = front(m + 1) if m + 1 < BIG else None
-            back(m, means)
-            means = ahead
-
-    lane_tiles(events, second_gelu)
+                y_ref[rows, block] = out
+
+    first_sums(0)
+    for m in range(BIG):
+        if m + 1 < BIG:
+            first_sums(m + 1)
+        first_gelu(m)
+        pb_ref[part(m), :] = tn(w2_ref[m], h_ref[part(m), :])
+        if m:
+            for here in spans:
+                second_gelu(m - 1, here)
+    for here in spans:
+        second_gelu(BIG - 1, here)
     orders = [(t * SLOTS, t * SLOTS + 1, t * SLOTS + 2, (1 - t) * SLOTS + 2) for t in range(2)]
 
     prob_ref[...] = jnp.ones_like(prob_ref)
@@ -521,72 +521,79 @@
         rows = [wide(miscs[t], 2 * (SLOTS + s)) for s in range(EXPERTS)] + [jnp.zeros((8 - EXPERTS, HID), F32)]
         ds_ref[8 * t : 8 * t + 8, :] = nn(jnp.concatenate(rows, axis=0).astype(BF), dmb_ref[part(t), :])
 
-    def mix_back(j, here):
-        probs = [[prob_ref[8 * t + k : 8 * t + k + 1, here] for k in range(GATES)] for t in range(2)]
-        d_probs = [[None] * GATES for _ in range(2)]
+    def probs_of(t, k, here):
+        return prob_ref[8 * t + k : 8 * t + k + 1, here]
+
+    def shared_probs(here):
         for t in range(2):
             for k in range(EXPERTS, GATES):
                 total = None
                 for mine, rows in zip(pieces_of(t), pieces_of(orders[t][k])):
                     total = plus(total, by_eight(dm_ref[mine, here] * y_ref[rows, here]))
-                d_probs[t][k] = col_sum(total)
-
-        def turned_gain(m, rows):
-            t, s = divmod(m, SLOTS)
+                dp_ref[8 * t + k : 8 * t + k + 1, here] = col_sum(total)
+
+    def norm_back(m, here):
+        t, s = divmod(m, SLOTS)
+        one, two = None, None
+        for rows in pieces_of(m):
             mine = slice(rows.start - m * HID + t * HID, rows.stop - m * HID + t * HID)
-            up = dm_ref[mine, here]
-            if s == SLOTS - 1:
-                theirs = slice(mine.start + (1 - 2 * t) * HID, mine.stop + (1 - 2 * t) * HID)
-                up = probs[t][s] * up + probs[1 - t][SLOTS] * dm_ref[theirs, here]
-            return up * gain_ref[rows, :]
-
-        def front(m):
-            one, two = None, None
+            for lanes in range(here.start, here.stop, LANES):
+                block = slice(lanes, lanes + LANES)
+                up = dm_ref[mine, block]
+                if s == SLOTS - 1:
+                    theirs = slice(mine.start + (1 - 2 * t) * HID, mine.stop + (1 - 2 * t) * HID)
+                    up = probs_of(t, s, block) * up + probs_of(1 - t, SLOTS, block) * dm_ref[theirs, block]
+                y_ref[rows, block] = up * gain_ref[rows, :]
+            d_normed = y_ref[rows, here]
+            product = d_normed * pb_ref[rows, here]
+            dn_ref[rows, here] = product.astype(BF)
+            one = plus(one, by_eight(d_normed))
+            two = plus(two, by_eight(product))
+        one, two = col_sum(one), col_sum(two)
+        outer = scale_ref[m : m + 1, here]
+        if s < EXPERTS:
+            outer = outer * probs_of(t, s, here)
+            dp_ref[8 * t + s : 8 * t + s + 1, here] = two + ds_ref[8 * t + s : 8 * t + s + 1, here]
+        one, two = one * (1.0 / HID), two * (1.0 / HID)
+        for rows in pieces_of(m):
+            inner = y_ref[rows, here] - one - pb_ref[rows, here] * two
+            e_ref[rows, here] = (s2_ref[rows, here] * outer * inner).astype(BF)
+
+    def put(m, first, value, scale):
+        t, s = divmod(m, SLOTS)
+        held = (g1_ref if first else g2_ref).at[m % 2]
+        held[...] = value
+        for out, (small_first, pieces) in zip((own_outs, oth_outs)[t], plan):
+            for g, piece in enumerate(pieces):
+                mine = rows_of(t, piece)[0 if first else 1]
+                at = g * SLOTS * (rows1 + rows2) + (SMALL_ROWS if small_first else 0)
+                at, size = (at + s * rows1, rows1) if first else (at + SLOTS * rows1 + s * rows2, rows2)
+                out[at : at + size, :] = (scale * held[mine, :]).astype(BF)
+
+    for here in spans:
+        shared_probs(here)
+    for here in spans:
+        norm_back(0, here)
+    for m in range(BIG):
+        y_ref[part(m), :] = nn(w2_ref[m], e_ref[part(m), :])
+        put(m, False, nt(h_ref[part(m), :], e_ref[part(m), :]), 0.5)
+        if m + 1 < BIG:
+            for here in spans:
+                norm_back(m + 1, here)
+        for here in spans:
             for rows in pieces_of(m):
-                d_normed = turned_gain(m, rows)
-                y_ref[rows, here] = d_normed
-                product = d_normed * pb_ref[rows, here]
-                dn_ref[rows, here] = product.astype(BF)
-                one = plus(one, by_eight(d_normed))
-                two = plus(two, by_eight(product))
-            return col_sum(one), col_sum(two)
-
-        def back(m, one, two):
-            t, s = divmod(m, SLOTS)
-            one, two = one * (1.0 / HID), two * (1.0 / HID)
-            outer = scale_ref[m : m + 1, here]
-            if s < EXPERTS:
-                outer = outer * probs[t][s]
-            for rows in pieces_of(m):
-                inner = y_ref[rows, here] - one - pb_ref[rows, here] * two
-                e_ref[rows, here] = (s2_ref[rows, here] * outer * inner).astype(BF)
-
-        sums = front(0)
-        for m in range(BIG):
-            ahead = front(m + 1) if m + 1 < BIG else None
-            t, s = divmod(m, SLOTS)
-            if s < EXPERTS:
-                d_probs[t][s] = sums[1] + ds_ref[8 * t + s : 8 * t + s + 1, here]
-            back(m, *sums)
-            sums = ahead
-        codes = []
-        for t in range(2):
-            weighted = probs[t][0] * d_probs[t][0]
-            for k in range(1, GATES):
-                weighted = weighted + probs[t][k] * d_probs[t][k]
-            codes += [probs[t][k] * (d_probs[t][k] - weighted) for k in range(GATES)]
-            codes.append(jnp.zeros((8 - GATES, LANES), F32))
-        fc_ref[WIDE : WIDE + 16, here] = jnp.concatenate(codes, axis=0).astype(BF)
-
-    lane_tiles(events, mix_back)
-    for m in range(BIG):
-        s2_ref[part(m), :] = nn(w2_ref[m], e_ref[part(m), :])
-
-    def first_back(j, here):
-        for m in range(BIG):
-            fc_ref[part(m), here] = (pc_ref[part(m), here] * s2_ref[part(m), here]).astype(BF)
-
-    lane_tiles(events, first_back)
+                fc_ref[rows, here] = (pc_ref[rows, here] * y_ref[rows, here]).astype(BF)
+        put(m, True, nt(x_ref[...], fc_ref[part(m), :]), 1.0)
+    codes = []
+    for t in range(2):
+        probs = [probs_of(t, k, slice(None)) for k in range(GATES)]
+        d_probs = [dp_ref[8 * t + k : 8 * t + k + 1, :] for k in range(GATES)]
+        weighted = probs[0] * d_probs[0]
+        for k in range(1, GATES):
+            weighted = weighted + probs[k] * d_probs[k]
+        codes += [probs[k] * (d_probs[k] - weighted) for k in range(GATES)]
+        codes.append(jnp.zeros((8 - GATES, events), F32))
+    fc_ref[WIDE : WIDE + 16, :] = jnp.concatenate(codes, axis=0).astype(BF)
     dx_ref[:events, :] = nn(wc_ref[...], fc_ref[...]).astype(BF).T
     pred = pred_ref[...]
     high = pred.astype(BF)
@@ -598,19 +605,6 @@
     shifts = [nt(weights, dmb_ref[part(t), :]) for t in range(2)]
     third_grad = col_sum(acc3_ref[...].T)
     for t, results in enumerate((own_outs, oth_outs)):
-        for s in range(SLOTS):
-            m = t * SLOTS + s
-            g1_ref[...] = nt(x_ref[...], fc_ref[part(m), :])
-            g2_ref[...] = nt(h_ref[part(m), :], e_ref[part(m), :])
-            p = 0
-            for out, (pieces, small_first) in zip(results, plan):
-                for g in range(pieces):
-                    one, two = rows_of(t, p)
-                    p += 1
-                    at = g * SLOTS * (rows1 + rows2) + (SMALL_ROWS if small_first else 0)
-                    out[at + s * rows1 : at + (s + 1) * rows1, :] = g1_ref[one, :].astype(BF)
-                    at = at + SLOTS * rows1 + s * rows2
-                    out[at : at + rows2, :] = (0.5 * g2_ref[two, :]).astype(BF)
         tower = slice(t * TOWER1, (t + 1) * TOWER1)
         half = slice(t * TOWER2, (t + 1) * TOWER2)
         lines = []
@@ -637,15 +631,15 @@
             axis=0,
         )
         small = jnp.concatenate([small[:SMALL_ROWS], small[SMALL_ROWS:]], axis=1).astype(BF)
-        for out, (_, small_first) in zip(results, plan):
+        for out, (small_first, _) in zip(results, plan):
             if small_first:
                 out[:SMALL_ROWS, :] = small
 
 
-def layer(ids, x_parts, own_groups, oth_groups, own_pack, oth_pack, plan, rows1, rows2):
+def layer(ids, x_parts, own_groups, oth_groups, own_pack, oth_pack, given, plan, rows1, rows2):
     events = sum(part.shape[0] for part in x_parts)
     rows = SLOTS * (rows1 + rows2)
-    grads = tuple(shape((pieces * rows + small * SMALL_ROWS, HID)) for pieces, small in plan)
+    grads = tuple(shape((len(pieces) * rows + small * SMALL_ROWS, HID)) for small, pieces in plan)
     results = (shape((events + 16, D)),) + grads + grads
     scratch = [
         ((D, events), BF),
@@ -677,12 +671,13 @@
         ((WIDE, events), BF),
         ((2 * TOWER2, LANES), F32),
         ((16, LANES), F32),
-        ((D, HID), F32),
-        ((HID, HID), F32),
+        ((2, D, HID), F32),
+        ((2, HID, HID), F32),
+        ((16, events), F32),
     ]
     arrays = [*x_parts, *own_groups, *oth_groups, own_pack, oth_pack]
     dx, *grads = pl.pallas_call(
-        functools.partial(main_kernel, len(x_parts), len(own_groups), plan, rows1, rows2),
+        functools.partial(main_kernel, len(x_parts), given, plan, rows1, rows2),
         out_shape=results,
         in_specs=[SSPEC] + [VSPEC] * len(arrays),
         out_specs=(VSPEC,) * len(results),
@@ -736,21 +731,22 @@
     return total.astype(BF)
 
 
-def small_sum_kernel(one_ref, two_ref, out_ref):
+def small_sum_kernel(one_ref, two_ref, *refs):
+    out_ref = refs[-1]
     out_ref[...] = (one_ref[...].astype(F32) + two_ref[...].astype(F32)).astype(BF)
 
 
-def small_sum(one, two):
+def small_sum(one, two, *after):
     lead = pl.BlockSpec((SMALL_ROWS, HID), lambda i: (0, 0))
     return pl.pallas_call(
         small_sum_kernel,
         grid=(1,),
         out_shape=shape((SMALL_ROWS, HID)),
-        in_specs=[lead, lead],
+        in_specs=[lead, lead] + [ASPEC] * len(after),
         out_specs=lead,
         compiler_params=params(4),
         cost_estimate=cost(8e9, 1e6),
-    )(one, two)
+    )(one, two, *after)
 
 
 def tie_kernel(*refs):
@@ -769,7 +765,7 @@
     )(value, after)
 
 
-def far_kernel(quarter, rows, keep_ref, got_ref, mid_ref, near_ref, *outs):
+def far_kernel(rows, keep_ref, got_ref, mid_ref, near_ref, *outs):
     for k, out in enumerate(outs):
         here = slice(k * rows, (k + 1) * rows)
         total = keep_ref[here, :].astype(F32) + got_ref[here, :].astype(F32)
@@ -778,59 +774,79 @@
         out[...] = (total + near_ref[here, :].astype(F32)).astype(BF)
 
 
-def far_messages(quarter, rows, keep, got, mid, near):
-    def lead(size):
-        return pl.BlockSpec((size, HID), lambda i: (0, 0))
-
-    size = quarter * rows
+def block(rows, at=0):
+    return pl.BlockSpec((rows, HID), lambda i: (at, 0))
+
+
+def far_messages(far, rows, keep, got, mid, near):
+    size = far * rows
     return pl.pallas_call(
-        functools.partial(far_kernel, quarter, rows),
+        functools.partial(far_kernel, rows),
         grid=(1,),
-        out_shape=(shape((rows, HID)),) * quarter,
-        in_specs=[lead(size), lead(size), lead(size + SMALL_ROWS), lead(size)],
-        out_specs=(lead(rows),) * quarter,
+        out_shape=(shape((rows, HID)),) * far,
+        in_specs=[block(size), block(size), block(size + SMALL_ROWS), block(size)],
+        out_specs=(block(rows),) * far,
         compiler_params=params(12),
         cost_estimate=cost(0, 4e6),
     )(keep, got, mid, near)
 
 
-def last_kernel(count, rows1, rows2, *refs):
+def home_kernel(rows, keep_ref, got_ref, mid_ref, *refs):
+    smalls, (message_ref, base_ref) = refs[:-2], refs[-2:]
+    total = keep_ref[...].astype(F32) + got_ref[...].astype(F32) + mid_ref[...].astype(F32)
+    base_ref[...] = total[:rows]
+    message_ref[SMALL_ROWS:, :] = total[rows:].astype(BF)
+    small = smalls[0][...].astype(F32)
+    for term in smalls[1:]:
+        small = small + term[...].astype(F32)
+    message_ref[:SMALL_ROWS, :] = small.astype(BF)
+
+
+def home_message(far, rows, keep, got, mid, smalls):
+    at = block(2 * rows, far)
+    return pl.pallas_call(
+        functools.partial(home_kernel, rows),
+        grid=(1,),
+        out_shape=(shape((SMALL_ROWS + rows, HID)), shape((rows, HID), F32)),
+        in_specs=[at, at, block(2 * rows)] + [block(SMALL_ROWS)] * len(smalls),
+        out_specs=(block(SMALL_ROWS + rows), block(rows)),
+        compiler_params=params(8),
+        cost_estimate=cost(0, 2e6),
+    )(keep, got, mid, *smalls)
+
+
+def total_kernel(*refs):
     total = refs[0][...].astype(F32)
-    for k in range(1, count):
-        total = total + refs[k][...].astype(F32)
-    w1_ref, w2_ref, o1_ref, o2_ref, token_ref = refs[count:]
-    token_ref[...] = total[:8, :LANES]
+    for term in refs[1:-1]:
+        total = total + term[...].astype(F32)
+    refs[-1][...] = total
+
+
+def totalled(*terms):
+    return pl.pallas_call(
+        total_kernel,
+        out_shape=shape(terms[0].shape, F32),
+        in_specs=[VSPEC] * len(terms),
+        out_specs=VSPEC,
+        compiler_params=params(4),
+        cost_estimate=cost(10e9, 1e6),
+    )(*terms)
+
+
+def last_kernel(rows1, rows2, paired, ids_ref, *refs):
+    if paired:
+        part_ref, sent_ref, near_ref = refs[:3]
+        total = part_ref[...] + near_ref[SMALL_ROWS:, :].astype(F32)
+        small = sent_ref[:SMALL_ROWS, :].astype(F32) + near_ref[:SMALL_ROWS, :].astype(F32)
+    else:
+        total, small = refs[0][...], refs[1][...]
+    w1_ref, w2_ref, o1_ref, o2_ref, sg_ref, ss_ref, og_ref, os_ref, gate_ref, t1_ref, t2_ref, t3_ref = refs[-12:]
     cut = SLOTS * rows1
     for s in range(EXPERTS):
         w1_ref[s] = total[s * rows1 : (s + 1) * rows1]
         w2_ref[s] = total[cut + s * rows2 : cut + (s + 1) * rows2]
     o1_ref[...] = total[EXPERTS * rows1 : cut]
     o2_ref[...] = total[cut + EXPERTS * rows2 :]
-
-
-def finish(parts, rows1, rows2):
-    outs = (
-        shape((EXPERTS, rows1, HID), F32),
-        shape((EXPERTS, rows2, HID), F32),
-        shape((rows1, HID), F32),
-        shape((rows2, HID), F32),
-        shape((8, LANES), F32),
-    )
-    return pl.pallas_call(
-        functools.partial(last_kernel, len(parts), rows1, rows2),
-        out_shape=outs,
-        in_specs=[VSPEC] * len(parts),
-        out_specs=(VSPEC,) * len(outs),
-        compiler_params=params(8),
-        cost_estimate=cost(10e9, 2e6),
-    )(*parts)
-
-
-def last_small_kernel(count, ids_ref, *refs):
-    small = refs[0][...].astype(F32)
-    for k in range(1, count):
-        small = small + refs[k][...].astype(F32)
-    sg_ref, ss_ref, og_ref, os_ref, gate_ref, t1_ref, t2_ref, t3_ref = refs[-8:]
     tiny = jnp.concatenate([small[:, :LANES], small[:, LANES:]], axis=0)
     t1_ref[...] = tiny[T1_AT : T1_AT + HID]
     t2_ref[...] = tiny[T2_AT : T2_AT + TOWER2]
@@ -854,8 +870,12 @@
     t3_ref[...] = tiny[MISC_AT + 12 : MISC_AT + 13, :TOWER2]
 
 
-def finish_small(ids, parts, after):
+def finish(ids, terms, rows1, rows2):
     outs = (
+        shape((EXPERTS, rows1, HID), F32),
+        shape((EXPERTS, rows2, HID), F32),
+        shape((rows1, HID), F32),
+        shape((rows2, HID), F32),
         shape((EXPERTS, HID), F32),
         shape((EXPERTS, HID), F32),
         shape((1, HID), F32),
@@ -866,13 +886,13 @@
         shape((1, TOWER2), F32),
     )
     return pl.pallas_call(
-        functools.partial(last_small_kernel, len(parts)),
+        functools.partial(last_kernel, rows1, rows2, len(terms) == 3),
         out_shape=outs,
-        in_specs=[SSPEC] + [VSPEC] * len(parts) + [ASPEC],
+        in_specs=[SSPEC] + [VSPEC] * len(terms),
         out_specs=(VSPEC,) * len(outs),
         compiler_params=params(8),
         cost_estimate=cost(0, 2e6),
-    )(ids, *parts, after)
+    )(ids, *terms)
 
 
 def per_device(
@@ -920,16 +940,21 @@
     )
     other_small = sibling(small)
     turned = entries.T
-    x_first = pool(0, 2, ids, meta, starts, ends, turned, small)
+    x_first = pool(0, 2, ids, meta, starts, ends, turned)
 
     if direct:
         zc = stacked(far)
         r1 = tied(crossed(zc, (1, 2)), x_first)
-        r2 = crossed(zc, (2, 1))
-        x_second = pool(1, 2, ids, meta, starts, ends, turned, r2)
+        r2 = crossed(tied(zc, x_first), (2, 1))
+        x_second = pool(1, 2, ids, meta, starts, ends, turned, other_small)
         r3 = tied(crossed(r1, (2, 1)), x_second)
         own = [zc, r2, r1, r3]
-        plan, used1, used2 = ((2 * quarter, 0), (2 * quarter, 1)), rows1, rows2
+        given = tuple(tuple((one, two, k) for k in range(quarter)) for one, two in ((0, 0), (0, 1), (1, 0), (1, 1)))
+        far_ones = [(two, k) for two in range(2) for k in range(1, quarter)]
+        home_ones = [(0, 0), (1, 0)]
+        send = [(1, *piece) for piece in far_ones]
+        keep = [(0, *piece) for piece in far_ones + home_ones] + [(1, *piece) for piece in home_ones]
+        plan, used1, used2 = ((0, tuple(keep)), (1, tuple(send))), rows1, rows2
     else:
         x_second = pool(1, 2, ids, meta, starts, ends, turned)
         every = lax.all_gather(pack, "dp", axis=0)
@@ -937,9 +962,9 @@
         w1 = every[:, :cut].reshape(n, SLOTS, rows1, HID).swapaxes(0, 1).reshape(-1, HID)
         w2 = every[:, cut:].reshape(n, SLOTS, rows2, HID).swapaxes(0, 1).reshape(-1, HID)
         own = [jnp.concatenate([w1, w2], axis=0)[None]]
-        plan, used1, used2 = ((1, 1),), D, HID
+        given, plan, used1, used2 = ((None,),), ((1, (None,)),), D, HID
     dx, own_grads, oth_grads = layer(
-        ids, [x_first, x_second], own, [sibling(group) for group in own], small, other_small, plan, used1, used2
+        ids, [x_first, x_second], own, [sibling(group) for group in own], small, other_small, given, plan, used1, used2
     )
 
     got = [sibling(grad) for grad in oth_grads[::-1]][::-1]
@@ -948,18 +973,21 @@
     piece = SLOTS * (rows1 + rows2)
     if direct:
         keep, send = own_grads
+        far, cut = quarter - 1, (quarter - 1) * piece
         send = summed(send, got[1])
         mid = tied(crossed(send, (1, 2)), expanded)
-        cut = quarter * piece
+        home = slice(2 * cut + 2 * piece, 2 * cut + 4 * piece)
+        home = summed(keep[home], got[0][home])
+        late = slice(cut, 2 * cut)
+        near = crossed(summed(keep[late], got[0][late], mid[SMALL_ROWS + cut :]), (2, 1))
         small = small_sum(send, mid)
-        send = summed(keep[cut:], got[0][cut:], mid[SMALL_ROWS + cut :])
-        near = crossed(send, (2, 1))
-        parts = far_messages(quarter, piece, keep, got[0], mid, near)
-        smalls = [small] + [tied(flipped(small, 4 * k), parts[0]) for k in range(1, quarter)]
-        parts = [parts[0]] + [flipped(parts[k], 4 * k) for k in range(1, quarter)]
-        small = summed(*smalls)
-        *grads, summed_up = finish(parts, rows1, rows2)
-        grads += finish_small(ids, [small, crossed(small, (2, 1))], summed_up)
+        home_mid = crossed(tied(home, mid), (1, 2))
+        smalls = [flipped(small, 4 * k) for k in range(1, quarter)]
+        parts = far_messages(far, piece, keep, got[0], mid, near)
+        smalls = [small] + [tied(term, parts[0]) for term in smalls]
+        message, base = home_message(far, piece, keep, got[0], home_mid, smalls)
+        parts = [flipped(part, 4 * (k + 1)) for k, part in enumerate(parts)]
+        grads = finish(ids, [totalled(base, *parts), message, crossed(message, (2, 1))], rows1, rows2)
     else:
         whole = own_grads[0].astype(F32) + got[0].astype(F32)
         small = lax.psum(whole[:SMALL_ROWS], "dp")
@@ -968,8 +996,7 @@
         g1 = lax.psum_scatter(whole[:cut].reshape(SLOTS, D, HID), "dp", scatter_dimension=1, tiled=True)
         g2 = lax.psum_scatter(whole[cut:].reshape(SLOTS, HID, HID), "dp", scatter_dimension=1, tiled=True)
         part = jnp.concatenate([g1.reshape(-1, HID), g2.reshape(-1, HID)], axis=0)
-        *grads, summed_up = finish([part], rows1, rows2)
-        grads += finish_small(ids, [small], summed_up)
+        grads = finish(ids, [part, small], rows1, rows2)
     w1, w2, o1, o2, sg, ss, og, os, gate, t1, t2, t3 = grads
     entry_grads = turned.T
     return (

time: 84.6 us -> 77.9 us (0.921)
  Pallas kernels: 37.6 us -> 32.6 us
  local copies, waits for them, and re-layouts: 1.7 us -> 0.04 us
  waiting for transfers between devices: 17.3 us -> 16.4 us
    pallas_call x4 -> x5, Pallas kernels: 23.1 us -> 18.5 us  [the longest x1 16.9 us: layer(): pl.pallas_call(functools.partial(main_kernel, len(x_parts), given, plan,...]
    ppermute x6 -> x7, waiting for transfers between devices: 10.1 us -> 7.33 us  [crossed(): return lax.ppermute(value, ('task', 'dp'), pairs)]
    ppermute x6 -> x7, starting transfers between devices: 7.88 us -> 10.3 us  [crossed(): return lax.ppermute(value, ('task', 'dp'), pairs)]
    ppermute x9, waiting for transfers between devices: 4.52 us -> 6.2 us  [flipped(): return lax.ppermute(value, 'dp', pairs)]
    unnamed x10 -> x9, local copies, waits for them, and re-layouts: 1.7 us -> 0.04 us
    ppermute x8, starting transfers between devices: 2.64 us -> 1.34 us  [sibling(): return lax.ppermute(value, 'task', [(0, 1), (1, 0)])]
  transfers between devices with their start and end apart: 23 -> 24, of which waited for: 9 -> 10; matrix products, arithmetic and copies ran while one was open for 1% -> 1% of each run, Pallas kernels for 18% -> 19%
where the time goes in v5:
time: 77.9 us; the launch traced here: 77.6 us
  Pallas kernels  32.6 us (42%)
  starting transfers between devices  25.9 us (33%)
  waiting for transfers between devices  16.4 us (21%)
  other arithmetic  1.67 us (2%)
  between operations  0.99 us (1%)
    pallas_call x1, Pallas kernels, layer(): pl.pallas_call(functools.partial(main_kernel, len(x_parts), given, plan,...  16.9 us
    ppermute x9, starting transfers between devices, flipped(): return lax.ppermute(value, 'dp', pairs)  14.3 us
    ppermute x7, starting transfers between devices, crossed(): return lax.ppermute(value, ('task', 'dp'), pairs)  10.3 us
    ppermute x7, waiting for transfers between devices, crossed(): return lax.ppermute(value, ('task', 'dp'), pairs)  7.33 us
    pallas_call x1, Pallas kernels, expand(): pl.pallas_call(functools.partial(expand_kernel, blocks // 2, group), grid...  6.52 us
    ppermute x9, waiting for transfers between devices, flipped(): return lax.ppermute(value, 'dp', pairs)  6.2 us
    pallas_call x2, Pallas kernels, pool(): pl.pallas_call(functools.partial(pool_kernel, part * count, count, half_b...  5.22 us
    ppermute x8, waiting for transfers between devices, sibling(): return lax.ppermute(value, 'task', [(0, 1), (1, 0)])  2.86 us
  transfers between devices with their start and end apart: 24, of which 10 were waited for; matrix products, arithmetic and copies ran while one was open for 1% of the time, Pallas kernels for 19%

profile of v5, /device:TPU:0, one launch (start us, length us, event | category | flops | bytes accessed | tf_op | source)
XLA Modules:
  0.0 77.6 jit_solution(8639159128135207968)
XLA Ops:
  1.5 5.0 %collective-permute-start.3 = (bf16[144,256]{1,0:T(8,128)(2,1)S(1)}, bf16[144,256]{1,0:T(8,128)(2,1)S(1)}, u32[]{:S(2)}, u32[]{:S(2)}) collective-permute-start(bf16[144,256]{1,0:T(8,128)(2,1)S(1)} %pad_maximum_fusion.refs_0_), channel_id=1, source_target_pairs={{0,12},{1,13},{2,14},{3,15},{4,8},{5,9},{6,10},{7,11},{8,4},{9,5},... | collective-permute-start | bytes 221192 | tf_op jit(solution)/shard_map/ppermute | solution.py:697
  7.7 1.7 %shard_map.256.refs_10_ = bf16[368,128]{1,0:T(8,128)(2,1)} custom-call(s32[2]{0:T(128)} %pad_add_fusion.ids_ref, s32[1,1536]{1,0:T(1,128)} %label_ref.1, bf16[2,256]{1,0:T(2,128)(2,1)} %bitcast.48, bf16[2,256]{1,0:T(2,128)(2,1)} %bitcast.49, bf16[1,256]{1,0:T(2,128)(2,1)} %ogain_ref.1, bf16[1,256]{1,0:T(2,128)(2,1)} %oshift_ref.1, bf16[4,512]{1,0:T(4,128)(2,1)} %bitcast.45, ...), custom_call_target="tpu_custom_call" | custom-call | flops 1000000000 | bytes 1000000 | tf_op jit(solution)/shard_map/pallas_call | solution.py:159
  9.7 3.0 %collective-permute-done.2.refs_2_ = bf16[144,256]{1,0:T(8,128)(2,1)S(1)} collective-permute-done((bf16[144,256]{1,0:T(8,128)(2,1)S(1)}, bf16[144,256]{1,0:T(8,128)(2,1)S(1)}, u32[]{:S(2)}, u32[]{:S(2)}) %collective-permute-start.2) | collective-permute-done | bytes 73760 | tf_op jit(solution)/shard_map/ppermute | solution.py:697
  13.1 1.6 %collective-permute-start.5 = (bf16[4,144,256]{2,1,0:T(8,128)(2,1)S(1)}, bf16[4,144,256]{2,1,0:T(8,128)(2,1)S(1)}, u32[]{:S(2)}, u32[]{:S(2)}) collective-permute-start(bf16[4,144,256]{2,1,0:T(8,128)(2,1)S(1)} %shard_map.258.refs_2_), channel_id=1, source_target_pairs={{0,1},{1,0},{2,3},{3,2},{4,5},{5,4},{6,7},{7,6},{8,9},{9,8},{10,11... | collective-permute-start | bytes 884744 | tf_op jit(solution)/shard_map/ppermute | solution.py:703
  14.7 2.5 %shard_map.255.refs_1_.refs_0_ = bf16[384,512]{1,0:T(8,128)(2,1)S(1)} custom-call(s32[2]{0:T(128)S(1)} %copy-done, s32[2,256]{1,0:T(2,128)S(1)} %get-tuple-element.42.meta_ref, s32[104,128]{1,0:T(8,128)S(1)} %get-tuple-element.43.st_ref, s32[104,128]{1,0:T(8,128)S(1)} %get-tuple-element.44.en_ref, bf16[64,18432]{1,0:T(8,128)(2,1)S(1)} %bitcast.30), custom_call_target="tpu_custom_call" | custom-call | flops 10000000000 | bytes 5000000 | tf_op jit(solution)/shard_map/pallas_call | solution.py:231
  17.3 1.6 %collective-permute-start.4 = (bf16[4,144,256]{2,1,0:T(8,128)(2,1)S(1)}, bf16[4,144,256]{2,1,0:T(8,128)(2,1)S(1)}, u32[]{:S(2)}, u32[]{:S(2)}) collective-permute-start(bf16[4,144,256]{2,1,0:T(8,128)(2,1)S(1)} %shard_map.259), channel_id=1, source_target_pairs={{0,2},{1,3},{2,0},{3,1},{4,6},{5,7},{6,4},{7,5},{8,10},{9,11},{10,... | collective-permute-start | bytes 884744 | tf_op jit(solution)/shard_map/ppermute | solution.py:703
  19.9 1.5 %collective-permute-start.6 = (bf16[4,144,256]{2,1,0:T(8,128)(2,1)S(1)}, bf16[4,144,256]{2,1,0:T(8,128)(2,1)S(1)}, u32[]{:S(2)}, u32[]{:S(2)}) collective-permute-start(bf16[4,144,256]{2,1,0:T(8,128)(2,1)S(1)} %shard_map.260.refs_4_), channel_id=1, source_target_pairs={{0,2},{1,3},{2,0},{3,1},{4,6},{5,7},{6,4},{7,5},{8,10},{9,11},{10,... | collective-permute-start | bytes 884744 | tf_op jit(solution)/shard_map/ppermute | solution.py:703
  21.5 2.7 %shard_map.257.refs_1_ = bf16[384,512]{1,0:T(8,128)(2,1)S(1)} custom-call(s32[2]{0:T(128)S(1)} %copy-done, s32[2,256]{1,0:T(2,128)S(1)} %get-tuple-element.42.meta_ref, s32[104,128]{1,0:T(8,128)S(1)} %get-tuple-element.43.st_ref, s32[104,128]{1,0:T(8,128)S(1)} %get-tuple-element.44.en_ref, bf16[64,18432]{1,0:T(8,128)(2,1)S(1)} %bitcast.31, ...), custom_call_target="tpu_custom_call" | custom-call | flops 10000000000 | bytes 5000000 | tf_op jit(solution)/shard_map/pallas_call | solution.py:231
  24.8 2.5 %collective-permute-done.6.refs_0_ = bf16[4,144,256]{2,1,0:T(8,128)(2,1)S(1)} collective-permute-done((bf16[4,144,256]{2,1,0:T(8,128)(2,1)S(1)}, bf16[4,144,256]{2,1,0:T(8,128)(2,1)S(1)}, u32[]{:S(2)}, u32[]{:S(2)}) %collective-permute-start.6) | collective-permute-done | bytes 294944 | tf_op jit(solution)/shard_map/ppermute | solution.py:703
  27.3 1.6 %collective-permute-done.10.refs_9_ = bf16[4,144,256]{2,1,0:T(8,128)(2,1)S(1)} collective-permute-done((bf16[4,144,256]{2,1,0:T(8,128)(2,1)S(1)}, bf16[4,144,256]{2,1,0:T(8,128)(2,1)S(1)}, u32[]{:S(2)}, u32[]{:S(2)}) %collective-permute-start.10) | collective-permute-done | bytes 294944 | tf_op jit(solution)/shard_map/ppermute | solution.py:692
  28.8 16.9 %shard_map.262 = (bf16[784,512]{1,0:T(8,128)(2,1)S(1)}, bf16[1440,256]{1,0:T(8,128)(2,1)S(1)}, bf16[1040,256]{1,0:T(8,128)(2,1)S(1)}, bf16[1440,256]{1,0:T(8,128)(2,1)S(1)}, bf16[1040,256]{1,0:T(8,128)(2,1)S(1)}) custom-call(s32[2]{0:T(128)S(1)} %copy-done, bf16[384,512]{1,0:T(8,128)(2,1)S(1)} %shard_map.255.refs_1_.refs_0_, ...), custom_call_target="tpu_custom_call" | custom-call | flops 5435817984 | bytes 10000000 | tf_op jit(solution)/shard_map/pallas_call | solution.py:679
  46.5 1.3 %collective-permute-done.13 = bf16[1040,256]{1,0:T(8,128)(2,1)S(1)} collective-permute-done((bf16[1040,256]{1,0:T(8,128)(2,1)S(1)}, bf16[1040,256]{1,0:T(8,128)(2,1)S(1)}, u32[]{:S(2)}, u32[]{:S(2)}) %collective-permute-start.13) | collective-permute-done | bytes 532512 | tf_op jit(solution)/shard_map/ppermute | solution.py:692
  47.9 1.1 %collective-permute-start.14 = (bf16[1040,256]{1,0:T(8,128)(2,1)S(1)}, bf16[1040,256]{1,0:T(8,128)(2,1)S(1)}, u32[]{:S(2)}, u32[]{:S(2)}) collective-permute-start(bf16[1040,256]{1,0:T(8,128)(2,1)S(1)} %add_convert_fusion.one_ref), channel_id=1, source_target_pairs={{0,1},{1,0},{2,3},{3,2},{4,5},{5,4},{6,7},{7,6},{8,9},{9,8},{10,11... | collective-permute-start | bytes 1597448 | tf_op jit(solution)/shard_map/ppermute | solution.py:703
  49.1 6.5 %shard_map.263 = (bf16[64,18432]{1,0:T(8,128)(2,1)}, f32[1,1536]{1,0:T(1,128)}, f32[8,128]{1,0:T(8,128)S(1)}) custom-call(s32[2]{0:T(128)S(1)} %copy-done, s32[2,256]{1,0:T(2,128)S(1)} %get-tuple-element.42.meta_ref, s32[104,128]{1,0:T(8,128)S(1)} %get-tuple-element.43.st_ref, s32[104,128]{1,0:T(8,128)S(1)} %get-tuple-element.44.en_ref, ...), custom_call_target="tpu_custom_call" | custom-call | flops 12000000000 | bytes 6000000 | tf_op jit(solution)/shard_map/pallas_call | solution.py:285
  55.6 1.7 %collective-permute-done.14.refs_0_ = bf16[1040,256]{1,0:T(8,128)(2,1)S(1)} collective-permute-done((bf16[1040,256]{1,0:T(8,128)(2,1)S(1)}, bf16[1040,256]{1,0:T(8,128)(2,1)S(1)}, u32[]{:S(2)}, u32[]{:S(2)}) %collective-permute-start.14) | collective-permute-done | bytes 532512 | tf_op jit(solution)/shard_map/ppermute | solution.py:703
  57.3 3.1 %collective-permute-start.19 = (bf16[176,256]{1,0:T(8,128)(2,1)S(1)}, bf16[176,256]{1,0:T(8,128)(2,1)S(1)}, u32[]{:S(2)}, u32[]{:S(2)}) collective-permute-start(bf16[176,256]{1,0:T(8,128)(2,1)S(1)} %shard_map.266.refs_0_), channel_id=1, source_target_pairs={{0,12},{1,13},{2,14},{3,15},{4,8},{5,9},{6,10},{7,11},{8,4},{9,5},... | collective-permute-start | bytes 270344 | tf_op jit(solution)/shard_map/ppermute | solution.py:697
  60.4 1.6 %collective-permute-start.17 = (bf16[432,256]{1,0:T(8,128)(2,1)S(1)}, bf16[432,256]{1,0:T(8,128)(2,1)S(1)}, u32[]{:S(2)}, u32[]{:S(2)}) collective-permute-start(bf16[432,256]{1,0:T(8,128)(2,1)S(1)} %add_convert_fusion.1), channel_id=1, source_target_pairs={{0,2},{1,3},{2,0},{3,1},{4,6},{5,7},{6,4},{7,5},{8,10},{9,11},{10,... | collective-permute-start | bytes 663560 | tf_op jit(solution)/shard_map/ppermute | solution.py:703
  63.2 1.7 %collective-permute-start.16 = (bf16[176,256]{1,0:T(8,128)(2,1)S(1)}, bf16[176,256]{1,0:T(8,128)(2,1)S(1)}, u32[]{:S(2)}, u32[]{:S(2)}) collective-permute-start(bf16[176,256]{1,0:T(8,128)(2,1)S(1)} %shard_map.266.refs_0_), channel_id=1, source_target_pairs={{0,4},{1,5},{2,6},{3,7},{4,0},{5,1},{6,2},{7,3},{8,12},{9,13},{10,... | collective-permute-start | bytes 270344 | tf_op jit(solution)/shard_map/ppermute | solution.py:697
  64.9 1.8 %collective-permute-done.17.near_ref = bf16[432,256]{1,0:T(8,128)(2,1)S(1)} collective-permute-done((bf16[432,256]{1,0:T(8,128)(2,1)S(1)}, bf16[432,256]{1,0:T(8,128)(2,1)S(1)}, u32[]{:S(2)}, u32[]{:S(2)}) %collective-permute-start.17) | collective-permute-done | bytes 221216 | tf_op jit(solution)/shard_map/ppermute | solution.py:703
  66.8 2.7 %collective-permute-start.21 = (bf16[144,256]{1,0:T(8,128)(2,1)S(1)}, bf16[144,256]{1,0:T(8,128)(2,1)S(1)}, u32[]{:S(2)}, u32[]{:S(2)}) collective-permute-start(bf16[144,256]{1,0:T(8,128)(2,1)S(1)} %get-tuple-element.55), channel_id=1, source_target_pairs={{0,8},{1,9},{2,10},{3,11},{4,12},{5,13},{6,14},{7,15},{8,0},{9,1},... | collective-permute-start | bytes 221192 | tf_op jit(solution)/shard_map/ppermute | solution.py:697
  69.5 1.1 %collective-permute-start.22 = (bf16[144,256]{1,0:T(8,128)(2,1)S(1)}, bf16[144,256]{1,0:T(8,128)(2,1)S(1)}, u32[]{:S(2)}, u32[]{:S(2)}) collective-permute-start(bf16[144,256]{1,0:T(8,128)(2,1)S(1)} %get-tuple-element.56), channel_id=1, source_target_pairs={{0,12},{1,13},{2,14},{3,15},{4,8},{5,9},{6,10},{7,11},{8,4},{9,5},... | collective-permute-start | bytes 221192 | tf_op jit(solution)/shard_map/ppermute | solution.py:697
  70.8 1.8 %collective-permute-start.23 = (bf16[320,256]{1,0:T(8,128)(2,1)S(1)}, bf16[320,256]{1,0:T(8,128)(2,1)S(1)}, u32[]{:S(2)}, u32[]{:S(2)}) collective-permute-start(bf16[320,256]{1,0:T(8,128)(2,1)S(1)} %get-tuple-element.57.refs_1_), channel_id=1, source_target_pairs={{0,2},{1,3},{2,0},{3,1},{4,6},{5,7},{6,4},{7,5},{8,10},{9,11},{10,... | collective-permute-start | bytes 491528 | tf_op jit(solution)/shard_map/ppermute | solution.py:703
  73.7 2.1 %collective-permute-done.22.refs_3_ = bf16[144,256]{1,0:T(8,128)(2,1)S(1)} collective-permute-done((bf16[144,256]{1,0:T(8,128)(2,1)S(1)}, bf16[144,256]{1,0:T(8,128)(2,1)S(1)}, u32[]{:S(2)}, u32[]{:S(2)}) %collective-permute-start.22) | collective-permute-done | bytes 73760 | tf_op jit(solution)/shard_map/ppermute | solution.py:697
  76.2 1.3 %shard_map.273 = (f32[2,32,256]{2,1,0:T(8,128)}, f32[2,16,256]{2,1,0:T(8,128)}, f32[32,256]{1,0:T(8,128)}, f32[16,256]{1,0:T(8,128)}, f32[2,256]{1,0:T(2,128)}, ...) custom-call(s32[2]{0:T(128)S(1)} %copy-done, ...), custom_call_target="tpu_custom_call" | custom-call | bytes 2000000 | tf_op jit(solution)/shard_map/pallas_call | solution.py:888
  (58 shorter events, 8.2 us)
Async XLA Ops:
  1.5 8.3 %collective-permute-start.3 = (bf16[144,256]{1,0:T(8,128)(2,1)S(1)}, bf16[144,256]{1,0:T(8,128)(2,1)S(1)}, u32[]{:S(2)}, u32[]{:S(2)}) collective-permute-start(bf16[144,256]{1,0:T(8,128)(2,1)S(1)} %pad_maximum_fusion.refs_0_), channel_id=1, source_target_pairs={{0,12},{1,13},{2,14},{3,15},{4,8},{5,9},{6,10},{7,11},{8,4},{9,5},... | collective-permute-start | bytes 221192 | tf_op jit(solution)/shard_map/ppermute | solution.py:697
  6.5 6.2 %collective-permute-start.2 = (bf16[144,256]{1,0:T(8,128)(2,1)S(1)}, bf16[144,256]{1,0:T(8,128)(2,1)S(1)}, u32[]{:S(2)}, u32[]{:S(2)}) collective-permute-start(bf16[144,256]{1,0:T(8,128)(2,1)S(1)} %pad_maximum_fusion.refs_0_), channel_id=1, source_target_pairs={{0,8},{1,9},{2,10},{3,11},{4,12},{5,13},{6,14},{7,15},{8,0},{9,1},... | collective-permute-start | bytes 221192 | tf_op jit(solution)/shard_map/ppermute | solution.py:697
  6.5 6.2 %collective-permute-start.1 = (bf16[144,256]{1,0:T(8,128)(2,1)S(1)}, bf16[144,256]{1,0:T(8,128)(2,1)S(1)}, u32[]{:S(2)}, u32[]{:S(2)}) collective-permute-start(bf16[144,256]{1,0:T(8,128)(2,1)S(1)} %pad_maximum_fusion.refs_0_), channel_id=1, source_target_pairs={{0,4},{1,5},{2,6},{3,7},{4,0},{5,1},{6,2},{7,3},{8,12},{9,13},{10,... | collective-permute-start | bytes 221192 | tf_op jit(solution)/shard_map/ppermute | solution.py:697
  9.4 12.0 %collective-permute-start = (bf16[368,128]{1,0:T(8,128)(2,1)}, bf16[368,128]{1,0:T(8,128)(2,1)S(1)}, u32[]{:S(2)}, u32[]{:S(2)}) collective-permute-start(bf16[368,128]{1,0:T(8,128)(2,1)} %shard_map.256.refs_10_), channel_id=1, source_target_pairs={{0,16},{16,0},{1,17},{17,1},{2,18},{18,2},{3,19},{19,3},{4,20},{20... | collective-permute-start | bytes 282632 | tf_op jit(solution)/shard_map/ppermute | solution.py:692
  13.1 6.8 %collective-permute-start.5 = (bf16[4,144,256]{2,1,0:T(8,128)(2,1)S(1)}, bf16[4,144,256]{2,1,0:T(8,128)(2,1)S(1)}, u32[]{:S(2)}, u32[]{:S(2)}) collective-permute-start(bf16[4,144,256]{2,1,0:T(8,128)(2,1)S(1)} %shard_map.258.refs_2_), channel_id=1, source_target_pairs={{0,1},{1,0},{2,3},{3,2},{4,5},{5,4},{6,7},{7,6},{8,9},{9,8},{10,11... | collective-permute-start | bytes 884744 | tf_op jit(solution)/shard_map/ppermute | solution.py:703
  17.2 10.0 %collective-permute-start.7 = (bf16[4,144,256]{2,1,0:T(8,128)(2,1)S(1)}, bf16[4,144,256]{2,1,0:T(8,128)(2,1)S(1)}, u32[]{:S(2)}, u32[]{:S(2)}) collective-permute-start(bf16[4,144,256]{2,1,0:T(8,128)(2,1)S(1)} %shard_map.258.refs_2_), channel_id=1, source_target_pairs={{0,16},{16,0},{1,17},{17,1},{2,18},{18,2},{3,19},{19,3},{4,20},{20... | collective-permute-start | bytes 884744 | tf_op jit(solution)/shard_map/ppermute | solution.py:692
  17.3 7.0 %collective-permute-start.4 = (bf16[4,144,256]{2,1,0:T(8,128)(2,1)S(1)}, bf16[4,144,256]{2,1,0:T(8,128)(2,1)S(1)}, u32[]{:S(2)}, u32[]{:S(2)}) collective-permute-start(bf16[4,144,256]{2,1,0:T(8,128)(2,1)S(1)} %shard_map.259), channel_id=1, source_target_pairs={{0,2},{1,3},{2,0},{3,1},{4,6},{5,7},{6,4},{7,5},{8,10},{9,11},{10,... | collective-permute-start | bytes 884744 | tf_op jit(solution)/shard_map/ppermute | solution.py:703
  19.9 7.3 %collective-permute-start.6 = (bf16[4,144,256]{2,1,0:T(8,128)(2,1)S(1)}, bf16[4,144,256]{2,1,0:T(8,128)(2,1)S(1)}, u32[]{:S(2)}, u32[]{:S(2)}) collective-permute-start(bf16[4,144,256]{2,1,0:T(8,128)(2,1)S(1)} %shard_map.260.refs_4_), channel_id=1, source_target_pairs={{0,2},{1,3},{2,0},{3,1},{4,6},{5,7},{6,4},{7,5},{8,10},{9,11},{10,... | collective-permute-start | bytes 884744 | tf_op jit(solution)/shard_map/ppermute | solution.py:703
  24.2 3.0 %collective-permute-start.9 = (bf16[4,144,256]{2,1,0:T(8,128)(2,1)S(1)}, bf16[4,144,256]{2,1,0:T(8,128)(2,1)S(1)}, u32[]{:S(2)}, u32[]{:S(2)}) collective-permute-start(bf16[4,144,256]{2,1,0:T(8,128)(2,1)S(1)} %shard_map.260.refs_4_), channel_id=1, source_target_pairs={{0,16},{16,0},{1,17},{17,1},{2,18},{18,2},{3,19},{19,3},{4,20},{20... | collective-permute-start | bytes 884744 | tf_op jit(solution)/shard_map/ppermute | solution.py:692
  24.3 3.0 %collective-permute-start.8 = (bf16[4,144,256]{2,1,0:T(8,128)(2,1)S(1)}, bf16[4,144,256]{2,1,0:T(8,128)(2,1)S(1)}, u32[]{:S(2)}, u32[]{:S(2)}) collective-permute-start(bf16[4,144,256]{2,1,0:T(8,128)(2,1)S(1)} %collective-permute-done.4.refs_3_), channel_id=1, source_target_pairs={{0,16},{16,0},{1,17},{17,1},{2,18},{18,2},{3,19},{19,3},{4,20},{20... | collective-permute-start | bytes 884744 | tf_op jit(solution)/shard_map/ppermute | solution.py:692
  27.2 1.6 %collective-permute-start.10 = (bf16[4,144,256]{2,1,0:T(8,128)(2,1)S(1)}, bf16[4,144,256]{2,1,0:T(8,128)(2,1)S(1)}, u32[]{:S(2)}, u32[]{:S(2)}) collective-permute-start(bf16[4,144,256]{2,1,0:T(8,128)(2,1)S(1)} %shard_map.261.refs_5_), channel_id=1, source_target_pairs={{0,16},{16,0},{1,17},{17,1},{2,18},{18,2},{3,19},{19,3},{4,20},{20... | collective-permute-start | bytes 884744 | tf_op jit(solution)/shard_map/ppermute | solution.py:692
  45.8 2.0 %collective-permute-start.13 = (bf16[1040,256]{1,0:T(8,128)(2,1)S(1)}, bf16[1040,256]{1,0:T(8,128)(2,1)S(1)}, u32[]{:S(2)}, u32[]{:S(2)}) collective-permute-start(bf16[1040,256]{1,0:T(8,128)(2,1)S(1)} %get-tuple-element.51), channel_id=1, source_target_pairs={{0,16},{16,0},{1,17},{17,1},{2,18},{18,2},{3,19},{19,3},{4,20},{20... | collective-permute-start | bytes 1597448 | tf_op jit(solution)/shard_map/ppermute | solution.py:692
  46.0 3.1 %collective-permute-start.11 = (bf16[784,512]{1,0:T(8,128)(2,1)S(1)}, bf16[784,512]{1,0:T(8,128)(2,1)S(1)}, u32[]{:S(2)}, u32[]{:S(2)}) collective-permute-start(bf16[784,512]{1,0:T(8,128)(2,1)S(1)} %get-tuple-element.45.own_ref), channel_id=1, source_target_pairs={{0,16},{16,0},{1,17},{17,1},{2,18},{18,2},{3,19},{19,3},{4,20},{20... | collective-permute-start | bytes 2408456 | tf_op jit(solution)/shard_map/ppermute | solution.py:692
  46.3 14.0 %collective-permute-start.12 = (bf16[1440,256]{1,0:T(8,128)(2,1)S(1)}, bf16[1440,256]{1,0:T(8,128)(2,1)S(1)}, u32[]{:S(2)}, u32[]{:S(2)}) collective-permute-start(bf16[1440,256]{1,0:T(8,128)(2,1)S(1)} %get-tuple-element.49), channel_id=1, source_target_pairs={{0,16},{16,0},{1,17},{17,1},{2,18},{18,2},{3,19},{19,3},{4,20},{20... | collective-permute-start | bytes 2211848 | tf_op jit(solution)/shard_map/ppermute | solution.py:692
  47.9 9.3 %collective-permute-start.14 = (bf16[1040,256]{1,0:T(8,128)(2,1)S(1)}, bf16[1040,256]{1,0:T(8,128)(2,1)S(1)}, u32[]{:S(2)}, u32[]{:S(2)}) collective-permute-start(bf16[1040,256]{1,0:T(8,128)(2,1)S(1)} %add_convert_fusion.one_ref), channel_id=1, source_target_pairs={{0,1},{1,0},{2,3},{3,2},{4,5},{5,4},{6,7},{7,6},{8,9},{9,8},{10,11... | collective-permute-start | bytes 1597448 | tf_op jit(solution)/shard_map/ppermute | solution.py:703
  57.3 12.3 %collective-permute-start.19 = (bf16[176,256]{1,0:T(8,128)(2,1)S(1)}, bf16[176,256]{1,0:T(8,128)(2,1)S(1)}, u32[]{:S(2)}, u32[]{:S(2)}) collective-permute-start(bf16[176,256]{1,0:T(8,128)(2,1)S(1)} %shard_map.266.refs_0_), channel_id=1, source_target_pairs={{0,12},{1,13},{2,14},{3,15},{4,8},{5,9},{6,10},{7,11},{8,4},{9,5},... | collective-permute-start | bytes 270344 | tf_op jit(solution)/shard_map/ppermute | solution.py:697
  60.3 10.3 %collective-permute-start.18 = (bf16[176,256]{1,0:T(8,128)(2,1)S(1)}, bf16[176,256]{1,0:T(8,128)(2,1)S(1)}, u32[]{:S(2)}, u32[]{:S(2)}) collective-permute-start(bf16[176,256]{1,0:T(8,128)(2,1)S(1)} %shard_map.266.refs_0_), channel_id=1, source_target_pairs={{0,8},{1,9},{2,10},{3,11},{4,12},{5,13},{6,14},{7,15},{8,0},{9,1},... | collective-permute-start | bytes 270344 | tf_op jit(solution)/shard_map/ppermute | solution.py:697
  60.4 6.3 %collective-permute-start.17 = (bf16[432,256]{1,0:T(8,128)(2,1)S(1)}, bf16[432,256]{1,0:T(8,128)(2,1)S(1)}, u32[]{:S(2)}, u32[]{:S(2)}) collective-permute-start(bf16[432,256]{1,0:T(8,128)(2,1)S(1)} %add_convert_fusion.1), channel_id=1, source_target_pairs={{0,2},{1,3},{2,0},{3,1},{4,6},{5,7},{6,4},{7,5},{8,10},{9,11},{10,... | collective-permute-start | bytes 663560 | tf_op jit(solution)/shard_map/ppermute | solution.py:703
  62.1 8.6 %collective-permute-start.15 = (bf16[288,256]{1,0:T(8,128)(2,1)S(1)}, bf16[288,256]{1,0:T(8,128)(2,1)S(1)}, u32[]{:S(2)}, u32[]{:S(2)}) collective-permute-start(bf16[288,256]{1,0:T(8,128)(2,1)S(1)} %shard_map.265), channel_id=1, source_target_pairs={{0,1},{1,0},{2,3},{3,2},{4,5},{5,4},{6,7},{7,6},{8,9},{9,8},{10,11... | collective-permute-start | bytes 442376 | tf_op jit(solution)/shard_map/ppermute | solution.py:703
  63.2 7.5 %collective-permute-start.16 = (bf16[176,256]{1,0:T(8,128)(2,1)S(1)}, bf16[176,256]{1,0:T(8,128)(2,1)S(1)}, u32[]{:S(2)}, u32[]{:S(2)}) collective-permute-start(bf16[176,256]{1,0:T(8,128)(2,1)S(1)} %shard_map.266.refs_0_), channel_id=1, source_target_pairs={{0,4},{1,5},{2,6},{3,7},{4,0},{5,1},{6,2},{7,3},{8,12},{9,13},{10,... | collective-permute-start | bytes 270344 | tf_op jit(solution)/shard_map/ppermute | solution.py:697
  66.8 6.8 %collective-permute-start.21 = (bf16[144,256]{1,0:T(8,128)(2,1)S(1)}, bf16[144,256]{1,0:T(8,128)(2,1)S(1)}, u32[]{:S(2)}, u32[]{:S(2)}) collective-permute-start(bf16[144,256]{1,0:T(8,128)(2,1)S(1)} %get-tuple-element.55), channel_id=1, source_target_pairs={{0,8},{1,9},{2,10},{3,11},{4,12},{5,13},{6,14},{7,15},{8,0},{9,1},... | collective-permute-start | bytes 221192 | tf_op jit(solution)/shard_map/ppermute | solution.py:697
  69.5 6.3 %collective-permute-start.22 = (bf16[144,256]{1,0:T(8,128)(2,1)S(1)}, bf16[144,256]{1,0:T(8,128)(2,1)S(1)}, u32[]{:S(2)}, u32[]{:S(2)}) collective-permute-start(bf16[144,256]{1,0:T(8,128)(2,1)S(1)} %get-tuple-element.56), channel_id=1, source_target_pairs={{0,12},{1,13},{2,14},{3,15},{4,8},{5,9},{6,10},{7,11},{8,4},{9,5},... | collective-permute-start | bytes 221192 | tf_op jit(solution)/shard_map/ppermute | solution.py:697
  70.7 5.1 %collective-permute-start.20 = (bf16[144,256]{1,0:T(8,128)(2,1)S(1)}, bf16[144,256]{1,0:T(8,128)(2,1)S(1)}, u32[]{:S(2)}, u32[]{:S(2)}) collective-permute-start(bf16[144,256]{1,0:T(8,128)(2,1)S(1)} %get-tuple-element.53.refs_1_), channel_id=1, source_target_pairs={{0,4},{1,5},{2,6},{3,7},{4,0},{5,1},{6,2},{7,3},{8,12},{9,13},{10,... | collective-permute-start | bytes 221192 | tf_op jit(solution)/shard_map/ppermute | solution.py:697
  70.8 5.4 %collective-permute-start.23 = (bf16[320,256]{1,0:T(8,128)(2,1)S(1)}, bf16[320,256]{1,0:T(8,128)(2,1)S(1)}, u32[]{:S(2)}, u32[]{:S(2)}) collective-permute-start(bf16[320,256]{1,0:T(8,128)(2,1)S(1)} %get-tuple-element.57.refs_1_), channel_id=1, source_target_pairs={{0,2},{1,3},{2,0},{3,1},{4,6},{5,7},{6,4},{7,5},{8,10},{9,11},{10,... | collective-permute-start | bytes 491528 | tf_op jit(solution)/shard_map/ppermute | solution.py:703
  (4 other events, 21.2 us)

commit v6 on v5

--- a/solution.py
+++ b/solution.py
@@ -25,6 +25,7 @@
 SLOTS = 3
 BIG = 2 * SLOTS
 WIDE = BIG * HID
+HALF = SLOTS * HID
 PIECE = 32
 SPAN = 256
 BF = jnp.bfloat16
@@ -340,47 +341,152 @@
     lax.fori_loop(0, events // LANES, step, 0)
 
 
-def main_kernel(xs, given, plan, rows1, rows2, ids_ref, *refs):
+def part(m):
+    return slice(m * HID, (m + 1) * HID)
+
+
+def pick(own, other, rows):
+    if rows.start < HALF:
+        return own.at[rows]
+    return other.at[slice(rows.start - HALF, rows.stop - HALF)]
+
+
+def spans_of(events):
+    span = next(size for size in (SPAN, 2 * LANES, LANES) if events % size == 0)
+    return [slice(at, at + span) for at in range(0, events, span)]
+
+
+def rows_of(ids_ref, t, piece, rows1, rows2):
+    if piece is None:
+        return pl.ds(0, rows1), pl.ds(0, rows2)
+    where = ids_ref[0] if t == 0 else 1 - ids_ref[0]
+    d = ids_ref[1] ^ (4 * piece[2])
+    if piece[1]:
+        d = d ^ (2 - where)
+    if piece[0]:
+        d = d ^ (1 + where)
+    return (
+        pl.ds(pl.multiple_of(d * rows1, rows1), rows1),
+        pl.ds(pl.multiple_of(d * rows2, rows2), rows2),
+    )
+
+
+def assemble(ids_ref, t, groups, given, rows1, rows2, w1_ref, w2_ref):
+    for group, pieces in zip(groups, given):
+        for g, piece in enumerate(pieces):
+            one, two = rows_of(ids_ref, t, piece, rows1, rows2)
+            for s in range(SLOTS):
+                w1_ref[one, part(s)] = group[g, s * rows1 : (s + 1) * rows1, :]
+                low = SLOTS * rows1 + s * rows2
+                w2_ref[s, two, :] = (0.5 * group[g, low : low + rows2, :].astype(F32)).astype(BF)
+
+
+def put(ids_ref, t, s, outs, plan, rows1, rows2, held_ref, first, value):
+    held_ref[...] = value
+    for out, (small_first, pieces) in zip(outs, plan):
+        for g, piece in enumerate(pieces):
+            mine = rows_of(ids_ref, t, piece, rows1, rows2)[0 if first else 1]
+            at = g * SLOTS * (rows1 + rows2) + (SMALL_ROWS if small_first else 0)
+            at, size = (at + s * rows1, rows1) if first else (at + SLOTS * rows1 + s * rows2, rows2)
+            value = held_ref[mine, :]
+            out[at : at + size, :] = (value if first else 0.5 * value).astype(BF)
+
+
+def first_layer(s, w1_ref, x_ref, pc_ref):
+    pc_ref[part(s), :] = tn(w1_ref[:, part(s)], x_ref[...])
+
+
+def first_gelu(s, pc_ref, h_ref):
+    for here in spans_of(pc_ref.shape[1]):
+        for rows in pieces_of(s):
+            act, slope = gelu_twice(pc_ref[rows, here])
+            pc_ref[rows, here] = slope
+            h_ref[rows, here] = act.astype(BF)
+
+
+def front_kernel(xs, given, rows1, rows2, ids_ref, *refs):
     refs = list(refs)
     take = lambda n: [refs.pop(0) for _ in range(n)]
-    x_parts = take(xs)
-    own_groups, oth_groups = take(len(given)), take(len(given))
+    x_parts, groups = take(xs), take(len(given))
+    x_ref, w1_ref, w2_ref, pc_ref, h_ref = refs
+    size = x_ref.shape[1] // xs
+    for k, piece in enumerate(x_parts):
+        x_ref[:, k * size : (k + 1) * size] = piece[...].T
+    assemble(ids_ref, 0, groups, given, rows1, rows2, w1_ref, w2_ref)
+    first_layer(0, w1_ref, x_ref, pc_ref)
+    for s in range(SLOTS):
+        if s + 1 < SLOTS:
+            first_layer(s + 1, w1_ref, x_ref, pc_ref)
+        first_gelu(s, pc_ref, h_ref)
+
+
+def front(ids, x_parts, groups, given, rows1, rows2):
+    events = sum(part.shape[0] for part in x_parts)
+    outs = (
+        shape((D, events)),
+        shape((D, HALF)),
+        shape((SLOTS, HID, HID)),
+        shape((HALF, events), F32),
+        shape((HALF, events)),
+    )
+    return pl.pallas_call(
+        functools.partial(front_kernel, len(x_parts), given, rows1, rows2),
+        out_shape=outs,
+        in_specs=[SSPEC] + [VSPEC] * (len(x_parts) + len(groups)),
+        out_specs=(VSPEC,) * len(outs),
+        compiler_params=params(16),
+        cost_estimate=cost(6e9, 4e6),
+    )(ids, *x_parts, *groups)
+
+
+def back_kernel(plan, rows1, rows2, ids_ref, x_ref, h_ref, e_ref, f_ref, small_ref, *refs):
+    outs, (g1_ref, g2_ref) = refs[:-2], refs[-2:]
+    for s in range(SLOTS):
+        g2 = nt(h_ref[part(s), :], e_ref[part(s), :])
+        put(ids_ref, 0, s, outs, plan, rows1, rows2, g2_ref.at[s % 2], False, g2)
+        g1 = nt(x_ref[...], f_ref[part(s), :])
+        put(ids_ref, 0, s, outs, plan, rows1, rows2, g1_ref.at[s % 2], True, g1)
+    for out, (small_first, _) in zip(outs, plan):
+        if small_first:
+            out[:SMALL_ROWS, :] = small_ref[...]
+
+
+def grad_shapes(plan, rows1, rows2):
+    rows = SLOTS * (rows1 + rows2)
+    return tuple(shape((len(pieces) * rows + small * SMALL_ROWS, HID)) for small, pieces in plan)
+
+
+def back(ids, x, h, e, f, small, plan, rows1, rows2):
+    outs = grad_shapes(plan, rows1, rows2)
+    return pl.pallas_call(
+        functools.partial(back_kernel, plan, rows1, rows2),
+        out_shape=outs,
+        in_specs=[SSPEC] + [VSPEC] * 5,
+        out_specs=(VSPEC,) * len(outs),
+        scratch_shapes=[pltpu.VMEM((2, D, HID), F32), pltpu.VMEM((2, HID, HID), F32)],
+        compiler_params=params(16),
+        cost_estimate=cost(6e9, 4e6),
+    )(ids, x, h, e, f, small)
+
+
+def main_kernel(given, plan, rows1, rows2, ids_ref, *refs):
+    refs = list(refs)
+    take = lambda n: [refs.pop(0) for _ in range(n)]
+    x_ref, w1own_ref, w2own_ref, pcown_ref, hown_ref = take(5)
+    oth_groups = take(len(given))
     packs = take(2)
-    (dx_ref,) = take(1)
-    own_outs, oth_outs = take(len(plan)), take(len(plan))
-    x_ref, wc_ref, w2_ref, gain_ref, third_ref, lab_ref, pc_ref, pb_ref, s2_ref, y_ref, h_ref, e_ref, fc_ref = take(13)
-    scale_ref, lg_ref, prob_ref, q_ref, pt_ref, u1_ref, p4_ref, e2_ref, e1_ref, du_ref, dm_ref, dmb_ref, ds_ref, dn_ref, acc3_ref, pred_ref, g1_ref, g2_ref, dp_ref = take(19)
+    dx_ref, eown_ref, fown_ref, small_ref = take(4)
+    oth_outs = take(len(plan))
+    wc_ref, w2_ref, gain_ref, third_ref, lab_ref, pc_ref, pb_ref, s2_ref, y_ref, h_ref, e_ref, fc_ref = take(12)
+    scale_ref, lg_ref, prob_ref, q_ref, pt_ref, u1_ref, p4_ref, e2_ref, e1_ref, du_ref, dm_ref, dmb_ref = take(12)
+    ds_ref, dn_ref, acc3_ref, pred_ref, g1_ref, g2_ref, dp_ref = take(7)
     position = ids_ref[0]
     events = x_ref.shape[1]
 
-    def part(m):
-        return slice(m * HID, (m + 1) * HID)
-
-    def rows_of(t, piece):
-        if piece is None:
-            return pl.ds(0, rows1), pl.ds(0, rows2)
-        where = position if t == 0 else 1 - position
-        d = ids_ref[1] ^ (4 * piece[2])
-        if piece[1]:
-            d = d ^ (2 - where)
-        if piece[0]:
-            d = d ^ (1 + where)
-        return (
-            pl.ds(pl.multiple_of(d * rows1, rows1), rows1),
-            pl.ds(pl.multiple_of(d * rows2, rows2), rows2),
-        )
-
-    size = events // xs
-    for k, piece in enumerate(x_parts):
-        x_ref[:, k * size : (k + 1) * size] = piece[...].T
-    for t, whole in enumerate((own_groups, oth_groups)):
-        for group, pieces in zip(whole, given):
-            for g, piece in enumerate(pieces):
-                one, two = rows_of(t, piece)
-                for s in range(SLOTS):
-                    wc_ref[one, part(t * SLOTS + s)] = group[g, s * rows1 : (s + 1) * rows1, :]
-                    low = SLOTS * rows1 + s * rows2
-                    w2_ref[t * SLOTS + s, two, :] = (0.5 * group[g, low : low + rows2, :].astype(F32)).astype(BF)
+    def second_weights(m):
+        return w2own_ref[m] if m < SLOTS else w2_ref[m - SLOTS]
+
+    assemble(ids_ref, 1, oth_groups, given, rows1, rows2, wc_ref, w2_ref)
     lines = []
     for t in range(2):
         block = packs[t][GATE_AT : GATE_AT + 16, :].astype(F32)
@@ -390,8 +496,8 @@
             )
         lines.append(jnp.zeros((8 - GATES, D), F32))
     gates = jnp.concatenate(lines, axis=0).astype(BF)
-    wc_ref[:, WIDE:] = jnp.concatenate([gates, jnp.zeros((LANES - 16, D), BF)], axis=0).T
-    fc_ref[WIDE:, :] = jnp.zeros((LANES, events), BF)
+    wc_ref[:, HALF:] = jnp.concatenate([gates, jnp.zeros((LANES - 16, D), BF)], axis=0).T
+    fc_ref[HALF:, :] = jnp.zeros((LANES, events), BF)
     acc3_ref[...] = jnp.zeros_like(acc3_ref)
     miscs = [packs[t][MISC_AT : MISC_AT + 16, :].astype(F32) for t in range(2)]
     for t in range(2):
@@ -407,18 +513,7 @@
         lab_ref[t * 16 : (t + 1) * 16, :] = packs[t][LABEL_AT : LABEL_AT + 16, :].astype(F32)
 
     lg_ref[...] = nn(gates, x_ref[...])
-    span = next(size for size in (SPAN, 2 * LANES, LANES) if events % size == 0)
-    spans = [slice(at, at + span) for at in range(0, events, span)]
-
-    def first_sums(m):
-        pc_ref[part(m), :] = tn(wc_ref[:, part(m)], x_ref[...])
-
-    def first_gelu(m):
-        for here in spans:
-            for rows in pieces_of(m):
-                act, slope = gelu_twice(pc_ref[rows, here])
-                pc_ref[rows, here] = slope
-                h_ref[rows, here] = act.astype(BF)
+    spans = spans_of(events)
 
     def second_gelu(m, here):
         total = None
@@ -445,17 +540,20 @@
                     out = out.astype(BF).astype(F32)
                 y_ref[rows, block] = out
 
-    first_sums(0)
-    for m in range(BIG):
-        if m + 1 < BIG:
-            first_sums(m + 1)
-        first_gelu(m)
-        pb_ref[part(m), :] = tn(w2_ref[m], h_ref[part(m), :])
-        if m:
+    turn = [m for s in range(SLOTS) for m in (s, SLOTS + s)]
+    first_layer(0, wc_ref, x_ref, pc_ref)
+    for i, m in enumerate(turn):
+        s = m - SLOTS
+        if s >= 0:
+            if s + 1 < SLOTS:
+                first_layer(s + 1, wc_ref, x_ref, pc_ref)
+            first_gelu(s, pc_ref, h_ref)
+        pb_ref[part(m), :] = tn(second_weights(m), pick(hown_ref, h_ref, part(m))[...])
+        if i:
             for here in spans:
-                second_gelu(m - 1, here)
+                second_gelu(turn[i - 1], here)
     for here in spans:
-        second_gelu(BIG - 1, here)
+        second_gelu(turn[-1], here)
     orders = [(t * SLOTS, t * SLOTS + 1, t * SLOTS + 2, (1 - t) * SLOTS + 2) for t in range(2)]
 
     prob_ref[...] = jnp.ones_like(prob_ref)
@@ -557,33 +655,29 @@
         one, two = one * (1.0 / HID), two * (1.0 / HID)
         for rows in pieces_of(m):
             inner = y_ref[rows, here] - one - pb_ref[rows, here] * two
-            e_ref[rows, here] = (s2_ref[rows, here] * outer * inner).astype(BF)
-
-    def put(m, first, value, scale):
-        t, s = divmod(m, SLOTS)
-        held = (g1_ref if first else g2_ref).at[m % 2]
-        held[...] = value
-        for out, (small_first, pieces) in zip((own_outs, oth_outs)[t], plan):
-            for g, piece in enumerate(pieces):
-                mine = rows_of(t, piece)[0 if first else 1]
-                at = g * SLOTS * (rows1 + rows2) + (SMALL_ROWS if small_first else 0)
-                at, size = (at + s * rows1, rows1) if first else (at + SLOTS * rows1 + s * rows2, rows2)
-                out[at : at + size, :] = (scale * held[mine, :]).astype(BF)
+            pick(eown_ref, e_ref, rows)[:, here] = (s2_ref[rows, here] * outer * inner).astype(BF)
 
     for here in spans:
         shared_probs(here)
+    turn = [m for s in range(SLOTS) for m in (SLOTS + s, s)]
     for here in spans:
-        norm_back(0, here)
-    for m in range(BIG):
-        y_ref[part(m), :] = nn(w2_ref[m], e_ref[part(m), :])
-        put(m, False, nt(h_ref[part(m), :], e_ref[part(m), :]), 0.5)
-        if m + 1 < BIG:
+        norm_back(turn[0], here)
+    for i, m in enumerate(turn):
+        y_ref[part(m), :] = nn(second_weights(m), pick(eown_ref, e_ref, part(m))[...])
+        s = m - SLOTS
+        if s >= 0:
+            g2 = nt(h_ref[part(s), :], e_ref[part(s), :])
+            put(ids_ref, 1, s, oth_outs, plan, rows1, rows2, g2_ref.at[s % 2], False, g2)
+        if i + 1 < BIG:
             for here in spans:
-                norm_back(m + 1, here)
+                norm_back(turn[i + 1], here)
         for here in spans:
             for rows in pieces_of(m):
-                fc_ref[rows, here] = (pc_ref[rows, here] * y_ref[rows, here]).astype(BF)
-        put(m, True, nt(x_ref[...], fc_ref[part(m), :]), 1.0)
+                value = pick(pcown_ref, pc_ref, rows)[:, here] * y_ref[rows, here]
+                pick(fown_ref, fc_ref, rows)[:, here] = value.astype(BF)
+        if s >= 0:
+            g1 = nt(x_ref[...], fc_ref[part(s), :])
+            put(ids_ref, 1, s, oth_outs, plan, rows1, rows2, g1_ref.at[s % 2], True, g1)
     codes = []
     for t in range(2):
         probs = [probs_of(t, k, slice(None)) for k in range(GATES)]
@@ -593,18 +687,19 @@
             weighted = weighted + probs[k] * d_probs[k]
         codes += [probs[k] * (d_probs[k] - weighted) for k in range(GATES)]
         codes.append(jnp.zeros((8 - GATES, events), F32))
-    fc_ref[WIDE : WIDE + 16, :] = jnp.concatenate(codes, axis=0).astype(BF)
-    dx_ref[:events, :] = nn(wc_ref[...], fc_ref[...]).astype(BF).T
+    fc_ref[HALF : HALF + 16, :] = jnp.concatenate(codes, axis=0).astype(BF)
+    dx = nn(w1own_ref[...], fown_ref[...]) + nn(wc_ref[...], fc_ref[...])
+    dx_ref[:events, :] = dx.astype(BF).T
     pred = pred_ref[...]
     high = pred.astype(BF)
     low = (pred - high.astype(F32)).astype(BF)
     dx_ref[events:, :] = jnp.concatenate([high, low, high, low], axis=1)
 
-    gate_grad = nt(fc_ref[WIDE : WIDE + 16, :], x_ref[...])
+    gate_grad = nt(fc_ref[HALF : HALF + 16, :], x_ref[...])
     weights = prob_ref[...].astype(BF)
     shifts = [nt(weights, dmb_ref[part(t), :]) for t in range(2)]
     third_grad = col_sum(acc3_ref[...].T)
-    for t, results in enumerate((own_outs, oth_outs)):
+    for t in range(2):
         tower = slice(t * TOWER1, (t + 1) * TOWER1)
         half = slice(t * TOWER2, (t + 1) * TOWER2)
         lines = []
@@ -631,30 +726,31 @@
             axis=0,
         )
         small = jnp.concatenate([small[:SMALL_ROWS], small[SMALL_ROWS:]], axis=1).astype(BF)
-        for out, (small_first, _) in zip(results, plan):
+        if t == 0:
+            small_ref[...] = small
+            continue
+        for out, (small_first, _) in zip(oth_outs, plan):
             if small_first:
                 out[:SMALL_ROWS, :] = small
 
 
-def layer(ids, x_parts, own_groups, oth_groups, own_pack, oth_pack, given, plan, rows1, rows2):
-    events = sum(part.shape[0] for part in x_parts)
-    rows = SLOTS * (rows1 + rows2)
-    grads = tuple(shape((len(pieces) * rows + small * SMALL_ROWS, HID)) for small, pieces in plan)
-    results = (shape((events + 16, D)),) + grads + grads
+def layer(ids, started, oth_groups, own_pack, oth_pack, given, plan, rows1, rows2):
+    events = started[0].shape[1]
+    half = shape((HALF, events))
+    results = (shape((events + 16, D)), half, half, shape((SMALL_ROWS, HID))) + grad_shapes(plan, rows1, rows2)
     scratch = [
-        ((D, events), BF),
-        ((D, WIDE + LANES), BF),
-        ((BIG, HID, HID), BF),
+        ((D, HALF + LANES), BF),
+        ((SLOTS, HID, HID), BF),
         ((2 * WIDE, LANES), F32),
         ((2 * TOWER2, LANES), F32),
         ((32, LANES), F32),
+        ((HALF, events), F32),
         ((WIDE, events), F32),
         ((WIDE, events), F32),
         ((WIDE, events), F32),
-        ((WIDE, events), F32),
-        ((WIDE, events), BF),
-        ((WIDE, events), BF),
-        ((WIDE + LANES, events), BF),
+        ((HALF, events), BF),
+        ((HALF, events), BF),
+        ((HALF + LANES, events), BF),
         ((8, events), F32),
         ((16, events), F32),
         ((16, events), F32),
@@ -675,17 +771,16 @@
         ((2, HID, HID), F32),
         ((16, events), F32),
     ]
-    arrays = [*x_parts, *own_groups, *oth_groups, own_pack, oth_pack]
-    dx, *grads = pl.pallas_call(
-        functools.partial(main_kernel, len(x_parts), given, plan, rows1, rows2),
+    arrays = [*started, *oth_groups, own_pack, oth_pack]
+    return pl.pallas_call(
+        functools.partial(main_kernel, given, plan, rows1, rows2),
         out_shape=results,
         in_specs=[SSPEC] + [VSPEC] * len(arrays),
         out_specs=(VSPEC,) * len(results),
         scratch_shapes=[pltpu.VMEM(dims, kind) for dims, kind in scratch],
-        compiler_params=params(46),
+        compiler_params=params(42),
         cost_estimate=cost(events * BIG * 196608 * 6, 10e6),
     )(ids, *arrays)
-    return dx, grads[: len(plan)], grads[len(plan) :]
 
 
 def sibling(value):
@@ -963,11 +1058,11 @@
         w2 = every[:, cut:].reshape(n, SLOTS, rows2, HID).swapaxes(0, 1).reshape(-1, HID)
         own = [jnp.concatenate([w1, w2], axis=0)[None]]
         given, plan, used1, used2 = ((None,),), ((1, (None,)),), D, HID
-    dx, own_grads, oth_grads = layer(
-        ids, [x_first, x_second], own, [sibling(group) for group in own], small, other_small, given, plan, used1, used2
-    )
-
+    other = [sibling(group) for group in own]
+    started = front(ids, [x_first, x_second], own, given, used1, used2)
+    dx, e, f, own_small, *oth_grads = layer(ids, started, other, small, other_small, given, plan, used1, used2)
     got = [sibling(grad) for grad in oth_grads[::-1]][::-1]
+    own_grads = back(ids, started[0], started[4], e, f, own_small, plan, used1, used2)
     other_dx = sibling(dx)
     turned, predictions, expanded = expand(ids, meta, starts, ends, dx, other_dx, rows)
     piece = SLOTS * (rows1 + rows2)
@@ -982,7 +1077,11 @@
         near = crossed(summed(keep[late], got[0][late], mid[SMALL_ROWS + cut :]), (2, 1))
         small = small_sum(send, mid)
         home_mid = crossed(tied(home, mid), (1, 2))
-        smalls = [flipped(small, 4 * k) for k in range(1, quarter)]
+        mask = 4
+        while 2 * mask < n:
+            small = summed(small, flipped(small, mask))
+            mask *= 2
+        smalls = [flipped(small, mask)]
         parts = far_messages(far, piece, keep, got[0], mid, near)
         smalls = [small] + [tied(term, parts[0]) for term in smalls]
         message, base = home_message(far, piece, keep, got[0], home_mid, smalls)

time: 77.9 us -> 76.9 us (0.987)
  Pallas kernels: 32.6 us -> 34.6 us
  starting transfers between devices: 25.9 us -> 23.9 us
  waiting for transfers between devices: 16.4 us -> 14.8 us
    ppermute x8, waiting for transfers between devices: 2.86 us -> 0.15 us  [sibling(): return lax.ppermute(value, 'task', [(0, 1), (1, 0)])]
    ppermute x9 -> x8, starting transfers between devices: 14.3 us -> 11.8 us  [flipped(): return lax.ppermute(value, 'dp', pairs)]
    pallas_call x1 -> x3, Pallas kernels: 16.9 us -> 19 us  [the longest x1 15.2 us: layer(): pl.pallas_call(functools.partial(main_kernel, given, plan, rows1, rows2),...]
    ppermute x9 -> x8, waiting for transfers between devices: 6.2 us -> 7.34 us  [flipped(): return lax.ppermute(value, 'dp', pairs)]
  transfers between devices with their start and end apart: 24 -> 23, of which waited for: 10 -> 10; matrix products, arithmetic and copies ran while one was open for 1% -> 1% of each run, Pallas kernels for 19% -> 24%
where the time goes in v6:
time: 76.9 us; the launch traced here: 76.1 us
  Pallas kernels  34.6 us (45%)
  starting transfers between devices  23.9 us (31%)
  waiting for transfers between devices  14.8 us (19%)
  other arithmetic  1.71 us (2%)
  between operations  1.02 us (1%)
    pallas_call x1, Pallas kernels, layer(): pl.pallas_call(functools.partial(main_kernel, given, plan, rows1, rows2),...  15.2 us
    ppermute x8, starting transfers between devices, flipped(): return lax.ppermute(value, 'dp', pairs)  11.8 us
    ppermute x7, starting transfers between devices, crossed(): return lax.ppermute(value, ('task', 'dp'), pairs)  10.3 us
    ppermute x8, waiting for transfers between devices, flipped(): return lax.ppermute(value, 'dp', pairs)  7.34 us
    ppermute x7, waiting for transfers between devices, crossed(): return lax.ppermute(value, ('task', 'dp'), pairs)  7.29 us
    pallas_call x1, Pallas kernels, expand(): pl.pallas_call(functools.partial(expand_kernel, blocks // 2, group), grid...  6.52 us
    pallas_call x2, Pallas kernels, pool(): pl.pallas_call(functools.partial(pool_kernel, part * count, count, half_b...  5.22 us
    pallas_call x1, Pallas kernels, front(): pl.pallas_call(functools.partial(front_kernel, len(x_parts), given, rows1...  2.09 us
  transfers between devices with their start and end apart: 23, of which 10 were waited for; matrix products, arithmetic and copies ran while one was open for 1% of the time, Pallas kernels for 24%

profile of v6, /device:TPU:0, one launch (start us, length us, event | category | flops | bytes accessed | tf_op | source)
XLA Modules:
  0.0 76.1 jit_solution(12475425526256763408)
XLA Ops:
  1.5 5.0 %collective-permute-start.3 = (bf16[144,256]{1,0:T(8,128)(2,1)S(1)}, bf16[144,256]{1,0:T(8,128)(2,1)S(1)}, u32[]{:S(2)}, u32[]{:S(2)}) collective-permute-start(bf16[144,256]{1,0:T(8,128)(2,1)S(1)} %pad_maximum_fusion.refs_0_), channel_id=1, source_target_pairs={{0,12},{1,13},{2,14},{3,15},{4,8},{5,9},{6,10},{7,11},{8,4},{9,5},... | collective-permute-start | bytes 221192 | tf_op jit(solution)/shard_map/ppermute | solution.py:792
  7.7 1.7 %shard_map.256.refs_9_ = bf16[368,128]{1,0:T(8,128)(2,1)} custom-call(s32[2]{0:T(128)} %pad_add_fusion.ids_ref, s32[1,1536]{1,0:T(1,128)} %label_ref.1, bf16[2,256]{1,0:T(2,128)(2,1)} %bitcast.48, bf16[2,256]{1,0:T(2,128)(2,1)} %bitcast.49, bf16[1,256]{1,0:T(2,128)(2,1)} %ogain_ref.1, bf16[1,256]{1,0:T(2,128)(2,1)} %oshift_ref.1, bf16[4,512]{1,0:T(4,128)(2,1)} %bitcast.45, ...), custom_call_target="tpu_custom_call" | custom-call | flops 1000000000 | bytes 1000000 | tf_op jit(solution)/shard_map/pallas_call | solution.py:160
  9.7 3.0 %collective-permute-done.2.refs_2_ = bf16[144,256]{1,0:T(8,128)(2,1)S(1)} collective-permute-done((bf16[144,256]{1,0:T(8,128)(2,1)S(1)}, bf16[144,256]{1,0:T(8,128)(2,1)S(1)}, u32[]{:S(2)}, u32[]{:S(2)}) %collective-permute-start.2) | collective-permute-done | bytes 73760 | tf_op jit(solution)/shard_map/ppermute | solution.py:792
  13.1 1.6 %collective-permute-start.5 = (bf16[4,144,256]{2,1,0:T(8,128)(2,1)S(1)}, bf16[4,144,256]{2,1,0:T(8,128)(2,1)S(1)}, u32[]{:S(2)}, u32[]{:S(2)}) collective-permute-start(bf16[4,144,256]{2,1,0:T(8,128)(2,1)S(1)} %shard_map.258.refs_2_), channel_id=1, source_target_pairs={{0,1},{1,0},{2,3},{3,2},{4,5},{5,4},{6,7},{7,6},{8,9},{9,8},{10,11... | collective-permute-start | bytes 884744 | tf_op jit(solution)/shard_map/ppermute | solution.py:798
  14.7 2.5 %shard_map.255.refs_1_.refs_0_ = bf16[384,512]{1,0:T(8,128)(2,1)S(1)} custom-call(s32[2]{0:T(128)S(1)} %copy-done, s32[2,256]{1,0:T(2,128)S(1)} %get-tuple-element.50.meta_ref, s32[104,128]{1,0:T(8,128)S(1)} %get-tuple-element.51.st_ref, s32[104,128]{1,0:T(8,128)S(1)} %get-tuple-element.52.en_ref, bf16[64,18432]{1,0:T(8,128)(2,1)S(1)} %bitcast.30), custom_call_target="tpu_custom_call" | custom-call | flops 10000000000 | bytes 5000000 | tf_op jit(solution)/shard_map/pallas_call | solution.py:232
  17.3 1.6 %collective-permute-start.4 = (bf16[4,144,256]{2,1,0:T(8,128)(2,1)S(1)}, bf16[4,144,256]{2,1,0:T(8,128)(2,1)S(1)}, u32[]{:S(2)}, u32[]{:S(2)}) collective-permute-start(bf16[4,144,256]{2,1,0:T(8,128)(2,1)S(1)} %shard_map.259), channel_id=1, source_target_pairs={{0,2},{1,3},{2,0},{3,1},{4,6},{5,7},{6,4},{7,5},{8,10},{9,11},{10,... | collective-permute-start | bytes 884744 | tf_op jit(solution)/shard_map/ppermute | solution.py:798
  19.9 1.5 %collective-permute-start.6 = (bf16[4,144,256]{2,1,0:T(8,128)(2,1)S(1)}, bf16[4,144,256]{2,1,0:T(8,128)(2,1)S(1)}, u32[]{:S(2)}, u32[]{:S(2)}) collective-permute-start(bf16[4,144,256]{2,1,0:T(8,128)(2,1)S(1)} %shard_map.260.refs_4_), channel_id=1, source_target_pairs={{0,2},{1,3},{2,0},{3,1},{4,6},{5,7},{6,4},{7,5},{8,10},{9,11},{10,... | collective-permute-start | bytes 884744 | tf_op jit(solution)/shard_map/ppermute | solution.py:798
  21.5 2.7 %shard_map.257.refs_1_ = bf16[384,512]{1,0:T(8,128)(2,1)S(1)} custom-call(s32[2]{0:T(128)S(1)} %copy-done, s32[2,256]{1,0:T(2,128)S(1)} %get-tuple-element.50.meta_ref, s32[104,128]{1,0:T(8,128)S(1)} %get-tuple-element.51.st_ref, s32[104,128]{1,0:T(8,128)S(1)} %get-tuple-element.52.en_ref, bf16[64,18432]{1,0:T(8,128)(2,1)S(1)} %bitcast.31, ...), custom_call_target="tpu_custom_call" | custom-call | flops 10000000000 | bytes 5000000 | tf_op jit(solution)/shard_map/pallas_call | solution.py:232
  24.8 2.5 %collective-permute-done.6.refs_0_ = bf16[4,144,256]{2,1,0:T(8,128)(2,1)S(1)} collective-permute-done((bf16[4,144,256]{2,1,0:T(8,128)(2,1)S(1)}, bf16[4,144,256]{2,1,0:T(8,128)(2,1)S(1)}, u32[]{:S(2)}, u32[]{:S(2)}) %collective-permute-start.6) | collective-permute-done | bytes 294944 | tf_op jit(solution)/shard_map/ppermute | solution.py:798
  27.3 2.1 %shard_map.262 = (bf16[512,768]{1,0:T(8,128)(2,1)S(1)}, bf16[512,768]{1,0:T(8,128)(2,1)S(1)}, bf16[3,256,256]{2,1,0:T(8,128)(2,1)S(1)}, f32[768,768]{1,0:T(8,128)S(1)}, bf16[768,768]{1,0:T(8,128)(2,1)S(1)}) custom-call(s32[2]{0:T(128)S(1)} %copy-done, bf16[384,512]{1,0:T(8,128)(2,1)S(1)} %shard_map.255.refs_1_.refs_0_, ...), custom_call_target="tpu_custom_call" | custom-call | flops 6000000000 | bytes 4000000 | tf_op jit(solution)/shard_map/pallas_call | solution.py:432
  29.4 15.2 %shard_map.263 = (bf16[784,512]{1,0:T(8,128)(2,1)S(1)}, bf16[768,768]{1,0:T(8,128)(2,1)S(1)}, bf16[768,768]{1,0:T(8,128)(2,1)S(1)}, bf16[176,256]{1,0:T(8,128)(2...) custom-call(s32[2]{0:T(128)S(1)} %copy-done, ...), custom_call_target="tpu_custom_call" | custom-call | flops 5435817984 | bytes 10000000 | tf_op jit(solution)/shard_map/pallas_call | solution.py:775
  45.7 1.7 %shard_map.265 = (bf16[1440,256]{1,0:T(8,128)(2,1)S(1)}, bf16[1040,256]{1,0:T(8,128)(2,1)S(1)}) custom-call(s32[2]{0:T(128)S(1)} %copy-done, bf16[512,768]{1,0:T(8,128)(2,1)S(1)} %get-tuple-element.53.refs_0_.x_ref, bf16[768,768]{1,0:T(8,128)(2,1)S(1)} %get-tuple-element.57.refs_4_.h_ref, bf16[768,768]{1,0:T(8,128)(2,1)S(1)} %get-tuple-element.61.e_ref, ...), custom_call_target="tpu_custom_call" | custom-call | flops 6000000000 | bytes 4000000 | tf_op jit(solution)/shard_map/pallas_call | solution.py:461
  47.6 1.1 %collective-permute-start.14 = (bf16[1040,256]{1,0:T(8,128)(2,1)S(1)}, bf16[1040,256]{1,0:T(8,128)(2,1)S(1)}, u32[]{:S(2)}, u32[]{:S(2)}) collective-permute-start(bf16[1040,256]{1,0:T(8,128)(2,1)S(1)} %add_convert_fusion.one_ref), channel_id=1, source_target_pairs={{0,1},{1,0},{2,3},{3,2},{4,5},{5,4},{6,7},{7,6},{8,9},{9,8},{10,11... | collective-permute-start | bytes 1597448 | tf_op jit(solution)/shard_map/ppermute | solution.py:798
  48.9 6.5 %shard_map.264 = (bf16[64,18432]{1,0:T(8,128)(2,1)}, f32[1,1536]{1,0:T(1,128)}, f32[8,128]{1,0:T(8,128)S(1)}) custom-call(s32[2]{0:T(128)S(1)} %copy-done, s32[2,256]{1,0:T(2,128)S(1)} %get-tuple-element.50.meta_ref, s32[104,128]{1,0:T(8,128)S(1)} %get-tuple-element.51.st_ref, s32[104,128]{1,0:T(8,128)S(1)} %get-tuple-element.52.en_ref, ...), custom_call_target="tpu_custom_call" | custom-call | flops 12000000000 | bytes 6000000 | tf_op jit(solution)/shard_map/pallas_call | solution.py:286
  55.4 1.5 %collective-permute-done.14.refs_0_ = bf16[1040,256]{1,0:T(8,128)(2,1)S(1)} collective-permute-done((bf16[1040,256]{1,0:T(8,128)(2,1)S(1)}, bf16[1040,256]{1,0:T(8,128)(2,1)S(1)}, u32[]{:S(2)}, u32[]{:S(2)}) %collective-permute-start.14) | collective-permute-done | bytes 532512 | tf_op jit(solution)/shard_map/ppermute | solution.py:798
  58.0 1.3 %collective-permute-start.15 = (bf16[288,256]{1,0:T(8,128)(2,1)S(1)}, bf16[288,256]{1,0:T(8,128)(2,1)S(1)}, u32[]{:S(2)}, u32[]{:S(2)}) collective-permute-start(bf16[288,256]{1,0:T(8,128)(2,1)S(1)} %shard_map.267), channel_id=1, source_target_pairs={{0,1},{1,0},{2,3},{3,2},{4,5},{5,4},{6,7},{7,6},{8,9},{9,8},{10,11... | collective-permute-start | bytes 442376 | tf_op jit(solution)/shard_map/ppermute | solution.py:798
  59.4 1.3 %collective-permute-start.18 = (bf16[432,256]{1,0:T(8,128)(2,1)S(1)}, bf16[432,256]{1,0:T(8,128)(2,1)S(1)}, u32[]{:S(2)}, u32[]{:S(2)}) collective-permute-start(bf16[432,256]{1,0:T(8,128)(2,1)S(1)} %add_convert_fusion.1), channel_id=1, source_target_pairs={{0,2},{1,3},{2,0},{3,1},{4,6},{5,7},{6,4},{7,5},{8,10},{9,11},{10,... | collective-permute-start | bytes 663560 | tf_op jit(solution)/shard_map/ppermute | solution.py:798
  61.6 1.5 %collective-permute-start.17 = (bf16[176,256]{1,0:T(8,128)(2,1)S(1)}, bf16[176,256]{1,0:T(8,128)(2,1)S(1)}, u32[]{:S(2)}, u32[]{:S(2)}) collective-permute-start(bf16[176,256]{1,0:T(8,128)(2,1)S(1)} %add_convert_fusion.3.refs_0_), channel_id=1, source_target_pairs={{0,8},{1,9},{2,10},{3,11},{4,12},{5,13},{6,14},{7,15},{8,0},{9,1},... | collective-permute-start | bytes 270344 | tf_op jit(solution)/shard_map/ppermute | solution.py:792
  63.1 2.3 %collective-permute-done.18.near_ref = bf16[432,256]{1,0:T(8,128)(2,1)S(1)} collective-permute-done((bf16[432,256]{1,0:T(8,128)(2,1)S(1)}, bf16[432,256]{1,0:T(8,128)(2,1)S(1)}, u32[]{:S(2)}, u32[]{:S(2)}) %collective-permute-start.18) | collective-permute-done | bytes 221216 | tf_op jit(solution)/shard_map/ppermute | solution.py:798
  65.5 2.4 %collective-permute-start.20 = (bf16[144,256]{1,0:T(8,128)(2,1)S(1)}, bf16[144,256]{1,0:T(8,128)(2,1)S(1)}, u32[]{:S(2)}, u32[]{:S(2)}) collective-permute-start(bf16[144,256]{1,0:T(8,128)(2,1)S(1)} %get-tuple-element.71), channel_id=1, source_target_pairs={{0,8},{1,9},{2,10},{3,11},{4,12},{5,13},{6,14},{7,15},{8,0},{9,1},... | collective-permute-start | bytes 221192 | tf_op jit(solution)/shard_map/ppermute | solution.py:792
  69.2 1.9 %collective-permute-start.22 = (bf16[320,256]{1,0:T(8,128)(2,1)S(1)}, bf16[320,256]{1,0:T(8,128)(2,1)S(1)}, u32[]{:S(2)}, u32[]{:S(2)}) collective-permute-start(bf16[320,256]{1,0:T(8,128)(2,1)S(1)} %get-tuple-element.73.refs_1_), channel_id=1, source_target_pairs={{0,2},{1,3},{2,0},{3,1},{4,6},{5,7},{6,4},{7,5},{8,10},{9,11},{10,... | collective-permute-start | bytes 491528 | tf_op jit(solution)/shard_map/ppermute | solution.py:798
  71.1 2.2 %collective-permute-done.20.refs_2_ = bf16[144,256]{1,0:T(8,128)(2,1)S(1)} collective-permute-done((bf16[144,256]{1,0:T(8,128)(2,1)S(1)}, bf16[144,256]{1,0:T(8,128)(2,1)S(1)}, u32[]{:S(2)}, u32[]{:S(2)}) %collective-permute-start.20) | collective-permute-done | bytes 73760 | tf_op jit(solution)/shard_map/ppermute | solution.py:792
  73.3 1.1 %collective-permute-done.21.refs_3_ = bf16[144,256]{1,0:T(8,128)(2,1)S(1)} collective-permute-done((bf16[144,256]{1,0:T(8,128)(2,1)S(1)}, bf16[144,256]{1,0:T(8,128)(2,1)S(1)}, u32[]{:S(2)}, u32[]{:S(2)}) %collective-permute-start.21) | collective-permute-done | bytes 73760 | tf_op jit(solution)/shard_map/ppermute | solution.py:792
  74.6 1.3 %shard_map.273 = (f32[2,32,256]{2,1,0:T(8,128)}, f32[2,16,256]{2,1,0:T(8,128)}, f32[32,256]{1,0:T(8,128)}, f32[16,256]{1,0:T(8,128)}, f32[2,256]{1,0:T(2,128)}, ...) custom-call(s32[2]{0:T(128)S(1)} %copy-done, ...), custom_call_target="tpu_custom_call" | custom-call | bytes 2000000 | tf_op jit(solution)/shard_map/pallas_call | solution.py:983
  (57 shorter events, 9.5 us)
Async XLA Ops:
  1.5 8.3 %collective-permute-start.3 = (bf16[144,256]{1,0:T(8,128)(2,1)S(1)}, bf16[144,256]{1,0:T(8,128)(2,1)S(1)}, u32[]{:S(2)}, u32[]{:S(2)}) collective-permute-start(bf16[144,256]{1,0:T(8,128)(2,1)S(1)} %pad_maximum_fusion.refs_0_), channel_id=1, source_target_pairs={{0,12},{1,13},{2,14},{3,15},{4,8},{5,9},{6,10},{7,11},{8,4},{9,5},... | collective-permute-start | bytes 221192 | tf_op jit(solution)/shard_map/ppermute | solution.py:792
  6.5 6.2 %collective-permute-start.2 = (bf16[144,256]{1,0:T(8,128)(2,1)S(1)}, bf16[144,256]{1,0:T(8,128)(2,1)S(1)}, u32[]{:S(2)}, u32[]{:S(2)}) collective-permute-start(bf16[144,256]{1,0:T(8,128)(2,1)S(1)} %pad_maximum_fusion.refs_0_), channel_id=1, source_target_pairs={{0,8},{1,9},{2,10},{3,11},{4,12},{5,13},{6,14},{7,15},{8,0},{9,1},... | collective-permute-start | bytes 221192 | tf_op jit(solution)/shard_map/ppermute | solution.py:792
  6.5 6.2 %collective-permute-start.1 = (bf16[144,256]{1,0:T(8,128)(2,1)S(1)}, bf16[144,256]{1,0:T(8,128)(2,1)S(1)}, u32[]{:S(2)}, u32[]{:S(2)}) collective-permute-start(bf16[144,256]{1,0:T(8,128)(2,1)S(1)} %pad_maximum_fusion.refs_0_), channel_id=1, source_target_pairs={{0,4},{1,5},{2,6},{3,7},{4,0},{5,1},{6,2},{7,3},{8,12},{9,13},{10,... | collective-permute-start | bytes 221192 | tf_op jit(solution)/shard_map/ppermute | solution.py:792
  9.4 5.3 %copy-start.1 = (bf16[18432,64]{0,1:T(8,128)(2,1)S(1)}, bf16[18432,64]{0,1:T(8,128)(2,1)}, u32[]{:S(2)}) copy-start(bf16[18432,64]{0,1:T(8,128)(2,1)} %param.15) | copy-start | bytes 7077892
  9.4 12.0 %collective-permute-start = (bf16[368,128]{1,0:T(8,128)(2,1)}, bf16[368,128]{1,0:T(8,128)(2,1)S(1)}, u32[]{:S(2)}, u32[]{:S(2)}) collective-permute-start(bf16[368,128]{1,0:T(8,128)(2,1)} %shard_map.256.refs_9_), channel_id=1, source_target_pairs={{0,16},{16,0},{1,17},{17,1},{2,18},{18,2},{3,19},{19,3},{4,20},{20... | collective-permute-start | bytes 282632 | tf_op jit(solution)/shard_map/ppermute | solution.py:787
  13.1 6.8 %collective-permute-start.5 = (bf16[4,144,256]{2,1,0:T(8,128)(2,1)S(1)}, bf16[4,144,256]{2,1,0:T(8,128)(2,1)S(1)}, u32[]{:S(2)}, u32[]{:S(2)}) collective-permute-start(bf16[4,144,256]{2,1,0:T(8,128)(2,1)S(1)} %shard_map.258.refs_2_), channel_id=1, source_target_pairs={{0,1},{1,0},{2,3},{3,2},{4,5},{5,4},{6,7},{7,6},{8,9},{9,8},{10,11... | collective-permute-start | bytes 884744 | tf_op jit(solution)/shard_map/ppermute | solution.py:798
  17.2 12.1 %collective-permute-start.7 = (bf16[4,144,256]{2,1,0:T(8,128)(2,1)S(1)}, bf16[4,144,256]{2,1,0:T(8,128)(2,1)S(1)}, u32[]{:S(2)}, u32[]{:S(2)}) collective-permute-start(bf16[4,144,256]{2,1,0:T(8,128)(2,1)S(1)} %shard_map.258.refs_2_), channel_id=1, source_target_pairs={{0,16},{16,0},{1,17},{17,1},{2,18},{18,2},{3,19},{19,3},{4,20},{20... | collective-permute-start | bytes 884744 | tf_op jit(solution)/shard_map/ppermute | solution.py:787
  17.3 7.0 %collective-permute-start.4 = (bf16[4,144,256]{2,1,0:T(8,128)(2,1)S(1)}, bf16[4,144,256]{2,1,0:T(8,128)(2,1)S(1)}, u32[]{:S(2)}, u32[]{:S(2)}) collective-permute-start(bf16[4,144,256]{2,1,0:T(8,128)(2,1)S(1)} %shard_map.259), channel_id=1, source_target_pairs={{0,2},{1,3},{2,0},{3,1},{4,6},{5,7},{6,4},{7,5},{8,10},{9,11},{10,... | collective-permute-start | bytes 884744 | tf_op jit(solution)/shard_map/ppermute | solution.py:798
  19.9 7.3 %collective-permute-start.6 = (bf16[4,144,256]{2,1,0:T(8,128)(2,1)S(1)}, bf16[4,144,256]{2,1,0:T(8,128)(2,1)S(1)}, u32[]{:S(2)}, u32[]{:S(2)}) collective-permute-start(bf16[4,144,256]{2,1,0:T(8,128)(2,1)S(1)} %shard_map.260.refs_4_), channel_id=1, source_target_pairs={{0,2},{1,3},{2,0},{3,1},{4,6},{5,7},{6,4},{7,5},{8,10},{9,11},{10,... | collective-permute-start | bytes 884744 | tf_op jit(solution)/shard_map/ppermute | solution.py:798
  24.2 5.2 %collective-permute-start.9 = (bf16[4,144,256]{2,1,0:T(8,128)(2,1)S(1)}, bf16[4,144,256]{2,1,0:T(8,128)(2,1)S(1)}, u32[]{:S(2)}, u32[]{:S(2)}) collective-permute-start(bf16[4,144,256]{2,1,0:T(8,128)(2,1)S(1)} %shard_map.260.refs_4_), channel_id=1, source_target_pairs={{0,16},{16,0},{1,17},{17,1},{2,18},{18,2},{3,19},{19,3},{4,20},{20... | collective-permute-start | bytes 884744 | tf_op jit(solution)/shard_map/ppermute | solution.py:787
  24.3 5.1 %collective-permute-start.8 = (bf16[4,144,256]{2,1,0:T(8,128)(2,1)S(1)}, bf16[4,144,256]{2,1,0:T(8,128)(2,1)S(1)}, u32[]{:S(2)}, u32[]{:S(2)}) collective-permute-start(bf16[4,144,256]{2,1,0:T(8,128)(2,1)S(1)} %collective-permute-done.4.refs_3_), channel_id=1, source_target_pairs={{0,16},{16,0},{1,17},{17,1},{2,18},{18,2},{3,19},{19,3},{4,20},{20... | collective-permute-start | bytes 884744 | tf_op jit(solution)/shard_map/ppermute | solution.py:787
  27.2 2.1 %collective-permute-start.10 = (bf16[4,144,256]{2,1,0:T(8,128)(2,1)S(1)}, bf16[4,144,256]{2,1,0:T(8,128)(2,1)S(1)}, u32[]{:S(2)}, u32[]{:S(2)}) collective-permute-start(bf16[4,144,256]{2,1,0:T(8,128)(2,1)S(1)} %shard_map.261.refs_5_), channel_id=1, source_target_pairs={{0,16},{16,0},{1,17},{17,1},{2,18},{18,2},{3,19},{19,3},{4,20},{20... | collective-permute-start | bytes 884744 | tf_op jit(solution)/shard_map/ppermute | solution.py:787
  44.6 2.8 %collective-permute-start.13 = (bf16[1040,256]{1,0:T(8,128)(2,1)S(1)}, bf16[1040,256]{1,0:T(8,128)(2,1)S(1)}, u32[]{:S(2)}, u32[]{:S(2)}) collective-permute-start(bf16[1040,256]{1,0:T(8,128)(2,1)S(1)} %get-tuple-element.67), channel_id=1, source_target_pairs={{0,16},{16,0},{1,17},{17,1},{2,18},{18,2},{3,19},{19,3},{4,20},{20... | collective-permute-start | bytes 1597448 | tf_op jit(solution)/shard_map/ppermute | solution.py:787
  45.1 3.6 %collective-permute-start.12 = (bf16[1440,256]{1,0:T(8,128)(2,1)S(1)}, bf16[1440,256]{1,0:T(8,128)(2,1)S(1)}, u32[]{:S(2)}, u32[]{:S(2)}) collective-permute-start(bf16[1440,256]{1,0:T(8,128)(2,1)S(1)} %get-tuple-element.65), channel_id=1, source_target_pairs={{0,16},{16,0},{1,17},{17,1},{2,18},{18,2},{3,19},{19,3},{4,20},{20... | collective-permute-start | bytes 2211848 | tf_op jit(solution)/shard_map/ppermute | solution.py:787
  45.2 3.7 %collective-permute-start.11 = (bf16[784,512]{1,0:T(8,128)(2,1)S(1)}, bf16[784,512]{1,0:T(8,128)(2,1)S(1)}, u32[]{:S(2)}, u32[]{:S(2)}) collective-permute-start(bf16[784,512]{1,0:T(8,128)(2,1)S(1)} %get-tuple-element.58.own_ref), channel_id=1, source_target_pairs={{0,16},{16,0},{1,17},{17,1},{2,18},{18,2},{3,19},{19,3},{4,20},{20... | collective-permute-start | bytes 2408456 | tf_op jit(solution)/shard_map/ppermute | solution.py:787
  47.6 9.3 %collective-permute-start.14 = (bf16[1040,256]{1,0:T(8,128)(2,1)S(1)}, bf16[1040,256]{1,0:T(8,128)(2,1)S(1)}, u32[]{:S(2)}, u32[]{:S(2)}) collective-permute-start(bf16[1040,256]{1,0:T(8,128)(2,1)S(1)} %add_convert_fusion.one_ref), channel_id=1, source_target_pairs={{0,1},{1,0},{2,3},{3,2},{4,5},{5,4},{6,7},{7,6},{8,9},{9,8},{10,11... | collective-permute-start | bytes 1597448 | tf_op jit(solution)/shard_map/ppermute | solution.py:798
  56.9 4.6 %collective-permute-start.16 = (bf16[176,256]{1,0:T(8,128)(2,1)S(1)}, bf16[176,256]{1,0:T(8,128)(2,1)S(1)}, u32[]{:S(2)}, u32[]{:S(2)}) collective-permute-start(bf16[176,256]{1,0:T(8,128)(2,1)S(1)} %shard_map.268), channel_id=1, source_target_pairs={{0,4},{1,5},{2,6},{3,7},{4,0},{5,1},{6,2},{7,3},{8,12},{9,13},{10,... | collective-permute-start | bytes 270344 | tf_op jit(solution)/shard_map/ppermute | solution.py:792
  58.0 11.1 %collective-permute-start.15 = (bf16[288,256]{1,0:T(8,128)(2,1)S(1)}, bf16[288,256]{1,0:T(8,128)(2,1)S(1)}, u32[]{:S(2)}, u32[]{:S(2)}) collective-permute-start(bf16[288,256]{1,0:T(8,128)(2,1)S(1)} %shard_map.267), channel_id=1, source_target_pairs={{0,1},{1,0},{2,3},{3,2},{4,5},{5,4},{6,7},{7,6},{8,9},{9,8},{10,11... | collective-permute-start | bytes 442376 | tf_op jit(solution)/shard_map/ppermute | solution.py:798
  59.4 6.0 %collective-permute-start.18 = (bf16[432,256]{1,0:T(8,128)(2,1)S(1)}, bf16[432,256]{1,0:T(8,128)(2,1)S(1)}, u32[]{:S(2)}, u32[]{:S(2)}) collective-permute-start(bf16[432,256]{1,0:T(8,128)(2,1)S(1)} %add_convert_fusion.1), channel_id=1, source_target_pairs={{0,2},{1,3},{2,0},{3,1},{4,6},{5,7},{6,4},{7,5},{8,10},{9,11},{10,... | collective-permute-start | bytes 663560 | tf_op jit(solution)/shard_map/ppermute | solution.py:798
  61.6 7.5 %collective-permute-start.17 = (bf16[176,256]{1,0:T(8,128)(2,1)S(1)}, bf16[176,256]{1,0:T(8,128)(2,1)S(1)}, u32[]{:S(2)}, u32[]{:S(2)}) collective-permute-start(bf16[176,256]{1,0:T(8,128)(2,1)S(1)} %add_convert_fusion.3.refs_0_), channel_id=1, source_target_pairs={{0,8},{1,9},{2,10},{3,11},{4,12},{5,13},{6,14},{7,15},{8,0},{9,1},... | collective-permute-start | bytes 270344 | tf_op jit(solution)/shard_map/ppermute | solution.py:792
  65.5 7.7 %collective-permute-start.20 = (bf16[144,256]{1,0:T(8,128)(2,1)S(1)}, bf16[144,256]{1,0:T(8,128)(2,1)S(1)}, u32[]{:S(2)}, u32[]{:S(2)}) collective-permute-start(bf16[144,256]{1,0:T(8,128)(2,1)S(1)} %get-tuple-element.71), channel_id=1, source_target_pairs={{0,8},{1,9},{2,10},{3,11},{4,12},{5,13},{6,14},{7,15},{8,0},{9,1},... | collective-permute-start | bytes 221192 | tf_op jit(solution)/shard_map/ppermute | solution.py:792
  67.9 6.5 %collective-permute-start.21 = (bf16[144,256]{1,0:T(8,128)(2,1)S(1)}, bf16[144,256]{1,0:T(8,128)(2,1)S(1)}, u32[]{:S(2)}, u32[]{:S(2)}) collective-permute-start(bf16[144,256]{1,0:T(8,128)(2,1)S(1)} %get-tuple-element.72), channel_id=1, source_target_pairs={{0,12},{1,13},{2,14},{3,15},{4,8},{5,9},{6,10},{7,11},{8,4},{9,5},... | collective-permute-start | bytes 221192 | tf_op jit(solution)/shard_map/ppermute | solution.py:792
  68.7 5.8 %collective-permute-start.19 = (bf16[144,256]{1,0:T(8,128)(2,1)S(1)}, bf16[144,256]{1,0:T(8,128)(2,1)S(1)}, u32[]{:S(2)}, u32[]{:S(2)}) collective-permute-start(bf16[144,256]{1,0:T(8,128)(2,1)S(1)} %get-tuple-element.69.refs_1_), channel_id=1, source_target_pairs={{0,4},{1,5},{2,6},{3,7},{4,0},{5,1},{6,2},{7,3},{8,12},{9,13},{10,... | collective-permute-start | bytes 221192 | tf_op jit(solution)/shard_map/ppermute | solution.py:792
  69.2 5.5 %collective-permute-start.22 = (bf16[320,256]{1,0:T(8,128)(2,1)S(1)}, bf16[320,256]{1,0:T(8,128)(2,1)S(1)}, u32[]{:S(2)}, u32[]{:S(2)}) collective-permute-start(bf16[320,256]{1,0:T(8,128)(2,1)S(1)} %get-tuple-element.73.refs_1_), channel_id=1, source_target_pairs={{0,2},{1,3},{2,0},{3,1},{4,6},{5,7},{6,4},{7,5},{8,10},{9,11},{10,... | collective-permute-start | bytes 491528 | tf_op jit(solution)/shard_map/ppermute | solution.py:798
  (3 other events, 9.1 us)

commit v7 on v6

--- a/solution.py
+++ b/solution.py
@@ -258,7 +258,7 @@
                     rows_ref[pl.ds(to + (2 * pair + 1) * EVB, EVB), :] = tile[:, EMB:]
                 return carry
 
-            lax.fori_loop(0, half_blocks, place, 0, unroll=12)
+            lax.fori_loop(0, half_blocks, place, 0, unroll=48)
         rows_ref[pl.ds(2 * half_blocks * BAGS, BAGS), :] = jnp.zeros((BAGS, EMB), BF)
         own = own_ref[events : events + 16, : 2 * LANES].astype(F32)
         other = other_ref[events : events + 16, : 2 * LANES].astype(F32)
@@ -280,7 +280,7 @@
 def expand(ids, meta, starts, ends, own, other, rows):
     blocks = starts.shape[0] - 8
     chunks = rows // ROWS
-    group = 36
+    group = 72
     while chunks % group:
         group -= 1
     return pl.pallas_call(
@@ -1076,11 +1076,11 @@
         late = slice(cut, 2 * cut)
         near = crossed(summed(keep[late], got[0][late], mid[SMALL_ROWS + cut :]), (2, 1))
         small = small_sum(send, mid)
-        home_mid = crossed(tied(home, mid), (1, 2))
-        mask = 4
-        while 2 * mask < n:
+        home_mid = tied(crossed(home, (1, 2)), expanded)
+        mask = n // 2
+        while mask > 4:
             small = summed(small, flipped(small, mask))
-            mask *= 2
+            mask //= 2
         smalls = [flipped(small, mask)]
         parts = far_messages(far, piece, keep, got[0], mid, near)
         smalls = [small] + [tied(term, parts[0]) for term in smalls]

time: 76.9 us -> 76.2 us (level)
  waiting for transfers between devices: 14.8 us -> 16.1 us
  Pallas kernels: 34.6 us -> 33.7 us
    ppermute x8, waiting for transfers between devices: 7.34 us -> 9.6 us  [flipped(): return lax.ppermute(value, 'dp', pairs)]
    pallas_call x1, Pallas kernels: 6.52 us -> 5.65 us  [expand(): pl.pallas_call(functools.partial(expand_kernel, blocks // 2, group), grid...]
    ppermute x7, waiting for transfers between devices: 7.29 us -> 6.46 us  [crossed(): return lax.ppermute(value, ('task', 'dp'), pairs)]
  transfers between devices with their start and end apart: 23 -> 23, of which waited for: 10 -> 9; matrix products, arithmetic and copies ran while one was open for 1% -> 1% of each run, Pallas kernels for 24% -> 23%
where the time goes in v7:
time: 76.2 us; the launch traced here: 75.8 us
  Pallas kernels  33.7 us (44%)
  starting transfers between devices  23.2 us (30%)
  waiting for transfers between devices  16.1 us (21%)
  other arithmetic  1.73 us (2%)
  between operations  1.03 us (1%)
    pallas_call x1, Pallas kernels, layer(): pl.pallas_call(functools.partial(main_kernel, given, plan, rows1, rows2),...  15.2 us
    ppermute x8, starting transfers between devices, flipped(): return lax.ppermute(value, 'dp', pairs)  11.5 us
    ppermute x7, starting transfers between devices, crossed(): return lax.ppermute(value, ('task', 'dp'), pairs)  9.98 us
    ppermute x8, waiting for transfers between devices, flipped(): return lax.ppermute(value, 'dp', pairs)  9.6 us
    ppermute x7, waiting for transfers between devices, crossed(): return lax.ppermute(value, ('task', 'dp'), pairs)  6.46 us
    pallas_call x1, Pallas kernels, expand(): pl.pallas_call(functools.partial(expand_kernel, blocks // 2, group), grid...  5.65 us
    pallas_call x2, Pallas kernels, pool(): pl.pallas_call(functools.partial(pool_kernel, part * count, count, half_b...  5.22 us
    pallas_call x1, Pallas kernels, front(): pl.pallas_call(functools.partial(front_kernel, len(x_parts), given, rows1...  2.09 us
  transfers between devices with their start and end apart: 23, of which 9 were waited for; matrix products, arithmetic and copies ran while one was open for 1% of the time, Pallas kernels for 23%

profile of v7, /device:TPU:0, one launch (start us, length us, event | category | flops | bytes accessed | tf_op | source)
XLA Modules:
  0.0 75.8 jit_solution(5751412289228177906)
XLA Ops:
  1.5 5.0 %collective-permute-start.3 = (bf16[144,256]{1,0:T(8,128)(2,1)S(1)}, bf16[144,256]{1,0:T(8,128)(2,1)S(1)}, u32[]{:S(2)}, u32[]{:S(2)}) collective-permute-start(bf16[144,256]{1,0:T(8,128)(2,1)S(1)} %pad_maximum_fusion.refs_0_), channel_id=1, source_target_pairs={{0,12},{1,13},{2,14},{3,15},{4,8},{5,9},{6,10},{7,11},{8,4},{9,5},... | collective-permute-start | bytes 221192 | tf_op jit(solution)/shard_map/ppermute | solution.py:792
  7.7 1.7 %shard_map.256.refs_9_ = bf16[368,128]{1,0:T(8,128)(2,1)} custom-call(s32[2]{0:T(128)} %pad_add_fusion.ids_ref, s32[1,1536]{1,0:T(1,128)} %label_ref.1, bf16[2,256]{1,0:T(2,128)(2,1)} %bitcast.48, bf16[2,256]{1,0:T(2,128)(2,1)} %bitcast.49, bf16[1,256]{1,0:T(2,128)(2,1)} %ogain_ref.1, bf16[1,256]{1,0:T(2,128)(2,1)} %oshift_ref.1, bf16[4,512]{1,0:T(4,128)(2,1)} %bitcast.45, ...), custom_call_target="tpu_custom_call" | custom-call | flops 1000000000 | bytes 1000000 | tf_op jit(solution)/shard_map/pallas_call | solution.py:160
  9.7 3.0 %collective-permute-done.2.refs_2_ = bf16[144,256]{1,0:T(8,128)(2,1)S(1)} collective-permute-done((bf16[144,256]{1,0:T(8,128)(2,1)S(1)}, bf16[144,256]{1,0:T(8,128)(2,1)S(1)}, u32[]{:S(2)}, u32[]{:S(2)}) %collective-permute-start.2) | collective-permute-done | bytes 73760 | tf_op jit(solution)/shard_map/ppermute | solution.py:792
  13.1 1.6 %collective-permute-start.5 = (bf16[4,144,256]{2,1,0:T(8,128)(2,1)S(1)}, bf16[4,144,256]{2,1,0:T(8,128)(2,1)S(1)}, u32[]{:S(2)}, u32[]{:S(2)}) collective-permute-start(bf16[4,144,256]{2,1,0:T(8,128)(2,1)S(1)} %shard_map.258.refs_2_), channel_id=1, source_target_pairs={{0,1},{1,0},{2,3},{3,2},{4,5},{5,4},{6,7},{7,6},{8,9},{9,8},{10,11... | collective-permute-start | bytes 884744 | tf_op jit(solution)/shard_map/ppermute | solution.py:798
  14.7 2.5 %shard_map.255.refs_1_.refs_0_ = bf16[384,512]{1,0:T(8,128)(2,1)S(1)} custom-call(s32[2]{0:T(128)S(1)} %copy-done, s32[2,256]{1,0:T(2,128)S(1)} %get-tuple-element.50.meta_ref, s32[104,128]{1,0:T(8,128)S(1)} %get-tuple-element.51.st_ref, s32[104,128]{1,0:T(8,128)S(1)} %get-tuple-element.52.en_ref, bf16[64,18432]{1,0:T(8,128)(2,1)S(1)} %bitcast.30), custom_call_target="tpu_custom_call" | custom-call | flops 10000000000 | bytes 5000000 | tf_op jit(solution)/shard_map/pallas_call | solution.py:232
  17.3 1.6 %collective-permute-start.4 = (bf16[4,144,256]{2,1,0:T(8,128)(2,1)S(1)}, bf16[4,144,256]{2,1,0:T(8,128)(2,1)S(1)}, u32[]{:S(2)}, u32[]{:S(2)}) collective-permute-start(bf16[4,144,256]{2,1,0:T(8,128)(2,1)S(1)} %shard_map.259), channel_id=1, source_target_pairs={{0,2},{1,3},{2,0},{3,1},{4,6},{5,7},{6,4},{7,5},{8,10},{9,11},{10,... | collective-permute-start | bytes 884744 | tf_op jit(solution)/shard_map/ppermute | solution.py:798
  18.9 1.0 %collective-permute-done.5.refs_0_ = bf16[4,144,256]{2,1,0:T(8,128)(2,1)S(1)} collective-permute-done((bf16[4,144,256]{2,1,0:T(8,128)(2,1)S(1)}, bf16[4,144,256]{2,1,0:T(8,128)(2,1)S(1)}, u32[]{:S(2)}, u32[]{:S(2)}) %collective-permute-start.5) | collective-permute-done | bytes 294944 | tf_op jit(solution)/shard_map/ppermute | solution.py:798
  19.9 1.5 %collective-permute-start.6 = (bf16[4,144,256]{2,1,0:T(8,128)(2,1)S(1)}, bf16[4,144,256]{2,1,0:T(8,128)(2,1)S(1)}, u32[]{:S(2)}, u32[]{:S(2)}) collective-permute-start(bf16[4,144,256]{2,1,0:T(8,128)(2,1)S(1)} %shard_map.260.refs_4_), channel_id=1, source_target_pairs={{0,2},{1,3},{2,0},{3,1},{4,6},{5,7},{6,4},{7,5},{8,10},{9,11},{10,... | collective-permute-start | bytes 884744 | tf_op jit(solution)/shard_map/ppermute | solution.py:798
  21.5 2.7 %shard_map.257.refs_1_ = bf16[384,512]{1,0:T(8,128)(2,1)S(1)} custom-call(s32[2]{0:T(128)S(1)} %copy-done, s32[2,256]{1,0:T(2,128)S(1)} %get-tuple-element.50.meta_ref, s32[104,128]{1,0:T(8,128)S(1)} %get-tuple-element.51.st_ref, s32[104,128]{1,0:T(8,128)S(1)} %get-tuple-element.52.en_ref, bf16[64,18432]{1,0:T(8,128)(2,1)S(1)} %bitcast.31, ...), custom_call_target="tpu_custom_call" | custom-call | flops 10000000000 | bytes 5000000 | tf_op jit(solution)/shard_map/pallas_call | solution.py:232
  24.8 2.5 %collective-permute-done.6.refs_0_ = bf16[4,144,256]{2,1,0:T(8,128)(2,1)S(1)} collective-permute-done((bf16[4,144,256]{2,1,0:T(8,128)(2,1)S(1)}, bf16[4,144,256]{2,1,0:T(8,128)(2,1)S(1)}, u32[]{:S(2)}, u32[]{:S(2)}) %collective-permute-start.6) | collective-permute-done | bytes 294944 | tf_op jit(solution)/shard_map/ppermute | solution.py:798
  27.3 2.1 %shard_map.262 = (bf16[512,768]{1,0:T(8,128)(2,1)S(1)}, bf16[512,768]{1,0:T(8,128)(2,1)S(1)}, bf16[3,256,256]{2,1,0:T(8,128)(2,1)S(1)}, f32[768,768]{1,0:T(8,128)S(1)}, bf16[768,768]{1,0:T(8,128)(2,1)S(1)}) custom-call(s32[2]{0:T(128)S(1)} %copy-done, bf16[384,512]{1,0:T(8,128)(2,1)S(1)} %shard_map.255.refs_1_.refs_0_, ...), custom_call_target="tpu_custom_call" | custom-call | flops 6000000000 | bytes 4000000 | tf_op jit(solution)/shard_map/pallas_call | solution.py:432
  29.4 15.2 %shard_map.263 = (bf16[784,512]{1,0:T(8,128)(2,1)S(1)}, bf16[768,768]{1,0:T(8,128)(2,1)S(1)}, bf16[768,768]{1,0:T(8,128)(2,1)S(1)}, bf16[176,256]{1,0:T(8,128)(2...) custom-call(s32[2]{0:T(128)S(1)} %copy-done, ...), custom_call_target="tpu_custom_call" | custom-call | flops 5435817984 | bytes 10000000 | tf_op jit(solution)/shard_map/pallas_call | solution.py:775
  45.7 1.7 %shard_map.265 = (bf16[1440,256]{1,0:T(8,128)(2,1)S(1)}, bf16[1040,256]{1,0:T(8,128)(2,1)S(1)}) custom-call(s32[2]{0:T(128)S(1)} %copy-done, bf16[512,768]{1,0:T(8,128)(2,1)S(1)} %get-tuple-element.53.refs_0_.x_ref, bf16[768,768]{1,0:T(8,128)(2,1)S(1)} %get-tuple-element.57.refs_4_.h_ref, bf16[768,768]{1,0:T(8,128)(2,1)S(1)} %get-tuple-element.61.e_ref, ...), custom_call_target="tpu_custom_call" | custom-call | flops 6000000000 | bytes 4000000 | tf_op jit(solution)/shard_map/pallas_call | solution.py:461
  47.6 1.4 %collective-permute-start.15 = (bf16[1040,256]{1,0:T(8,128)(2,1)S(1)}, bf16[1040,256]{1,0:T(8,128)(2,1)S(1)}, u32[]{:S(2)}, u32[]{:S(2)}) collective-permute-start(bf16[1040,256]{1,0:T(8,128)(2,1)S(1)} %add_convert_fusion.one_ref), channel_id=1, source_target_pairs={{0,1},{1,0},{2,3},{3,2},{4,5},{5,4},{6,7},{7,6},{8,9},{9,8},{10,11... | collective-permute-start | bytes 1597448 | tf_op jit(solution)/shard_map/ppermute | solution.py:798
  49.8 5.7 %shard_map.264 = (bf16[64,18432]{1,0:T(8,128)(2,1)}, f32[1,1536]{1,0:T(1,128)}, f32[8,128]{1,0:T(8,128)S(1)}) custom-call(s32[2]{0:T(128)S(1)} %copy-done, s32[2,256]{1,0:T(2,128)S(1)} %get-tuple-element.50.meta_ref, s32[104,128]{1,0:T(8,128)S(1)} %get-tuple-element.51.st_ref, s32[104,128]{1,0:T(8,128)S(1)} %get-tuple-element.52.en_ref, ...), custom_call_target="tpu_custom_call" | custom-call | flops 12000000000 | bytes 6000000 | tf_op jit(solution)/shard_map/pallas_call | solution.py:286
  55.4 1.5 %collective-permute-done.15.refs_0_ = bf16[1040,256]{1,0:T(8,128)(2,1)S(1)} collective-permute-done((bf16[1040,256]{1,0:T(8,128)(2,1)S(1)}, bf16[1040,256]{1,0:T(8,128)(2,1)S(1)}, u32[]{:S(2)}, u32[]{:S(2)}) %collective-permute-start.15) | collective-permute-done | bytes 532512 | tf_op jit(solution)/shard_map/ppermute | solution.py:798
  56.9 1.2 %collective-permute-start.16 = (bf16[176,256]{1,0:T(8,128)(2,1)S(1)}, bf16[176,256]{1,0:T(8,128)(2,1)S(1)}, u32[]{:S(2)}, u32[]{:S(2)}) collective-permute-start(bf16[176,256]{1,0:T(8,128)(2,1)S(1)} %shard_map.268), channel_id=1, source_target_pairs={{0,8},{1,9},{2,10},{3,11},{4,12},{5,13},{6,14},{7,15},{8,0},{9,1},... | collective-permute-start | bytes 270344 | tf_op jit(solution)/shard_map/ppermute | solution.py:792
  58.2 1.6 %collective-permute-start.18 = (bf16[432,256]{1,0:T(8,128)(2,1)S(1)}, bf16[432,256]{1,0:T(8,128)(2,1)S(1)}, u32[]{:S(2)}, u32[]{:S(2)}) collective-permute-start(bf16[432,256]{1,0:T(8,128)(2,1)S(1)} %add_convert_fusion.1), channel_id=1, source_target_pairs={{0,2},{1,3},{2,0},{3,1},{4,6},{5,7},{6,4},{7,5},{8,10},{9,11},{10,... | collective-permute-start | bytes 663560 | tf_op jit(solution)/shard_map/ppermute | solution.py:798
  59.8 3.8 %collective-permute-done.16 = bf16[176,256]{1,0:T(8,128)(2,1)S(1)} collective-permute-done((bf16[176,256]{1,0:T(8,128)(2,1)S(1)}, bf16[176,256]{1,0:T(8,128)(2,1)S(1)}, u32[]{:S(2)}, u32[]{:S(2)}) %collective-permute-start.16) | collective-permute-done | bytes 90144 | tf_op jit(solution)/shard_map/ppermute | solution.py:792
  64.3 2.1 %collective-permute-start.20 = (bf16[144,256]{1,0:T(8,128)(2,1)S(1)}, bf16[144,256]{1,0:T(8,128)(2,1)S(1)}, u32[]{:S(2)}, u32[]{:S(2)}) collective-permute-start(bf16[144,256]{1,0:T(8,128)(2,1)S(1)} %get-tuple-element.71), channel_id=1, source_target_pairs={{0,8},{1,9},{2,10},{3,11},{4,12},{5,13},{6,14},{7,15},{8,0},{9,1},... | collective-permute-start | bytes 221192 | tf_op jit(solution)/shard_map/ppermute | solution.py:792
  66.4 2.5 %collective-permute-start.21 = (bf16[144,256]{1,0:T(8,128)(2,1)S(1)}, bf16[144,256]{1,0:T(8,128)(2,1)S(1)}, u32[]{:S(2)}, u32[]{:S(2)}) collective-permute-start(bf16[144,256]{1,0:T(8,128)(2,1)S(1)} %get-tuple-element.72), channel_id=1, source_target_pairs={{0,12},{1,13},{2,14},{3,15},{4,8},{5,9},{6,10},{7,11},{8,4},{9,5},... | collective-permute-start | bytes 221192 | tf_op jit(solution)/shard_map/ppermute | solution.py:792
  69.0 1.6 %collective-permute-start.22 = (bf16[320,256]{1,0:T(8,128)(2,1)S(1)}, bf16[320,256]{1,0:T(8,128)(2,1)S(1)}, u32[]{:S(2)}, u32[]{:S(2)}) collective-permute-start(bf16[320,256]{1,0:T(8,128)(2,1)S(1)} %get-tuple-element.73.refs_1_), channel_id=1, source_target_pairs={{0,2},{1,3},{2,0},{3,1},{4,6},{5,7},{6,4},{7,5},{8,10},{9,11},{10,... | collective-permute-start | bytes 491528 | tf_op jit(solution)/shard_map/ppermute | solution.py:798
  70.6 2.0 %collective-permute-done.21.refs_3_ = bf16[144,256]{1,0:T(8,128)(2,1)S(1)} collective-permute-done((bf16[144,256]{1,0:T(8,128)(2,1)S(1)}, bf16[144,256]{1,0:T(8,128)(2,1)S(1)}, u32[]{:S(2)}, u32[]{:S(2)}) %collective-permute-start.21) | collective-permute-done | bytes 73760 | tf_op jit(solution)/shard_map/ppermute | solution.py:792
  74.4 1.3 %shard_map.273 = (f32[2,32,256]{2,1,0:T(8,128)}, f32[2,16,256]{2,1,0:T(8,128)}, f32[32,256]{1,0:T(8,128)}, f32[16,256]{1,0:T(8,128)}, f32[2,256]{1,0:T(2,128)}, ...) custom-call(s32[2]{0:T(128)S(1)} %copy-done, ...), custom_call_target="tpu_custom_call" | custom-call | bytes 2000000 | tf_op jit(solution)/shard_map/pallas_call | solution.py:983
  (57 shorter events, 8.2 us)
Async XLA Ops:
  1.5 8.3 %collective-permute-start.3 = (bf16[144,256]{1,0:T(8,128)(2,1)S(1)}, bf16[144,256]{1,0:T(8,128)(2,1)S(1)}, u32[]{:S(2)}, u32[]{:S(2)}) collective-permute-start(bf16[144,256]{1,0:T(8,128)(2,1)S(1)} %pad_maximum_fusion.refs_0_), channel_id=1, source_target_pairs={{0,12},{1,13},{2,14},{3,15},{4,8},{5,9},{6,10},{7,11},{8,4},{9,5},... | collective-permute-start | bytes 221192 | tf_op jit(solution)/shard_map/ppermute | solution.py:792
  6.5 6.2 %collective-permute-start.2 = (bf16[144,256]{1,0:T(8,128)(2,1)S(1)}, bf16[144,256]{1,0:T(8,128)(2,1)S(1)}, u32[]{:S(2)}, u32[]{:S(2)}) collective-permute-start(bf16[144,256]{1,0:T(8,128)(2,1)S(1)} %pad_maximum_fusion.refs_0_), channel_id=1, source_target_pairs={{0,8},{1,9},{2,10},{3,11},{4,12},{5,13},{6,14},{7,15},{8,0},{9,1},... | collective-permute-start | bytes 221192 | tf_op jit(solution)/shard_map/ppermute | solution.py:792
  6.5 6.2 %collective-permute-start.1 = (bf16[144,256]{1,0:T(8,128)(2,1)S(1)}, bf16[144,256]{1,0:T(8,128)(2,1)S(1)}, u32[]{:S(2)}, u32[]{:S(2)}) collective-permute-start(bf16[144,256]{1,0:T(8,128)(2,1)S(1)} %pad_maximum_fusion.refs_0_), channel_id=1, source_target_pairs={{0,4},{1,5},{2,6},{3,7},{4,0},{5,1},{6,2},{7,3},{8,12},{9,13},{10,... | collective-permute-start | bytes 221192 | tf_op jit(solution)/shard_map/ppermute | solution.py:792
  9.4 5.3 %copy-start.1 = (bf16[18432,64]{0,1:T(8,128)(2,1)S(1)}, bf16[18432,64]{0,1:T(8,128)(2,1)}, u32[]{:S(2)}) copy-start(bf16[18432,64]{0,1:T(8,128)(2,1)} %param.15) | copy-start | bytes 7077892
  9.4 12.0 %collective-permute-start = (bf16[368,128]{1,0:T(8,128)(2,1)}, bf16[368,128]{1,0:T(8,128)(2,1)S(1)}, u32[]{:S(2)}, u32[]{:S(2)}) collective-permute-start(bf16[368,128]{1,0:T(8,128)(2,1)} %shard_map.256.refs_9_), channel_id=1, source_target_pairs={{0,16},{16,0},{1,17},{17,1},{2,18},{18,2},{3,19},{19,3},{4,20},{20... | collective-permute-start | bytes 282632 | tf_op jit(solution)/shard_map/ppermute | solution.py:787
  13.1 6.8 %collective-permute-start.5 = (bf16[4,144,256]{2,1,0:T(8,128)(2,1)S(1)}, bf16[4,144,256]{2,1,0:T(8,128)(2,1)S(1)}, u32[]{:S(2)}, u32[]{:S(2)}) collective-permute-start(bf16[4,144,256]{2,1,0:T(8,128)(2,1)S(1)} %shard_map.258.refs_2_), channel_id=1, source_target_pairs={{0,1},{1,0},{2,3},{3,2},{4,5},{5,4},{6,7},{7,6},{8,9},{9,8},{10,11... | collective-permute-start | bytes 884744 | tf_op jit(solution)/shard_map/ppermute | solution.py:798
  17.2 12.1 %collective-permute-start.7 = (bf16[4,144,256]{2,1,0:T(8,128)(2,1)S(1)}, bf16[4,144,256]{2,1,0:T(8,128)(2,1)S(1)}, u32[]{:S(2)}, u32[]{:S(2)}) collective-permute-start(bf16[4,144,256]{2,1,0:T(8,128)(2,1)S(1)} %shard_map.258.refs_2_), channel_id=1, source_target_pairs={{0,16},{16,0},{1,17},{17,1},{2,18},{18,2},{3,19},{19,3},{4,20},{20... | collective-permute-start | bytes 884744 | tf_op jit(solution)/shard_map/ppermute | solution.py:787
  17.3 7.0 %collective-permute-start.4 = (bf16[4,144,256]{2,1,0:T(8,128)(2,1)S(1)}, bf16[4,144,256]{2,1,0:T(8,128)(2,1)S(1)}, u32[]{:S(2)}, u32[]{:S(2)}) collective-permute-start(bf16[4,144,256]{2,1,0:T(8,128)(2,1)S(1)} %shard_map.259), channel_id=1, source_target_pairs={{0,2},{1,3},{2,0},{3,1},{4,6},{5,7},{6,4},{7,5},{8,10},{9,11},{10,... | collective-permute-start | bytes 884744 | tf_op jit(solution)/shard_map/ppermute | solution.py:798
  19.9 7.3 %collective-permute-start.6 = (bf16[4,144,256]{2,1,0:T(8,128)(2,1)S(1)}, bf16[4,144,256]{2,1,0:T(8,128)(2,1)S(1)}, u32[]{:S(2)}, u32[]{:S(2)}) collective-permute-start(bf16[4,144,256]{2,1,0:T(8,128)(2,1)S(1)} %shard_map.260.refs_4_), channel_id=1, source_target_pairs={{0,2},{1,3},{2,0},{3,1},{4,6},{5,7},{6,4},{7,5},{8,10},{9,11},{10,... | collective-permute-start | bytes 884744 | tf_op jit(solution)/shard_map/ppermute | solution.py:798
  24.2 5.2 %collective-permute-start.9 = (bf16[4,144,256]{2,1,0:T(8,128)(2,1)S(1)}, bf16[4,144,256]{2,1,0:T(8,128)(2,1)S(1)}, u32[]{:S(2)}, u32[]{:S(2)}) collective-permute-start(bf16[4,144,256]{2,1,0:T(8,128)(2,1)S(1)} %shard_map.260.refs_4_), channel_id=1, source_target_pairs={{0,16},{16,0},{1,17},{17,1},{2,18},{18,2},{3,19},{19,3},{4,20},{20... | collective-permute-start | bytes 884744 | tf_op jit(solution)/shard_map/ppermute | solution.py:787
  24.3 5.1 %collective-permute-start.8 = (bf16[4,144,256]{2,1,0:T(8,128)(2,1)S(1)}, bf16[4,144,256]{2,1,0:T(8,128)(2,1)S(1)}, u32[]{:S(2)}, u32[]{:S(2)}) collective-permute-start(bf16[4,144,256]{2,1,0:T(8,128)(2,1)S(1)} %collective-permute-done.4.refs_3_), channel_id=1, source_target_pairs={{0,16},{16,0},{1,17},{17,1},{2,18},{18,2},{3,19},{19,3},{4,20},{20... | collective-permute-start | bytes 884744 | tf_op jit(solution)/shard_map/ppermute | solution.py:787
  27.2 2.1 %collective-permute-start.10 = (bf16[4,144,256]{2,1,0:T(8,128)(2,1)S(1)}, bf16[4,144,256]{2,1,0:T(8,128)(2,1)S(1)}, u32[]{:S(2)}, u32[]{:S(2)}) collective-permute-start(bf16[4,144,256]{2,1,0:T(8,128)(2,1)S(1)} %shard_map.261.refs_5_), channel_id=1, source_target_pairs={{0,16},{16,0},{1,17},{17,1},{2,18},{18,2},{3,19},{19,3},{4,20},{20... | collective-permute-start | bytes 884744 | tf_op jit(solution)/shard_map/ppermute | solution.py:787
  44.6 2.8 %collective-permute-start.14 = (bf16[1040,256]{1,0:T(8,128)(2,1)S(1)}, bf16[1040,256]{1,0:T(8,128)(2,1)S(1)}, u32[]{:S(2)}, u32[]{:S(2)}) collective-permute-start(bf16[1040,256]{1,0:T(8,128)(2,1)S(1)} %get-tuple-element.68), channel_id=1, source_target_pairs={{0,16},{16,0},{1,17},{17,1},{2,18},{18,2},{3,19},{19,3},{4,20},{20... | collective-permute-start | bytes 1597448 | tf_op jit(solution)/shard_map/ppermute | solution.py:787
  45.1 3.8 %collective-permute-start.12 = (bf16[1440,256]{1,0:T(8,128)(2,1)S(1)}, bf16[1440,256]{1,0:T(8,128)(2,1)S(1)}, u32[]{:S(2)}, u32[]{:S(2)}) collective-permute-start(bf16[1440,256]{1,0:T(8,128)(2,1)S(1)} %get-tuple-element.65), channel_id=1, source_target_pairs={{0,16},{16,0},{1,17},{17,1},{2,18},{18,2},{3,19},{19,3},{4,20},{20... | collective-permute-start | bytes 2211848 | tf_op jit(solution)/shard_map/ppermute | solution.py:787
  45.2 4.6 %collective-permute-start.11 = (bf16[784,512]{1,0:T(8,128)(2,1)S(1)}, bf16[784,512]{1,0:T(8,128)(2,1)S(1)}, u32[]{:S(2)}, u32[]{:S(2)}) collective-permute-start(bf16[784,512]{1,0:T(8,128)(2,1)S(1)} %get-tuple-element.58.own_ref), channel_id=1, source_target_pairs={{0,16},{16,0},{1,17},{17,1},{2,18},{18,2},{3,19},{19,3},{4,20},{20... | collective-permute-start | bytes 2408456 | tf_op jit(solution)/shard_map/ppermute | solution.py:787
  47.6 9.3 %collective-permute-start.15 = (bf16[1040,256]{1,0:T(8,128)(2,1)S(1)}, bf16[1040,256]{1,0:T(8,128)(2,1)S(1)}, u32[]{:S(2)}, u32[]{:S(2)}) collective-permute-start(bf16[1040,256]{1,0:T(8,128)(2,1)S(1)} %add_convert_fusion.one_ref), channel_id=1, source_target_pairs={{0,1},{1,0},{2,3},{3,2},{4,5},{5,4},{6,7},{7,6},{8,9},{9,8},{10,11... | collective-permute-start | bytes 1597448 | tf_op jit(solution)/shard_map/ppermute | solution.py:798
  49.0 19.9 %collective-permute-start.13 = (bf16[288,256]{1,0:T(8,128)(2,1)S(1)}, bf16[288,256]{1,0:T(8,128)(2,1)S(1)}, u32[]{:S(2)}, u32[]{:S(2)}) collective-permute-start(bf16[288,256]{1,0:T(8,128)(2,1)S(1)} %add_convert_fusion.2), channel_id=1, source_target_pairs={{0,1},{1,0},{2,3},{3,2},{4,5},{5,4},{6,7},{7,6},{8,9},{9,8},{10,11... | collective-permute-start | bytes 442376 | tf_op jit(solution)/shard_map/ppermute | solution.py:798
  56.9 6.6 %collective-permute-start.16 = (bf16[176,256]{1,0:T(8,128)(2,1)S(1)}, bf16[176,256]{1,0:T(8,128)(2,1)S(1)}, u32[]{:S(2)}, u32[]{:S(2)}) collective-permute-start(bf16[176,256]{1,0:T(8,128)(2,1)S(1)} %shard_map.268), channel_id=1, source_target_pairs={{0,8},{1,9},{2,10},{3,11},{4,12},{5,13},{6,14},{7,15},{8,0},{9,1},... | collective-permute-start | bytes 270344 | tf_op jit(solution)/shard_map/ppermute | solution.py:792
  58.2 6.0 %collective-permute-start.18 = (bf16[432,256]{1,0:T(8,128)(2,1)S(1)}, bf16[432,256]{1,0:T(8,128)(2,1)S(1)}, u32[]{:S(2)}, u32[]{:S(2)}) collective-permute-start(bf16[432,256]{1,0:T(8,128)(2,1)S(1)} %add_convert_fusion.1), channel_id=1, source_target_pairs={{0,2},{1,3},{2,0},{3,1},{4,6},{5,7},{6,4},{7,5},{8,10},{9,11},{10,... | collective-permute-start | bytes 663560 | tf_op jit(solution)/shard_map/ppermute | solution.py:798
  63.6 5.3 %collective-permute-start.17 = (bf16[176,256]{1,0:T(8,128)(2,1)S(1)}, bf16[176,256]{1,0:T(8,128)(2,1)S(1)}, u32[]{:S(2)}, u32[]{:S(2)}) collective-permute-start(bf16[176,256]{1,0:T(8,128)(2,1)S(1)} %add_convert_fusion.3.refs_0_), channel_id=1, source_target_pairs={{0,4},{1,5},{2,6},{3,7},{4,0},{5,1},{6,2},{7,3},{8,12},{9,13},{10,... | collective-permute-start | bytes 270344 | tf_op jit(solution)/shard_map/ppermute | solution.py:792
  64.3 6.3 %collective-permute-start.20 = (bf16[144,256]{1,0:T(8,128)(2,1)S(1)}, bf16[144,256]{1,0:T(8,128)(2,1)S(1)}, u32[]{:S(2)}, u32[]{:S(2)}) collective-permute-start(bf16[144,256]{1,0:T(8,128)(2,1)S(1)} %get-tuple-element.71), channel_id=1, source_target_pairs={{0,8},{1,9},{2,10},{3,11},{4,12},{5,13},{6,14},{7,15},{8,0},{9,1},... | collective-permute-start | bytes 221192 | tf_op jit(solution)/shard_map/ppermute | solution.py:792
  66.4 6.2 %collective-permute-start.21 = (bf16[144,256]{1,0:T(8,128)(2,1)S(1)}, bf16[144,256]{1,0:T(8,128)(2,1)S(1)}, u32[]{:S(2)}, u32[]{:S(2)}) collective-permute-start(bf16[144,256]{1,0:T(8,128)(2,1)S(1)} %get-tuple-element.72), channel_id=1, source_target_pairs={{0,12},{1,13},{2,14},{3,15},{4,8},{5,9},{6,10},{7,11},{8,4},{9,5},... | collective-permute-start | bytes 221192 | tf_op jit(solution)/shard_map/ppermute | solution.py:792
  68.9 4.5 %collective-permute-start.19 = (bf16[144,256]{1,0:T(8,128)(2,1)S(1)}, bf16[144,256]{1,0:T(8,128)(2,1)S(1)}, u32[]{:S(2)}, u32[]{:S(2)}) collective-permute-start(bf16[144,256]{1,0:T(8,128)(2,1)S(1)} %get-tuple-element.69.refs_1_), channel_id=1, source_target_pairs={{0,4},{1,5},{2,6},{3,7},{4,0},{5,1},{6,2},{7,3},{8,12},{9,13},{10,... | collective-permute-start | bytes 221192 | tf_op jit(solution)/shard_map/ppermute | solution.py:792
  69.0 5.4 %collective-permute-start.22 = (bf16[320,256]{1,0:T(8,128)(2,1)S(1)}, bf16[320,256]{1,0:T(8,128)(2,1)S(1)}, u32[]{:S(2)}, u32[]{:S(2)}) collective-permute-start(bf16[320,256]{1,0:T(8,128)(2,1)S(1)} %get-tuple-element.73.refs_1_), channel_id=1, source_target_pairs={{0,2},{1,3},{2,0},{3,1},{4,6},{5,7},{6,4},{7,5},{8,10},{9,11},{10,... | collective-permute-start | bytes 491528 | tf_op jit(solution)/shard_map/ppermute | solution.py:798
  (3 other events, 9.1 us)

commit v8 on v7

--- a/solution.py
+++ b/solution.py
@@ -382,14 +382,13 @@
 
 
 def put(ids_ref, t, s, outs, plan, rows1, rows2, held_ref, first, value):
-    held_ref[...] = value
+    held_ref[...] = (value if first else 0.5 * value).astype(BF)
     for out, (small_first, pieces) in zip(outs, plan):
         for g, piece in enumerate(pieces):
             mine = rows_of(ids_ref, t, piece, rows1, rows2)[0 if first else 1]
             at = g * SLOTS * (rows1 + rows2) + (SMALL_ROWS if small_first else 0)
             at, size = (at + s * rows1, rows1) if first else (at + SLOTS * rows1 + s * rows2, rows2)
-            value = held_ref[mine, :]
-            out[at : at + size, :] = (value if first else 0.5 * value).astype(BF)
+            out[at : at + size, :] = held_ref[mine, :]
 
 
 def first_layer(s, w1_ref, x_ref, pc_ref):
@@ -463,7 +462,7 @@
         out_shape=outs,
         in_specs=[SSPEC] + [VSPEC] * 5,
         out_specs=(VSPEC,) * len(outs),
-        scratch_shapes=[pltpu.VMEM((2, D, HID), F32), pltpu.VMEM((2, HID, HID), F32)],
+        scratch_shapes=[pltpu.VMEM((2, D, HID), BF), pltpu.VMEM((2, HID, HID), BF)],
         compiler_params=params(16),
         cost_estimate=cost(6e9, 4e6),
     )(ids, x, h, e, f, small)
@@ -767,8 +766,8 @@
         ((WIDE, events), BF),
         ((2 * TOWER2, LANES), F32),
         ((16, LANES), F32),
-        ((2, D, HID), F32),
-        ((2, HID, HID), F32),
+        ((2, D, HID), BF),
+        ((2, HID, HID), BF),
         ((16, events), F32),
     ]
     arrays = [*started, *oth_groups, own_pack, oth_pack]

time: 76.2 us -> 76.1 us (level)
  transfers between devices with their start and end apart: 23 -> 23, of which waited for: 9 -> 10; matrix products, arithmetic and copies ran while one was open for 1% -> 1% of each run, Pallas kernels for 23% -> 23%
where the time goes in v8:
time: 76.1 us; the launch traced here: 76 us
  Pallas kernels  33.9 us (45%)
  starting transfers between devices  23.2 us (30%)
  waiting for transfers between devices  16.1 us (21%)
  other arithmetic  1.73 us (2%)
  between operations  1.02 us (1%)
    pallas_call x1, Pallas kernels, layer(): pl.pallas_call(functools.partial(main_kernel, given, plan, rows1, rows2),...  15.1 us
    ppermute x8, starting transfers between devices, flipped(): return lax.ppermute(value, 'dp', pairs)  11.5 us
    ppermute x7, starting transfers between devices, crossed(): return lax.ppermute(value, ('task', 'dp'), pairs)  9.98 us
    ppermute x8, waiting for transfers between devices, flipped(): return lax.ppermute(value, 'dp', pairs)  9.61 us
    ppermute x7, waiting for transfers between devices, crossed(): return lax.ppermute(value, ('task', 'dp'), pairs)  6.52 us
    pallas_call x1, Pallas kernels, expand(): pl.pallas_call(functools.partial(expand_kernel, blocks // 2, group), grid...  5.66 us
    pallas_call x2, Pallas kernels, pool(): pl.pallas_call(functools.partial(pool_kernel, part * count, count, half_b...  5.5 us
    pallas_call x1, Pallas kernels, front(): pl.pallas_call(functools.partial(front_kernel, len(x_parts), given, rows1...  2.09 us
  transfers between devices with their start and end apart: 23, of which 10 were waited for; matrix products, arithmetic and copies ran while one was open for 1% of the time, Pallas kernels for 23%

profile of v8, /device:TPU:0, one launch (start us, length us, event | category | flops | bytes accessed | tf_op | source)
XLA Modules:
  0.0 76.0 jit_solution(3623945415269658517)
XLA Ops:
  1.5 5.0 %collective-permute-start.3 = (bf16[144,256]{1,0:T(8,128)(2,1)S(1)}, bf16[144,256]{1,0:T(8,128)(2,1)S(1)}, u32[]{:S(2)}, u32[]{:S(2)}) collective-permute-start(bf16[144,256]{1,0:T(8,128)(2,1)S(1)} %pad_maximum_fusion.refs_0_), channel_id=1, source_target_pairs={{0,12},{1,13},{2,14},{3,15},{4,8},{5,9},{6,10},{7,11},{8,4},{9,5},... | collective-permute-start | bytes 221192 | tf_op jit(solution)/shard_map/ppermute | solution.py:791
  7.7 1.7 %shard_map.256.refs_9_ = bf16[368,128]{1,0:T(8,128)(2,1)} custom-call(s32[2]{0:T(128)} %pad_add_fusion.ids_ref, s32[1,1536]{1,0:T(1,128)} %label_ref.1, bf16[2,256]{1,0:T(2,128)(2,1)} %bitcast.48, bf16[2,256]{1,0:T(2,128)(2,1)} %bitcast.49, bf16[1,256]{1,0:T(2,128)(2,1)} %ogain_ref.1, bf16[1,256]{1,0:T(2,128)(2,1)} %oshift_ref.1, bf16[4,512]{1,0:T(4,128)(2,1)} %bitcast.45, ...), custom_call_target="tpu_custom_call" | custom-call | flops 1000000000 | bytes 1000000 | tf_op jit(solution)/shard_map/pallas_call | solution.py:160
  9.7 3.0 %collective-permute-done.2.refs_2_ = bf16[144,256]{1,0:T(8,128)(2,1)S(1)} collective-permute-done((bf16[144,256]{1,0:T(8,128)(2,1)S(1)}, bf16[144,256]{1,0:T(8,128)(2,1)S(1)}, u32[]{:S(2)}, u32[]{:S(2)}) %collective-permute-start.2) | collective-permute-done | bytes 73760 | tf_op jit(solution)/shard_map/ppermute | solution.py:791
  13.1 1.6 %collective-permute-start.5 = (bf16[4,144,256]{2,1,0:T(8,128)(2,1)S(1)}, bf16[4,144,256]{2,1,0:T(8,128)(2,1)S(1)}, u32[]{:S(2)}, u32[]{:S(2)}) collective-permute-start(bf16[4,144,256]{2,1,0:T(8,128)(2,1)S(1)} %shard_map.258.refs_2_), channel_id=1, source_target_pairs={{0,1},{1,0},{2,3},{3,2},{4,5},{5,4},{6,7},{7,6},{8,9},{9,8},{10,11... | collective-permute-start | bytes 884744 | tf_op jit(solution)/shard_map/ppermute | solution.py:797
  14.7 2.7 %shard_map.255.refs_1_.refs_0_ = bf16[384,512]{1,0:T(8,128)(2,1)S(1)} custom-call(s32[2]{0:T(128)S(1)} %copy-done, s32[2,256]{1,0:T(2,128)S(1)} %get-tuple-element.50.meta_ref, s32[104,128]{1,0:T(8,128)S(1)} %get-tuple-element.51.st_ref, s32[104,128]{1,0:T(8,128)S(1)} %get-tuple-element.52.en_ref, bf16[64,18432]{1,0:T(8,128)(2,1)S(1)} %bitcast.30), custom_call_target="tpu_custom_call" | custom-call | flops 10000000000 | bytes 5000000 | tf_op jit(solution)/shard_map/pallas_call | solution.py:232
  17.6 1.6 %collective-permute-start.4 = (bf16[4,144,256]{2,1,0:T(8,128)(2,1)S(1)}, bf16[4,144,256]{2,1,0:T(8,128)(2,1)S(1)}, u32[]{:S(2)}, u32[]{:S(2)}) collective-permute-start(bf16[4,144,256]{2,1,0:T(8,128)(2,1)S(1)} %shard_map.259), channel_id=1, source_target_pairs={{0,2},{1,3},{2,0},{3,1},{4,6},{5,7},{6,4},{7,5},{8,10},{9,11},{10,... | collective-permute-start | bytes 884744 | tf_op jit(solution)/shard_map/ppermute | solution.py:797
  19.9 1.5 %collective-permute-start.6 = (bf16[4,144,256]{2,1,0:T(8,128)(2,1)S(1)}, bf16[4,144,256]{2,1,0:T(8,128)(2,1)S(1)}, u32[]{:S(2)}, u32[]{:S(2)}) collective-permute-start(bf16[4,144,256]{2,1,0:T(8,128)(2,1)S(1)} %shard_map.260.refs_4_), channel_id=1, source_target_pairs={{0,2},{1,3},{2,0},{3,1},{4,6},{5,7},{6,4},{7,5},{8,10},{9,11},{10,... | collective-permute-start | bytes 884744 | tf_op jit(solution)/shard_map/ppermute | solution.py:797
  21.5 2.7 %shard_map.257.refs_1_ = bf16[384,512]{1,0:T(8,128)(2,1)S(1)} custom-call(s32[2]{0:T(128)S(1)} %copy-done, s32[2,256]{1,0:T(2,128)S(1)} %get-tuple-element.50.meta_ref, s32[104,128]{1,0:T(8,128)S(1)} %get-tuple-element.51.st_ref, s32[104,128]{1,0:T(8,128)S(1)} %get-tuple-element.52.en_ref, bf16[64,18432]{1,0:T(8,128)(2,1)S(1)} %bitcast.31, ...), custom_call_target="tpu_custom_call" | custom-call | flops 10000000000 | bytes 5000000 | tf_op jit(solution)/shard_map/pallas_call | solution.py:232
  24.8 2.7 %collective-permute-done.6.refs_0_ = bf16[4,144,256]{2,1,0:T(8,128)(2,1)S(1)} collective-permute-done((bf16[4,144,256]{2,1,0:T(8,128)(2,1)S(1)}, bf16[4,144,256]{2,1,0:T(8,128)(2,1)S(1)}, u32[]{:S(2)}, u32[]{:S(2)}) %collective-permute-start.6) | collective-permute-done | bytes 294944 | tf_op jit(solution)/shard_map/ppermute | solution.py:797
  27.5 2.1 %shard_map.262 = (bf16[512,768]{1,0:T(8,128)(2,1)S(1)}, bf16[512,768]{1,0:T(8,128)(2,1)S(1)}, bf16[3,256,256]{2,1,0:T(8,128)(2,1)S(1)}, f32[768,768]{1,0:T(8,128)S(1)}, bf16[768,768]{1,0:T(8,128)(2,1)S(1)}) custom-call(s32[2]{0:T(128)S(1)} %copy-done, bf16[384,512]{1,0:T(8,128)(2,1)S(1)} %shard_map.255.refs_1_.refs_0_, ...), custom_call_target="tpu_custom_call" | custom-call | flops 6000000000 | bytes 4000000 | tf_op jit(solution)/shard_map/pallas_call | solution.py:431
  29.7 15.1 %shard_map.263 = (bf16[784,512]{1,0:T(8,128)(2,1)S(1)}, bf16[768,768]{1,0:T(8,128)(2,1)S(1)}, bf16[768,768]{1,0:T(8,128)(2,1)S(1)}, bf16[176,256]{1,0:T(8,128)(2...) custom-call(s32[2]{0:T(128)S(1)} %copy-done, ...), custom_call_target="tpu_custom_call" | custom-call | flops 5435817984 | bytes 10000000 | tf_op jit(solution)/shard_map/pallas_call | solution.py:774
  45.9 1.7 %shard_map.265 = (bf16[1440,256]{1,0:T(8,128)(2,1)S(1)}, bf16[1040,256]{1,0:T(8,128)(2,1)S(1)}) custom-call(s32[2]{0:T(128)S(1)} %copy-done, bf16[512,768]{1,0:T(8,128)(2,1)S(1)} %get-tuple-element.53.refs_0_.x_ref, bf16[768,768]{1,0:T(8,128)(2,1)S(1)} %get-tuple-element.57.refs_4_.h_ref, bf16[768,768]{1,0:T(8,128)(2,1)S(1)} %get-tuple-element.61.e_ref, ...), custom_call_target="tpu_custom_call" | custom-call | flops 6000000000 | bytes 4000000 | tf_op jit(solution)/shard_map/pallas_call | solution.py:460
  48.7 1.3 %collective-permute-start.13 = (bf16[288,256]{1,0:T(8,128)(2,1)S(1)}, bf16[288,256]{1,0:T(8,128)(2,1)S(1)}, u32[]{:S(2)}, u32[]{:S(2)}) collective-permute-start(bf16[288,256]{1,0:T(8,128)(2,1)S(1)} %add_convert_fusion.2), channel_id=1, source_target_pairs={{0,1},{1,0},{2,3},{3,2},{4,5},{5,4},{6,7},{7,6},{8,9},{9,8},{10,11... | collective-permute-start | bytes 442376 | tf_op jit(solution)/shard_map/ppermute | solution.py:797
  50.0 5.7 %shard_map.264 = (bf16[64,18432]{1,0:T(8,128)(2,1)}, f32[1,1536]{1,0:T(1,128)}, f32[8,128]{1,0:T(8,128)S(1)}) custom-call(s32[2]{0:T(128)S(1)} %copy-done, s32[2,256]{1,0:T(2,128)S(1)} %get-tuple-element.50.meta_ref, s32[104,128]{1,0:T(8,128)S(1)} %get-tuple-element.51.st_ref, s32[104,128]{1,0:T(8,128)S(1)} %get-tuple-element.52.en_ref, ...), custom_call_target="tpu_custom_call" | custom-call | flops 12000000000 | bytes 6000000 | tf_op jit(solution)/shard_map/pallas_call | solution.py:286
  55.6 1.5 %collective-permute-done.15.refs_0_ = bf16[1040,256]{1,0:T(8,128)(2,1)S(1)} collective-permute-done((bf16[1040,256]{1,0:T(8,128)(2,1)S(1)}, bf16[1040,256]{1,0:T(8,128)(2,1)S(1)}, u32[]{:S(2)}, u32[]{:S(2)}) %collective-permute-start.15) | collective-permute-done | bytes 532512 | tf_op jit(solution)/shard_map/ppermute | solution.py:797
  57.1 1.2 %collective-permute-start.16 = (bf16[176,256]{1,0:T(8,128)(2,1)S(1)}, bf16[176,256]{1,0:T(8,128)(2,1)S(1)}, u32[]{:S(2)}, u32[]{:S(2)}) collective-permute-start(bf16[176,256]{1,0:T(8,128)(2,1)S(1)} %shard_map.268), channel_id=1, source_target_pairs={{0,8},{1,9},{2,10},{3,11},{4,12},{5,13},{6,14},{7,15},{8,0},{9,1},... | collective-permute-start | bytes 270344 | tf_op jit(solution)/shard_map/ppermute | solution.py:791
  58.4 1.6 %collective-permute-start.18 = (bf16[432,256]{1,0:T(8,128)(2,1)S(1)}, bf16[432,256]{1,0:T(8,128)(2,1)S(1)}, u32[]{:S(2)}, u32[]{:S(2)}) collective-permute-start(bf16[432,256]{1,0:T(8,128)(2,1)S(1)} %add_convert_fusion.1), channel_id=1, source_target_pairs={{0,2},{1,3},{2,0},{3,1},{4,6},{5,7},{6,4},{7,5},{8,10},{9,11},{10,... | collective-permute-start | bytes 663560 | tf_op jit(solution)/shard_map/ppermute | solution.py:797
  60.0 3.8 %collective-permute-done.16 = bf16[176,256]{1,0:T(8,128)(2,1)S(1)} collective-permute-done((bf16[176,256]{1,0:T(8,128)(2,1)S(1)}, bf16[176,256]{1,0:T(8,128)(2,1)S(1)}, u32[]{:S(2)}, u32[]{:S(2)}) %collective-permute-start.16) | collective-permute-done | bytes 90144 | tf_op jit(solution)/shard_map/ppermute | solution.py:791
  64.5 2.1 %collective-permute-start.20 = (bf16[144,256]{1,0:T(8,128)(2,1)S(1)}, bf16[144,256]{1,0:T(8,128)(2,1)S(1)}, u32[]{:S(2)}, u32[]{:S(2)}) collective-permute-start(bf16[144,256]{1,0:T(8,128)(2,1)S(1)} %get-tuple-element.71), channel_id=1, source_target_pairs={{0,8},{1,9},{2,10},{3,11},{4,12},{5,13},{6,14},{7,15},{8,0},{9,1},... | collective-permute-start | bytes 221192 | tf_op jit(solution)/shard_map/ppermute | solution.py:791
  66.6 2.5 %collective-permute-start.21 = (bf16[144,256]{1,0:T(8,128)(2,1)S(1)}, bf16[144,256]{1,0:T(8,128)(2,1)S(1)}, u32[]{:S(2)}, u32[]{:S(2)}) collective-permute-start(bf16[144,256]{1,0:T(8,128)(2,1)S(1)} %get-tuple-element.72), channel_id=1, source_target_pairs={{0,12},{1,13},{2,14},{3,15},{4,8},{5,9},{6,10},{7,11},{8,4},{9,5},... | collective-permute-start | bytes 221192 | tf_op jit(solution)/shard_map/ppermute | solution.py:791
  69.2 1.6 %collective-permute-start.22 = (bf16[320,256]{1,0:T(8,128)(2,1)S(1)}, bf16[320,256]{1,0:T(8,128)(2,1)S(1)}, u32[]{:S(2)}, u32[]{:S(2)}) collective-permute-start(bf16[320,256]{1,0:T(8,128)(2,1)S(1)} %get-tuple-element.73.refs_1_), channel_id=1, source_target_pairs={{0,2},{1,3},{2,0},{3,1},{4,6},{5,7},{6,4},{7,5},{8,10},{9,11},{10,... | collective-permute-start | bytes 491528 | tf_op jit(solution)/shard_map/ppermute | solution.py:797
  70.8 2.0 %collective-permute-done.21.refs_3_ = bf16[144,256]{1,0:T(8,128)(2,1)S(1)} collective-permute-done((bf16[144,256]{1,0:T(8,128)(2,1)S(1)}, bf16[144,256]{1,0:T(8,128)(2,1)S(1)}, u32[]{:S(2)}, u32[]{:S(2)}) %collective-permute-start.21) | collective-permute-done | bytes 73760 | tf_op jit(solution)/shard_map/ppermute | solution.py:791
  73.7 0.9 %collective-permute-done.22.refs_2_ = bf16[320,256]{1,0:T(8,128)(2,1)S(1)} collective-permute-done((bf16[320,256]{1,0:T(8,128)(2,1)S(1)}, bf16[320,256]{1,0:T(8,128)(2,1)S(1)}, u32[]{:S(2)}, u32[]{:S(2)}) %collective-permute-start.22) | collective-permute-done | bytes 163872 | tf_op jit(solution)/shard_map/ppermute | solution.py:797
  74.6 1.3 %shard_map.273 = (f32[2,32,256]{2,1,0:T(8,128)}, f32[2,16,256]{2,1,0:T(8,128)}, f32[32,256]{1,0:T(8,128)}, f32[16,256]{1,0:T(8,128)}, f32[2,256]{1,0:T(2,128)}, ...) custom-call(s32[2]{0:T(128)S(1)} %copy-done, ...), custom_call_target="tpu_custom_call" | custom-call | bytes 2000000 | tf_op jit(solution)/shard_map/pallas_call | solution.py:982
  (57 shorter events, 8.1 us)
Async XLA Ops:
  1.5 8.3 %collective-permute-start.3 = (bf16[144,256]{1,0:T(8,128)(2,1)S(1)}, bf16[144,256]{1,0:T(8,128)(2,1)S(1)}, u32[]{:S(2)}, u32[]{:S(2)}) collective-permute-start(bf16[144,256]{1,0:T(8,128)(2,1)S(1)} %pad_maximum_fusion.refs_0_), channel_id=1, source_target_pairs={{0,12},{1,13},{2,14},{3,15},{4,8},{5,9},{6,10},{7,11},{8,4},{9,5},... | collective-permute-start | bytes 221192 | tf_op jit(solution)/shard_map/ppermute | solution.py:791
  6.5 6.2 %collective-permute-start.2 = (bf16[144,256]{1,0:T(8,128)(2,1)S(1)}, bf16[144,256]{1,0:T(8,128)(2,1)S(1)}, u32[]{:S(2)}, u32[]{:S(2)}) collective-permute-start(bf16[144,256]{1,0:T(8,128)(2,1)S(1)} %pad_maximum_fusion.refs_0_), channel_id=1, source_target_pairs={{0,8},{1,9},{2,10},{3,11},{4,12},{5,13},{6,14},{7,15},{8,0},{9,1},... | collective-permute-start | bytes 221192 | tf_op jit(solution)/shard_map/ppermute | solution.py:791
  6.5 6.2 %collective-permute-start.1 = (bf16[144,256]{1,0:T(8,128)(2,1)S(1)}, bf16[144,256]{1,0:T(8,128)(2,1)S(1)}, u32[]{:S(2)}, u32[]{:S(2)}) collective-permute-start(bf16[144,256]{1,0:T(8,128)(2,1)S(1)} %pad_maximum_fusion.refs_0_), channel_id=1, source_target_pairs={{0,4},{1,5},{2,6},{3,7},{4,0},{5,1},{6,2},{7,3},{8,12},{9,13},{10,... | collective-permute-start | bytes 221192 | tf_op jit(solution)/shard_map/ppermute | solution.py:791
  9.4 5.3 %copy-start.1 = (bf16[18432,64]{0,1:T(8,128)(2,1)S(1)}, bf16[18432,64]{0,1:T(8,128)(2,1)}, u32[]{:S(2)}) copy-start(bf16[18432,64]{0,1:T(8,128)(2,1)} %param.15) | copy-start | bytes 7077892
  9.4 12.0 %collective-permute-start = (bf16[368,128]{1,0:T(8,128)(2,1)}, bf16[368,128]{1,0:T(8,128)(2,1)S(1)}, u32[]{:S(2)}, u32[]{:S(2)}) collective-permute-start(bf16[368,128]{1,0:T(8,128)(2,1)} %shard_map.256.refs_9_), channel_id=1, source_target_pairs={{0,16},{16,0},{1,17},{17,1},{2,18},{18,2},{3,19},{19,3},{4,20},{20... | collective-permute-start | bytes 282632 | tf_op jit(solution)/shard_map/ppermute | solution.py:786
  13.1 6.8 %collective-permute-start.5 = (bf16[4,144,256]{2,1,0:T(8,128)(2,1)S(1)}, bf16[4,144,256]{2,1,0:T(8,128)(2,1)S(1)}, u32[]{:S(2)}, u32[]{:S(2)}) collective-permute-start(bf16[4,144,256]{2,1,0:T(8,128)(2,1)S(1)} %shard_map.258.refs_2_), channel_id=1, source_target_pairs={{0,1},{1,0},{2,3},{3,2},{4,5},{5,4},{6,7},{7,6},{8,9},{9,8},{10,11... | collective-permute-start | bytes 884744 | tf_op jit(solution)/shard_map/ppermute | solution.py:797
  17.5 12.1 %collective-permute-start.7 = (bf16[4,144,256]{2,1,0:T(8,128)(2,1)S(1)}, bf16[4,144,256]{2,1,0:T(8,128)(2,1)S(1)}, u32[]{:S(2)}, u32[]{:S(2)}) collective-permute-start(bf16[4,144,256]{2,1,0:T(8,128)(2,1)S(1)} %shard_map.258.refs_2_), channel_id=1, source_target_pairs={{0,16},{16,0},{1,17},{17,1},{2,18},{18,2},{3,19},{19,3},{4,20},{20... | collective-permute-start | bytes 884744 | tf_op jit(solution)/shard_map/ppermute | solution.py:786
  17.6 6.8 %collective-permute-start.4 = (bf16[4,144,256]{2,1,0:T(8,128)(2,1)S(1)}, bf16[4,144,256]{2,1,0:T(8,128)(2,1)S(1)}, u32[]{:S(2)}, u32[]{:S(2)}) collective-permute-start(bf16[4,144,256]{2,1,0:T(8,128)(2,1)S(1)} %shard_map.259), channel_id=1, source_target_pairs={{0,2},{1,3},{2,0},{3,1},{4,6},{5,7},{6,4},{7,5},{8,10},{9,11},{10,... | collective-permute-start | bytes 884744 | tf_op jit(solution)/shard_map/ppermute | solution.py:797
  19.9 7.6 %collective-permute-start.6 = (bf16[4,144,256]{2,1,0:T(8,128)(2,1)S(1)}, bf16[4,144,256]{2,1,0:T(8,128)(2,1)S(1)}, u32[]{:S(2)}, u32[]{:S(2)}) collective-permute-start(bf16[4,144,256]{2,1,0:T(8,128)(2,1)S(1)} %shard_map.260.refs_4_), channel_id=1, source_target_pairs={{0,2},{1,3},{2,0},{3,1},{4,6},{5,7},{6,4},{7,5},{8,10},{9,11},{10,... | collective-permute-start | bytes 884744 | tf_op jit(solution)/shard_map/ppermute | solution.py:797
  24.2 5.4 %collective-permute-start.9 = (bf16[4,144,256]{2,1,0:T(8,128)(2,1)S(1)}, bf16[4,144,256]{2,1,0:T(8,128)(2,1)S(1)}, u32[]{:S(2)}, u32[]{:S(2)}) collective-permute-start(bf16[4,144,256]{2,1,0:T(8,128)(2,1)S(1)} %shard_map.260.refs_4_), channel_id=1, source_target_pairs={{0,16},{16,0},{1,17},{17,1},{2,18},{18,2},{3,19},{19,3},{4,20},{20... | collective-permute-start | bytes 884744 | tf_op jit(solution)/shard_map/ppermute | solution.py:786
  24.4 5.3 %collective-permute-start.8 = (bf16[4,144,256]{2,1,0:T(8,128)(2,1)S(1)}, bf16[4,144,256]{2,1,0:T(8,128)(2,1)S(1)}, u32[]{:S(2)}, u32[]{:S(2)}) collective-permute-start(bf16[4,144,256]{2,1,0:T(8,128)(2,1)S(1)} %collective-permute-done.4.refs_3_), channel_id=1, source_target_pairs={{0,16},{16,0},{1,17},{17,1},{2,18},{18,2},{3,19},{19,3},{4,20},{20... | collective-permute-start | bytes 884744 | tf_op jit(solution)/shard_map/ppermute | solution.py:786
  27.5 2.1 %collective-permute-start.10 = (bf16[4,144,256]{2,1,0:T(8,128)(2,1)S(1)}, bf16[4,144,256]{2,1,0:T(8,128)(2,1)S(1)}, u32[]{:S(2)}, u32[]{:S(2)}) collective-permute-start(bf16[4,144,256]{2,1,0:T(8,128)(2,1)S(1)} %shard_map.261.refs_5_), channel_id=1, source_target_pairs={{0,16},{16,0},{1,17},{17,1},{2,18},{18,2},{3,19},{19,3},{4,20},{20... | collective-permute-start | bytes 884744 | tf_op jit(solution)/shard_map/ppermute | solution.py:786
  44.8 2.8 %collective-permute-start.14 = (bf16[1040,256]{1,0:T(8,128)(2,1)S(1)}, bf16[1040,256]{1,0:T(8,128)(2,1)S(1)}, u32[]{:S(2)}, u32[]{:S(2)}) collective-permute-start(bf16[1040,256]{1,0:T(8,128)(2,1)S(1)} %get-tuple-element.68), channel_id=1, source_target_pairs={{0,16},{16,0},{1,17},{17,1},{2,18},{18,2},{3,19},{19,3},{4,20},{20... | collective-permute-start | bytes 1597448 | tf_op jit(solution)/shard_map/ppermute | solution.py:786
  45.4 3.3 %collective-permute-start.12 = (bf16[1440,256]{1,0:T(8,128)(2,1)S(1)}, bf16[1440,256]{1,0:T(8,128)(2,1)S(1)}, u32[]{:S(2)}, u32[]{:S(2)}) collective-permute-start(bf16[1440,256]{1,0:T(8,128)(2,1)S(1)} %get-tuple-element.65), channel_id=1, source_target_pairs={{0,16},{16,0},{1,17},{17,1},{2,18},{18,2},{3,19},{19,3},{4,20},{20... | collective-permute-start | bytes 2211848 | tf_op jit(solution)/shard_map/ppermute | solution.py:786
  45.5 4.5 %collective-permute-start.11 = (bf16[784,512]{1,0:T(8,128)(2,1)S(1)}, bf16[784,512]{1,0:T(8,128)(2,1)S(1)}, u32[]{:S(2)}, u32[]{:S(2)}) collective-permute-start(bf16[784,512]{1,0:T(8,128)(2,1)S(1)} %get-tuple-element.58.own_ref), channel_id=1, source_target_pairs={{0,16},{16,0},{1,17},{17,1},{2,18},{18,2},{3,19},{19,3},{4,20},{20... | collective-permute-start | bytes 2408456 | tf_op jit(solution)/shard_map/ppermute | solution.py:786
  47.8 9.3 %collective-permute-start.15 = (bf16[1040,256]{1,0:T(8,128)(2,1)S(1)}, bf16[1040,256]{1,0:T(8,128)(2,1)S(1)}, u32[]{:S(2)}, u32[]{:S(2)}) collective-permute-start(bf16[1040,256]{1,0:T(8,128)(2,1)S(1)} %add_convert_fusion.one_ref), channel_id=1, source_target_pairs={{0,1},{1,0},{2,3},{3,2},{4,5},{5,4},{6,7},{7,6},{8,9},{9,8},{10,11... | collective-permute-start | bytes 1597448 | tf_op jit(solution)/shard_map/ppermute | solution.py:797
  48.7 20.4 %collective-permute-start.13 = (bf16[288,256]{1,0:T(8,128)(2,1)S(1)}, bf16[288,256]{1,0:T(8,128)(2,1)S(1)}, u32[]{:S(2)}, u32[]{:S(2)}) collective-permute-start(bf16[288,256]{1,0:T(8,128)(2,1)S(1)} %add_convert_fusion.2), channel_id=1, source_target_pairs={{0,1},{1,0},{2,3},{3,2},{4,5},{5,4},{6,7},{7,6},{8,9},{9,8},{10,11... | collective-permute-start | bytes 442376 | tf_op jit(solution)/shard_map/ppermute | solution.py:797
  57.1 6.6 %collective-permute-start.16 = (bf16[176,256]{1,0:T(8,128)(2,1)S(1)}, bf16[176,256]{1,0:T(8,128)(2,1)S(1)}, u32[]{:S(2)}, u32[]{:S(2)}) collective-permute-start(bf16[176,256]{1,0:T(8,128)(2,1)S(1)} %shard_map.268), channel_id=1, source_target_pairs={{0,8},{1,9},{2,10},{3,11},{4,12},{5,13},{6,14},{7,15},{8,0},{9,1},... | collective-permute-start | bytes 270344 | tf_op jit(solution)/shard_map/ppermute | solution.py:791
  58.4 6.0 %collective-permute-start.18 = (bf16[432,256]{1,0:T(8,128)(2,1)S(1)}, bf16[432,256]{1,0:T(8,128)(2,1)S(1)}, u32[]{:S(2)}, u32[]{:S(2)}) collective-permute-start(bf16[432,256]{1,0:T(8,128)(2,1)S(1)} %add_convert_fusion.1), channel_id=1, source_target_pairs={{0,2},{1,3},{2,0},{3,1},{4,6},{5,7},{6,4},{7,5},{8,10},{9,11},{10,... | collective-permute-start | bytes 663560 | tf_op jit(solution)/shard_map/ppermute | solution.py:797
  63.8 5.3 %collective-permute-start.17 = (bf16[176,256]{1,0:T(8,128)(2,1)S(1)}, bf16[176,256]{1,0:T(8,128)(2,1)S(1)}, u32[]{:S(2)}, u32[]{:S(2)}) collective-permute-start(bf16[176,256]{1,0:T(8,128)(2,1)S(1)} %add_convert_fusion.3.refs_0_), channel_id=1, source_target_pairs={{0,4},{1,5},{2,6},{3,7},{4,0},{5,1},{6,2},{7,3},{8,12},{9,13},{10,... | collective-permute-start | bytes 270344 | tf_op jit(solution)/shard_map/ppermute | solution.py:791
  64.5 6.3 %collective-permute-start.20 = (bf16[144,256]{1,0:T(8,128)(2,1)S(1)}, bf16[144,256]{1,0:T(8,128)(2,1)S(1)}, u32[]{:S(2)}, u32[]{:S(2)}) collective-permute-start(bf16[144,256]{1,0:T(8,128)(2,1)S(1)} %get-tuple-element.71), channel_id=1, source_target_pairs={{0,8},{1,9},{2,10},{3,11},{4,12},{5,13},{6,14},{7,15},{8,0},{9,1},... | collective-permute-start | bytes 221192 | tf_op jit(solution)/shard_map/ppermute | solution.py:791
  66.6 6.2 %collective-permute-start.21 = (bf16[144,256]{1,0:T(8,128)(2,1)S(1)}, bf16[144,256]{1,0:T(8,128)(2,1)S(1)}, u32[]{:S(2)}, u32[]{:S(2)}) collective-permute-start(bf16[144,256]{1,0:T(8,128)(2,1)S(1)} %get-tuple-element.72), channel_id=1, source_target_pairs={{0,12},{1,13},{2,14},{3,15},{4,8},{5,9},{6,10},{7,11},{8,4},{9,5},... | collective-permute-start | bytes 221192 | tf_op jit(solution)/shard_map/ppermute | solution.py:791
  69.1 4.5 %collective-permute-start.19 = (bf16[144,256]{1,0:T(8,128)(2,1)S(1)}, bf16[144,256]{1,0:T(8,128)(2,1)S(1)}, u32[]{:S(2)}, u32[]{:S(2)}) collective-permute-start(bf16[144,256]{1,0:T(8,128)(2,1)S(1)} %get-tuple-element.69.refs_1_), channel_id=1, source_target_pairs={{0,4},{1,5},{2,6},{3,7},{4,0},{5,1},{6,2},{7,3},{8,12},{9,13},{10,... | collective-permute-start | bytes 221192 | tf_op jit(solution)/shard_map/ppermute | solution.py:791
  69.2 5.4 %collective-permute-start.22 = (bf16[320,256]{1,0:T(8,128)(2,1)S(1)}, bf16[320,256]{1,0:T(8,128)(2,1)S(1)}, u32[]{:S(2)}, u32[]{:S(2)}) collective-permute-start(bf16[320,256]{1,0:T(8,128)(2,1)S(1)} %get-tuple-element.73.refs_1_), channel_id=1, source_target_pairs={{0,2},{1,3},{2,0},{3,1},{4,6},{5,7},{6,4},{7,5},{8,10},{9,11},{10,... | collective-permute-start | bytes 491528 | tf_op jit(solution)/shard_map/ppermute | solution.py:797
  (3 other events, 9.1 us)
